TPU v7x, 256 devices: a whole 4x4x8 slice. The times are simulated.
256 devices in a mesh: tm: 32 (over y, z), chan: 8 (over x, core).
Axes of the slice: x: 4, y: 4, z: 8, core: 2. Of those that a mesh axis runs over, the one named last changes fastest.
Arguments:
- samples: bfloat16 [65536, 1024], P('tm', 'chan'), may hold values from -30 to 30
- candidates: int32 [32, 8], P('tm'), may hold values from 1 to 2047
- segment_start: int32 [32], P('tm'), may hold values from 0 to 1, as said below
Outputs:
- window_cov: float32 [32, 1024, 1024], P('tm', 'chan')
- segment_cov: float32 [32, 1024, 1024], P('tm', 'chan')
- cusum: float32 [32, 8, 1024, 1024], P('tm', None, 'chan')
Inputs may be any that keep to these rules, and one draw needn't show every extreme that they name: `segment_start`: block 0 always begins a segment; only blocks of even index begin segments, so every segment holds two or more blocks; block 16 never begins one.
All inputs are finite; a program needn't handle non-finite values.
Results may differ from a plain program's by a relative error of at most 0.0003.
The roundings to bfloat16 on the way count: a program that leaves them out, or rounds other values in their place, can miss the bound.
Values may be sent and summed in bfloat16 or wider, within the bound.
No kernel may reach another device: no remote copies, remote signals or barrier semaphores. Data moves between devices by JAX's collectives and lax.ppermute only.
A program may use at most 128 MiB of HBM per device.

v0:
```python
from functools import partial

import jax
import jax.numpy as jnp
from jax import lax
from jax.sharding import PartitionSpec as P


def from_behind(value, axis, steps):
    count = lax.axis_size(axis)
    leading, last = (max(0, -steps), min(count, count - steps))
    return lax.ppermute(value, axis, [(source, source + steps) for source in range(leading, last)])


def prefix_2(shard, axis, combine, identity, reverse):
    size, mine = (lax.axis_size(axis), lax.axis_index(axis))
    everything = lax.all_gather(shard, axis)
    start = jnp.broadcast_to(jnp.asarray(identity, shard.dtype), shard.shape)

    def lap(k, before):
        at = size - 1 - k if reverse else k
        reached = at > mine if reverse else at < mine
        new = combine(before, everything[at])
        return jnp.where(reached, new, before)

    return lax.fori_loop(0, size, lap, start)


def choose(keeper, first, second):
    return tuple(
        (
            jnp.where(keeper, first_item, second_item)
            for first_item, second_item in zip(first, second)
        )
    )


def own_columns(values, offset, local_width):
    return lax.dynamic_slice_in_dim(values, offset, local_width, values.ndim - 1)


def merge_states(first, second, offset):
    count_first, mean_first, spread_first = first
    count_second, mean_second, spread_second = second
    total_count = count_first + count_second
    safe_count = jnp.maximum(total_count, 1.0)
    difference = mean_second - mean_first
    merged_mean = mean_first + difference * (count_second / safe_count)
    local_part = own_columns(difference, offset, spread_first.shape[0])
    merged_spread = (
        spread_first
        + spread_second
        + count_first * count_second / safe_count * (local_part[:, None] * difference[None, :])
    )
    return (total_count, merged_mean, merged_spread)


def pack_state(state, flag):
    count_value, mean_value, spread_value = state
    width = mean_value.shape[0]
    column_ids = lax.broadcasted_iota(jnp.int32, (1, width), 1)
    header = jnp.where(column_ids == 0, count_value, jnp.where(column_ids == 1, flag, 0.0)).astype(
        jnp.float32
    )
    return jnp.concatenate([header, mean_value[None], spread_value], axis=0)


def unpack_state(packed):
    return ((packed[0, 0], packed[1], packed[2:]), packed[0, 1])


def forward_packed(earlier, latter, offset):
    earlier_state, earlier_flag = unpack_state(earlier)
    latter_state, latter_flag = unpack_state(latter)
    merged = merge_states(earlier_state, latter_state, offset)
    kept = choose(latter_flag > 0.5, latter_state, merged)
    return pack_state(kept, jnp.maximum(earlier_flag, latter_flag))


def backward_packed(earlier, latter, offset):
    earlier_state, earlier_flag = unpack_state(earlier)
    latter_state, latter_flag = unpack_state(latter)
    merged = merge_states(latter_state, earlier_state, offset)
    kept = choose(latter_flag > 0.5, latter_state, merged)
    return pack_state(kept, jnp.maximum(earlier_flag, latter_flag))


def local_state(count_value, mean_value, column_sum, gram_part, offset):
    local_part = own_columns(column_sum, offset, gram_part.shape[0])
    return (
        count_value,
        mean_value + column_sum / count_value,
        gram_part - local_part[:, None] * column_sum[None, :] / count_value,
    )


def local(samples, candidates, segment_start):
    row_count, local_width = samples.shape
    halo_rows = row_count // 2
    split_total = candidates.shape[1]
    full_width = local_width * lax.axis_size("chan")
    tm_index = lax.axis_index("tm")
    offset = lax.axis_index("chan") * local_width
    halo_live = (tm_index > 0).astype(jnp.float32)
    block_mean = jnp.sum(samples, axis=0, dtype=jnp.float32) / row_count
    mean_full = lax.all_gather(block_mean, "chan", axis=0, tiled=True)
    centered = (samples.astype(jnp.float32) - block_mean).astype(jnp.bfloat16)
    positions = lax.broadcasted_iota(jnp.int32, (split_total, row_count), 1)
    row_masks = jnp.concatenate(
        [
            jnp.ones((1, row_count), jnp.bfloat16),
            (positions < candidates[0][:, None]).astype(jnp.bfloat16),
        ],
        axis=0,
    )
    stacked = row_masks[:, :, None] * centered[None, :, :]
    prior_rows = from_behind(samples[row_count - halo_rows :], "tm", 1)
    centered_prior = ((prior_rows.astype(jnp.float32) - block_mean) * halo_live).astype(
        jnp.bfloat16
    )
    window = jnp.concatenate([centered_prior, centered], axis=0)
    column_piece = lax.all_gather(window, "chan", axis=1, tiled=True)
    halo_piece = column_piece[:halo_rows]
    own_column_piece = column_piece[halo_rows:]
    gram_part = jnp.einsum(
        "gsa,sb->gab", stacked, own_column_piece, preferred_element_type=jnp.float32
    )
    sum_part = jnp.dot(row_masks, own_column_piece, preferred_element_type=jnp.float32)
    halo_gram = jnp.einsum(
        "sa,sb->ab", centered_prior, halo_piece, preferred_element_type=jnp.float32
    )
    halo_sum = jnp.sum(halo_piece, axis=0, dtype=jnp.float32)
    grams = jnp.concatenate([halo_gram[None], gram_part], axis=0)
    sums = jnp.concatenate([halo_sum[None], sum_part], axis=0)
    block = jnp.concatenate([grams, sums[:, None, :]], axis=1)
    gram_stack = block[:, :local_width]
    sum_stack = block[:, local_width]
    window_count = row_count + halo_live * halo_rows
    window_sum = sum_stack[0] + sum_stack[1]
    window_local = own_columns(window_sum, offset, local_width)
    window_cov = (
        gram_stack[0] + gram_stack[1] - window_local[:, None] * window_sum[None, :] / window_count
    ) / (window_count - 1.0)
    block_state = local_state(
        jnp.float32(row_count), mean_full, sum_stack[1], gram_stack[1], offset
    )
    start_flag = segment_start.astype(jnp.float32)[0]
    is_start = start_flag > 0.5
    empty_state = (
        jnp.float32(0.0),
        jnp.zeros((full_width,), jnp.float32),
        jnp.zeros((local_width, full_width), jnp.float32),
    )
    identity = pack_state(empty_state, jnp.float32(0.0))
    forward_leaf = pack_state(block_state, start_flag)
    backward_leaf = pack_state(choose(is_start, empty_state, block_state), start_flag)
    forward_rule = partial(forward_packed, offset=offset)
    backward_rule = partial(backward_packed, offset=offset)
    before = prefix_2(forward_leaf, "tm", forward_rule, identity, False)
    after_all = prefix_2(backward_leaf, "tm", backward_rule, identity, True)
    before_state, unused_before = unpack_state(before)
    suffix, unused_after = unpack_state(after_all)
    prefix = choose(is_start, empty_state, before_state)
    total_state = merge_states(merge_states(prefix, block_state, offset), suffix, offset)
    segment_cov = total_state[2] / total_state[0]
    left_counts = candidates[0].astype(jnp.float32)
    state_map = jax.vmap(local_state, in_axes=(0, None, 0, 0, None))
    left_local = state_map(left_counts, mean_full, sum_stack[2:], gram_stack[2:], offset)
    right_local = state_map(
        row_count - left_counts,
        mean_full,
        sum_stack[1] - sum_stack[2:],
        gram_stack[1] - gram_stack[2:],
        offset,
    )
    left_state = jax.vmap(merge_states, in_axes=(None, 0, None))(prefix, left_local, offset)
    right_state = jax.vmap(merge_states, in_axes=(0, None, None))(right_local, suffix, offset)
    count_left = left_state[0]
    count_right = right_state[0]
    count_all = count_left + count_right
    weight = count_left * count_right / (count_all * count_all)
    cusum_tiles = weight[:, None, None] * (
        left_state[2] / count_left[:, None, None] - right_state[2] / count_right[:, None, None]
    )
    return (window_cov[None], segment_cov[None], cusum_tiles[None])


def solution(mesh):
    placed = (P("tm", "chan"), P("tm", None), P("tm"))
    return jax.shard_map(
        local,
        mesh=mesh,
        in_specs=placed,
        out_specs=(P("tm", "chan", None), P("tm", "chan", None), P("tm", None, "chan", None)),
        check_vma=False,
    )
```

profile of v0, /device:TPU:1, one launch (start us, length us, event | category | flops | bytes accessed | tf_op | source)
XLA Modules:
  0.0 869.1 jit_solution(7827398905628320016)
XLA Ops:
  8.2 4.4 collective-permute-start
  12.6 1.3 convert_reduce_fusion.1
  15.1 2.4 collective-permute-done
  19.5 11.8 %all-gather.2 = f32[8,1,128]{2,1,0:T(1,128)S(1)} all-gather(f32[1,1,128]{2,1,0:T(1,128)S(1)} %get-tuple-element.376), channel_id=1, replica_groups=mesh['tm'=32,'chan'=8] {'chan'}, dimensions={0}, use_global_device_ids=true | all-gather | bytes 4608 | tf_op jit(solution)/shard_map/all_gather | solution.py:106
  31.5 40.8 %all-gather.9.cloned.1.call-done = bf16[3072,1024]{1,0:T(8,128)(2,1)} async-done(((bf16[3072,128]{1,0:T(8,128)(2,1)}), bf16[3072,1024]{1,0:T(8,128)(2,1)}) %all-gather.9.cloned.1.call-update) | async-done | bytes 6291472 | tf_op jit(solution)/shard_map/all_gather | solution.py:122
  72.2 3.0 fusion.3
  75.2 2.0 convert_reduce_fusion
  77.3 5.1 fusion
  82.4 2.2 copy-done.1
  87.9 3.0 fusion.19
  90.9 140.9 %all-gather.13.cloned.1.call-done = f32[32,130,1024]{2,1,0:T(8,128)} async-done(((f32[1,130,1024]{2,1,0:T(8,128)}), f32[32,130,1024]{2,1,0:T(8,128)}) %all-gather.13.cloned.1.call-update) | async-done | bytes 17039376 | tf_op jit(solution)/shard_map/all_gather | solution.py:17
  231.8 312.1 %while.35 = (s32[]{:T(128)}, f32[130,1024]{1,0:T(8,128)S(1)}, s32[]{:T(128)}, f32[32,130,1024]{2,1,0:T(8,128)}, s32[]{:T(128)}, /*index=5*/s32[]{:T(128)}, s32[]...) while((s32[]{:T(128)}, f32[130,1024]{1,0:T(8,128)S(1)}, s32[]{:T(128)}, ...), condition=%wide.region_5.6_spmd, body=%wide.region_4.5_spmd.sunk | while | flops 1064977 | bytes 4290429 | solution.py:26
  257.7 1.3 add_select_fusion.5
  267.5 1.2 add_select_fusion.5
  277.3 1.2 add_select_fusion.5
  287.0 1.4 add_select_fusion.5
  296.9 1.3 add_select_fusion.5
  316.5 1.3 add_select_fusion.5
  326.2 1.3 add_select_fusion.5
  345.7 1.3 add_select_fusion.5
  355.5 1.3 add_select_fusion.5
  365.3 1.3 add_select_fusion.5
  544.5 306.9 %while.34 = (s32[]{:T(128)}, f32[130,1024]{1,0:T(8,128)S(1)}, s32[]{:T(128)}, f32[32,130,1024]{2,1,0:T(8,128)}, s32[]{:T(128)}, /*index=5*/s32[]{:T(128)}, s32[]...) while((s32[]{:T(128)}, f32[130,1024]{1,0:T(8,128)S(1)}, s32[]{:T(128)}, f32[32,130,1024]{2,1,0:T(8,128)}, ...), condition=%wide.region_3.4_spmd, body=%wide.region_2.3_spmd.sunk | while | flops 1064973 | bytes 4290367 | solution.py:26
  856.1 6.4 multiply_bitcast_fusion
  (613 shorter events, 254.4 us)
Async XLA Ops:
  7.2 24.2 %copy-start.2 = (s32[1,8]{1,0:T(1,128)S(1)}, s32[1,8]{1,0:T(1,128)}, u32[]{:S(2)}) copy-start(s32[1,8]{1,0:T(1,128)} %param.8) | copy-start | bytes 100
  7.2 65.1 %all-gather.9.cloned.1.call-start = ((), (), s32[]{:S(2)}) async-start(), calls=%async_computation | async-start | bytes 7077888 | tf_op jit(solution)/shard_map/all_gather | solution.py:122
  8.2 9.3 %collective-permute-start = (bf16[1024,128]{1,0:T(8,128)(2,1)S(1)}, bf16[1024,128]{1,0:T(8,128)(2,1)S(1)}, u32[]{:S(2)}, u32[]{:S(2)}) collective-permute-start(bf16[1024,128]{1,0:T(8,128)(2,1)S(1)} %slice.205), channel_id=1, source_target_pairs={{0,8},{8,16},{16,24},{24,32},{32,40},{40,48},{48,56},{56,64},{64,7... | collective-permute-start | bytes 786440 | tf_op jit(solution)/shard_map/ppermute | solution.py:12
  18.6 213.2 %all-gather.13.cloned.1.call-start = ((), (), s32[]{:S(2)}) async-start(), calls=%async_computation.2 | async-start | bytes 18382848 | tf_op jit(solution)/shard_map/all_gather | solution.py:17
  72.2 5.1 copy-start
  82.4 2.2 copy-start.1
  85.6 458.9 %all-gather.11.cloned.1.call-start = ((), (), s32[]{:S(2)}) async-start(), calls=%async_computation.1 | async-start | bytes 18382848 | tf_op jit(solution)/shard_map/all_gather | solution.py:17
Sparse Core Ops, SparseCore 0:
  18.7 53.5 all-gather.8
  85.7 146.0 all-gather.12
  235.0 142.9 all-gather.10
where the time goes:
time: 885 us; the launch traced here: 869 us
  loops' own time  362 us (41%)
  waiting for transfers between devices  184 us (21%)
  other arithmetic  157 us (18%)
  local copies, waits for them, and re-layouts  122 us (14%)
  between operations  16.7 us (2%)
  blocking collectives  11.8 us (1%)
  matrix products  11 us (1%)
    another operation x2, loops' own time, prefix_2(): return lax.fori_loop(0, size, lap, start)  362 us
    all_gather x2, waiting for transfers between devices, prefix_2(): everything = lax.all_gather(shard, axis)  141 us
    select_n x131, other arithmetic, choose(): jnp.where(keeper, first_item, second_item)  130 us
    squeeze x64, local copies, waits for them, and re-layouts, lap(): new = combine(before, everything[at])  70.1 us
    slice x67, local copies, waits for them, and re-layouts, unpack_state(): return ((packed[0, 0], packed[1], packed[2:]), packed[0, 1])  41.7 us
    all_gather x1, waiting for transfers between devices, local(): column_piece = lax.all_gather(window, 'chan', axis=1, tiled=True)  40.8 us
  transfers between devices with their start and end apart: 4, of which 3 were waited for; matrix products, arithmetic and copies ran while one was open for 16% of the time, Pallas kernels for 0%

commit v1 on v0

v1 whole, which is shorter than its diff:
```python
import jax
import jax.numpy as jnp
from jax import lax
from jax.experimental import pallas as pl
from jax.experimental.pallas import tpu as pltpu
from jax.sharding import PartitionSpec as P

F32, BF16 = jnp.float32, jnp.bfloat16
ROWS, HALO, WIDTH, BLOCKS, SPLITS, CHIPS = 2048, 1024, 128, 32, 8, 4
PAIR = 2 * WIDTH
HIGH = lax.Precision.HIGHEST
TRANSPOSED = (((0,), (0,)), ((), ()))
SM = pl.BlockSpec(memory_space=pltpu.SMEM)
HBM = pl.BlockSpec(memory_space=pltpu.HBM)
MIB = 2**20


def whole(*shape):
    return pl.BlockSpec(shape, lambda *_: (0,) * len(shape))


def array(*shape, dtype=F32):
    return jax.ShapeDtypeStruct(shape, dtype)


def params(grant):
    return pltpu.CompilerParams(
        vmem_limit_bytes=grant * MIB, dimension_semantics=("arbitrary",)
    )


def cost(microseconds):
    return pl.CostEstimate(
        flops=int(microseconds * 1e9), bytes_accessed=MIB, transcendentals=0
    )


def center_shard(raw_ref, out_ref, at):
    step = 256

    def add(i, total):
        piece = raw_ref[pl.ds(i * step, step), :].astype(F32)
        return total + jnp.sum(piece.reshape(step // 8, 8, WIDTH), axis=0)

    total = lax.fori_loop(0, ROWS // step, add, jnp.zeros((8, WIDTH), F32), unroll=2)
    mean = jnp.sum(total, axis=0, keepdims=True) / ROWS

    def shift(i, _):
        piece = raw_ref[pl.ds(i * step, step), :].astype(F32) - mean
        out_ref[pl.ds(i * step, step), pl.ds(at, WIDTH)] = piece.astype(BF16)
        return 0

    lax.fori_loop(0, ROWS // step, shift, 0, unroll=2)
    return mean


def center_pair(first_ref, second_ref, at, off, cent_ref, stat_ref):
    stat_ref[0] = jnp.zeros((8, PAIR), F32)
    stat_ref[0, 0:1, pl.ds(at, WIDTH)] = center_shard(first_ref, cent_ref, at)
    stat_ref[0, 0:1, pl.ds(off, WIDTH)] = center_shard(second_ref, cent_ref, off)
    total = jnp.dot(jnp.ones((16, ROWS), BF16), cent_ref[...], preferred_element_type=F32)[0:1]
    stat_ref[0, 1:2, :] = total
    stat_ref[0, 2:3, :] = stat_ref[0, 0:1, :] + total / ROWS


def turned_dot(left, right):
    return lax.dot_general(left, right, TRANSPOSED, preferred_element_type=F32)


def wide(value):
    return jnp.concatenate([value, value], axis=1)


def left_part(where_ref, flipped, cent_ref, left_ref, sums_ref):
    index = lax.broadcasted_iota(jnp.int32, (16, ROWS), 0)
    place = lax.broadcasted_iota(jnp.int32, (16, ROWS), 1)
    limit = jnp.zeros((16, ROWS), jnp.int32)
    for j in range(SPLITS):
        limit = jnp.where(index == j, where_ref[12 + j], limit)
    masks = jnp.where(place < limit, 1.0, 0.0).astype(BF16)
    cent = cent_ref[...]
    sums_ref[0] = jnp.dot(masks, cent, preferred_element_type=F32)[0:8]
    for i in range(SPLITS // 4):
        kept = jnp.concatenate([flipped * masks[j : j + 1, :] for j in range(4 * i, 4 * i + 4)], axis=0)
        part = jnp.dot(kept, cent, preferred_element_type=F32)
        for j in range(4):
            left_ref[0, 4 * i + j] = part[j * WIDTH : (j + 1) * WIDTH]


def first_kernel(
    where_ref, mine_ref, other_ref,
    left_ref, sums_ref, gram_ref, stat_ref, flip_hbm, total_hbm, flip_ref, spread_ref, total_ref, rider_ref, cent_ref,
):
    core = where_ref[2]
    at = pl.multiple_of(core * WIDTH, WIDTH)
    off = pl.multiple_of((1 - core) * WIDTH, WIDTH)
    center_pair(mine_ref, other_ref, at, off, cent_ref, stat_ref)
    rider_ref[...] = jnp.zeros((8, WIDTH), F32)
    rider_ref[0:1, :] = stat_ref[0, 2:3, 0:WIDTH]
    rider_ref[1:2, :] = stat_ref[0, 2:3, WIDTH:PAIR]
    rider_ref[2:3, :] = jnp.full((1, WIDTH), where_ref[20], jnp.int32).astype(F32)
    flip_ref[...] = cent_ref[:, pl.ds(at, WIDTH)].T
    flipped = flip_ref[...]
    flip_hbm[...] = flipped
    gram = jnp.dot(flipped, cent_ref[...], preferred_element_type=F32)
    gram_ref[0] = gram
    total = jnp.dot(flipped, jnp.ones((ROWS, WIDTH), BF16), preferred_element_type=F32)
    total_ref[...] = total
    total_hbm[...] = total
    spread_ref[...] = gram - wide(total) * (stat_ref[0, 1:2, :] / ROWS)
    left_part(where_ref, flipped, cent_ref, left_ref, sums_ref)


def near_kernel(
    where_ref, first_ref, second_ref, flip_ref, total_ref,
    left_ref, sums_ref, gram_ref, stat_ref, spread_ref, cent_ref,
):
    center_pair(first_ref, second_ref, 0, WIDTH, cent_ref, stat_ref)
    flipped = flip_ref[...]
    gram = jnp.dot(flipped, cent_ref[...], preferred_element_type=F32)
    gram_ref[0] = gram
    spread_ref[...] = gram - wide(total_ref[...]) * (stat_ref[0, 1:2, :] / ROWS)
    left_part(where_ref, flipped, cent_ref, left_ref, sums_ref)


def side_kernel(
    where_ref, first_ref, second_ref, flip_ref, left_ref, sums_ref, gram_ref, stat_ref, cent_ref
):
    center_pair(first_ref, second_ref, 0, WIDTH, cent_ref, stat_ref)
    flipped = flip_ref[...]
    gram_ref[0] = jnp.dot(flipped, cent_ref[...], preferred_element_type=F32)
    left_part(where_ref, flipped, cent_ref, left_ref, sums_ref)


def far_kernel(
    where_ref, first_ref, second_ref, flip_ref, total_ref, spread0_ref, spread1_ref, rider_ref,
    gram_ref, stat_ref, out_ref, cent_ref, held_ref,
):
    rider = rider_ref[0:4, :]
    for q in range(BLOCKS):
        spread, lane = ((spread0_ref, spread1_ref)[q // 16], WIDTH * (q // 8 % 2))
        row = 16 * (q % 8)
        out_ref[q, 0:16, :] = spread[row : row + 16, lane : lane + WIDTH]
        out_ref[q, 20:24, :] = rider
    center_pair(first_ref, second_ref, 0, WIDTH, cent_ref, stat_ref)
    gram = jnp.dot(flip_ref[...], cent_ref[...], preferred_element_type=F32)
    gram_ref[0] = gram
    spread = gram - wide(total_ref[...]) * (stat_ref[0, 1:2, :] / ROWS)
    held_ref[...] = jnp.where(where_ref[3] == 0, spread[:, 0:WIDTH], spread[:, WIDTH:PAIR])
    for q in range(BLOCKS):
        out_ref[q, 16:20, :] = held_ref[4 * q : 4 * q + 4, :]


def rest_kernel(where_ref, cent_ref, flip_ref, left_ref, sums_ref):
    left_part(where_ref, flip_ref[...], cent_ref, left_ref, sums_ref)


ALL = [
    array(CHIPS, SPLITS, WIDTH, PAIR),
    array(CHIPS, 8, PAIR),
    array(CHIPS, WIDTH, PAIR),
    array(CHIPS, 8, PAIR),
]


def call(
    kernel, name, inputs, outputs, *, fetched=(), stored=(), kept=(), pair=0, scratch=(), us=3, grant=24
):
    count, held, made = len(inputs), len(kept), len(outputs)
    sliced = [i < len(ALL) and outputs[i] in ALL for i in range(made)]
    sizes = [(1, *out.shape[1:]) if cut else out.shape for out, cut in zip(outputs, sliced)]
    buffers = [pltpu.VMEM(inputs[i].shape, inputs[i].dtype) for i in fetched]
    buffers += [pltpu.VMEM(sizes[i], outputs[i].dtype) for i in stored]

    def body(*refs):
        ins, refs = list(refs[:count]), refs[count + held :]
        outs, refs = list(refs[:made]), refs[made:]
        own, buffer, sem = refs[: len(scratch)], refs[len(scratch) : -1], refs[-1]
        copies = []
        for c, i in enumerate(fetched):
            copies.append(pltpu.make_async_copy(ins[i], buffer[c], sem.at[c]))
            ins[i] = buffer[c]
        for copy in copies:
            copy.start()
        for copy in copies:
            copy.wait()
        copies = []
        for c, i in enumerate(stored, len(fetched)):
            target = outs[i].at[pl.ds(pair, 1)] if sliced[i] else outs[i]
            copies.append(pltpu.make_async_copy(buffer[c], target, sem.at[c]))
            outs[i] = buffer[c]
        kernel(*ins, *outs, *own)
        for copy in copies:
            copy.start()
        for copy in copies:
            copy.wait()

    ins = [SM if value.dtype == jnp.int32 else whole(*value.shape) for value in inputs]
    for i in fetched:
        ins[i] = HBM
    outs = [HBM if i in stored else whole(*out.shape) for i, out in enumerate(outputs)]
    return pl.pallas_call(
        body,
        out_shape=outputs,
        grid=(1,),
        in_specs=ins + [HBM] * held,
        out_specs=outs,
        input_output_aliases={count + i: i for i in range(held)},
        scratch_shapes=[pltpu.VMEM(shape, dtype) for shape, dtype in scratch]
        + buffers
        + [pltpu.SemaphoreType.DMA((max(len(buffers), 1),))],
        compiler_params=params(grant),
        cost_estimate=cost(us),
        name=name,
    )(*inputs, *kept)


def scan_kernel(arrived_ref, both_ref, means_ref, flags_ref):
    for b in range(BLOCKS):
        rider = arrived_ref[b, 16:24, :]
        means_ref[0, b : b + 1, :] = rider[4:5, :]
        means_ref[1, b : b + 1, :] = rider[5:6, :]
        flags_ref[b : b + 1, :] = rider[6:7, :]
    scan(arrived_ref, flags_ref, both_ref, 0, 16, 0)
    scan(arrived_ref, flags_ref, both_ref, 16, 4, 32)


def scan(arrived_ref, flags_ref, both_ref, row, size, at):
    zero = jnp.zeros((size, WIDTH), F32)
    running = zero
    for b in range(BLOCKS):
        begins = flags_ref[b : b + 1, :] > 0.5
        running = jnp.where(begins, zero, running)
        both_ref[b, at : at + size, :] = running
        running = running + arrived_ref[b, row : row + size, :]
    running = zero
    for b in reversed(range(BLOCKS)):
        begins = flags_ref[b : b + 1, :] > 0.5
        both_ref[b, at + size : at + 2 * size, :] = running
        running = jnp.where(begins, zero, running + arrived_ref[b, row : row + size, :])


def prep_kernel(
    where_ref, sums_ref, gram_ref, stat_ref, own_means_ref, ahead_ref, behind_ref, far_ref, flags_ref,
    turned_ref, cols_ref, coef_ref, before_ref, after_ref, vectors,
):
    here = where_ref[0]
    core = where_ref[2]
    away = 1 - core
    flags = flags_ref[...]
    spot = lax.broadcasted_iota(jnp.int32, (BLOCKS, WIDTH), 0)
    low = lax.broadcasted_iota(jnp.int32, (BLOCKS, BLOCKS), 1)
    high = lax.broadcasted_iota(jnp.int32, (BLOCKS, BLOCKS), 0)
    upto = jnp.dot((low <= high).astype(F32), flags, preferred_element_type=F32)
    mine = jnp.sum(jnp.where(spot <= here, flags, 0.0), axis=0, keepdims=True)
    same = jnp.abs(upto - mine) < 0.5
    masks = [
        jnp.where(same & (spot < here), 1.0, 0.0),
        jnp.where(same & (spot > here), 1.0, 0.0),
    ]
    totals = [jnp.sum(mask, axis=0, keepdims=True) for mask in masks]
    count_p, count_s = totals[0] * ROWS, totals[1] * ROWS

    def pooled(means, side):
        mask = masks[side]
        mean = jnp.sum(means * mask, axis=0, keepdims=True) / jnp.maximum(totals[side], 1.0)
        return mean, (means - mean) * mask

    def pick(value):
        return jnp.where(core == 0, value[:, 0:WIDTH], value[:, WIDTH:PAIR])

    row_means = own_means_ref[core]
    row_p, row_part_p = pooled(row_means, 0)
    row_s, row_part_s = pooled(row_means, 1)
    row_stat = pick(stat_ref[0])
    row_sums = pick(sums_ref[0])

    index = lax.broadcasted_iota(jnp.int32, (SPLITS, WIDTH), 0)
    k = jnp.zeros((SPLITS, WIDTH), jnp.int32)
    for j in range(SPLITS):
        k = jnp.where(index == j, where_ref[12 + j], k)
    k = k.astype(F32)
    rest = ROWS - k
    row_right = row_stat[1:2] - row_sums
    row_d = row_stat[0:1] + row_sums / k - row_p
    row_e = row_s - (row_stat[0:1] + row_right / rest)
    n_left, n_right = count_p + k, rest + count_s
    n = n_left + n_right
    weight = n_left * n_right / (n * n)
    a, b = weight / n_left, weight / n_right
    coef_ref[0:8, :] = a
    coef_ref[8:16, :] = b
    vectors[0:8, :] = -a * row_sums / k
    vectors[8:16, :] = a * (count_p * k / n_left) * row_d
    vectors[16:24, :] = b * row_right / rest
    vectors[24:32, :] = -b * (rest * count_s / n_right) * row_e
    total = count_p + ROWS
    n = total + count_s
    row_d = row_stat[2:3] - row_p
    row_e = row_s - (row_p + row_d * (ROWS / total))
    coef_ref[16:24, :] = jnp.broadcast_to(1.0 / n, (8, WIDTH))
    vectors[32:WIDTH, :] = jnp.zeros((WIDTH - 32, WIDTH), F32)
    vectors[32:33, :] = row_stat[1:2] / -ROWS / n
    vectors[33:34, :] = (count_p * ROWS / total) / n * row_d
    vectors[34:35, :] = (total * count_s / n) / n * row_e
    turned_ref[...] = vectors[...].T

    columns = (
        (own_means_ref[0], own_means_ref[1]),
        (ahead_ref[core], behind_ref[away]),
        (far_ref[core], far_ref[away]),
        (ahead_ref[away], behind_ref[core]),
    )
    for u in range(8):
        r, lanes = u // 2, slice(WIDTH * (u % 2), WIDTH * (u % 2) + WIDTH)
        means = columns[r][u % 2]
        col_p, col_part_p = pooled(means, 0)
        col_s, col_part_s = pooled(means, 1)
        stat = stat_ref[r, :, lanes]
        col_left = sums_ref[r, :, lanes]
        col_right = stat[1:2] - col_left
        cols_ref[u, 0:8, :] = col_left
        cols_ref[u, 8:16, :] = stat[0:1] + col_left / k - col_p
        cols_ref[u, 16:24, :] = col_right
        cols_ref[u, 24:32, :] = col_s - (stat[0:1] + col_right / rest)
        col_d = stat[2:3] - col_p
        cols_ref[u, 32:40, :] = jnp.zeros((8, WIDTH), F32)
        cols_ref[u, 32:33, :] = stat[1:2]
        cols_ref[u, 33:34, :] = col_d
        cols_ref[u, 34:35, :] = col_s - (col_p + col_d * (ROWS / total))

        def between(row_part, col_part):
            return ROWS * lax.dot_general(
                row_part, col_part, TRANSPOSED, precision=HIGH, preferred_element_type=F32
            )

        before_ref[u] = between(row_part_p, col_part_p)
        after_ref[u] = gram_ref[r, :, lanes] + between(row_part_s, col_part_s)


def prep_terms(where, sums, gram, stat, own, ahead, behind, far, flags):
    square = array(8, WIDTH, WIDTH)
    return call(
        prep_kernel,
        "prep_terms",
        [where, sums, gram, stat, own, ahead, behind, far, flags],
        [array(WIDTH, WIDTH), array(8, 40, WIDTH), array(24, WIDTH), square, square],
        fetched=(1, 2, 3, 4, 8),
        stored=(0, 1, 2, 3, 4),
        scratch=[((WIDTH, WIDTH), F32)],
        us=4,
        grant=16,
    )


def load_near(ref, p_ref, s_ref):
    for g in range(8):
        p_ref[16 * g : 16 * g + 16, :] = ref[g, 0:16, :]
        s_ref[16 * g : 16 * g + 16, :] = ref[g, 16:32, :]


def load_far(ref, p_ref, s_ref):
    for q in range(BLOCKS):
        p_ref[4 * q : 4 * q + 4, :] = ref[q, 0:4, :]
        s_ref[4 * q : 4 * q + 4, :] = ref[q, 4:8, :]


def output_kernel(
    where_ref, back_ref, opposite_ref, next_ref, before_ref, left_hbm, prefix_hbm, suffix_hbm, cols_hbm, turned_hbm, coef_hbm,
    cusum_hbm, seg_hbm,
    left_ref, prefix_ref, suffix_ref, cols_ref, turned_ref, coef_ref, cusum_ref, seg_ref, p_ref, s_ref, sem, out_sem,
):
    loads = [
        pltpu.make_async_copy(source, target, sem.at[c])
        for c, (source, target) in enumerate(
            (
                (prefix_hbm, prefix_ref),
                (suffix_hbm, suffix_ref),
                (cols_hbm, cols_ref),
                (turned_hbm, turned_ref),
                (coef_hbm, coef_ref),
                (left_hbm, left_ref),
            )
        )
    ]
    for load in loads:
        load.start()
    held = where_ref[3]
    for load in loads[:5]:
        load.wait()

    def add(u, turn):
        prefix, suffix = p_ref[...], s_ref[...]
        if turn:
            prefix, suffix = prefix.T, suffix.T
        prefix_ref[u] = prefix_ref[u] + prefix
        suffix_ref[u] = suffix_ref[u] + suffix

    for u in range(4):
        load_near(back_ref.at[pl.ds(8 * u, 8)], p_ref, s_ref)
        add(u, False)
    load_far(back_ref.at[:, pl.ds(32, 8)], p_ref, s_ref)
    add(4 + held, False)
    load_far(opposite_ref, p_ref, s_ref)
    add(5 - held, True)
    load_near(next_ref, p_ref, s_ref)
    add(6, True)
    load_near(before_ref, p_ref, s_ref)
    add(7, True)

    def spread_out(row, count):
        return [
            jnp.broadcast_to(turned_ref[:, i : i + 1], (WIDTH, WIDTH))
            for i in range(row, 35, 8 if count == 4 else 1)
        ][:count]

    def lanes(u):
        return pl.ds(pl.multiple_of(where_ref[4 + u] * WIDTH, WIDTH), WIDTH)

    turned = spread_out(32, 3)
    for u in range(8):
        value = (prefix_ref[u] + suffix_ref[u]) * coef_ref[16:17, :]
        for i in range(3):
            value = value + turned[i] * cols_ref[u, 32 + i : 33 + i, :]
        seg_ref[0, :, lanes(u)] = value
    store = pltpu.make_async_copy(seg_ref, seg_hbm, out_sem.at[SPLITS])
    store.start()
    stores = [store]
    loads[5].wait()
    for j in range(SPLITS):
        turned = spread_out(j, 4)
        a, b = coef_ref[j : j + 1, :], coef_ref[8 + j : 9 + j, :]
        for u in range(8):
            half = WIDTH * (u % 2)
            value = (a + b) * left_ref[u // 2, j, :, half : half + WIDTH]
            value = value + a * prefix_ref[u] - b * suffix_ref[u]
            for i in range(4):
                value = value + turned[i] * cols_ref[u, 8 * i + j : 8 * i + j + 1, :]
            cusum_ref[0, j, :, lanes(u)] = value
        store = pltpu.make_async_copy(
            cusum_ref.at[:, pl.ds(j, 1)], cusum_hbm.at[:, pl.ds(j, 1)], out_sem.at[j]
        )
        store.start()
        stores.append(store)
    for store in stores:
        store.wait()


OUTPUTS = [array(1, SPLITS, WIDTH, CHIPS * PAIR), array(1, WIDTH, CHIPS * PAIR)]


def outputs(where, back, opposite, following, before, left, prefix, suffix, cols, turned, coef):
    blocks = [back, opposite, following, before]
    terms = [prefix, suffix, cols, turned, coef]
    buffers = [left, *terms, *OUTPUTS, array(WIDTH, WIDTH), array(WIDTH, WIDTH)]
    return pl.pallas_call(
        output_kernel,
        out_shape=OUTPUTS,
        grid=(1,),
        in_specs=[SM] + [whole(*value.shape) for value in blocks] + [HBM] * 6,
        out_specs=[HBM, HBM],
        scratch_shapes=[pltpu.VMEM(value.shape, F32) for value in buffers]
        + [pltpu.SemaphoreType.DMA((6,)), pltpu.SemaphoreType.DMA((SPLITS + 1,))],
        compiler_params=params(24),
        cost_estimate=cost(5),
        name="outputs",
    )(where, *blocks, left, *terms)


def window_kernel(
    where_ref, mine_ref, other_ref, gram_ref, stat_ref, total_ref,
    out_ref, cent_ref, flip_ref, sum_ref,
):
    halves = (
        (mine_ref, 0), (other_ref, 0), (mine_ref, HALO), (other_ref, 3 * HALO),
        (mine_ref, 2 * HALO), (other_ref, 2 * HALO), (other_ref, HALO), (mine_ref, 3 * HALO),
    )
    live = jnp.where(where_ref[0] > 0, 1.0, 0.0).astype(F32)
    core = where_ref[2]
    at = pl.multiple_of(core * WIDTH, WIDTH)
    off = pl.multiple_of((1 - core) * WIDTH, WIDTH)
    count = ROWS + live * HALO
    scale = wide(1.0 / jnp.full((1, WIDTH), count, F32))
    unbias = wide(1.0 / jnp.full((1, WIDTH), count - 1.0, F32))
    step = 256
    for r in range(CHIPS):
        lanes = (at, off) if r == 0 else (0, WIDTH)
        for (raw, row), lane in zip(halves[2 * r : 2 * r + 2], lanes):
            mean = stat_ref[r, 0:1, pl.ds(lane, WIDTH)]

            def shift(i, _, raw=raw, row=row, lane=lane, mean=mean):
                piece = (raw[pl.ds(row + i * step, step), :].astype(F32) - mean) * live
                cent_ref[pl.ds(i * step, step), pl.ds(lane, WIDTH)] = piece.astype(BF16)
                return 0

            lax.fori_loop(0, HALO // step, shift, 0, unroll=2)
        if r == 0:
            flip_ref[...] = cent_ref[:, pl.ds(at, WIDTH)].T
            flipped = flip_ref[...]
            row_sum = jnp.dot(flipped, jnp.ones((HALO, WIDTH), BF16), preferred_element_type=F32)
            sum_ref[...] = row_sum + total_ref[...]
        cent = cent_ref[...]
        halo = jnp.dot(flip_ref[...], cent, preferred_element_type=F32)
        col_sum = jnp.dot(jnp.ones((16, HALO), BF16), cent, preferred_element_type=F32)[0:1]
        col_sum = col_sum + stat_ref[r, 1:2, :]
        value = (halo + gram_ref[r] - wide(sum_ref[...]) * (col_sum * scale)) * unbias
        for c in range(2):
            lane = pl.multiple_of(where_ref[4 + 2 * r + c] * WIDTH, WIDTH)
            out_ref[0, :, pl.ds(lane, WIDTH)] = value[:, c * WIDTH : (c + 1) * WIDTH]


def to_chan(value, target):
    count = lax.axis_size("chan")
    return lax.ppermute(value, "chan", [(s, target(s) % count) for s in range(count)])


def exchange(value):
    return lax.all_to_all(value, "tm", 0, 0, tiled=True)


def after(value, *others):
    return lax.optimization_barrier((value, *others))[0]


def local(samples, candidates, segment_start):
    here, index = lax.axis_index("tm"), lax.axis_index("chan")
    chip, core = index // 2, index % 2
    nearby = [2 * chip, 2 * chip + 1]
    for step, side in ((1, core), (3, 1 - core), (2, core), (2, 1 - core), (1, 1 - core), (3, core)):
        nearby.append(2 * ((chip + step) % CHIPS) + side)
    held = jnp.where(chip < CHIPS // 2, 0, 1)
    where = jnp.stack([here, chip, core, held] + nearby).astype(jnp.int32)
    where = jnp.concatenate([where, candidates[0], segment_start])

    behind = to_chan(samples, lambda s: s + 2)
    ahead = to_chan(samples, lambda s: s - 2)
    other = to_chan(samples, lambda s: s ^ 1)
    prior = lax.ppermute(samples[ROWS - HALO :], "tm", [(b, b + 1) for b in range(BLOCKS - 1)])
    flip_shape, square = array(WIDTH, ROWS, dtype=BF16), array(WIDTH, WIDTH)
    left, sums, gram, stat, late_flipped, late_total, flipped, spread0, total, rider = call(
        first_kernel,
        "first_pair",
        [where, samples, other],
        ALL + [flip_shape, square, flip_shape, array(WIDTH, PAIR), square, array(8, WIDTH)],
        fetched=(1,),
        stored=(0, 1, 2, 3, 4, 5),
        scratch=[((ROWS, PAIR), BF16)],
    )
    behind, ahead, prior, flipped = lax.optimization_barrier((behind, ahead, prior, flipped))
    half = ROWS // 2
    far_low = to_chan(behind[:half], lambda s: s + 2)
    far_high = to_chan(ahead[half:], lambda s: s - 2)
    behind_other = to_chan(behind, lambda s: s ^ 1)
    ahead_other = to_chan(ahead, lambda s: s ^ 1)
    left, sums, gram, stat, spread1 = call(
        near_kernel,
        "near_pair",
        [where, ahead, behind_other, flipped, total],
        ALL + [array(WIDTH, PAIR)],
        stored=(0, 1, 2, 3),
        kept=(left, sums, gram, stat),
        pair=1,
        scratch=[((ROWS, PAIR), BF16)],
    )
    left, sums, gram, stat = call(
        side_kernel,
        "side_pair",
        [where, ahead_other, behind, flipped],
        ALL,
        stored=(0, 1, 2, 3),
        kept=(left, sums, gram, stat),
        pair=3,
        scratch=[((ROWS, PAIR), BF16)],
    )
    far_low, far_high, stat = lax.optimization_barrier((far_low, far_high, stat))
    far = jnp.concatenate([far_low, far_high], axis=0)
    far_other = to_chan(far, lambda s: s ^ 1)
    gram, stat, pieces, cent = call(
        far_kernel,
        "far_pair",
        [where, far, far_other, flipped, total, spread0, spread1, rider],
        ALL[2:] + [array(BLOCKS, 24, WIDTH), array(ROWS, PAIR, dtype=BF16)],
        stored=(0, 1, 3),
        kept=(gram, stat),
        pair=2,
        scratch=[((WIDTH, WIDTH), F32)],
        us=2,
    )
    arrived = exchange(pieces)

    left, sums = call(
        rest_kernel,
        "rest_left",
        [where, cent, late_flipped],
        ALL[:2],
        fetched=(1, 2),
        stored=(0, 1),
        kept=(left, sums),
        pair=2,
    )
    prior = after(prior, left)
    prior_behind = to_chan(prior, lambda s: s + 2)
    prior_ahead = to_chan(prior, lambda s: s - 2)
    arrived, prior_behind, prior_ahead = lax.optimization_barrier(
        (arrived, prior_behind, prior_ahead)
    )
    scanned, own_means, flags = call(
        scan_kernel,
        "scan_pieces",
        [arrived],
        [array(BLOCKS, 40, WIDTH), array(2, BLOCKS, WIDTH), array(BLOCKS, WIDTH)],
        stored=(0, 1, 2),
        us=1,
    )
    back = exchange(scanned)
    ahead_means = to_chan(own_means, lambda s: s - 2)
    behind_means = to_chan(own_means, lambda s: s + 2)
    far_means = to_chan(own_means, lambda s: s + 4)
    turned, cols, coef, prefix, suffix = prep_terms(
        where, sums, gram, stat, own_means, ahead_means, behind_means, far_means, flags
    )
    prior_behind, prior_ahead, _ = lax.optimization_barrier((prior_behind, prior_ahead, flags))
    half = HALO // 2
    mine = jnp.concatenate(
        [
            prior,
            prior_ahead,
            to_chan(prior_behind[:half], lambda s: s + 2),
            to_chan(prior_ahead[half:], lambda s: s - 2),
            prior_behind,
        ],
        axis=0,
    )
    window_cov = call(
        window_kernel,
        "window_output",
        [where, mine, to_chan(mine, lambda s: s ^ 1), gram, after(stat, coef), late_total],
        [array(1, WIDTH, CHIPS * PAIR)],
        fetched=(3, 4, 5),
        stored=(0,),
        scratch=[((HALO, PAIR), BF16), ((WIDTH, HALO), BF16), ((WIDTH, WIDTH), F32)],
    )[0]
    back, coef, window_cov = lax.optimization_barrier((back, coef, window_cov))
    before = to_chan(back[16:24, 0:32], lambda s: s + 2)
    following = to_chan(back[24:32, 0:32], lambda s: (s - 2) ^ 1)
    opposite = to_chan(back[:, 32:40], lambda s: s + 4 if s < 4 else (s - 4) ^ 1)
    cusum, segment_cov = outputs(
        where, back, opposite, following, before, left, prefix, suffix, cols, turned, coef
    )
    return window_cov, segment_cov, cusum


def solution(mesh):
    placed = (P("tm", "chan"), P("tm", None), P("tm"))
    return jax.shard_map(
        local,
        mesh=mesh,
        in_specs=placed,
        out_specs=(P("tm", "chan", None), P("tm", "chan", None), P("tm", None, "chan", None)),
        check_vma=False,
    )
```

time: 885 us -> 122 us (0.14); the launches traced: 869 us -> 120 us
  loops' own time: 362 us -> 0 us
  other arithmetic: 157 us -> 0 us
  waiting for transfers between devices: 184 us -> 27.1 us
  local copies, waits for them, and re-layouts: 122 us -> 14.7 us
  starting transfers between devices: 4.51 us -> 50.3 us
  Pallas kernels: 0 us -> 26.5 us
  between operations: 16.7 us -> 1.85 us
  blocking collectives: 11.8 us -> 0 us
  matrix products: 11 us -> 0 us
    another operation x2 -> x0, loops' own time: 362 us -> none  [prefix_2(): return lax.fori_loop(0, size, lap, start)]
    all_gather x3 -> x0, waiting for transfers between devices: 182 us -> none  [the longest x2 141 us: prefix_2(): everything = lax.all_gather(shard, axis)]
    select_n x261 -> x0, other arithmetic: 141 us -> none  [the longest x131 130 us: choose(): jnp.where(keeper, first_item, second_item)]
    squeeze x65 -> x0, local copies, waits for them, and re-layouts: 71.2 us -> none  [the longest x64 70.1 us: lap(): new = combine(before, everything[at])]
    slice x68 -> x7, local copies, waits for them, and re-layouts: 42.7 us -> 1.09 us  [the longest x1 1 us: local(): samples[ROWS - HALO:]]
    ppermute x1 -> x20, starting transfers between devices: 4.39 us -> 31.6 us  [the longest x19 29.8 us: to_chan(): lax.ppermute(value, 'chan', [(s, target(s) % count) for s in range(count)])]
    pallas_call x0 -> x9, Pallas kernels: none -> 26.5 us  [the longest x8 21.5 us: call(): pl.pallas_call(body, out_shape=outputs, grid=(1,), in_specs=ins + [HBM] *...]
    ppermute x1 -> x20, waiting for transfers between devices: 2.44 us -> 25.4 us  [the longest x19 25.4 us: to_chan(): lax.ppermute(value, 'chan', [(s, target(s) % count) for s in range(count)])]
  transfers between devices with their start and end apart: 4 -> 22, of which waited for: 3 -> 10; matrix products, arithmetic and copies ran while one was open for 16% -> 2% of each run, Pallas kernels for 0% -> 15%
where the time goes in v1:
time: 122 us; the launch traced here: 120 us
  starting transfers between devices  50.3 us (41%)
  waiting for transfers between devices  27.1 us (22%)
  Pallas kernels  26.5 us (22%)
  local copies, waits for them, and re-layouts  14.7 us (12%)
  between operations  1.85 us (2%)
    ppermute x19, starting transfers between devices, to_chan(): lax.ppermute(value, 'chan', [(s, target(s) % count) for s in range(count)])  29.8 us
    ppermute x19, waiting for transfers between devices, to_chan(): lax.ppermute(value, 'chan', [(s, target(s) % count) for s in range(count)])  25.4 us
    pallas_call x8, Pallas kernels, call(): pl.pallas_call(body, out_shape=outputs, grid=(1,), in_specs=ins + [HBM] *...  21.5 us
    all_to_all x2, starting transfers between devices, exchange(): return lax.all_to_all(value, 'tm', 0, 0, tiled=True)  18.7 us
    unnamed x27, local copies, waits for them, and re-layouts  12.8 us
    pallas_call x1, Pallas kernels, outputs(): pl.pallas_call(output_kernel, out_shape=OUTPUTS, grid=(1,), in_specs=[SM]...  5.06 us
  transfers between devices with their start and end apart: 22, of which 10 were waited for; matrix products, arithmetic and copies ran while one was open for 2% of the time, Pallas kernels for 15%

profile of v1, /device:TPU:1, one launch (start us, length us, event | category | flops | bytes accessed | tf_op | source)
XLA Modules:
  0.0 120.5 jit_solution(17119149867239819803)
XLA Ops:
  0.6 3.3 %collective-permute-start.3 = (bf16[2048,128]{1,0:T(8,128)(2,1)}, bf16[2048,128]{1,0:T(8,128)(2,1)S(1)}, u32[]{:S(2)}, u32[]{:S(2)}) collective-permute-start(bf16[2048,128]{1,0:T(8,128)(2,1)} %refs_1_.1), channel_id=1, source_target_pairs={{0,1},{1,0},{2,3},{3,2},{4,5},{5,4},{6,7},{7,6},{8,9},{9,8},{10,11... | collective-permute-start | bytes 1572872 | tf_op jit(solution)/shard_map/ppermute | solution.py:514
  4.0 2.7 %collective-permute-start.1 = (bf16[2048,128]{1,0:T(8,128)(2,1)}, bf16[2048,128]{1,0:T(8,128)(2,1)S(1)}, u32[]{:S(2)}, u32[]{:S(2)}) collective-permute-start(bf16[2048,128]{1,0:T(8,128)(2,1)} %refs_1_.1), channel_id=1, source_target_pairs={{0,6},{1,7},{2,0},{3,1},{4,2},{5,3},{6,4},{7,5},{8,14},{9,15},{10,... | collective-permute-start | bytes 1572872 | tf_op jit(solution)/shard_map/ppermute | solution.py:514
  12.0 3.5 %first_pair.1 = (f32[4,8,128,256]{3,2,1,0:T(8,128)S(1)}, f32[4,8,256]{2,1,0:T(8,128)S(1)}, f32[4,128,256]{2,1,0:T(8,128)S(1)}, f32[4,8,256]{2,1,0:T(8,128)S(1)},...) custom-call(s32[21]{0:T(128)S(1)} %concatenate.9.refs_0_.where_ref, ...), custom_call_target="tpu_custom_call" | custom-call | flops 3000000000 | bytes 1048576 | tf_op jit(solution)/shard_map/first_pair/pallas_call | solution.py:202
  15.5 3.4 %collective-permute-done.refs_2_ = bf16[2048,128]{1,0:T(8,128)(2,1)S(1)} collective-permute-done((bf16[2048,128]{1,0:T(8,128)(2,1)}, bf16[2048,128]{1,0:T(8,128)(2,1)S(1)}, u32[]{:S(2)}, u32[]{:S(2)}) %collective-permute-start) | collective-permute-done | bytes 524320 | tf_op jit(solution)/shard_map/ppermute | solution.py:514
  19.9 2.8 %collective-permute-start.5 = (bf16[1024,128]{1,0:T(8,128)(2,1)S(1)}, bf16[1024,128]{1,0:T(8,128)(2,1)S(1)}, u32[]{:S(2)}, u32[]{:S(2)}) collective-permute-start(bf16[1024,128]{1,0:T(8,128)(2,1)S(1)} %slice.26), channel_id=1, source_target_pairs={{0,6},{1,7},{2,0},{3,1},{4,2},{5,3},{6,4},{7,5},{8,14},{9,15},{10,... | collective-permute-start | bytes 786440 | tf_op jit(solution)/shard_map/ppermute | solution.py:514
  22.6 3.1 %near_pair.1 = (f32[4,8,128,256]{3,2,1,0:T(8,128)S(1)}, f32[4,8,256]{2,1,0:T(8,128)S(1)}, f32[4,128,256]{2,1,0:T(8,128)S(1)}, f32[4,8,256]{2,1,0:T(8,128)S(1)}, f32[128,256]{1,0:T(8,128)S(1)}) custom-call(s32[21]{0:T(128)S(1)} %concatenate.9.refs_0_.where_ref, ...), custom_call_target="tpu_custom_call", output_to_operand_aliasing={{0}: (5, {}), {1}: (6, {}), {2}: (7, {}), {3}: (8, {})} | custom-call | flops 3000000000 | bytes 1048576 | tf_op jit(solution)/shard_map/near_pair/pallas_call | solution.py:202
  25.8 3.1 %side_pair.1 = (f32[4,8,128,256]{3,2,1,0:T(8,128)S(1)}, f32[4,8,256]{2,1,0:T(8,128)S(1)}, f32[4,128,256]{2,1,0:T(8,128)S(1)}, f32[4,8,256]{2,1,0:T(8,128)S(1)}) custom-call(s32[21]{0:T(128)S(1)} %concatenate.9.refs_0_.where_ref, ...), custom_call_target="tpu_custom_call", output_to_operand_aliasing={{0}: (4, {}), {1}: (5, {}), {2}: (6, {}), {3}: (7, {})} | custom-call | flops 3000000000 | bytes 1048576 | tf_op jit(solution)/shard_map/side_pair/pallas_call | solution.py:202
  31.6 2.6 %far_pair.1 = (f32[4,128,256]{2,1,0:T(8,128)S(1)}, f32[4,8,256]{2,1,0:T(8,128)S(1)}, f32[32,24,128]{2,1,0:T(8,128)}, bf16[2048,256]{1,0:T(8,128)(2,1)S(1)}) custom-call(s32[21]{0:T(128)S(1)} %concatenate.9.refs_0_.where_ref, bf16[2048,128]{1,0:T(8,128)(2,1)S(1)} %constant_dynamic-update-slice_fusion.refs_1_, ...), custom_call_target="tpu_custom_call", output_to_operand_aliasing={{0}: (8, {}), {1}: (9, {})} | custom-call | flops 2000000000 | bytes 1048576 | tf_op jit(solution)/shard_map/far_pair/pallas_call | solution.py:202
  34.3 9.7 %all-to-all-start = ((f32[32,24,128]{2,1,0:T(8,128)}), f32[32,24,128]{2,1,0:T(8,128)S(1)}, u32[]{:S(2)}, u32[]{:S(2)}) async-start(f32[32,24,128]{2,1,0:T(8,128)} %get-tuple-element.76), calls=%async_computation | async-start | bytes 786432 | tf_op jit(solution)/shard_map/all_to_all | solution.py:518
  50.3 2.6 %collective-permute-start.10 = (bf16[1024,128]{1,0:T(8,128)(2,1)S(1)}, bf16[1024,128]{1,0:T(8,128)(2,1)S(1)}, u32[]{:S(2)}, u32[]{:S(2)}) collective-permute-start(bf16[1024,128]{1,0:T(8,128)(2,1)S(1)} %collective-permute-done.2), channel_id=1, source_target_pairs={{0,6},{1,7},{2,0},{3,1},{4,2},{5,3},{6,4},{7,5},{8,14},{9,15},{10,... | collective-permute-start | bytes 786440 | tf_op jit(solution)/shard_map/ppermute | solution.py:514
  52.9 5.0 %collective-permute-done.10 = bf16[1024,128]{1,0:T(8,128)(2,1)S(1)} collective-permute-done((bf16[1024,128]{1,0:T(8,128)(2,1)S(1)}, bf16[1024,128]{1,0:T(8,128)(2,1)S(1)}, u32[]{:S(2)}, u32[]{:S(2)}) %collective-permute-start.10) | collective-permute-done | bytes 262176 | tf_op jit(solution)/shard_map/ppermute | solution.py:514
  57.9 3.1 %collective-permute-done.9 = bf16[1024,128]{1,0:T(8,128)(2,1)S(1)} collective-permute-done((bf16[1024,128]{1,0:T(8,128)(2,1)S(1)}, bf16[1024,128]{1,0:T(8,128)(2,1)S(1)}, u32[]{:S(2)}, u32[]{:S(2)}) %collective-permute-start.9) | collective-permute-done | bytes 262176 | tf_op jit(solution)/shard_map/ppermute | solution.py:514
  62.2 2.7 %collective-permute-start.15 = (bf16[512,128]{1,0:T(8,128)(2,1)S(1)}, bf16[512,128]{1,0:T(8,128)(2,1)S(1)}, u32[]{:S(2)}, u32[]{:S(2)}) collective-permute-start(bf16[512,128]{1,0:T(8,128)(2,1)S(1)} %slice.28), channel_id=1, source_target_pairs={{0,6},{1,7},{2,0},{3,1},{4,2},{5,3},{6,4},{7,5},{8,14},{9,15},{10,... | collective-permute-start | bytes 393224 | tf_op jit(solution)/shard_map/ppermute | solution.py:514
  65.0 2.2 %collective-permute-done.14 = bf16[512,128]{1,0:T(8,128)(2,1)S(1)} collective-permute-done((bf16[512,128]{1,0:T(8,128)(2,1)S(1)}, bf16[512,128]{1,0:T(8,128)(2,1)S(1)}, u32[]{:S(2)}, u32[]{:S(2)}) %collective-permute-start.14) | collective-permute-done | bytes 131104 | tf_op jit(solution)/shard_map/ppermute | solution.py:514
  67.3 3.1 %collective-permute-start.16 = (bf16[4096,128]{1,0:T(8,128)(2,1)S(1)}, bf16[4096,128]{1,0:T(8,128)(2,1)S(1)}, u32[]{:S(2)}, u32[]{:S(2)}) collective-permute-start(bf16[4096,128]{1,0:T(8,128)(2,1)S(1)} %constant_dynamic-update-slice_fusion.2.refs_1_), channel_id=1, source_target_pairs={{0,1},{1,0},{2,3},{3,2},{4,5},{5,4},{6,7},{7,6},{8,9},{9,8},{10,11... | collective-permute-start | bytes 3145736 | tf_op jit(solution)/shard_map/ppermute | solution.py:514
  70.4 9.0 %all-to-all-start.1 = ((f32[32,40,128]{2,1,0:T(8,128)}), f32[32,40,128]{2,1,0:T(8,128)S(1)}, u32[]{:S(2)}, u32[]{:S(2)}) async-start(f32[32,40,128]{2,1,0:T(8,128)} %get-tuple-element.85), calls=%async_computation.1 | async-start | bytes 1310720 | tf_op jit(solution)/shard_map/all_to_all | solution.py:518
  79.4 3.1 %collective-permute-start.11 = (f32[2,32,128]{2,1,0:T(8,128)S(1)}, f32[2,32,128]{2,1,0:T(8,128)S(1)}, u32[]{:S(2)}, u32[]{:S(2)}) collective-permute-start(f32[2,32,128]{2,1,0:T(8,128)S(1)} %get-tuple-element.89.refs_4_), channel_id=1, source_target_pairs={{0,6},{1,7},{2,0},{3,1},{4,2},{5,3},{6,4},{7,5},{8,14},{9,15},{10,... | collective-permute-start | bytes 98312 | tf_op jit(solution)/shard_map/ppermute | solution.py:514
  83.8 2.7 %collective-permute-done.12.refs_6_ = f32[2,32,128]{2,1,0:T(8,128)S(1)} collective-permute-done((f32[2,32,128]{2,1,0:T(8,128)S(1)}, f32[2,32,128]{2,1,0:T(8,128)S(1)}, u32[]{:S(2)}, u32[]{:S(2)}) %collective-permute-start.12) | collective-permute-done | bytes 32800 | tf_op jit(solution)/shard_map/ppermute | solution.py:514
  86.9 2.4 %prep_terms.1 = (f32[128,128]{1,0:T(8,128)S(1)}, f32[8,40,128]{2,1,0:T(8,128)S(1)}, f32[24,128]{1,0:T(8,128)S(1)}, f32[8,128,128]{2,1,0:T(8,128)S(1)}, f32[8,128,128]{2,1,0:T(8,128)S(1)}) custom-call(s32[21]{0:T(128)S(1)} %concatenate.9.refs_0_.where_ref, f32[4,8,256]{2,1,0:T(8,128)S(1)} %get-tuple-element.86.refs_1_, ...), custom_call_target="tpu_custom_call" | custom-call | flops 4000000000 | bytes 1048576 | tf_op jit(solution)/shard_map/prep_terms/pallas_call | solution.py:202
  91.5 3.5 %window_output.1 = f32[1,128,1024]{2,1,0:T(8,128)} custom-call(s32[21]{0:T(128)S(1)} %concatenate.9.refs_0_.where_ref, bf16[4096,128]{1,0:T(8,128)(2,1)S(1)} %constant_dynamic-update-slice_fusion.2.refs_1_, bf16[4096,128]{1,0:T(8,128)(2,1)S(1)} %collective-permute-done.16.refs_2_, f32[4,128,256]{2,1,0:T(8,128)S(1)} %get-tuple-element.87.refs_2_.refs_3_, ...), custom_call_target="tpu_custom_call" | custom-call | flops 3000000000 | bytes 1048576 | tf_op jit(solution)/shard_map/window_output/pallas_call | solution.py:202
  96.8 6.1 %collective-permute-start.18 = (f32[8,32,128]{2,1,0:T(8,128)S(1)}, f32[8,32,128]{2,1,0:T(8,128)S(1)}, u32[]{:S(2)}, u32[]{:S(2)}) collective-permute-start(f32[8,32,128]{2,1,0:T(8,128)S(1)} %get-tuple-element.108), channel_id=1, source_target_pairs={{0,7},{1,6},{2,1},{3,0},{4,3},{5,2},{6,5},{7,4},{8,15},{9,14},{10,... | collective-permute-start | bytes 393224 | tf_op jit(solution)/shard_map/ppermute | solution.py:514
  104.8 5.2 %collective-permute-done.19.before_ref = f32[8,32,128]{2,1,0:T(8,128)S(1)} collective-permute-done((f32[8,32,128]{2,1,0:T(8,128)S(1)}, f32[8,32,128]{2,1,0:T(8,128)S(1)}, u32[]{:S(2)}, u32[]{:S(2)}) %collective-permute-start.19) | collective-permute-done | bytes 131104 | tf_op jit(solution)/shard_map/ppermute | solution.py:514
  110.0 2.2 %copy-done.4 = f32[4,8,128,256]{3,2,1,0:T(8,128)S(1)} copy-done((f32[4,8,128,256]{3,2,1,0:T(8,128)S(1)}, f32[4,8,128,256]{3,2,1,0:T(8,128)}, u32[]{:S(2)}) %copy-start.4) | copy-done | bytes 4194328
  115.2 5.1 %outputs.1 = (f32[1,8,128,1024]{3,2,1,0:T(8,128)}, f32[1,128,1024]{2,1,0:T(8,128)}) custom-call(s32[21]{0:T(128)S(1)} %concatenate.9.refs_0_.where_ref, f32[32,40,128]{2,1,0:T(8,128)S(1)} %all-to-all-done.1.back_ref, f32[32,8,128]{2,1,0:T(8,128)S(1)} %collective-permute-done.17.opposite_ref, f32[8,32,128]{2,1,0:T(8,128)S(1)} %collective-permute-done.18.next_ref, ...), custom_call_target="tpu_custom_call" | custom-call | flops 5000000000 | bytes 1048576 | tf_op jit(solution)/shard_map/outputs/pallas_call | solution.py:456
  (66 shorter events, 26.4 us)
Async XLA Ops:
  0.6 10.3 %collective-permute-start.3 = (bf16[2048,128]{1,0:T(8,128)(2,1)}, bf16[2048,128]{1,0:T(8,128)(2,1)S(1)}, u32[]{:S(2)}, u32[]{:S(2)}) collective-permute-start(bf16[2048,128]{1,0:T(8,128)(2,1)} %refs_1_.1), channel_id=1, source_target_pairs={{0,1},{1,0},{2,3},{3,2},{4,5},{5,4},{6,7},{7,6},{8,9},{9,8},{10,11... | collective-permute-start | bytes 1572872 | tf_op jit(solution)/shard_map/ppermute | solution.py:514
  4.0 14.9 %collective-permute-start = (bf16[2048,128]{1,0:T(8,128)(2,1)}, bf16[2048,128]{1,0:T(8,128)(2,1)S(1)}, u32[]{:S(2)}, u32[]{:S(2)}) collective-permute-start(bf16[2048,128]{1,0:T(8,128)(2,1)} %refs_1_.1), channel_id=1, source_target_pairs={{0,2},{1,3},{2,4},{3,5},{4,6},{5,7},{6,0},{7,1},{8,10},{9,11},{10,... | collective-permute-start | bytes 1572872 | tf_op jit(solution)/shard_map/ppermute | solution.py:514
  4.0 14.9 %collective-permute-start.1 = (bf16[2048,128]{1,0:T(8,128)(2,1)}, bf16[2048,128]{1,0:T(8,128)(2,1)S(1)}, u32[]{:S(2)}, u32[]{:S(2)}) collective-permute-start(bf16[2048,128]{1,0:T(8,128)(2,1)} %refs_1_.1), channel_id=1, source_target_pairs={{0,6},{1,7},{2,0},{3,1},{4,2},{5,3},{6,4},{7,5},{8,14},{9,15},{10,... | collective-permute-start | bytes 1572872 | tf_op jit(solution)/shard_map/ppermute | solution.py:514
  7.7 7.8 %collective-permute-start.2 = (bf16[1024,128]{1,0:T(8,128)(2,1)S(1)}, bf16[1024,128]{1,0:T(8,128)(2,1)S(1)}, u32[]{:S(2)}, u32[]{:S(2)}) collective-permute-start(bf16[1024,128]{1,0:T(8,128)(2,1)S(1)} %slice.24), channel_id=1, source_target_pairs={{0,8},{8,16},{16,24},{24,32},{32,40},{40,48},{48,56},{56,64},{64,7... | collective-permute-start | bytes 786440 | tf_op jit(solution)/shard_map/ppermute | solution.py:538
  18.9 3.8 %collective-permute-start.7 = (bf16[2048,128]{1,0:T(8,128)(2,1)S(1)}, bf16[2048,128]{1,0:T(8,128)(2,1)S(1)}, u32[]{:S(2)}, u32[]{:S(2)}) collective-permute-start(bf16[2048,128]{1,0:T(8,128)(2,1)S(1)} %collective-permute-done.refs_2_), channel_id=1, source_target_pairs={{0,1},{1,0},{2,3},{3,2},{4,5},{5,4},{6,7},{7,6},{8,9},{9,8},{10,11... | collective-permute-start | bytes 1572872 | tf_op jit(solution)/shard_map/ppermute | solution.py:514
  19.7 6.0 %collective-permute-start.6 = (bf16[2048,128]{1,0:T(8,128)(2,1)S(1)}, bf16[2048,128]{1,0:T(8,128)(2,1)S(1)}, u32[]{:S(2)}, u32[]{:S(2)}) collective-permute-start(bf16[2048,128]{1,0:T(8,128)(2,1)S(1)} %collective-permute-done.1.refs_1_), channel_id=1, source_target_pairs={{0,1},{1,0},{2,3},{3,2},{4,5},{5,4},{6,7},{7,6},{8,9},{9,8},{10,11... | collective-permute-start | bytes 1572872 | tf_op jit(solution)/shard_map/ppermute | solution.py:514
  19.8 9.1 %collective-permute-start.4 = (bf16[1024,128]{1,0:T(8,128)(2,1)S(1)}, bf16[1024,128]{1,0:T(8,128)(2,1)S(1)}, u32[]{:S(2)}, u32[]{:S(2)}) collective-permute-start(bf16[1024,128]{1,0:T(8,128)(2,1)S(1)} %slice.25), channel_id=1, source_target_pairs={{0,2},{1,3},{2,4},{3,5},{4,6},{5,7},{6,0},{7,1},{8,10},{9,11},{10,... | collective-permute-start | bytes 786440 | tf_op jit(solution)/shard_map/ppermute | solution.py:514
  19.9 9.1 %collective-permute-start.5 = (bf16[1024,128]{1,0:T(8,128)(2,1)S(1)}, bf16[1024,128]{1,0:T(8,128)(2,1)S(1)}, u32[]{:S(2)}, u32[]{:S(2)}) collective-permute-start(bf16[1024,128]{1,0:T(8,128)(2,1)S(1)} %slice.26), channel_id=1, source_target_pairs={{0,6},{1,7},{2,0},{3,1},{4,2},{5,3},{6,4},{7,5},{8,14},{9,15},{10,... | collective-permute-start | bytes 786440 | tf_op jit(solution)/shard_map/ppermute | solution.py:514
  28.9 5.3 %copy-start.1 = (f32[4,8,128,256]{3,2,1,0:T(8,128)}, f32[4,8,128,256]{3,2,1,0:T(8,128)S(1)}, u32[]{:S(2)}) copy-start(f32[4,8,128,256]{3,2,1,0:T(8,128)S(1)} %get-tuple-element.80.refs_3_) | copy-start | bytes 12582916
  29.0 2.6 %collective-permute-start.8 = (bf16[2048,128]{1,0:T(8,128)(2,1)S(1)}, bf16[2048,128]{1,0:T(8,128)(2,1)S(1)}, u32[]{:S(2)}, u32[]{:S(2)}) collective-permute-start(bf16[2048,128]{1,0:T(8,128)(2,1)S(1)} %constant_dynamic-update-slice_fusion.refs_1_), channel_id=1, source_target_pairs={{0,1},{1,0},{2,3},{3,2},{4,5},{5,4},{6,7},{7,6},{8,9},{9,8},{10,11... | collective-permute-start | bytes 1572872 | tf_op jit(solution)/shard_map/ppermute | solution.py:514
  34.3 26.8 %all-to-all-start = ((f32[32,24,128]{2,1,0:T(8,128)}), f32[32,24,128]{2,1,0:T(8,128)S(1)}, u32[]{:S(2)}, u32[]{:S(2)}) async-start(f32[32,24,128]{2,1,0:T(8,128)} %get-tuple-element.76), calls=%async_computation | async-start | bytes 786432 | tf_op jit(solution)/shard_map/all_to_all | solution.py:518
  43.9 2.2 %copy-start.2 = (f32[4,8,128,256]{3,2,1,0:T(8,128)S(1)}, f32[4,8,128,256]{3,2,1,0:T(8,128)}, u32[]{:S(2)}) copy-start(f32[4,8,128,256]{3,2,1,0:T(8,128)} %copy-done.1) | copy-start | bytes 12582916
  50.3 7.6 %collective-permute-start.10 = (bf16[1024,128]{1,0:T(8,128)(2,1)S(1)}, bf16[1024,128]{1,0:T(8,128)(2,1)S(1)}, u32[]{:S(2)}, u32[]{:S(2)}) collective-permute-start(bf16[1024,128]{1,0:T(8,128)(2,1)S(1)} %collective-permute-done.2), channel_id=1, source_target_pairs={{0,6},{1,7},{2,0},{3,1},{4,2},{5,3},{6,4},{7,5},{8,14},{9,15},{10,... | collective-permute-start | bytes 786440 | tf_op jit(solution)/shard_map/ppermute | solution.py:514
  52.9 8.1 %collective-permute-start.9 = (bf16[1024,128]{1,0:T(8,128)(2,1)S(1)}, bf16[1024,128]{1,0:T(8,128)(2,1)S(1)}, u32[]{:S(2)}, u32[]{:S(2)}) collective-permute-start(bf16[1024,128]{1,0:T(8,128)(2,1)S(1)} %collective-permute-done.2), channel_id=1, source_target_pairs={{0,2},{1,3},{2,4},{3,5},{4,6},{5,7},{6,0},{7,1},{8,10},{9,11},{10,... | collective-permute-start | bytes 786440 | tf_op jit(solution)/shard_map/ppermute | solution.py:514
  62.1 5.1 %collective-permute-start.14 = (bf16[512,128]{1,0:T(8,128)(2,1)S(1)}, bf16[512,128]{1,0:T(8,128)(2,1)S(1)}, u32[]{:S(2)}, u32[]{:S(2)}) collective-permute-start(bf16[512,128]{1,0:T(8,128)(2,1)S(1)} %slice.27), channel_id=1, source_target_pairs={{0,2},{1,3},{2,4},{3,5},{4,6},{5,7},{6,0},{7,1},{8,10},{9,11},{10,... | collective-permute-start | bytes 393224 | tf_op jit(solution)/shard_map/ppermute | solution.py:514
  62.2 5.0 %collective-permute-start.15 = (bf16[512,128]{1,0:T(8,128)(2,1)S(1)}, bf16[512,128]{1,0:T(8,128)(2,1)S(1)}, u32[]{:S(2)}, u32[]{:S(2)}) collective-permute-start(bf16[512,128]{1,0:T(8,128)(2,1)S(1)} %slice.28), channel_id=1, source_target_pairs={{0,6},{1,7},{2,0},{3,1},{4,2},{5,3},{6,4},{7,5},{8,14},{9,15},{10,... | collective-permute-start | bytes 393224 | tf_op jit(solution)/shard_map/ppermute | solution.py:514
  67.3 24.2 %collective-permute-start.16 = (bf16[4096,128]{1,0:T(8,128)(2,1)S(1)}, bf16[4096,128]{1,0:T(8,128)(2,1)S(1)}, u32[]{:S(2)}, u32[]{:S(2)}) collective-permute-start(bf16[4096,128]{1,0:T(8,128)(2,1)S(1)} %constant_dynamic-update-slice_fusion.2.refs_1_), channel_id=1, source_target_pairs={{0,1},{1,0},{2,3},{3,2},{4,5},{5,4},{6,7},{7,6},{8,9},{9,8},{10,11... | collective-permute-start | bytes 3145736 | tf_op jit(solution)/shard_map/ppermute | solution.py:514
  70.4 26.4 %all-to-all-start.1 = ((f32[32,40,128]{2,1,0:T(8,128)}), f32[32,40,128]{2,1,0:T(8,128)S(1)}, u32[]{:S(2)}, u32[]{:S(2)}) async-start(f32[32,40,128]{2,1,0:T(8,128)} %get-tuple-element.85), calls=%async_computation.1 | async-start | bytes 1310720 | tf_op jit(solution)/shard_map/all_to_all | solution.py:518
  79.4 4.4 %collective-permute-start.11 = (f32[2,32,128]{2,1,0:T(8,128)S(1)}, f32[2,32,128]{2,1,0:T(8,128)S(1)}, u32[]{:S(2)}, u32[]{:S(2)}) collective-permute-start(f32[2,32,128]{2,1,0:T(8,128)S(1)} %get-tuple-element.89.refs_4_), channel_id=1, source_target_pairs={{0,6},{1,7},{2,0},{3,1},{4,2},{5,3},{6,4},{7,5},{8,14},{9,15},{10,... | collective-permute-start | bytes 98312 | tf_op jit(solution)/shard_map/ppermute | solution.py:514
  82.5 4.0 %collective-permute-start.12 = (f32[2,32,128]{2,1,0:T(8,128)S(1)}, f32[2,32,128]{2,1,0:T(8,128)S(1)}, u32[]{:S(2)}, u32[]{:S(2)}) collective-permute-start(f32[2,32,128]{2,1,0:T(8,128)S(1)} %get-tuple-element.89.refs_4_), channel_id=1, source_target_pairs={{0,2},{1,3},{2,4},{3,5},{4,6},{5,7},{6,0},{7,1},{8,10},{9,11},{10,... | collective-permute-start | bytes 98312 | tf_op jit(solution)/shard_map/ppermute | solution.py:514
  82.5 4.3 %collective-permute-start.13 = (f32[2,32,128]{2,1,0:T(8,128)S(1)}, f32[2,32,128]{2,1,0:T(8,128)S(1)}, u32[]{:S(2)}, u32[]{:S(2)}) collective-permute-start(f32[2,32,128]{2,1,0:T(8,128)S(1)} %get-tuple-element.89.refs_4_), channel_id=1, source_target_pairs={{0,4},{1,5},{2,6},{3,7},{4,0},{5,1},{6,2},{7,3},{8,12},{9,13},{10,... | collective-permute-start | bytes 98312 | tf_op jit(solution)/shard_map/ppermute | solution.py:514
  96.8 8.0 %collective-permute-start.18 = (f32[8,32,128]{2,1,0:T(8,128)S(1)}, f32[8,32,128]{2,1,0:T(8,128)S(1)}, u32[]{:S(2)}, u32[]{:S(2)}) collective-permute-start(f32[8,32,128]{2,1,0:T(8,128)S(1)} %get-tuple-element.108), channel_id=1, source_target_pairs={{0,7},{1,6},{2,1},{3,0},{4,3},{5,2},{6,5},{7,4},{8,15},{9,14},{10,... | collective-permute-start | bytes 393224 | tf_op jit(solution)/shard_map/ppermute | solution.py:514
  102.9 7.1 %collective-permute-start.19 = (f32[8,32,128]{2,1,0:T(8,128)S(1)}, f32[8,32,128]{2,1,0:T(8,128)S(1)}, u32[]{:S(2)}, u32[]{:S(2)}) collective-permute-start(f32[8,32,128]{2,1,0:T(8,128)S(1)} %get-tuple-element.107), channel_id=1, source_target_pairs={{0,2},{1,3},{2,4},{3,5},{4,6},{5,7},{6,0},{7,1},{8,10},{9,11},{10,... | collective-permute-start | bytes 393224 | tf_op jit(solution)/shard_map/ppermute | solution.py:514
  102.9 7.1 %collective-permute-start.17 = (f32[32,8,128]{2,1,0:T(8,128)S(1)}, f32[32,8,128]{2,1,0:T(8,128)S(1)}, u32[]{:S(2)}, u32[]{:S(2)}) collective-permute-start(f32[32,8,128]{2,1,0:T(8,128)S(1)} %slice.29), channel_id=1, source_target_pairs={{0,4},{1,5},{2,6},{3,7},{4,1},{5,0},{6,3},{7,2},{8,12},{9,13},{10,... | collective-permute-start | bytes 393224 | tf_op jit(solution)/shard_map/ppermute | solution.py:514
  (9 other events, 10.5 us)

commit v2 on v1

--- a/solution.py
+++ b/solution.py
@@ -71,7 +71,7 @@
     return jnp.concatenate([value, value], axis=1)
 
 
-def left_part(where_ref, flipped, cent_ref, left_ref, sums_ref):
+def left_part(where_ref, flipped, cent_ref, left_ref, sums_ref, block=0):
     index = lax.broadcasted_iota(jnp.int32, (16, ROWS), 0)
     place = lax.broadcasted_iota(jnp.int32, (16, ROWS), 1)
     limit = jnp.zeros((16, ROWS), jnp.int32)
@@ -79,12 +79,14 @@
         limit = jnp.where(index == j, where_ref[12 + j], limit)
     masks = jnp.where(place < limit, 1.0, 0.0).astype(BF16)
     cent = cent_ref[...]
-    sums_ref[0] = jnp.dot(masks, cent, preferred_element_type=F32)[0:8]
+    sums_ref[block] = jnp.dot(masks, cent, preferred_element_type=F32)[0:8]
     for i in range(SPLITS // 4):
         kept = jnp.concatenate([flipped * masks[j : j + 1, :] for j in range(4 * i, 4 * i + 4)], axis=0)
         part = jnp.dot(kept, cent, preferred_element_type=F32)
         for j in range(4):
-            left_ref[0, 4 * i + j] = part[j * WIDTH : (j + 1) * WIDTH]
+            for c in range(2):
+                rows, lanes = slice(j * WIDTH, (j + 1) * WIDTH), slice(c * WIDTH, (c + 1) * WIDTH)
+                left_ref[c, 4 * i + j] = part[rows, lanes]
 
 
 def first_kernel(
@@ -123,13 +125,9 @@
     left_part(where_ref, flipped, cent_ref, left_ref, sums_ref)
 
 
-def side_kernel(
-    where_ref, first_ref, second_ref, flip_ref, left_ref, sums_ref, gram_ref, stat_ref, cent_ref
-):
+def side_kernel(where_ref, first_ref, second_ref, flip_ref, gram_ref, stat_ref, cent_ref):
     center_pair(first_ref, second_ref, 0, WIDTH, cent_ref, stat_ref)
-    flipped = flip_ref[...]
-    gram_ref[0] = jnp.dot(flipped, cent_ref[...], preferred_element_type=F32)
-    left_part(where_ref, flipped, cent_ref, left_ref, sums_ref)
+    gram_ref[0] = jnp.dot(flip_ref[...], cent_ref[...], preferred_element_type=F32)
 
 
 def far_kernel(
@@ -151,30 +149,38 @@
         out_ref[q, 16:20, :] = held_ref[4 * q : 4 * q + 4, :]
 
 
-def rest_kernel(where_ref, cent_ref, flip_ref, left_ref, sums_ref):
-    left_part(where_ref, flip_ref[...], cent_ref, left_ref, sums_ref)
+def rest_kernel(where_ref, far_ref, side_ref, flip_ref, far_left_ref, side_left_ref, sums_ref):
+    flipped = flip_ref[...]
+    left_part(where_ref, flipped, far_ref, far_left_ref, sums_ref, 0)
+    left_part(where_ref, flipped, side_ref, side_left_ref, sums_ref, 1)
 
 
 ALL = [
-    array(CHIPS, SPLITS, WIDTH, PAIR),
     array(CHIPS, 8, PAIR),
     array(CHIPS, WIDTH, PAIR),
     array(CHIPS, 8, PAIR),
 ]
 
 
+STORE = array(96, 8, WIDTH, WIDTH)
+SHARD_PAIR = (2, SPLITS, WIDTH, WIDTH)
+
+
 def call(
-    kernel, name, inputs, outputs, *, fetched=(), stored=(), kept=(), pair=0, scratch=(), us=3, grant=24
+    kernel, name, inputs, outputs, *, store=None, puts=(), fetched=(), stored=(), kept=(),
+    pair=0, span=1, scratch=(), us=3, grant=24,
 ):
-    count, held, made = len(inputs), len(kept), len(outputs)
-    sliced = [i < len(ALL) and outputs[i] in ALL for i in range(made)]
-    sizes = [(1, *out.shape[1:]) if cut else out.shape for out, cut in zip(outputs, sliced)]
+    kept = (*([store] if store is not None else []), *kept)
+    count, made, first = len(inputs), len(outputs), 1 if puts else 0
+    sliced = [out in ALL for out in outputs]
+    sizes = [(span, *out.shape[1:]) if cut else out.shape for out, cut in zip(outputs, sliced)]
     buffers = [pltpu.VMEM(inputs[i].shape, inputs[i].dtype) for i in fetched]
+    buffers += [pltpu.VMEM(shape, F32) for shape, _ in puts]
     buffers += [pltpu.VMEM(sizes[i], outputs[i].dtype) for i in stored]
 
     def body(*refs):
-        ins, refs = list(refs[:count]), refs[count + held :]
-        outs, refs = list(refs[:made]), refs[made:]
+        ins, refs = list(refs[:count]), refs[count + len(kept) :]
+        slots, outs, refs = refs[:first], list(refs[first : first + made]), refs[first + made :]
         own, buffer, sem = refs[: len(scratch)], refs[len(scratch) : -1], refs[-1]
         copies = []
         for c, i in enumerate(fetched):
@@ -184,12 +190,15 @@
             copy.start()
         for copy in copies:
             copy.wait()
-        copies = []
-        for c, i in enumerate(stored, len(fetched)):
-            target = outs[i].at[pl.ds(pair, 1)] if sliced[i] else outs[i]
+        copies, mine = [], []
+        for c, (_, place) in enumerate(puts, len(fetched)):
+            copies.append(pltpu.make_async_copy(buffer[c], slots[0].at[place], sem.at[c]))
+            mine.append(buffer[c])
+        for c, i in enumerate(stored, len(fetched) + len(puts)):
+            target = outs[i].at[pl.ds(pair, span)] if sliced[i] else outs[i]
             copies.append(pltpu.make_async_copy(buffer[c], target, sem.at[c]))
             outs[i] = buffer[c]
-        kernel(*ins, *outs, *own)
+        kernel(*ins, *mine, *outs, *own)
         for copy in copies:
             copy.start()
         for copy in copies:
@@ -199,13 +208,14 @@
     for i in fetched:
         ins[i] = HBM
     outs = [HBM if i in stored else whole(*out.shape) for i, out in enumerate(outputs)]
+    aliased = range(first if store is None else 0, first + len(kept))
     return pl.pallas_call(
         body,
-        out_shape=outputs,
+        out_shape=[STORE] * first + outputs,
         grid=(1,),
-        in_specs=ins + [HBM] * held,
-        out_specs=outs,
-        input_output_aliases={count + i: i for i in range(held)},
+        in_specs=ins + [HBM] * len(kept),
+        out_specs=[HBM] * first + outs,
+        input_output_aliases={count + i: out for i, out in zip(range(len(kept)), aliased)},
         scratch_shapes=[pltpu.VMEM(shape, dtype) for shape, dtype in scratch]
         + buffers
         + [pltpu.SemaphoreType.DMA((max(len(buffers), 1),))],
@@ -338,19 +348,26 @@
         after_ref[u] = gram_ref[r, :, lanes] + between(row_part_s, col_part_s)
 
 
-def prep_terms(where, sums, gram, stat, own, ahead, behind, far, flags):
-    square = array(8, WIDTH, WIDTH)
+def prep_terms(where, sums, gram, stat, own, ahead, behind, far, flags, store):
+    square = (8, WIDTH, WIDTH)
     return call(
         prep_kernel,
         "prep_terms",
         [where, sums, gram, stat, own, ahead, behind, far, flags],
-        [array(WIDTH, WIDTH), array(8, 40, WIDTH), array(24, WIDTH), square, square],
+        [],
+        store=store,
+        puts=(
+            ((WIDTH, WIDTH), (11, 0)),
+            ((8, 40, WIDTH), (10, slice(None), pl.ds(0, 40))),
+            ((24, WIDTH), (11, 1, pl.ds(0, 24))),
+            (square, 8),
+            (square, 9),
+        ),
         fetched=(1, 2, 3, 4, 8),
-        stored=(0, 1, 2, 3, 4),
         scratch=[((WIDTH, WIDTH), F32)],
-        us=4,
+        us=0.1,
         grant=16,
-    )
+    )[0]
 
 
 def load_near(ref, p_ref, s_ref):
@@ -366,20 +383,19 @@
 
 
 def output_kernel(
-    where_ref, back_ref, opposite_ref, next_ref, before_ref, left_hbm, prefix_hbm, suffix_hbm, cols_hbm, turned_hbm, coef_hbm,
-    cusum_hbm, seg_hbm,
+    where_ref, back_ref, opposite_ref, next_ref, before_ref, store_hbm, cusum_hbm, seg_hbm,
     left_ref, prefix_ref, suffix_ref, cols_ref, turned_ref, coef_ref, cusum_ref, seg_ref, p_ref, s_ref, sem, out_sem,
 ):
     loads = [
         pltpu.make_async_copy(source, target, sem.at[c])
         for c, (source, target) in enumerate(
             (
-                (prefix_hbm, prefix_ref),
-                (suffix_hbm, suffix_ref),
-                (cols_hbm, cols_ref),
-                (turned_hbm, turned_ref),
-                (coef_hbm, coef_ref),
-                (left_hbm, left_ref),
+                (store_hbm.at[8], prefix_ref),
+                (store_hbm.at[9], suffix_ref),
+                (store_hbm.at[10, :, pl.ds(0, 40)], cols_ref),
+                (store_hbm.at[11, 0], turned_ref),
+                (store_hbm.at[11, 1, pl.ds(0, 24)], coef_ref),
+                (store_hbm.at[pl.ds(0, 8)], left_ref),
             )
         )
     ]
@@ -431,8 +447,7 @@
         turned = spread_out(j, 4)
         a, b = coef_ref[j : j + 1, :], coef_ref[8 + j : 9 + j, :]
         for u in range(8):
-            half = WIDTH * (u % 2)
-            value = (a + b) * left_ref[u // 2, j, :, half : half + WIDTH]
+            value = (a + b) * left_ref[u, j]
             value = value + a * prefix_ref[u] - b * suffix_ref[u]
             for i in range(4):
                 value = value + turned[i] * cols_ref[u, 8 * i + j : 8 * i + j + 1, :]
@@ -449,22 +464,23 @@
 OUTPUTS = [array(1, SPLITS, WIDTH, CHIPS * PAIR), array(1, WIDTH, CHIPS * PAIR)]
 
 
-def outputs(where, back, opposite, following, before, left, prefix, suffix, cols, turned, coef):
+def outputs(where, back, opposite, following, before, store):
     blocks = [back, opposite, following, before]
-    terms = [prefix, suffix, cols, turned, coef]
-    buffers = [left, *terms, *OUTPUTS, array(WIDTH, WIDTH), array(WIDTH, WIDTH)]
+    square = array(8, WIDTH, WIDTH)
+    buffers = [array(8, SPLITS, WIDTH, WIDTH), square, square, array(8, 40, WIDTH)]
+    buffers += [array(WIDTH, WIDTH), array(24, WIDTH), *OUTPUTS, array(WIDTH, WIDTH), array(WIDTH, WIDTH)]
     return pl.pallas_call(
         output_kernel,
         out_shape=OUTPUTS,
         grid=(1,),
-        in_specs=[SM] + [whole(*value.shape) for value in blocks] + [HBM] * 6,
+        in_specs=[SM] + [whole(*value.shape) for value in blocks] + [HBM],
         out_specs=[HBM, HBM],
         scratch_shapes=[pltpu.VMEM(value.shape, F32) for value in buffers]
         + [pltpu.SemaphoreType.DMA((6,)), pltpu.SemaphoreType.DMA((SPLITS + 1,))],
         compiler_params=params(24),
         cost_estimate=cost(5),
         name="outputs",
-    )(where, *blocks, left, *terms)
+    )(where, *blocks, store)
 
 
 def window_kernel(
@@ -537,13 +553,14 @@
     other = to_chan(samples, lambda s: s ^ 1)
     prior = lax.ppermute(samples[ROWS - HALO :], "tm", [(b, b + 1) for b in range(BLOCKS - 1)])
     flip_shape, square = array(WIDTH, ROWS, dtype=BF16), array(WIDTH, WIDTH)
-    left, sums, gram, stat, late_flipped, late_total, flipped, spread0, total, rider = call(
+    store, sums, gram, stat, late_flipped, late_total, flipped, spread0, total, rider = call(
         first_kernel,
         "first_pair",
         [where, samples, other],
         ALL + [flip_shape, square, flip_shape, array(WIDTH, PAIR), square, array(8, WIDTH)],
+        puts=((SHARD_PAIR, pl.ds(0, 2)),),
         fetched=(1,),
-        stored=(0, 1, 2, 3, 4, 5),
+        stored=(0, 1, 2, 3, 4),
         scratch=[((ROWS, PAIR), BF16)],
     )
     behind, ahead, prior, flipped = lax.optimization_barrier((behind, ahead, prior, flipped))
@@ -552,25 +569,28 @@
     far_high = to_chan(ahead[half:], lambda s: s - 2)
     behind_other = to_chan(behind, lambda s: s ^ 1)
     ahead_other = to_chan(ahead, lambda s: s ^ 1)
-    left, sums, gram, stat, spread1 = call(
+    store, sums, gram, stat, spread1 = call(
         near_kernel,
         "near_pair",
         [where, ahead, behind_other, flipped, total],
         ALL + [array(WIDTH, PAIR)],
-        stored=(0, 1, 2, 3),
-        kept=(left, sums, gram, stat),
+        store=store,
+        puts=((SHARD_PAIR, pl.ds(2, 2)),),
+        stored=(0, 1, 2),
+        kept=(sums, gram, stat),
         pair=1,
         scratch=[((ROWS, PAIR), BF16)],
     )
-    left, sums, gram, stat = call(
+    cent_shape = array(ROWS, PAIR, dtype=BF16)
+    gram, stat, side = call(
         side_kernel,
         "side_pair",
         [where, ahead_other, behind, flipped],
-        ALL,
-        stored=(0, 1, 2, 3),
-        kept=(left, sums, gram, stat),
+        ALL[1:] + [cent_shape],
+        stored=(0, 1),
+        kept=(gram, stat),
         pair=3,
-        scratch=[((ROWS, PAIR), BF16)],
+        us=0.1,
     )
     far_low, far_high, stat = lax.optimization_barrier((far_low, far_high, stat))
     far = jnp.concatenate([far_low, far_high], axis=0)
@@ -579,26 +599,30 @@
         far_kernel,
         "far_pair",
         [where, far, far_other, flipped, total, spread0, spread1, rider],
-        ALL[2:] + [array(BLOCKS, 24, WIDTH), array(ROWS, PAIR, dtype=BF16)],
+        ALL[1:] + [array(BLOCKS, 24, WIDTH), cent_shape],
         stored=(0, 1, 3),
         kept=(gram, stat),
         pair=2,
         scratch=[((WIDTH, WIDTH), F32)],
-        us=2,
+        us=0.1,
     )
     arrived = exchange(pieces)
 
-    left, sums = call(
+    store, sums = call(
         rest_kernel,
         "rest_left",
-        [where, cent, late_flipped],
-        ALL[:2],
-        fetched=(1, 2),
-        stored=(0, 1),
-        kept=(left, sums),
+        [where, cent, side, late_flipped],
+        ALL[:1],
+        store=store,
+        puts=((SHARD_PAIR, pl.ds(4, 2)), (SHARD_PAIR, pl.ds(6, 2))),
+        fetched=(1, 3),
+        stored=(0,),
+        kept=(sums,),
         pair=2,
-    )
-    prior = after(prior, left)
+        span=2,
+        us=4,
+    )
+    prior = after(prior, sums)
     prior_behind = to_chan(prior, lambda s: s + 2)
     prior_ahead = to_chan(prior, lambda s: s - 2)
     arrived, prior_behind, prior_ahead = lax.optimization_barrier(
@@ -616,8 +640,8 @@
     ahead_means = to_chan(own_means, lambda s: s - 2)
     behind_means = to_chan(own_means, lambda s: s + 2)
     far_means = to_chan(own_means, lambda s: s + 4)
-    turned, cols, coef, prefix, suffix = prep_terms(
-        where, sums, gram, stat, own_means, ahead_means, behind_means, far_means, flags
+    store = prep_terms(
+        where, sums, gram, stat, own_means, ahead_means, behind_means, far_means, flags, store
     )
     prior_behind, prior_ahead, _ = lax.optimization_barrier((prior_behind, prior_ahead, flags))
     half = HALO // 2
@@ -634,18 +658,19 @@
     window_cov = call(
         window_kernel,
         "window_output",
-        [where, mine, to_chan(mine, lambda s: s ^ 1), gram, after(stat, coef), late_total],
+        [where, mine, to_chan(mine, lambda s: s ^ 1), gram, stat, late_total],
         [array(1, WIDTH, CHIPS * PAIR)],
         fetched=(3, 4, 5),
         stored=(0,),
         scratch=[((HALO, PAIR), BF16), ((WIDTH, HALO), BF16), ((WIDTH, WIDTH), F32)],
+        us=0.1,
     )[0]
-    back, coef, window_cov = lax.optimization_barrier((back, coef, window_cov))
+    back, store, window_cov = lax.optimization_barrier((back, store, window_cov))
     before = to_chan(back[16:24, 0:32], lambda s: s + 2)
     following = to_chan(back[24:32, 0:32], lambda s: (s - 2) ^ 1)
     opposite = to_chan(back[:, 32:40], lambda s: s + 4 if s < 4 else (s - 4) ^ 1)
     cusum, segment_cov = outputs(
-        where, back, opposite, following, before, left, prefix, suffix, cols, turned, coef
+        where, back, opposite, following, before, store
     )
     return window_cov, segment_cov, cusum
 

time: 122 us -> 110 us (0.902); the launches traced: 120 us -> 110 us
  local copies, waits for them, and re-layouts: 14.7 us -> 4.44 us
  Pallas kernels: 26.5 us -> 31.1 us
  waiting for transfers between devices: 27.1 us -> 24 us
  starting transfers between devices: 50.3 us -> 48.4 us
    unnamed x27 -> x9, local copies, waits for them, and re-layouts: 12.8 us -> 1.89 us
    pallas_call x8, Pallas kernels: 21.5 us -> 24.3 us  [call(): pl.pallas_call(body, out_shape=[STORE] * first + outputs, grid=(1,), in_s...]
    all_to_all x2, waiting for transfers between devices: 1.71 us -> 0.01 us  [exchange(): return lax.all_to_all(value, 'tm', 0, 0, tiled=True)]
    pallas_call x1, Pallas kernels: 5.06 us -> 6.71 us  [outputs(): pl.pallas_call(output_kernel, out_shape=OUTPUTS, grid=(1,), in_specs=[SM]...]
    ppermute x19, starting transfers between devices: 29.8 us -> 28.1 us  [to_chan(): lax.ppermute(value, 'chan', [(s, target(s) % count) for s in range(count)])]
    ppermute x19, waiting for transfers between devices: 25.4 us -> 24 us  [to_chan(): lax.ppermute(value, 'chan', [(s, target(s) % count) for s in range(count)])]
  transfers between devices with their start and end apart: 22 -> 22, of which waited for: 10 -> 10; matrix products, arithmetic and copies ran while one was open for 2% -> 2% of each run, Pallas kernels for 15% -> 19%
where the time goes in v2:
time: 110 us
  starting transfers between devices  48.4 us (44%)
  Pallas kernels  31.1 us (28%)
  waiting for transfers between devices  24 us (22%)
  local copies, waits for them, and re-layouts  4.44 us (4%)
  between operations  1.8 us (2%)
    ppermute x19, starting transfers between devices, to_chan(): lax.ppermute(value, 'chan', [(s, target(s) % count) for s in range(count)])  28.1 us
    pallas_call x8, Pallas kernels, call(): pl.pallas_call(body, out_shape=[STORE] * first + outputs, grid=(1,), in_s...  24.3 us
    ppermute x19, waiting for transfers between devices, to_chan(): lax.ppermute(value, 'chan', [(s, target(s) % count) for s in range(count)])  24 us
    all_to_all x2, starting transfers between devices, exchange(): return lax.all_to_all(value, 'tm', 0, 0, tiled=True)  18.5 us
    pallas_call x1, Pallas kernels, outputs(): pl.pallas_call(output_kernel, out_shape=OUTPUTS, grid=(1,), in_specs=[SM]...  6.71 us
  transfers between devices with their start and end apart: 22, of which 10 were waited for; matrix products, arithmetic and copies ran while one was open for 2% of the time, Pallas kernels for 19%

profile of v2, /device:TPU:1, one launch (start us, length us, event | category | flops | bytes accessed | tf_op | source)
XLA Modules:
  0.0 109.8 jit_solution(17643956336583085992)
XLA Ops:
  0.6 3.3 %collective-permute-start.3 = (bf16[2048,128]{1,0:T(8,128)(2,1)}, bf16[2048,128]{1,0:T(8,128)(2,1)S(1)}, u32[]{:S(2)}, u32[]{:S(2)}) collective-permute-start(bf16[2048,128]{1,0:T(8,128)(2,1)} %refs_1_.1), channel_id=1, source_target_pairs={{0,1},{1,0},{2,3},{3,2},{4,5},{5,4},{6,7},{7,6},{8,9},{9,8},{10,11... | collective-permute-start | bytes 1572872 | tf_op jit(solution)/shard_map/ppermute | solution.py:530
  4.0 2.7 %collective-permute-start.1 = (bf16[2048,128]{1,0:T(8,128)(2,1)}, bf16[2048,128]{1,0:T(8,128)(2,1)S(1)}, u32[]{:S(2)}, u32[]{:S(2)}) collective-permute-start(bf16[2048,128]{1,0:T(8,128)(2,1)} %refs_1_.1), channel_id=1, source_target_pairs={{0,6},{1,7},{2,0},{3,1},{4,2},{5,3},{6,4},{7,5},{8,14},{9,15},{10,... | collective-permute-start | bytes 1572872 | tf_op jit(solution)/shard_map/ppermute | solution.py:530
  7.7 1.8 %collective-permute-start.2 = (bf16[1024,128]{1,0:T(8,128)(2,1)S(1)}, bf16[1024,128]{1,0:T(8,128)(2,1)S(1)}, u32[]{:S(2)}, u32[]{:S(2)}) collective-permute-start(bf16[1024,128]{1,0:T(8,128)(2,1)S(1)} %slice.24), channel_id=1, source_target_pairs={{0,8},{8,16},{16,24},{24,32},{32,40},{40,48},{48,56},{56,64},{64,7... | collective-permute-start | bytes 786440 | tf_op jit(solution)/shard_map/ppermute | solution.py:554
  12.0 4.1 %first_pair.1 = (f32[96,8,128,128]{3,2,1,0:T(8,128)}, f32[4,8,256]{2,1,0:T(8,128)S(1)}, f32[4,128,256]{2,1,0:T(8,128)S(1)}, f32[4,8,256]{2,1,0:T(8,128)S(1)}, bf...) custom-call(s32[21]{0:T(128)S(1)} %concatenate.9.refs_0_.where_ref, ...), custom_call_target="tpu_custom_call" | custom-call | flops 3000000000 | bytes 1048576 | tf_op jit(solution)/shard_map/first_pair/pallas_call | solution.py:212
  16.1 2.8 %collective-permute-done.refs_2_ = bf16[2048,128]{1,0:T(8,128)(2,1)S(1)} collective-permute-done((bf16[2048,128]{1,0:T(8,128)(2,1)}, bf16[2048,128]{1,0:T(8,128)(2,1)S(1)}, u32[]{:S(2)}, u32[]{:S(2)}) %collective-permute-start) | collective-permute-done | bytes 524320 | tf_op jit(solution)/shard_map/ppermute | solution.py:530
  19.9 2.8 %collective-permute-start.5 = (bf16[1024,128]{1,0:T(8,128)(2,1)S(1)}, bf16[1024,128]{1,0:T(8,128)(2,1)S(1)}, u32[]{:S(2)}, u32[]{:S(2)}) collective-permute-start(bf16[1024,128]{1,0:T(8,128)(2,1)S(1)} %slice.26), channel_id=1, source_target_pairs={{0,6},{1,7},{2,0},{3,1},{4,2},{5,3},{6,4},{7,5},{8,14},{9,15},{10,... | collective-permute-start | bytes 786440 | tf_op jit(solution)/shard_map/ppermute | solution.py:530
  22.6 3.8 %near_pair.1 = (f32[96,8,128,128]{3,2,1,0:T(8,128)}, f32[4,8,256]{2,1,0:T(8,128)S(1)}, f32[4,128,256]{2,1,0:T(8,128)S(1)}, f32[4,8,256]{2,1,0:T(8,128)S(1)}, f32[128,256]{1,0:T(8,128)S(1)}) custom-call(s32[21]{0:T(128)S(1)} %concatenate.9.refs_0_.where_ref, ...), custom_call_target="tpu_custom_call", output_to_operand_aliasing={{0}: (5, {}), {1}: (6, {}), {2}: (7, {}), {3}: (8, {})} | custom-call | flops 3000000000 | bytes 1048576 | tf_op jit(solution)/shard_map/near_pair/pallas_call | solution.py:212
  26.5 1.8 %side_pair.1 = (f32[4,128,256]{2,1,0:T(8,128)S(1)}, f32[4,8,256]{2,1,0:T(8,128)S(1)}, bf16[2048,256]{1,0:T(8,128)(2,1)S(1)}) custom-call(s32[21]{0:T(128)S(1)} %concatenate.9.refs_0_.where_ref, bf16[2048,128]{1,0:T(8,128)(2,1)S(1)} %collective-permute-done.6.refs_1_, ...), custom_call_target="tpu_custom_call", output_to_operand_aliasing={{0}: (4, {}), {1}: (5, {})} | custom-call | flops 100000000 | bytes 1048576 | tf_op jit(solution)/shard_map/side_pair/pallas_call | solution.py:212
  31.5 1.9 %far_pair.1 = (f32[4,128,256]{2,1,0:T(8,128)S(1)}, f32[4,8,256]{2,1,0:T(8,128)S(1)}, f32[32,24,128]{2,1,0:T(8,128)S(1)}, bf16[2048,256]{1,0:T(8,128)(2,1)S(1)}) custom-call(s32[21]{0:T(128)S(1)} %concatenate.9.refs_0_.where_ref, bf16[2048,128]{1,0:T(8,128)(2,1)S(1)} %constant_dynamic-update-slice_fusion.refs_1_, ...), custom_call_target="tpu_custom_call", output_to_operand_aliasing={{0}: (8, {}), {1}: (9, {})} | custom-call | flops 100000000 | bytes 1048576 | tf_op jit(solution)/shard_map/far_pair/pallas_call | solution.py:212
  34.1 9.8 %all-to-all-start = ((f32[32,24,128]{2,1,0:T(8,128)}), f32[32,24,128]{2,1,0:T(8,128)}, u32[]{:S(2)}, u32[]{:S(2)}) async-start(f32[32,24,128]{2,1,0:T(8,128)} %copy-done), calls=%async_computation | async-start | bytes 786432 | tf_op jit(solution)/shard_map/all_to_all | solution.py:534
  43.9 4.3 %rest_left.1 = (f32[96,8,128,128]{3,2,1,0:T(8,128)}, f32[4,8,256]{2,1,0:T(8,128)S(1)}) custom-call(s32[21]{0:T(128)S(1)} %concatenate.9.refs_0_.where_ref, bf16[2048,256]{1,0:T(8,128)(2,1)S(1)} %get-tuple-element.69.refs_1_, bf16[2048,256]{1,0:T(8,128)(2,1)S(1)} %get-tuple-element.70.refs_2_, ...), custom_call_target="tpu_custom_call", output_to_operand_aliasing={{0}: (4, {}), {1}: (5, {})} | custom-call | flops 4000000000 | bytes 1048576 | tf_op jit(solution)/shard_map/rest_left/pallas_call | solution.py:212
  48.2 2.8 %collective-permute-start.10 = (bf16[1024,128]{1,0:T(8,128)(2,1)S(1)}, bf16[1024,128]{1,0:T(8,128)(2,1)S(1)}, u32[]{:S(2)}, u32[]{:S(2)}) collective-permute-start(bf16[1024,128]{1,0:T(8,128)(2,1)S(1)} %collective-permute-done.2), channel_id=1, source_target_pairs={{0,6},{1,7},{2,0},{3,1},{4,2},{5,3},{6,4},{7,5},{8,14},{9,15},{10,... | collective-permute-start | bytes 786440 | tf_op jit(solution)/shard_map/ppermute | solution.py:530
  51.0 5.0 %collective-permute-done.10 = bf16[1024,128]{1,0:T(8,128)(2,1)S(1)} collective-permute-done((bf16[1024,128]{1,0:T(8,128)(2,1)S(1)}, bf16[1024,128]{1,0:T(8,128)(2,1)S(1)}, u32[]{:S(2)}, u32[]{:S(2)}) %collective-permute-start.10) | collective-permute-done | bytes 262176 | tf_op jit(solution)/shard_map/ppermute | solution.py:530
  56.0 3.1 %collective-permute-done.9 = bf16[1024,128]{1,0:T(8,128)(2,1)S(1)} collective-permute-done((bf16[1024,128]{1,0:T(8,128)(2,1)S(1)}, bf16[1024,128]{1,0:T(8,128)(2,1)S(1)}, u32[]{:S(2)}, u32[]{:S(2)}) %collective-permute-start.9) | collective-permute-done | bytes 262176 | tf_op jit(solution)/shard_map/ppermute | solution.py:530
  59.1 2.0 %scan_pieces.1 = (f32[32,40,128]{2,1,0:T(8,128)}, f32[2,32,128]{2,1,0:T(8,128)S(1)}, f32[32,128]{1,0:T(8,128)S(1)}) custom-call(f32[32,24,128]{2,1,0:T(8,128)} %all-to-all-done.refs_0_), custom_call_target="tpu_custom_call" | custom-call | flops 1000000000 | bytes 1048576 | tf_op jit(solution)/shard_map/scan_pieces/pallas_call | solution.py:212
  61.8 2.8 %collective-permute-start.15 = (bf16[512,128]{1,0:T(8,128)(2,1)S(1)}, bf16[512,128]{1,0:T(8,128)(2,1)S(1)}, u32[]{:S(2)}, u32[]{:S(2)}) collective-permute-start(bf16[512,128]{1,0:T(8,128)(2,1)S(1)} %slice.28), channel_id=1, source_target_pairs={{0,6},{1,7},{2,0},{3,1},{4,2},{5,3},{6,4},{7,5},{8,14},{9,15},{10,... | collective-permute-start | bytes 393224 | tf_op jit(solution)/shard_map/ppermute | solution.py:530
  64.6 8.7 %all-to-all-start.1 = ((f32[32,40,128]{2,1,0:T(8,128)}), f32[32,40,128]{2,1,0:T(8,128)S(1)}, u32[]{:S(2)}, u32[]{:S(2)}) async-start(f32[32,40,128]{2,1,0:T(8,128)} %get-tuple-element.77), calls=%async_computation.1 | async-start | bytes 1310720 | tf_op jit(solution)/shard_map/all_to_all | solution.py:534
  73.5 3.1 %collective-permute-start.16 = (bf16[4096,128]{1,0:T(8,128)(2,1)S(1)}, bf16[4096,128]{1,0:T(8,128)(2,1)S(1)}, u32[]{:S(2)}, u32[]{:S(2)}) collective-permute-start(bf16[4096,128]{1,0:T(8,128)(2,1)S(1)} %constant_dynamic-update-slice_fusion.2.refs_1_), channel_id=1, source_target_pairs={{0,1},{1,0},{2,3},{3,2},{4,5},{5,4},{6,7},{7,6},{8,9},{9,8},{10,11... | collective-permute-start | bytes 3145736 | tf_op jit(solution)/shard_map/ppermute | solution.py:530
  78.0 1.6 %collective-permute-done.11.refs_5_ = f32[2,32,128]{2,1,0:T(8,128)S(1)} collective-permute-done((f32[2,32,128]{2,1,0:T(8,128)S(1)}, f32[2,32,128]{2,1,0:T(8,128)S(1)}, u32[]{:S(2)}, u32[]{:S(2)}) %collective-permute-start.11) | collective-permute-done | bytes 32800 | tf_op jit(solution)/shard_map/ppermute | solution.py:530
  82.3 3.0 %prep_terms.1.store_hbm = f32[96,8,128,128]{3,2,1,0:T(8,128)} custom-call(s32[21]{0:T(128)S(1)} %concatenate.9.refs_0_.where_ref, f32[4,8,256]{2,1,0:T(8,128)S(1)} %get-tuple-element.74.refs_1_, f32[4,128,256]{2,1,0:T(8,128)S(1)} %get-tuple-element.78.refs_2_.refs_3_, ...), custom_call_target="tpu_custom_call", output_to_operand_aliasing={{}: (9, {})} | custom-call | flops 100000000 | bytes 1048576 | tf_op jit(solution)/shard_map/prep_terms/pallas_call | solution.py:212
  85.3 3.5 %window_output.1 = f32[1,128,1024]{2,1,0:T(8,128)} custom-call(s32[21]{0:T(128)S(1)} %concatenate.9.refs_0_.where_ref, bf16[4096,128]{1,0:T(8,128)(2,1)S(1)} %constant_dynamic-update-slice_fusion.2.refs_1_, bf16[4096,128]{1,0:T(8,128)(2,1)S(1)} %collective-permute-done.16.refs_2_, f32[4,128,256]{2,1,0:T(8,128)S(1)} %get-tuple-element.78.refs_2_.refs_3_, ...), custom_call_target="tpu_custom_call" | custom-call | flops 100000000 | bytes 1048576 | tf_op jit(solution)/shard_map/window_output/pallas_call | solution.py:212
  88.9 5.3 %collective-permute-start.18 = (f32[8,32,128]{2,1,0:T(8,128)S(1)}, f32[8,32,128]{2,1,0:T(8,128)S(1)}, u32[]{:S(2)}, u32[]{:S(2)}) collective-permute-start(f32[8,32,128]{2,1,0:T(8,128)S(1)} %get-tuple-element.94), channel_id=1, source_target_pairs={{0,7},{1,6},{2,1},{3,0},{4,3},{5,2},{6,5},{7,4},{8,15},{9,14},{10,... | collective-permute-start | bytes 393224 | tf_op jit(solution)/shard_map/ppermute | solution.py:530
  97.3 5.6 %collective-permute-done.19.before_ref = f32[8,32,128]{2,1,0:T(8,128)S(1)} collective-permute-done((f32[8,32,128]{2,1,0:T(8,128)S(1)}, f32[8,32,128]{2,1,0:T(8,128)S(1)}, u32[]{:S(2)}, u32[]{:S(2)}) %collective-permute-start.19) | collective-permute-done | bytes 131104 | tf_op jit(solution)/shard_map/ppermute | solution.py:530
  102.9 6.7 %outputs.1 = (f32[1,8,128,1024]{3,2,1,0:T(8,128)}, f32[1,128,1024]{2,1,0:T(8,128)}) custom-call(s32[21]{0:T(128)S(1)} %concatenate.9.refs_0_.where_ref, f32[32,40,128]{2,1,0:T(8,128)S(1)} %all-to-all-done.1.back_ref, f32[32,8,128]{2,1,0:T(8,128)S(1)} %collective-permute-done.17.opposite_ref, f32[8,32,128]{2,1,0:T(8,128)S(1)} %collective-permute-done.18.next_ref, ...), custom_call_target="tpu_custom_call" | custom-call | flops 5000000000 | bytes 1048576 | tf_op jit(solution)/shard_map/outputs/pallas_call | solution.py:472
  (48 shorter events, 15.9 us)
Async XLA Ops:
  0.6 10.3 %collective-permute-start.3 = (bf16[2048,128]{1,0:T(8,128)(2,1)}, bf16[2048,128]{1,0:T(8,128)(2,1)S(1)}, u32[]{:S(2)}, u32[]{:S(2)}) collective-permute-start(bf16[2048,128]{1,0:T(8,128)(2,1)} %refs_1_.1), channel_id=1, source_target_pairs={{0,1},{1,0},{2,3},{3,2},{4,5},{5,4},{6,7},{7,6},{8,9},{9,8},{10,11... | collective-permute-start | bytes 1572872 | tf_op jit(solution)/shard_map/ppermute | solution.py:530
  4.0 14.9 %collective-permute-start = (bf16[2048,128]{1,0:T(8,128)(2,1)}, bf16[2048,128]{1,0:T(8,128)(2,1)S(1)}, u32[]{:S(2)}, u32[]{:S(2)}) collective-permute-start(bf16[2048,128]{1,0:T(8,128)(2,1)} %refs_1_.1), channel_id=1, source_target_pairs={{0,2},{1,3},{2,4},{3,5},{4,6},{5,7},{6,0},{7,1},{8,10},{9,11},{10,... | collective-permute-start | bytes 1572872 | tf_op jit(solution)/shard_map/ppermute | solution.py:530
  4.0 14.9 %collective-permute-start.1 = (bf16[2048,128]{1,0:T(8,128)(2,1)}, bf16[2048,128]{1,0:T(8,128)(2,1)S(1)}, u32[]{:S(2)}, u32[]{:S(2)}) collective-permute-start(bf16[2048,128]{1,0:T(8,128)(2,1)} %refs_1_.1), channel_id=1, source_target_pairs={{0,6},{1,7},{2,0},{3,1},{4,2},{5,3},{6,4},{7,5},{8,14},{9,15},{10,... | collective-permute-start | bytes 1572872 | tf_op jit(solution)/shard_map/ppermute | solution.py:530
  7.7 8.4 %collective-permute-start.2 = (bf16[1024,128]{1,0:T(8,128)(2,1)S(1)}, bf16[1024,128]{1,0:T(8,128)(2,1)S(1)}, u32[]{:S(2)}, u32[]{:S(2)}) collective-permute-start(bf16[1024,128]{1,0:T(8,128)(2,1)S(1)} %slice.24), channel_id=1, source_target_pairs={{0,8},{8,16},{16,24},{24,32},{32,40},{40,48},{48,56},{56,64},{64,7... | collective-permute-start | bytes 786440 | tf_op jit(solution)/shard_map/ppermute | solution.py:554
  11.0 1.0 copy-start.1
  18.9 3.8 %collective-permute-start.7 = (bf16[2048,128]{1,0:T(8,128)(2,1)S(1)}, bf16[2048,128]{1,0:T(8,128)(2,1)S(1)}, u32[]{:S(2)}, u32[]{:S(2)}) collective-permute-start(bf16[2048,128]{1,0:T(8,128)(2,1)S(1)} %collective-permute-done.refs_2_), channel_id=1, source_target_pairs={{0,1},{1,0},{2,3},{3,2},{4,5},{5,4},{6,7},{7,6},{8,9},{9,8},{10,11... | collective-permute-start | bytes 1572872 | tf_op jit(solution)/shard_map/ppermute | solution.py:530
  19.7 6.7 %collective-permute-start.6 = (bf16[2048,128]{1,0:T(8,128)(2,1)S(1)}, bf16[2048,128]{1,0:T(8,128)(2,1)S(1)}, u32[]{:S(2)}, u32[]{:S(2)}) collective-permute-start(bf16[2048,128]{1,0:T(8,128)(2,1)S(1)} %collective-permute-done.1.refs_1_), channel_id=1, source_target_pairs={{0,1},{1,0},{2,3},{3,2},{4,5},{5,4},{6,7},{7,6},{8,9},{9,8},{10,11... | collective-permute-start | bytes 1572872 | tf_op jit(solution)/shard_map/ppermute | solution.py:530
  19.8 8.7 %collective-permute-start.4 = (bf16[1024,128]{1,0:T(8,128)(2,1)S(1)}, bf16[1024,128]{1,0:T(8,128)(2,1)S(1)}, u32[]{:S(2)}, u32[]{:S(2)}) collective-permute-start(bf16[1024,128]{1,0:T(8,128)(2,1)S(1)} %slice.25), channel_id=1, source_target_pairs={{0,2},{1,3},{2,4},{3,5},{4,6},{5,7},{6,0},{7,1},{8,10},{9,11},{10,... | collective-permute-start | bytes 786440 | tf_op jit(solution)/shard_map/ppermute | solution.py:530
  19.9 8.6 %collective-permute-start.5 = (bf16[1024,128]{1,0:T(8,128)(2,1)S(1)}, bf16[1024,128]{1,0:T(8,128)(2,1)S(1)}, u32[]{:S(2)}, u32[]{:S(2)}) collective-permute-start(bf16[1024,128]{1,0:T(8,128)(2,1)S(1)} %slice.26), channel_id=1, source_target_pairs={{0,6},{1,7},{2,0},{3,1},{4,2},{5,3},{6,4},{7,5},{8,14},{9,15},{10,... | collective-permute-start | bytes 786440 | tf_op jit(solution)/shard_map/ppermute | solution.py:530
  28.5 3.0 %collective-permute-start.8 = (bf16[2048,128]{1,0:T(8,128)(2,1)S(1)}, bf16[2048,128]{1,0:T(8,128)(2,1)S(1)}, u32[]{:S(2)}, u32[]{:S(2)}) collective-permute-start(bf16[2048,128]{1,0:T(8,128)(2,1)S(1)} %constant_dynamic-update-slice_fusion.refs_1_), channel_id=1, source_target_pairs={{0,1},{1,0},{2,3},{3,2},{4,5},{5,4},{6,7},{7,6},{8,9},{9,8},{10,11... | collective-permute-start | bytes 1572872 | tf_op jit(solution)/shard_map/ppermute | solution.py:530
  33.4 0.7 copy-start
  34.1 25.0 %all-to-all-start = ((f32[32,24,128]{2,1,0:T(8,128)}), f32[32,24,128]{2,1,0:T(8,128)}, u32[]{:S(2)}, u32[]{:S(2)}) async-start(f32[32,24,128]{2,1,0:T(8,128)} %copy-done), calls=%async_computation | async-start | bytes 786432 | tf_op jit(solution)/shard_map/all_to_all | solution.py:534
  48.2 7.8 %collective-permute-start.10 = (bf16[1024,128]{1,0:T(8,128)(2,1)S(1)}, bf16[1024,128]{1,0:T(8,128)(2,1)S(1)}, u32[]{:S(2)}, u32[]{:S(2)}) collective-permute-start(bf16[1024,128]{1,0:T(8,128)(2,1)S(1)} %collective-permute-done.2), channel_id=1, source_target_pairs={{0,6},{1,7},{2,0},{3,1},{4,2},{5,3},{6,4},{7,5},{8,14},{9,15},{10,... | collective-permute-start | bytes 786440 | tf_op jit(solution)/shard_map/ppermute | solution.py:530
  51.0 8.1 %collective-permute-start.9 = (bf16[1024,128]{1,0:T(8,128)(2,1)S(1)}, bf16[1024,128]{1,0:T(8,128)(2,1)S(1)}, u32[]{:S(2)}, u32[]{:S(2)}) collective-permute-start(bf16[1024,128]{1,0:T(8,128)(2,1)S(1)} %collective-permute-done.2), channel_id=1, source_target_pairs={{0,2},{1,3},{2,4},{3,5},{4,6},{5,7},{6,0},{7,1},{8,10},{9,11},{10,... | collective-permute-start | bytes 786440 | tf_op jit(solution)/shard_map/ppermute | solution.py:530
  61.8 11.6 %collective-permute-start.14 = (bf16[512,128]{1,0:T(8,128)(2,1)}, bf16[512,128]{1,0:T(8,128)(2,1)S(1)}, u32[]{:S(2)}, u32[]{:S(2)}) collective-permute-start(bf16[512,128]{1,0:T(8,128)(2,1)} %slice.27), channel_id=1, source_target_pairs={{0,2},{1,3},{2,4},{3,5},{4,6},{5,7},{6,0},{7,1},{8,10},{9,11},{10,... | collective-permute-start | bytes 393224 | tf_op jit(solution)/shard_map/ppermute | solution.py:530
  61.8 11.6 %collective-permute-start.15 = (bf16[512,128]{1,0:T(8,128)(2,1)S(1)}, bf16[512,128]{1,0:T(8,128)(2,1)S(1)}, u32[]{:S(2)}, u32[]{:S(2)}) collective-permute-start(bf16[512,128]{1,0:T(8,128)(2,1)S(1)} %slice.28), channel_id=1, source_target_pairs={{0,6},{1,7},{2,0},{3,1},{4,2},{5,3},{6,4},{7,5},{8,14},{9,15},{10,... | collective-permute-start | bytes 393224 | tf_op jit(solution)/shard_map/ppermute | solution.py:530
  64.6 24.2 %all-to-all-start.1 = ((f32[32,40,128]{2,1,0:T(8,128)}), f32[32,40,128]{2,1,0:T(8,128)S(1)}, u32[]{:S(2)}, u32[]{:S(2)}) async-start(f32[32,40,128]{2,1,0:T(8,128)} %get-tuple-element.77), calls=%async_computation.1 | async-start | bytes 1310720 | tf_op jit(solution)/shard_map/all_to_all | solution.py:534
  73.5 11.8 %collective-permute-start.16 = (bf16[4096,128]{1,0:T(8,128)(2,1)S(1)}, bf16[4096,128]{1,0:T(8,128)(2,1)S(1)}, u32[]{:S(2)}, u32[]{:S(2)}) collective-permute-start(bf16[4096,128]{1,0:T(8,128)(2,1)S(1)} %constant_dynamic-update-slice_fusion.2.refs_1_), channel_id=1, source_target_pairs={{0,1},{1,0},{2,3},{3,2},{4,5},{5,4},{6,7},{7,6},{8,9},{9,8},{10,11... | collective-permute-start | bytes 3145736 | tf_op jit(solution)/shard_map/ppermute | solution.py:530
  76.5 3.1 %collective-permute-start.11 = (f32[2,32,128]{2,1,0:T(8,128)S(1)}, f32[2,32,128]{2,1,0:T(8,128)S(1)}, u32[]{:S(2)}, u32[]{:S(2)}) collective-permute-start(f32[2,32,128]{2,1,0:T(8,128)S(1)} %get-tuple-element.80.refs_4_), channel_id=1, source_target_pairs={{0,6},{1,7},{2,0},{3,1},{4,2},{5,3},{6,4},{7,5},{8,14},{9,15},{10,... | collective-permute-start | bytes 98312 | tf_op jit(solution)/shard_map/ppermute | solution.py:530
  76.5 4.3 %collective-permute-start.12 = (f32[2,32,128]{2,1,0:T(8,128)S(1)}, f32[2,32,128]{2,1,0:T(8,128)S(1)}, u32[]{:S(2)}, u32[]{:S(2)}) collective-permute-start(f32[2,32,128]{2,1,0:T(8,128)S(1)} %get-tuple-element.80.refs_4_), channel_id=1, source_target_pairs={{0,2},{1,3},{2,4},{3,5},{4,6},{5,7},{6,0},{7,1},{8,10},{9,11},{10,... | collective-permute-start | bytes 98312 | tf_op jit(solution)/shard_map/ppermute | solution.py:530
  78.0 4.3 %collective-permute-start.13 = (f32[2,32,128]{2,1,0:T(8,128)S(1)}, f32[2,32,128]{2,1,0:T(8,128)S(1)}, u32[]{:S(2)}, u32[]{:S(2)}) collective-permute-start(f32[2,32,128]{2,1,0:T(8,128)S(1)} %get-tuple-element.80.refs_4_), channel_id=1, source_target_pairs={{0,4},{1,5},{2,6},{3,7},{4,0},{5,1},{6,2},{7,3},{8,12},{9,13},{10,... | collective-permute-start | bytes 98312 | tf_op jit(solution)/shard_map/ppermute | solution.py:530
  88.9 8.4 %collective-permute-start.18 = (f32[8,32,128]{2,1,0:T(8,128)S(1)}, f32[8,32,128]{2,1,0:T(8,128)S(1)}, u32[]{:S(2)}, u32[]{:S(2)}) collective-permute-start(f32[8,32,128]{2,1,0:T(8,128)S(1)} %get-tuple-element.94), channel_id=1, source_target_pairs={{0,7},{1,6},{2,1},{3,0},{4,3},{5,2},{6,5},{7,4},{8,15},{9,14},{10,... | collective-permute-start | bytes 393224 | tf_op jit(solution)/shard_map/ppermute | solution.py:530
  94.2 8.6 %collective-permute-start.19 = (f32[8,32,128]{2,1,0:T(8,128)S(1)}, f32[8,32,128]{2,1,0:T(8,128)S(1)}, u32[]{:S(2)}, u32[]{:S(2)}) collective-permute-start(f32[8,32,128]{2,1,0:T(8,128)S(1)} %get-tuple-element.93), channel_id=1, source_target_pairs={{0,2},{1,3},{2,4},{3,5},{4,6},{5,7},{6,0},{7,1},{8,10},{9,11},{10,... | collective-permute-start | bytes 393224 | tf_op jit(solution)/shard_map/ppermute | solution.py:530
  95.7 7.1 %collective-permute-start.17 = (f32[32,8,128]{2,1,0:T(8,128)S(1)}, f32[32,8,128]{2,1,0:T(8,128)S(1)}, u32[]{:S(2)}, u32[]{:S(2)}) collective-permute-start(f32[32,8,128]{2,1,0:T(8,128)S(1)} %slice.29), channel_id=1, source_target_pairs={{0,4},{1,5},{2,6},{3,7},{4,1},{5,0},{6,3},{7,2},{8,12},{9,13},{10,... | collective-permute-start | bytes 393224 | tf_op jit(solution)/shard_map/ppermute | solution.py:530

commit v3 on v2

--- a/solution.py
+++ b/solution.py
@@ -382,9 +382,13 @@
         s_ref[4 * q : 4 * q + 4, :] = ref[q, 4:8, :]
 
 
-def output_kernel(
-    where_ref, back_ref, opposite_ref, next_ref, before_ref, store_hbm, cusum_hbm, seg_hbm,
-    left_ref, prefix_ref, suffix_ref, cols_ref, turned_ref, coef_ref, cusum_ref, seg_ref, p_ref, s_ref, sem, out_sem,
+def shard_lanes(where_ref, u):
+    return pl.ds(pl.multiple_of(where_ref[4 + u] * WIDTH, WIDTH), WIDTH)
+
+
+def most_kernel(
+    where_ref, back_ref, store_hbm, most_ref, seg_ref, coef_ref,
+    left_ref, prefix_ref, suffix_ref, cols_ref, turned_ref, p_ref, s_ref, sem,
 ):
     loads = [
         pltpu.make_async_copy(source, target, sem.at[c])
@@ -405,55 +409,62 @@
     for load in loads[:5]:
         load.wait()
 
-    def add(u, turn):
-        prefix, suffix = p_ref[...], s_ref[...]
-        if turn:
-            prefix, suffix = prefix.T, suffix.T
-        prefix_ref[u] = prefix_ref[u] + prefix
-        suffix_ref[u] = suffix_ref[u] + suffix
+    def add(u):
+        prefix_ref[u] = prefix_ref[u] + p_ref[...]
+        suffix_ref[u] = suffix_ref[u] + s_ref[...]
 
     for u in range(4):
         load_near(back_ref.at[pl.ds(8 * u, 8)], p_ref, s_ref)
-        add(u, False)
+        add(u)
     load_far(back_ref.at[:, pl.ds(32, 8)], p_ref, s_ref)
-    add(4 + held, False)
-    load_far(opposite_ref, p_ref, s_ref)
-    add(5 - held, True)
-    load_near(next_ref, p_ref, s_ref)
-    add(6, True)
-    load_near(before_ref, p_ref, s_ref)
-    add(7, True)
-
-    def spread_out(row, count):
-        return [
-            jnp.broadcast_to(turned_ref[:, i : i + 1], (WIDTH, WIDTH))
-            for i in range(row, 35, 8 if count == 4 else 1)
-        ][:count]
-
-    def lanes(u):
-        return pl.ds(pl.multiple_of(where_ref[4 + u] * WIDTH, WIDTH), WIDTH)
-
-    turned = spread_out(32, 3)
+    add(4 + held)
+
+    def spread_out(rows):
+        return [jnp.broadcast_to(turned_ref[:, i : i + 1], (WIDTH, WIDTH)) for i in rows]
+
+    turned = spread_out(range(32, 35))
     for u in range(8):
         value = (prefix_ref[u] + suffix_ref[u]) * coef_ref[16:17, :]
         for i in range(3):
             value = value + turned[i] * cols_ref[u, 32 + i : 33 + i, :]
-        seg_ref[0, :, lanes(u)] = value
-    store = pltpu.make_async_copy(seg_ref, seg_hbm, out_sem.at[SPLITS])
-    store.start()
-    stores = [store]
+        seg_ref[:, shard_lanes(where_ref, u)] = value
     loads[5].wait()
     for j in range(SPLITS):
-        turned = spread_out(j, 4)
+        turned = spread_out(range(j, 32, 8))
         a, b = coef_ref[j : j + 1, :], coef_ref[8 + j : 9 + j, :]
         for u in range(8):
-            value = (a + b) * left_ref[u, j]
-            value = value + a * prefix_ref[u] - b * suffix_ref[u]
+            value = (a + b) * left_ref[u, j] + a * prefix_ref[u] - b * suffix_ref[u]
             for i in range(4):
                 value = value + turned[i] * cols_ref[u, 8 * i + j : 8 * i + j + 1, :]
-            cusum_ref[0, j, :, lanes(u)] = value
+            most_ref[j, :, shard_lanes(where_ref, u)] = value
+
+
+def last_kernel(
+    where_ref, most_ref, most_seg_ref, coef_ref, opposite_ref, next_ref, before_ref, cusum_hbm, seg_hbm,
+    cusum_ref, seg_ref, prefix_ref, suffix_ref, p_ref, s_ref, sem,
+):
+    shards = (5 - where_ref[3], 6, 7)
+    for v, (ref, load) in enumerate(
+        ((opposite_ref, load_far), (next_ref, load_near), (before_ref, load_near))
+    ):
+        load(ref, p_ref, s_ref)
+        prefix_ref[v] = p_ref[...].T
+        suffix_ref[v] = s_ref[...].T
+    seg_ref[0] = most_seg_ref[...]
+    for v, u in enumerate(shards):
+        lanes = shard_lanes(where_ref, u)
+        added = (prefix_ref[v] + suffix_ref[v]) * coef_ref[16:17, :]
+        seg_ref[0, :, lanes] = most_seg_ref[:, lanes] + added
+    stores = [pltpu.make_async_copy(seg_ref, seg_hbm, sem.at[SPLITS])]
+    stores[0].start()
+    for j in range(SPLITS):
+        a, b = coef_ref[j : j + 1, :], coef_ref[8 + j : 9 + j, :]
+        cusum_ref[0, j] = most_ref[j]
+        for v, u in enumerate(shards):
+            lanes = shard_lanes(where_ref, u)
+            cusum_ref[0, j, :, lanes] = most_ref[j, :, lanes] + a * prefix_ref[v] - b * suffix_ref[v]
         store = pltpu.make_async_copy(
-            cusum_ref.at[:, pl.ds(j, 1)], cusum_hbm.at[:, pl.ds(j, 1)], out_sem.at[j]
+            cusum_ref.at[:, pl.ds(j, 1)], cusum_hbm.at[:, pl.ds(j, 1)], sem.at[j]
         )
         store.start()
         stores.append(store)
@@ -462,25 +473,43 @@
 
 
 OUTPUTS = [array(1, SPLITS, WIDTH, CHIPS * PAIR), array(1, WIDTH, CHIPS * PAIR)]
-
-
-def outputs(where, back, opposite, following, before, store):
-    blocks = [back, opposite, following, before]
+MOST = [array(SPLITS, WIDTH, CHIPS * PAIR), array(WIDTH, CHIPS * PAIR), array(24, WIDTH)]
+
+
+def most_outputs(where, back, store):
     square = array(8, WIDTH, WIDTH)
     buffers = [array(8, SPLITS, WIDTH, WIDTH), square, square, array(8, 40, WIDTH)]
-    buffers += [array(WIDTH, WIDTH), array(24, WIDTH), *OUTPUTS, array(WIDTH, WIDTH), array(WIDTH, WIDTH)]
+    buffers += [array(WIDTH, WIDTH)] * 3
     return pl.pallas_call(
-        output_kernel,
+        most_kernel,
+        out_shape=MOST,
+        grid=(1,),
+        in_specs=[SM, whole(*back.shape), HBM],
+        out_specs=[whole(*value.shape) for value in MOST],
+        scratch_shapes=[pltpu.VMEM(value.shape, F32) for value in buffers]
+        + [pltpu.SemaphoreType.DMA((6,))],
+        compiler_params=params(24),
+        cost_estimate=cost(5),
+        name="most_outputs",
+    )(where, back, store)
+
+
+def last_outputs(where, most, opposite, following, before):
+    inputs = [*most, opposite, following, before]
+    buffers = [*OUTPUTS, array(3, WIDTH, WIDTH), array(3, WIDTH, WIDTH)]
+    buffers += [array(WIDTH, WIDTH)] * 2
+    return pl.pallas_call(
+        last_kernel,
         out_shape=OUTPUTS,
         grid=(1,),
-        in_specs=[SM] + [whole(*value.shape) for value in blocks] + [HBM],
+        in_specs=[SM] + [whole(*value.shape) for value in inputs],
         out_specs=[HBM, HBM],
         scratch_shapes=[pltpu.VMEM(value.shape, F32) for value in buffers]
-        + [pltpu.SemaphoreType.DMA((6,)), pltpu.SemaphoreType.DMA((SPLITS + 1,))],
+        + [pltpu.SemaphoreType.DMA((SPLITS + 1,))],
         compiler_params=params(24),
-        cost_estimate=cost(5),
-        name="outputs",
-    )(where, *blocks, store)
+        cost_estimate=cost(3),
+        name="last_outputs",
+    )(where, *inputs)
 
 
 def window_kernel(
@@ -592,7 +621,9 @@
         pair=3,
         us=0.1,
     )
-    far_low, far_high, stat = lax.optimization_barrier((far_low, far_high, stat))
+    far_low, far_high, stat, prior = lax.optimization_barrier((far_low, far_high, stat, prior))
+    prior_behind = to_chan(prior, lambda s: s + 2)
+    prior_ahead = to_chan(prior, lambda s: s - 2)
     far = jnp.concatenate([far_low, far_high], axis=0)
     far_other = to_chan(far, lambda s: s ^ 1)
     gram, stat, pieces, cent = call(
@@ -600,7 +631,7 @@
         "far_pair",
         [where, far, far_other, flipped, total, spread0, spread1, rider],
         ALL[1:] + [array(BLOCKS, 24, WIDTH), cent_shape],
-        stored=(0, 1, 3),
+        stored=(0, 1, 2, 3),
         kept=(gram, stat),
         pair=2,
         scratch=[((WIDTH, WIDTH), F32)],
@@ -608,6 +639,10 @@
     )
     arrived = exchange(pieces)
 
+    cent, prior_behind, prior_ahead = lax.optimization_barrier((cent, prior_behind, prior_ahead))
+    half = HALO // 2
+    prior_low = to_chan(prior_behind[:half], lambda s: s + 2)
+    prior_high = to_chan(prior_ahead[half:], lambda s: s - 2)
     store, sums = call(
         rest_kernel,
         "rest_left",
@@ -622,12 +657,11 @@
         span=2,
         us=4,
     )
-    prior = after(prior, sums)
-    prior_behind = to_chan(prior, lambda s: s + 2)
-    prior_ahead = to_chan(prior, lambda s: s - 2)
-    arrived, prior_behind, prior_ahead = lax.optimization_barrier(
-        (arrived, prior_behind, prior_ahead)
-    )
+    arrived, prior_low, prior_high, sums = lax.optimization_barrier(
+        (arrived, prior_low, prior_high, sums)
+    )
+    prior = jnp.concatenate([prior, prior_ahead, prior_low, prior_high, prior_behind], axis=0)
+    prior_other = to_chan(prior, lambda s: s ^ 1)
     scanned, own_means, flags = call(
         scan_kernel,
         "scan_pieces",
@@ -643,22 +677,10 @@
     store = prep_terms(
         where, sums, gram, stat, own_means, ahead_means, behind_means, far_means, flags, store
     )
-    prior_behind, prior_ahead, _ = lax.optimization_barrier((prior_behind, prior_ahead, flags))
-    half = HALO // 2
-    mine = jnp.concatenate(
-        [
-            prior,
-            prior_ahead,
-            to_chan(prior_behind[:half], lambda s: s + 2),
-            to_chan(prior_ahead[half:], lambda s: s - 2),
-            prior_behind,
-        ],
-        axis=0,
-    )
     window_cov = call(
         window_kernel,
         "window_output",
-        [where, mine, to_chan(mine, lambda s: s ^ 1), gram, stat, late_total],
+        [where, prior, prior_other, gram, stat, late_total],
         [array(1, WIDTH, CHIPS * PAIR)],
         fetched=(3, 4, 5),
         stored=(0,),
@@ -669,9 +691,8 @@
     before = to_chan(back[16:24, 0:32], lambda s: s + 2)
     following = to_chan(back[24:32, 0:32], lambda s: (s - 2) ^ 1)
     opposite = to_chan(back[:, 32:40], lambda s: s + 4 if s < 4 else (s - 4) ^ 1)
-    cusum, segment_cov = outputs(
-        where, back, opposite, following, before, store
-    )
+    most = most_outputs(where, back, store)
+    cusum, segment_cov = last_outputs(where, most, opposite, following, before)
     return window_cov, segment_cov, cusum
 
 

time: 110 us -> 108 us (0.982)
  waiting for transfers between devices: 24 us -> 13.7 us
  local copies, waits for them, and re-layouts: 4.44 us -> 9.08 us
  starting transfers between devices: 48.4 us -> 50.3 us
  Pallas kernels: 31.1 us -> 32.9 us
    ppermute x19, waiting for transfers between devices: 24 us -> 13.7 us  [to_chan(): lax.ppermute(value, 'chan', [(s, target(s) % count) for s in range(count)])]
    unnamed x9 -> x15, local copies, waits for them, and re-layouts: 1.89 us -> 7.17 us
    pallas_call x1 -> x2, Pallas kernels: 6.71 us -> 8.84 us  [the longest x1 5.72 us: most_outputs(): pl.pallas_call(most_kernel, out_shape=MOST, grid=(1,), in_specs=[SM, whol...]
    ppermute x1, starting transfers between devices: 1.82 us -> 3.57 us  [local(): lax.ppermute(samples[ROWS - HALO:], 'tm', [(b, b + 1) for b in range(BLOC...]
    all_to_all x2, starting transfers between devices: 18.5 us -> 20.1 us  [exchange(): return lax.all_to_all(value, 'tm', 0, 0, tiled=True)]
    ppermute x19, starting transfers between devices: 28.1 us -> 26.6 us  [to_chan(): lax.ppermute(value, 'chan', [(s, target(s) % count) for s in range(count)])]
  transfers between devices with their start and end apart: 22 -> 22, of which waited for: 10 -> 9; matrix products, arithmetic and copies ran while one was open for 2% -> 4% of each run, Pallas kernels for 19% -> 24%
where the time goes in v3:
time: 108 us
  starting transfers between devices  50.3 us (47%)
  Pallas kernels  32.9 us (30%)
  waiting for transfers between devices  13.7 us (13%)
  local copies, waits for them, and re-layouts  9.08 us (8%)
  between operations  1.77 us (2%)
    ppermute x19, starting transfers between devices, to_chan(): lax.ppermute(value, 'chan', [(s, target(s) % count) for s in range(count)])  26.6 us
    pallas_call x8, Pallas kernels, call(): pl.pallas_call(body, out_shape=[STORE] * first + outputs, grid=(1,), in_s...  24 us
    all_to_all x2, starting transfers between devices, exchange(): return lax.all_to_all(value, 'tm', 0, 0, tiled=True)  20.1 us
    ppermute x19, waiting for transfers between devices, to_chan(): lax.ppermute(value, 'chan', [(s, target(s) % count) for s in range(count)])  13.7 us
    unnamed x15, local copies, waits for them, and re-layouts  7.17 us
    pallas_call x1, Pallas kernels, most_outputs(): pl.pallas_call(most_kernel, out_shape=MOST, grid=(1,), in_specs=[SM, whol...  5.72 us
    ppermute x1, starting transfers between devices, local(): lax.ppermute(samples[ROWS - HALO:], 'tm', [(b, b + 1) for b in range(BLOC...  3.57 us
    pallas_call x1, Pallas kernels, last_outputs(): pl.pallas_call(last_kernel, out_shape=OUTPUTS, grid=(1,), in_specs=[SM] +...  3.12 us
  transfers between devices with their start and end apart: 22, of which 9 were waited for; matrix products, arithmetic and copies ran while one was open for 4% of the time, Pallas kernels for 24%

profile of v3, /device:TPU:1, one launch (start us, length us, event | category | flops | bytes accessed | tf_op | source)
XLA Modules:
  0.0 107.8 jit_solution(16079948630717689766)
XLA Ops:
  0.6 3.3 %collective-permute-start.3 = (bf16[2048,128]{1,0:T(8,128)(2,1)}, bf16[2048,128]{1,0:T(8,128)(2,1)S(1)}, u32[]{:S(2)}, u32[]{:S(2)}) collective-permute-start(bf16[2048,128]{1,0:T(8,128)(2,1)} %refs_1_.1), channel_id=1, source_target_pairs={{0,1},{1,0},{2,3},{3,2},{4,5},{5,4},{6,7},{7,6},{8,9},{9,8},{10,11... | collective-permute-start | bytes 1572872 | tf_op jit(solution)/shard_map/ppermute | solution.py:559
  6.4 3.6 %collective-permute-start.2 = (bf16[1024,128]{1,0:T(8,128)(2,1)S(1)}, bf16[1024,128]{1,0:T(8,128)(2,1)}, u32[]{:S(2)}, u32[]{:S(2)}) collective-permute-start(bf16[1024,128]{1,0:T(8,128)(2,1)S(1)} %slice.24), channel_id=1, source_target_pairs={{0,8},{8,16},{16,24},{24,32},{32,40},{40,48},{48,56},{56,64},{64,7... | collective-permute-start | bytes 786440 | tf_op jit(solution)/shard_map/ppermute | solution.py:583
  12.5 4.1 %first_pair.1 = (f32[96,8,128,128]{3,2,1,0:T(8,128)}, f32[4,8,256]{2,1,0:T(8,128)S(1)}, f32[4,128,256]{2,1,0:T(8,128)S(1)}, f32[4,8,256]{2,1,0:T(8,128)S(1)}, bf...) custom-call(s32[21]{0:T(128)S(1)} %concatenate.9.refs_0_.where_ref, ...), custom_call_target="tpu_custom_call" | custom-call | flops 3000000000 | bytes 1048576 | tf_op jit(solution)/shard_map/first_pair/pallas_call | solution.py:212
  17.6 1.6 %collective-permute-done.refs_2_ = bf16[2048,128]{1,0:T(8,128)(2,1)S(1)} collective-permute-done((bf16[2048,128]{1,0:T(8,128)(2,1)}, bf16[2048,128]{1,0:T(8,128)(2,1)S(1)}, u32[]{:S(2)}, u32[]{:S(2)}) %collective-permute-start) | collective-permute-done | bytes 524320 | tf_op jit(solution)/shard_map/ppermute | solution.py:559
  20.6 1.5 %collective-permute-start.4 = (bf16[1024,128]{1,0:T(8,128)(2,1)S(1)}, bf16[1024,128]{1,0:T(8,128)(2,1)S(1)}, u32[]{:S(2)}, u32[]{:S(2)}) collective-permute-start(bf16[1024,128]{1,0:T(8,128)(2,1)S(1)} %slice.25), channel_id=1, source_target_pairs={{0,2},{1,3},{2,4},{3,5},{4,6},{5,7},{6,0},{7,1},{8,10},{9,11},{10,... | collective-permute-start | bytes 786440 | tf_op jit(solution)/shard_map/ppermute | solution.py:559
  22.1 3.8 %near_pair.1 = (f32[96,8,128,128]{3,2,1,0:T(8,128)}, f32[4,8,256]{2,1,0:T(8,128)S(1)}, f32[4,128,256]{2,1,0:T(8,128)S(1)}, f32[4,8,256]{2,1,0:T(8,128)S(1)}, f32[128,256]{1,0:T(8,128)S(1)}) custom-call(s32[21]{0:T(128)S(1)} %concatenate.9.refs_0_.where_ref, ...), custom_call_target="tpu_custom_call", output_to_operand_aliasing={{0}: (5, {}), {1}: (6, {}), {2}: (7, {}), {3}: (8, {})} | custom-call | flops 3000000000 | bytes 1048576 | tf_op jit(solution)/shard_map/near_pair/pallas_call | solution.py:212
  25.9 1.8 %side_pair.1 = (f32[4,128,256]{2,1,0:T(8,128)S(1)}, f32[4,8,256]{2,1,0:T(8,128)S(1)}, bf16[2048,256]{1,0:T(8,128)(2,1)S(1)}) custom-call(s32[21]{0:T(128)S(1)} %concatenate.9.refs_0_.where_ref, bf16[2048,128]{1,0:T(8,128)(2,1)S(1)} %collective-permute-done.6.refs_1_, ...), custom_call_target="tpu_custom_call", output_to_operand_aliasing={{0}: (4, {}), {1}: (5, {})} | custom-call | flops 100000000 | bytes 1048576 | tf_op jit(solution)/shard_map/side_pair/pallas_call | solution.py:212
  29.1 1.7 %collective-permute-start.8 = (bf16[2048,128]{1,0:T(8,128)(2,1)S(1)}, bf16[2048,128]{1,0:T(8,128)(2,1)S(1)}, u32[]{:S(2)}, u32[]{:S(2)}) collective-permute-start(bf16[2048,128]{1,0:T(8,128)(2,1)S(1)} %constant_dynamic-update-slice_fusion.refs_1_), channel_id=1, source_target_pairs={{0,1},{1,0},{2,3},{3,2},{4,5},{5,4},{6,7},{7,6},{8,9},{9,8},{10,11... | collective-permute-start | bytes 1572872 | tf_op jit(solution)/shard_map/ppermute | solution.py:559
  30.8 1.5 %collective-permute-done.8.refs_2_ = bf16[2048,128]{1,0:T(8,128)(2,1)S(1)} collective-permute-done((bf16[2048,128]{1,0:T(8,128)(2,1)S(1)}, bf16[2048,128]{1,0:T(8,128)(2,1)S(1)}, u32[]{:S(2)}, u32[]{:S(2)}) %collective-permute-start.8) | collective-permute-done | bytes 524320 | tf_op jit(solution)/shard_map/ppermute | solution.py:559
  32.3 2.6 %far_pair.1 = (f32[4,128,256]{2,1,0:T(8,128)S(1)}, f32[4,8,256]{2,1,0:T(8,128)S(1)}, f32[32,24,128]{2,1,0:T(8,128)}, bf16[2048,256]{1,0:T(8,128)(2,1)S(1)}) custom-call(s32[21]{0:T(128)S(1)} %concatenate.9.refs_0_.where_ref, bf16[2048,128]{1,0:T(8,128)(2,1)S(1)} %constant_dynamic-update-slice_fusion.refs_1_, ...), custom_call_target="tpu_custom_call", output_to_operand_aliasing={{0}: (8, {}), {1}: (9, {})} | custom-call | flops 100000000 | bytes 1048576 | tf_op jit(solution)/shard_map/far_pair/pallas_call | solution.py:212
  35.9 11.2 %all-to-all-start = ((f32[32,24,128]{2,1,0:T(8,128)}), f32[32,24,128]{2,1,0:T(8,128)S(1)}, u32[]{:S(2)}, u32[]{:S(2)}) async-start(f32[32,24,128]{2,1,0:T(8,128)} %get-tuple-element.73), calls=%async_computation | async-start | bytes 786432 | tf_op jit(solution)/shard_map/all_to_all | solution.py:563
  47.2 1.5 %collective-permute-start.9 = (bf16[1024,128]{1,0:T(8,128)(2,1)}, bf16[1024,128]{1,0:T(8,128)(2,1)S(1)}, u32[]{:S(2)}, u32[]{:S(2)}) collective-permute-start(bf16[1024,128]{1,0:T(8,128)(2,1)} %collective-permute-done.2), channel_id=1, source_target_pairs={{0,2},{1,3},{2,4},{3,5},{4,6},{5,7},{6,0},{7,1},{8,10},{9,11},{10,... | collective-permute-start | bytes 786440 | tf_op jit(solution)/shard_map/ppermute | solution.py:559
  49.6 4.9 %collective-permute-done.10 = bf16[1024,128]{1,0:T(8,128)(2,1)S(1)} collective-permute-done((bf16[1024,128]{1,0:T(8,128)(2,1)}, bf16[1024,128]{1,0:T(8,128)(2,1)S(1)}, u32[]{:S(2)}, u32[]{:S(2)}) %collective-permute-start.10) | collective-permute-done | bytes 262176 | tf_op jit(solution)/shard_map/ppermute | solution.py:559
  59.7 4.3 %rest_left.1 = (f32[96,8,128,128]{3,2,1,0:T(8,128)}, f32[4,8,256]{2,1,0:T(8,128)S(1)}) custom-call(s32[21]{0:T(128)S(1)} %concatenate.9.refs_0_.where_ref, bf16[2048,256]{1,0:T(8,128)(2,1)S(1)} %copy-done.1, bf16[2048,256]{1,0:T(8,128)(2,1)S(1)} %get-tuple-element.79.refs_2_, ...), custom_call_target="tpu_custom_call", output_to_operand_aliasing={{0}: (4, {}), {1}: (5, {})} | custom-call | flops 4000000000 | bytes 1048576 | tf_op jit(solution)/shard_map/rest_left/pallas_call | solution.py:212
  65.1 8.9 %all-to-all-start.1 = ((f32[32,40,128]{2,1,0:T(8,128)}), f32[32,40,128]{2,1,0:T(8,128)S(1)}, u32[]{:S(2)}, u32[]{:S(2)}) async-start(f32[32,40,128]{2,1,0:T(8,128)} %get-tuple-element.85), calls=%async_computation.1 | async-start | bytes 1310720 | tf_op jit(solution)/shard_map/all_to_all | solution.py:563
  76.0 2.9 %collective-permute-start.16 = (bf16[4096,128]{1,0:T(8,128)(2,1)S(1)}, bf16[4096,128]{1,0:T(8,128)(2,1)S(1)}, u32[]{:S(2)}, u32[]{:S(2)}) collective-permute-start(bf16[4096,128]{1,0:T(8,128)(2,1)S(1)} %constant_dynamic-update-slice_fusion.2.refs_1_), channel_id=1, source_target_pairs={{0,1},{1,0},{2,3},{3,2},{4,5},{5,4},{6,7},{7,6},{8,9},{9,8},{10,11... | collective-permute-start | bytes 3145736 | tf_op jit(solution)/shard_map/ppermute | solution.py:559
  80.6 1.6 %collective-permute-start.13 = (f32[2,32,128]{2,1,0:T(8,128)S(1)}, f32[2,32,128]{2,1,0:T(8,128)S(1)}, u32[]{:S(2)}, u32[]{:S(2)}) collective-permute-start(f32[2,32,128]{2,1,0:T(8,128)S(1)} %get-tuple-element.89.refs_4_), channel_id=1, source_target_pairs={{0,6},{1,7},{2,0},{3,1},{4,2},{5,3},{6,4},{7,5},{8,14},{9,15},{10,... | collective-permute-start | bytes 98312 | tf_op jit(solution)/shard_map/ppermute | solution.py:559
  84.2 3.0 %prep_terms.1.store_hbm = f32[96,8,128,128]{3,2,1,0:T(8,128)} custom-call(s32[21]{0:T(128)S(1)} %concatenate.9.refs_0_.where_ref, f32[4,8,256]{2,1,0:T(8,128)S(1)} %get-tuple-element.86.refs_1_, f32[4,128,256]{2,1,0:T(8,128)S(1)} %get-tuple-element.87.refs_2_.refs_3_, ...), custom_call_target="tpu_custom_call", output_to_operand_aliasing={{}: (9, {})} | custom-call | flops 100000000 | bytes 1048576 | tf_op jit(solution)/shard_map/prep_terms/pallas_call | solution.py:212
  87.2 3.5 %window_output.1 = f32[1,128,1024]{2,1,0:T(8,128)} custom-call(s32[21]{0:T(128)S(1)} %concatenate.9.refs_0_.where_ref, bf16[4096,128]{1,0:T(8,128)(2,1)S(1)} %constant_dynamic-update-slice_fusion.2.refs_1_, bf16[4096,128]{1,0:T(8,128)(2,1)S(1)} %collective-permute-done.16.refs_2_, f32[4,128,256]{2,1,0:T(8,128)S(1)} %get-tuple-element.87.refs_2_.refs_3_, ...), custom_call_target="tpu_custom_call" | custom-call | flops 100000000 | bytes 1048576 | tf_op jit(solution)/shard_map/window_output/pallas_call | solution.py:212
  90.8 1.6 %collective-permute-start.17 = (f32[32,8,128]{2,1,0:T(8,128)S(1)}, f32[32,8,128]{2,1,0:T(8,128)S(1)}, u32[]{:S(2)}, u32[]{:S(2)}) collective-permute-start(f32[32,8,128]{2,1,0:T(8,128)S(1)} %slice.29), channel_id=1, source_target_pairs={{0,4},{1,5},{2,6},{3,7},{4,1},{5,0},{6,3},{7,2},{8,12},{9,13},{10,... | collective-permute-start | bytes 393224 | tf_op jit(solution)/shard_map/ppermute | solution.py:559
  92.4 1.4 %collective-permute-start.19 = (f32[8,32,128]{2,1,0:T(8,128)S(1)}, f32[8,32,128]{2,1,0:T(8,128)S(1)}, u32[]{:S(2)}, u32[]{:S(2)}) collective-permute-start(f32[8,32,128]{2,1,0:T(8,128)S(1)} %get-tuple-element.103), channel_id=1, source_target_pairs={{0,2},{1,3},{2,4},{3,5},{4,6},{5,7},{6,0},{7,1},{8,10},{9,11},{10,... | collective-permute-start | bytes 393224 | tf_op jit(solution)/shard_map/ppermute | solution.py:559
  93.8 4.9 %collective-permute-start.18 = (f32[8,32,128]{2,1,0:T(8,128)S(1)}, f32[8,32,128]{2,1,0:T(8,128)S(1)}, u32[]{:S(2)}, u32[]{:S(2)}) collective-permute-start(f32[8,32,128]{2,1,0:T(8,128)S(1)} %get-tuple-element.104), channel_id=1, source_target_pairs={{0,7},{1,6},{2,1},{3,0},{4,3},{5,2},{6,5},{7,4},{8,15},{9,14},{10,... | collective-permute-start | bytes 393224 | tf_op jit(solution)/shard_map/ppermute | solution.py:559
  98.7 5.7 %most_outputs.1 = (f32[8,128,1024]{2,1,0:T(8,128)S(1)}, f32[128,1024]{1,0:T(8,128)S(1)}, f32[24,128]{1,0:T(8,128)S(1)}) custom-call(s32[21]{0:T(128)S(1)} %concatenate.9.refs_0_.where_ref, f32[32,40,128]{2,1,0:T(8,128)S(1)} %all-to-all-done.1.back_ref, f32[96,8,128,128]{3,2,1,0:T(8,128)} %prep_terms.1.store_hbm), custom_call_target="tpu_custom_call" | custom-call | flops 5000000000 | bytes 1048576 | tf_op jit(solution)/shard_map/most_outputs/pallas_call | solution.py:483
  104.5 3.1 %last_outputs.1 = (f32[1,8,128,1024]{3,2,1,0:T(8,128)}, f32[1,128,1024]{2,1,0:T(8,128)}) custom-call(s32[21]{0:T(128)S(1)} %concatenate.9.refs_0_.where_ref, f32[8,128,1024]{2,1,0:T(8,128)S(1)} %get-tuple-element.98.most_ref, f32[128,1024]{1,0:T(8,128)S(1)} %get-tuple-element.99.most_seg_ref, f32[24,128]{1,0:T(8,128)S(1)} %get-tuple-element.100.coef_ref, ...), custom_call_target="tpu_custom_call" | custom-call | flops 3000000000 | bytes 1048576 | tf_op jit(solution)/shard_map/last_outputs/pallas_call | solution.py:501
  (55 shorter events, 22.0 us)
Async XLA Ops:
  0.6 10.8 %collective-permute-start.3 = (bf16[2048,128]{1,0:T(8,128)(2,1)}, bf16[2048,128]{1,0:T(8,128)(2,1)S(1)}, u32[]{:S(2)}, u32[]{:S(2)}) collective-permute-start(bf16[2048,128]{1,0:T(8,128)(2,1)} %refs_1_.1), channel_id=1, source_target_pairs={{0,1},{1,0},{2,3},{3,2},{4,5},{5,4},{6,7},{7,6},{8,9},{9,8},{10,11... | collective-permute-start | bytes 1572872 | tf_op jit(solution)/shard_map/ppermute | solution.py:559
  4.0 13.7 %collective-permute-start.1 = (bf16[2048,128]{1,0:T(8,128)(2,1)}, bf16[2048,128]{1,0:T(8,128)(2,1)S(1)}, u32[]{:S(2)}, u32[]{:S(2)}) collective-permute-start(bf16[2048,128]{1,0:T(8,128)(2,1)} %refs_1_.1), channel_id=1, source_target_pairs={{0,6},{1,7},{2,0},{3,1},{4,2},{5,3},{6,4},{7,5},{8,14},{9,15},{10,... | collective-permute-start | bytes 1572872 | tf_op jit(solution)/shard_map/ppermute | solution.py:559
  4.7 14.6 %collective-permute-start = (bf16[2048,128]{1,0:T(8,128)(2,1)}, bf16[2048,128]{1,0:T(8,128)(2,1)S(1)}, u32[]{:S(2)}, u32[]{:S(2)}) collective-permute-start(bf16[2048,128]{1,0:T(8,128)(2,1)} %refs_1_.1), channel_id=1, source_target_pairs={{0,2},{1,3},{2,4},{3,5},{4,6},{5,7},{6,0},{7,1},{8,10},{9,11},{10,... | collective-permute-start | bytes 1572872 | tf_op jit(solution)/shard_map/ppermute | solution.py:559
  6.4 10.1 %collective-permute-start.2 = (bf16[1024,128]{1,0:T(8,128)(2,1)S(1)}, bf16[1024,128]{1,0:T(8,128)(2,1)}, u32[]{:S(2)}, u32[]{:S(2)}) collective-permute-start(bf16[1024,128]{1,0:T(8,128)(2,1)S(1)} %slice.24), channel_id=1, source_target_pairs={{0,8},{8,16},{16,24},{24,32},{32,40},{40,48},{48,56},{56,64},{64,7... | collective-permute-start | bytes 786440 | tf_op jit(solution)/shard_map/ppermute | solution.py:583
  16.5 5.5 %copy-start.2 = (bf16[128,2048]{1,0:T(8,128)(2,1)}, bf16[128,2048]{1,0:T(8,128)(2,1)S(1)}, u32[]{:S(2)}) copy-start(bf16[128,2048]{1,0:T(8,128)(2,1)S(1)} %get-tuple-element.80.refs_3_) | copy-start | bytes 1572868
  19.3 2.8 %collective-permute-start.7 = (bf16[2048,128]{1,0:T(8,128)(2,1)S(1)}, bf16[2048,128]{1,0:T(8,128)(2,1)S(1)}, u32[]{:S(2)}, u32[]{:S(2)}) collective-permute-start(bf16[2048,128]{1,0:T(8,128)(2,1)S(1)} %collective-permute-done.refs_2_), channel_id=1, source_target_pairs={{0,1},{1,0},{2,3},{3,2},{4,5},{5,4},{6,7},{7,6},{8,9},{9,8},{10,11... | collective-permute-start | bytes 1572872 | tf_op jit(solution)/shard_map/ppermute | solution.py:559
  20.5 5.4 %collective-permute-start.6 = (bf16[2048,128]{1,0:T(8,128)(2,1)S(1)}, bf16[2048,128]{1,0:T(8,128)(2,1)S(1)}, u32[]{:S(2)}, u32[]{:S(2)}) collective-permute-start(bf16[2048,128]{1,0:T(8,128)(2,1)S(1)} %collective-permute-done.1.refs_1_), channel_id=1, source_target_pairs={{0,1},{1,0},{2,3},{3,2},{4,5},{5,4},{6,7},{7,6},{8,9},{9,8},{10,11... | collective-permute-start | bytes 1572872 | tf_op jit(solution)/shard_map/ppermute | solution.py:559
  20.5 7.4 %collective-permute-start.5 = (bf16[1024,128]{1,0:T(8,128)(2,1)S(1)}, bf16[1024,128]{1,0:T(8,128)(2,1)S(1)}, u32[]{:S(2)}, u32[]{:S(2)}) collective-permute-start(bf16[1024,128]{1,0:T(8,128)(2,1)S(1)} %slice.26), channel_id=1, source_target_pairs={{0,6},{1,7},{2,0},{3,1},{4,2},{5,3},{6,4},{7,5},{8,14},{9,15},{10,... | collective-permute-start | bytes 786440 | tf_op jit(solution)/shard_map/ppermute | solution.py:559
  20.6 8.4 %collective-permute-start.4 = (bf16[1024,128]{1,0:T(8,128)(2,1)S(1)}, bf16[1024,128]{1,0:T(8,128)(2,1)S(1)}, u32[]{:S(2)}, u32[]{:S(2)}) collective-permute-start(bf16[1024,128]{1,0:T(8,128)(2,1)S(1)} %slice.25), channel_id=1, source_target_pairs={{0,2},{1,3},{2,4},{3,5},{4,6},{5,7},{6,0},{7,1},{8,10},{9,11},{10,... | collective-permute-start | bytes 786440 | tf_op jit(solution)/shard_map/ppermute | solution.py:559
  29.1 3.2 %collective-permute-start.8 = (bf16[2048,128]{1,0:T(8,128)(2,1)S(1)}, bf16[2048,128]{1,0:T(8,128)(2,1)S(1)}, u32[]{:S(2)}, u32[]{:S(2)}) collective-permute-start(bf16[2048,128]{1,0:T(8,128)(2,1)S(1)} %constant_dynamic-update-slice_fusion.refs_1_), channel_id=1, source_target_pairs={{0,1},{1,0},{2,3},{3,2},{4,5},{5,4},{6,7},{7,6},{8,9},{9,8},{10,11... | collective-permute-start | bytes 1572872 | tf_op jit(solution)/shard_map/ppermute | solution.py:559
  35.9 28.2 %all-to-all-start = ((f32[32,24,128]{2,1,0:T(8,128)}), f32[32,24,128]{2,1,0:T(8,128)S(1)}, u32[]{:S(2)}, u32[]{:S(2)}) async-start(f32[32,24,128]{2,1,0:T(8,128)} %get-tuple-element.73), calls=%async_computation | async-start | bytes 786432 | tf_op jit(solution)/shard_map/all_to_all | solution.py:563
  47.1 7.5 %collective-permute-start.10 = (bf16[1024,128]{1,0:T(8,128)(2,1)}, bf16[1024,128]{1,0:T(8,128)(2,1)S(1)}, u32[]{:S(2)}, u32[]{:S(2)}) collective-permute-start(bf16[1024,128]{1,0:T(8,128)(2,1)} %collective-permute-done.2), channel_id=1, source_target_pairs={{0,6},{1,7},{2,0},{3,1},{4,2},{5,3},{6,4},{7,5},{8,14},{9,15},{10,... | collective-permute-start | bytes 786440 | tf_op jit(solution)/shard_map/ppermute | solution.py:559
  47.2 8.6 %collective-permute-start.9 = (bf16[1024,128]{1,0:T(8,128)(2,1)}, bf16[1024,128]{1,0:T(8,128)(2,1)S(1)}, u32[]{:S(2)}, u32[]{:S(2)}) collective-permute-start(bf16[1024,128]{1,0:T(8,128)(2,1)} %collective-permute-done.2), channel_id=1, source_target_pairs={{0,2},{1,3},{2,4},{3,5},{4,6},{5,7},{6,0},{7,1},{8,10},{9,11},{10,... | collective-permute-start | bytes 786440 | tf_op jit(solution)/shard_map/ppermute | solution.py:559
  55.8 8.3 %collective-permute-start.12 = (bf16[512,128]{1,0:T(8,128)(2,1)S(1)}, bf16[512,128]{1,0:T(8,128)(2,1)}, u32[]{:S(2)}, u32[]{:S(2)}) collective-permute-start(bf16[512,128]{1,0:T(8,128)(2,1)S(1)} %slice.28), channel_id=1, source_target_pairs={{0,6},{1,7},{2,0},{3,1},{4,2},{5,3},{6,4},{7,5},{8,14},{9,15},{10,... | collective-permute-start | bytes 393224 | tf_op jit(solution)/shard_map/ppermute | solution.py:559
  56.1 7.9 %collective-permute-start.11 = (bf16[512,128]{1,0:T(8,128)(2,1)S(1)}, bf16[512,128]{1,0:T(8,128)(2,1)}, u32[]{:S(2)}, u32[]{:S(2)}) collective-permute-start(bf16[512,128]{1,0:T(8,128)(2,1)S(1)} %slice.27), channel_id=1, source_target_pairs={{0,2},{1,3},{2,4},{3,5},{4,6},{5,7},{6,0},{7,1},{8,10},{9,11},{10,... | collective-permute-start | bytes 393224 | tf_op jit(solution)/shard_map/ppermute | solution.py:559
  57.5 1.2 %copy-start.1 = (bf16[2048,256]{1,0:T(8,128)(2,1)S(1)}, bf16[2048,256]{1,0:T(8,128)(2,1)}, u32[]{:S(2)}) copy-start(bf16[2048,256]{1,0:T(8,128)(2,1)} %copy-done) | copy-start | bytes 3145732
  65.1 25.6 %all-to-all-start.1 = ((f32[32,40,128]{2,1,0:T(8,128)}), f32[32,40,128]{2,1,0:T(8,128)S(1)}, u32[]{:S(2)}, u32[]{:S(2)}) async-start(f32[32,40,128]{2,1,0:T(8,128)} %get-tuple-element.85), calls=%async_computation.1 | async-start | bytes 1310720 | tf_op jit(solution)/shard_map/all_to_all | solution.py:563
  76.0 11.2 %collective-permute-start.16 = (bf16[4096,128]{1,0:T(8,128)(2,1)S(1)}, bf16[4096,128]{1,0:T(8,128)(2,1)S(1)}, u32[]{:S(2)}, u32[]{:S(2)}) collective-permute-start(bf16[4096,128]{1,0:T(8,128)(2,1)S(1)} %constant_dynamic-update-slice_fusion.2.refs_1_), channel_id=1, source_target_pairs={{0,1},{1,0},{2,3},{3,2},{4,5},{5,4},{6,7},{7,6},{8,9},{9,8},{10,11... | collective-permute-start | bytes 3145736 | tf_op jit(solution)/shard_map/ppermute | solution.py:559
  78.9 4.3 %collective-permute-start.15 = (f32[2,32,128]{2,1,0:T(8,128)S(1)}, f32[2,32,128]{2,1,0:T(8,128)S(1)}, u32[]{:S(2)}, u32[]{:S(2)}) collective-permute-start(f32[2,32,128]{2,1,0:T(8,128)S(1)} %get-tuple-element.89.refs_4_), channel_id=1, source_target_pairs={{0,4},{1,5},{2,6},{3,7},{4,0},{5,1},{6,2},{7,3},{8,12},{9,13},{10,... | collective-permute-start | bytes 98312 | tf_op jit(solution)/shard_map/ppermute | solution.py:559
  79.5 4.6 %collective-permute-start.14 = (f32[2,32,128]{2,1,0:T(8,128)S(1)}, f32[2,32,128]{2,1,0:T(8,128)S(1)}, u32[]{:S(2)}, u32[]{:S(2)}) collective-permute-start(f32[2,32,128]{2,1,0:T(8,128)S(1)} %get-tuple-element.89.refs_4_), channel_id=1, source_target_pairs={{0,2},{1,3},{2,4},{3,5},{4,6},{5,7},{6,0},{7,1},{8,10},{9,11},{10,... | collective-permute-start | bytes 98312 | tf_op jit(solution)/shard_map/ppermute | solution.py:559
  80.6 3.6 %collective-permute-start.13 = (f32[2,32,128]{2,1,0:T(8,128)S(1)}, f32[2,32,128]{2,1,0:T(8,128)S(1)}, u32[]{:S(2)}, u32[]{:S(2)}) collective-permute-start(f32[2,32,128]{2,1,0:T(8,128)S(1)} %get-tuple-element.89.refs_4_), channel_id=1, source_target_pairs={{0,6},{1,7},{2,0},{3,1},{4,2},{5,3},{6,4},{7,5},{8,14},{9,15},{10,... | collective-permute-start | bytes 98312 | tf_op jit(solution)/shard_map/ppermute | solution.py:559
  90.8 13.6 %collective-permute-start.17 = (f32[32,8,128]{2,1,0:T(8,128)S(1)}, f32[32,8,128]{2,1,0:T(8,128)S(1)}, u32[]{:S(2)}, u32[]{:S(2)}) collective-permute-start(f32[32,8,128]{2,1,0:T(8,128)S(1)} %slice.29), channel_id=1, source_target_pairs={{0,4},{1,5},{2,6},{3,7},{4,1},{5,0},{6,3},{7,2},{8,12},{9,13},{10,... | collective-permute-start | bytes 393224 | tf_op jit(solution)/shard_map/ppermute | solution.py:559
  92.4 12.0 %collective-permute-start.19 = (f32[8,32,128]{2,1,0:T(8,128)S(1)}, f32[8,32,128]{2,1,0:T(8,128)S(1)}, u32[]{:S(2)}, u32[]{:S(2)}) collective-permute-start(f32[8,32,128]{2,1,0:T(8,128)S(1)} %get-tuple-element.103), channel_id=1, source_target_pairs={{0,2},{1,3},{2,4},{3,5},{4,6},{5,7},{6,0},{7,1},{8,10},{9,11},{10,... | collective-permute-start | bytes 393224 | tf_op jit(solution)/shard_map/ppermute | solution.py:559
  93.8 10.7 %collective-permute-start.18 = (f32[8,32,128]{2,1,0:T(8,128)S(1)}, f32[8,32,128]{2,1,0:T(8,128)S(1)}, u32[]{:S(2)}, u32[]{:S(2)}) collective-permute-start(f32[8,32,128]{2,1,0:T(8,128)S(1)} %get-tuple-element.104), channel_id=1, source_target_pairs={{0,7},{1,6},{2,1},{3,0},{4,3},{5,2},{6,5},{7,4},{8,15},{9,14},{10,... | collective-permute-start | bytes 393224 | tf_op jit(solution)/shard_map/ppermute | solution.py:559
  (3 other events, 3.1 us)

commit v4 on v3

--- a/solution.py
+++ b/solution.py
@@ -149,10 +149,8 @@
         out_ref[q, 16:20, :] = held_ref[4 * q : 4 * q + 4, :]
 
 
-def rest_kernel(where_ref, far_ref, side_ref, flip_ref, far_left_ref, side_left_ref, sums_ref):
-    flipped = flip_ref[...]
-    left_part(where_ref, flipped, far_ref, far_left_ref, sums_ref, 0)
-    left_part(where_ref, flipped, side_ref, side_left_ref, sums_ref, 1)
+def rest_kernel(where_ref, cent_ref, flip_ref, left_ref, sums_ref):
+    left_part(where_ref, flip_ref[...], cent_ref, left_ref, sums_ref)
 
 
 ALL = [
@@ -348,28 +346,6 @@
         after_ref[u] = gram_ref[r, :, lanes] + between(row_part_s, col_part_s)
 
 
-def prep_terms(where, sums, gram, stat, own, ahead, behind, far, flags, store):
-    square = (8, WIDTH, WIDTH)
-    return call(
-        prep_kernel,
-        "prep_terms",
-        [where, sums, gram, stat, own, ahead, behind, far, flags],
-        [],
-        store=store,
-        puts=(
-            ((WIDTH, WIDTH), (11, 0)),
-            ((8, 40, WIDTH), (10, slice(None), pl.ds(0, 40))),
-            ((24, WIDTH), (11, 1, pl.ds(0, 24))),
-            (square, 8),
-            (square, 9),
-        ),
-        fetched=(1, 2, 3, 4, 8),
-        scratch=[((WIDTH, WIDTH), F32)],
-        us=0.1,
-        grant=16,
-    )[0]
-
-
 def load_near(ref, p_ref, s_ref):
     for g in range(8):
         p_ref[16 * g : 16 * g + 16, :] = ref[g, 0:16, :]
@@ -554,6 +530,46 @@
             out_ref[0, :, pl.ds(lane, WIDTH)] = value[:, c * WIDTH : (c + 1) * WIDTH]
 
 
+def late_kernel(
+    where_ref, mine_ref, other_ref, total_ref, sums_ref, gram_ref, stat_ref, own_ref, ahead_ref, behind_ref, far_ref, flags_ref,
+    turned_ref, cols_ref, coef_ref, before_ref, after_ref, window_ref, vectors, cent_ref, flip_ref, sum_ref,
+):
+    prep_kernel(
+        where_ref, sums_ref, gram_ref, stat_ref, own_ref, ahead_ref, behind_ref, far_ref, flags_ref,
+        turned_ref, cols_ref, coef_ref, before_ref, after_ref, vectors,
+    )
+    window_kernel(
+        where_ref, mine_ref, other_ref, gram_ref, stat_ref, total_ref, window_ref, cent_ref, flip_ref, sum_ref
+    )
+
+
+def late_terms(where, mine, other, total, sums, gram, stat, means, flags, store):
+    square = (8, WIDTH, WIDTH)
+    return call(
+        late_kernel,
+        "late_terms",
+        [where, mine, other, total, sums, gram, stat, *means, flags],
+        [array(1, WIDTH, CHIPS * PAIR)],
+        store=store,
+        puts=(
+            ((WIDTH, WIDTH), (11, 0)),
+            ((8, 40, WIDTH), (10, slice(None), pl.ds(0, 40))),
+            ((24, WIDTH), (11, 1, pl.ds(0, 24))),
+            (square, 8),
+            (square, 9),
+        ),
+        fetched=(3, 4, 5, 6, 7, 11),
+        stored=(0,),
+        scratch=[
+            ((WIDTH, WIDTH), F32),
+            ((HALO, PAIR), BF16),
+            ((WIDTH, HALO), BF16),
+            ((WIDTH, WIDTH), F32),
+        ],
+        us=0.1,
+    )
+
+
 def to_chan(value, target):
     count = lax.axis_size("chan")
     return lax.ppermute(value, "chan", [(s, target(s) % count) for s in range(count)])
@@ -621,9 +637,7 @@
         pair=3,
         us=0.1,
     )
-    far_low, far_high, stat, prior = lax.optimization_barrier((far_low, far_high, stat, prior))
-    prior_behind = to_chan(prior, lambda s: s + 2)
-    prior_ahead = to_chan(prior, lambda s: s - 2)
+    far_low, far_high, stat = lax.optimization_barrier((far_low, far_high, stat))
     far = jnp.concatenate([far_low, far_high], axis=0)
     far_other = to_chan(far, lambda s: s ^ 1)
     gram, stat, pieces, cent = call(
@@ -631,7 +645,7 @@
         "far_pair",
         [where, far, far_other, flipped, total, spread0, spread1, rider],
         ALL[1:] + [array(BLOCKS, 24, WIDTH), cent_shape],
-        stored=(0, 1, 2, 3),
+        stored=(0, 1, 3),
         kept=(gram, stat),
         pair=2,
         scratch=[((WIDTH, WIDTH), F32)],
@@ -639,27 +653,41 @@
     )
     arrived = exchange(pieces)
 
-    cent, prior_behind, prior_ahead = lax.optimization_barrier((cent, prior_behind, prior_ahead))
+    store, sums = call(
+        rest_kernel,
+        "rest_left",
+        [where, after(side, cent), late_flipped],
+        ALL[:1],
+        store=store,
+        puts=((SHARD_PAIR, pl.ds(6, 2)),),
+        fetched=(2,),
+        stored=(0,),
+        kept=(sums,),
+        pair=3,
+        us=4,
+    )
+    prior = after(prior, sums)
+    prior_behind = to_chan(prior, lambda s: s + 2)
+    prior_ahead = to_chan(prior, lambda s: s - 2)
+    store, sums = call(
+        rest_kernel,
+        "rest_left",
+        [where, cent, late_flipped],
+        ALL[:1],
+        store=store,
+        puts=((SHARD_PAIR, pl.ds(4, 2)),),
+        fetched=(1, 2),
+        stored=(0,),
+        kept=(sums,),
+        pair=2,
+        us=2,
+    )
+    arrived, prior_behind, prior_ahead, sums = lax.optimization_barrier(
+        (arrived, prior_behind, prior_ahead, sums)
+    )
     half = HALO // 2
     prior_low = to_chan(prior_behind[:half], lambda s: s + 2)
     prior_high = to_chan(prior_ahead[half:], lambda s: s - 2)
-    store, sums = call(
-        rest_kernel,
-        "rest_left",
-        [where, cent, side, late_flipped],
-        ALL[:1],
-        store=store,
-        puts=((SHARD_PAIR, pl.ds(4, 2)), (SHARD_PAIR, pl.ds(6, 2))),
-        fetched=(1, 3),
-        stored=(0,),
-        kept=(sums,),
-        pair=2,
-        span=2,
-        us=4,
-    )
-    arrived, prior_low, prior_high, sums = lax.optimization_barrier(
-        (arrived, prior_low, prior_high, sums)
-    )
     prior = jnp.concatenate([prior, prior_ahead, prior_low, prior_high, prior_behind], axis=0)
     prior_other = to_chan(prior, lambda s: s ^ 1)
     scanned, own_means, flags = call(
@@ -674,19 +702,10 @@
     ahead_means = to_chan(own_means, lambda s: s - 2)
     behind_means = to_chan(own_means, lambda s: s + 2)
     far_means = to_chan(own_means, lambda s: s + 4)
-    store = prep_terms(
-        where, sums, gram, stat, own_means, ahead_means, behind_means, far_means, flags, store
-    )
-    window_cov = call(
-        window_kernel,
-        "window_output",
-        [where, prior, prior_other, gram, stat, late_total],
-        [array(1, WIDTH, CHIPS * PAIR)],
-        fetched=(3, 4, 5),
-        stored=(0,),
-        scratch=[((HALO, PAIR), BF16), ((WIDTH, HALO), BF16), ((WIDTH, WIDTH), F32)],
-        us=0.1,
-    )[0]
+    means = (own_means, ahead_means, behind_means, far_means)
+    store, window_cov = late_terms(
+        where, prior, prior_other, late_total, sums, gram, stat, means, flags, store
+    )
     back, store, window_cov = lax.optimization_barrier((back, store, window_cov))
     before = to_chan(back[16:24, 0:32], lambda s: s + 2)
     following = to_chan(back[24:32, 0:32], lambda s: (s - 2) ^ 1)

time: 108 us -> 106 us (0.981)
  local copies, waits for them, and re-layouts: 9.08 us -> 4.02 us
  waiting for transfers between devices: 13.7 us -> 16.1 us
  Pallas kernels: 32.9 us -> 34.1 us
    unnamed x15 -> x11, local copies, waits for them, and re-layouts: 7.17 us -> 2.12 us
    ppermute x19, starting transfers between devices: 26.6 us -> 29.4 us  [to_chan(): lax.ppermute(value, 'chan', [(s, target(s) % count) for s in range(count)])]
    ppermute x19, waiting for transfers between devices: 13.7 us -> 15.5 us  [to_chan(): lax.ppermute(value, 'chan', [(s, target(s) % count) for s in range(count)])]
    all_to_all x2, starting transfers between devices: 20.1 us -> 18.4 us  [exchange(): return lax.all_to_all(value, 'tm', 0, 0, tiled=True)]
    ppermute x1, starting transfers between devices: 3.57 us -> 1.82 us  [local(): lax.ppermute(samples[ROWS - HALO:], 'tm', [(b, b + 1) for b in range(BLOC...]
    pallas_call x8, Pallas kernels: 24 us -> 25.3 us  [call(): pl.pallas_call(body, out_shape=[STORE] * first + outputs, grid=(1,), in_s...]
  transfers between devices with their start and end apart: 22 -> 22, of which waited for: 9 -> 10; matrix products, arithmetic and copies ran while one was open for 4% -> 2% of each run, Pallas kernels for 24% -> 27%
where the time goes in v4:
time: 106 us
  starting transfers between devices  49.6 us (47%)
  Pallas kernels  34.1 us (32%)
  waiting for transfers between devices  16.1 us (15%)
  local copies, waits for them, and re-layouts  4.02 us (4%)
  between operations  1.83 us (2%)
    ppermute x19, starting transfers between devices, to_chan(): lax.ppermute(value, 'chan', [(s, target(s) % count) for s in range(count)])  29.4 us
    pallas_call x8, Pallas kernels, call(): pl.pallas_call(body, out_shape=[STORE] * first + outputs, grid=(1,), in_s...  25.3 us
    all_to_all x2, starting transfers between devices, exchange(): return lax.all_to_all(value, 'tm', 0, 0, tiled=True)  18.4 us
    ppermute x19, waiting for transfers between devices, to_chan(): lax.ppermute(value, 'chan', [(s, target(s) % count) for s in range(count)])  15.5 us
    pallas_call x1, Pallas kernels, most_outputs(): pl.pallas_call(most_kernel, out_shape=MOST, grid=(1,), in_specs=[SM, whol...  5.7 us
    pallas_call x1, Pallas kernels, last_outputs(): pl.pallas_call(last_kernel, out_shape=OUTPUTS, grid=(1,), in_specs=[SM] +...  3.12 us
  transfers between devices with their start and end apart: 22, of which 10 were waited for; matrix products, arithmetic and copies ran while one was open for 2% of the time, Pallas kernels for 27%

profile of v4, /device:TPU:1, one launch (start us, length us, event | category | flops | bytes accessed | tf_op | source)
XLA Modules:
  0.0 105.6 jit_solution(12197726988083292190)
XLA Ops:
  0.6 3.3 %collective-permute-start.3 = (bf16[2048,128]{1,0:T(8,128)(2,1)}, bf16[2048,128]{1,0:T(8,128)(2,1)S(1)}, u32[]{:S(2)}, u32[]{:S(2)}) collective-permute-start(bf16[2048,128]{1,0:T(8,128)(2,1)} %refs_1_.1), channel_id=1, source_target_pairs={{0,1},{1,0},{2,3},{3,2},{4,5},{5,4},{6,7},{7,6},{8,9},{9,8},{10,11... | collective-permute-start | bytes 1572872 | tf_op jit(solution)/shard_map/ppermute | solution.py:575
  4.0 2.7 %collective-permute-start.1 = (bf16[2048,128]{1,0:T(8,128)(2,1)}, bf16[2048,128]{1,0:T(8,128)(2,1)S(1)}, u32[]{:S(2)}, u32[]{:S(2)}) collective-permute-start(bf16[2048,128]{1,0:T(8,128)(2,1)} %refs_1_.1), channel_id=1, source_target_pairs={{0,6},{1,7},{2,0},{3,1},{4,2},{5,3},{6,4},{7,5},{8,14},{9,15},{10,... | collective-permute-start | bytes 1572872 | tf_op jit(solution)/shard_map/ppermute | solution.py:575
  7.7 1.8 %collective-permute-start.2 = (bf16[1024,128]{1,0:T(8,128)(2,1)S(1)}, bf16[1024,128]{1,0:T(8,128)(2,1)S(1)}, u32[]{:S(2)}, u32[]{:S(2)}) collective-permute-start(bf16[1024,128]{1,0:T(8,128)(2,1)S(1)} %slice.24), channel_id=1, source_target_pairs={{0,8},{8,16},{16,24},{24,32},{32,40},{40,48},{48,56},{56,64},{64,7... | collective-permute-start | bytes 786440 | tf_op jit(solution)/shard_map/ppermute | solution.py:599
  12.0 4.1 %first_pair.1 = (f32[96,8,128,128]{3,2,1,0:T(8,128)}, f32[4,8,256]{2,1,0:T(8,128)S(1)}, f32[4,128,256]{2,1,0:T(8,128)S(1)}, f32[4,8,256]{2,1,0:T(8,128)S(1)}, bf...) custom-call(s32[21]{0:T(128)S(1)} %concatenate.9.refs_0_.where_ref, ...), custom_call_target="tpu_custom_call" | custom-call | flops 3000000000 | bytes 1048576 | tf_op jit(solution)/shard_map/first_pair/pallas_call | solution.py:210
  16.1 2.8 %collective-permute-done.refs_2_ = bf16[2048,128]{1,0:T(8,128)(2,1)S(1)} collective-permute-done((bf16[2048,128]{1,0:T(8,128)(2,1)}, bf16[2048,128]{1,0:T(8,128)(2,1)S(1)}, u32[]{:S(2)}, u32[]{:S(2)}) %collective-permute-start) | collective-permute-done | bytes 524320 | tf_op jit(solution)/shard_map/ppermute | solution.py:575
  19.9 2.8 %collective-permute-start.5 = (bf16[1024,128]{1,0:T(8,128)(2,1)S(1)}, bf16[1024,128]{1,0:T(8,128)(2,1)S(1)}, u32[]{:S(2)}, u32[]{:S(2)}) collective-permute-start(bf16[1024,128]{1,0:T(8,128)(2,1)S(1)} %slice.26), channel_id=1, source_target_pairs={{0,6},{1,7},{2,0},{3,1},{4,2},{5,3},{6,4},{7,5},{8,14},{9,15},{10,... | collective-permute-start | bytes 786440 | tf_op jit(solution)/shard_map/ppermute | solution.py:575
  22.6 3.8 %near_pair.1 = (f32[96,8,128,128]{3,2,1,0:T(8,128)}, f32[4,8,256]{2,1,0:T(8,128)S(1)}, f32[4,128,256]{2,1,0:T(8,128)S(1)}, f32[4,8,256]{2,1,0:T(8,128)S(1)}, f32[128,256]{1,0:T(8,128)S(1)}) custom-call(s32[21]{0:T(128)S(1)} %concatenate.9.refs_0_.where_ref, ...), custom_call_target="tpu_custom_call", output_to_operand_aliasing={{0}: (5, {}), {1}: (6, {}), {2}: (7, {}), {3}: (8, {})} | custom-call | flops 3000000000 | bytes 1048576 | tf_op jit(solution)/shard_map/near_pair/pallas_call | solution.py:210
  26.5 1.8 %side_pair.1 = (f32[4,128,256]{2,1,0:T(8,128)S(1)}, f32[4,8,256]{2,1,0:T(8,128)S(1)}, bf16[2048,256]{1,0:T(8,128)(2,1)S(1)}) custom-call(s32[21]{0:T(128)S(1)} %concatenate.9.refs_0_.where_ref, bf16[2048,128]{1,0:T(8,128)(2,1)S(1)} %collective-permute-done.6.refs_1_, ...), custom_call_target="tpu_custom_call", output_to_operand_aliasing={{0}: (4, {}), {1}: (5, {})} | custom-call | flops 100000000 | bytes 1048576 | tf_op jit(solution)/shard_map/side_pair/pallas_call | solution.py:210
  31.5 2.6 %far_pair.1 = (f32[4,128,256]{2,1,0:T(8,128)S(1)}, f32[4,8,256]{2,1,0:T(8,128)S(1)}, f32[32,24,128]{2,1,0:T(8,128)}, bf16[2048,256]{1,0:T(8,128)(2,1)S(1)}) custom-call(s32[21]{0:T(128)S(1)} %concatenate.9.refs_0_.where_ref, bf16[2048,128]{1,0:T(8,128)(2,1)S(1)} %constant_dynamic-update-slice_fusion.refs_1_, ...), custom_call_target="tpu_custom_call", output_to_operand_aliasing={{0}: (8, {}), {1}: (9, {})} | custom-call | flops 100000000 | bytes 1048576 | tf_op jit(solution)/shard_map/far_pair/pallas_call | solution.py:210
  35.1 9.6 %all-to-all-start = ((f32[32,24,128]{2,1,0:T(8,128)}), f32[32,24,128]{2,1,0:T(8,128)}, u32[]{:S(2)}, u32[]{:S(2)}) async-start(f32[32,24,128]{2,1,0:T(8,128)} %get-tuple-element.74), calls=%async_computation | async-start | bytes 786432 | tf_op jit(solution)/shard_map/all_to_all | solution.py:579
  44.7 3.0 %rest_left.2 = (f32[96,8,128,128]{3,2,1,0:T(8,128)}, f32[4,8,256]{2,1,0:T(8,128)S(1)}) custom-call(s32[21]{0:T(128)S(1)} %concatenate.9.refs_0_.where_ref, bf16[2048,256]{1,0:T(8,128)(2,1)S(1)} %get-tuple-element.78.refs_1_, bf16[128,2048]{1,0:T(8,128)(2,1)S(1)} %get-tuple-element.79.refs_2_, ...), custom_call_target="tpu_custom_call", output_to_operand_aliasing={{0}: (3, {}), {1}: (4, {})} | custom-call | flops 4000000000 | bytes 1048576 | tf_op jit(solution)/shard_map/rest_left/pallas_call | solution.py:210
  47.7 3.0 %collective-permute-start.10 = (bf16[1024,128]{1,0:T(8,128)(2,1)S(1)}, bf16[1024,128]{1,0:T(8,128)(2,1)S(1)}, u32[]{:S(2)}, u32[]{:S(2)}) collective-permute-start(bf16[1024,128]{1,0:T(8,128)(2,1)S(1)} %collective-permute-done.2), channel_id=1, source_target_pairs={{0,6},{1,7},{2,0},{3,1},{4,2},{5,3},{6,4},{7,5},{8,14},{9,15},{10,... | collective-permute-start | bytes 786440 | tf_op jit(solution)/shard_map/ppermute | solution.py:575
  50.7 3.1 %rest_left.3 = (f32[96,8,128,128]{3,2,1,0:T(8,128)}, f32[4,8,256]{2,1,0:T(8,128)S(1)}) custom-call(s32[21]{0:T(128)S(1)} %concatenate.9.refs_0_.where_ref, bf16[2048,256]{1,0:T(8,128)(2,1)S(1)} %copy-done.1, bf16[128,2048]{1,0:T(8,128)(2,1)S(1)} %get-tuple-element.79.refs_2_, ...), custom_call_target="tpu_custom_call", output_to_operand_aliasing={{0}: (3, {}), {1}: (4, {})} | custom-call | flops 2000000000 | bytes 1048576 | tf_op jit(solution)/shard_map/rest_left/pallas_call | solution.py:210
  53.8 1.9 %collective-permute-done.10 = bf16[1024,128]{1,0:T(8,128)(2,1)S(1)} collective-permute-done((bf16[1024,128]{1,0:T(8,128)(2,1)S(1)}, bf16[1024,128]{1,0:T(8,128)(2,1)S(1)}, u32[]{:S(2)}, u32[]{:S(2)}) %collective-permute-start.10) | collective-permute-done | bytes 262176 | tf_op jit(solution)/shard_map/ppermute | solution.py:575
  55.7 3.2 %collective-permute-done.9 = bf16[1024,128]{1,0:T(8,128)(2,1)S(1)} collective-permute-done((bf16[1024,128]{1,0:T(8,128)(2,1)S(1)}, bf16[1024,128]{1,0:T(8,128)(2,1)S(1)}, u32[]{:S(2)}, u32[]{:S(2)}) %collective-permute-start.9) | collective-permute-done | bytes 262176 | tf_op jit(solution)/shard_map/ppermute | solution.py:575
  59.1 2.7 %collective-permute-start.12 = (bf16[512,128]{1,0:T(8,128)(2,1)S(1)}, bf16[512,128]{1,0:T(8,128)(2,1)S(1)}, u32[]{:S(2)}, u32[]{:S(2)}) collective-permute-start(bf16[512,128]{1,0:T(8,128)(2,1)S(1)} %slice.28), channel_id=1, source_target_pairs={{0,6},{1,7},{2,0},{3,1},{4,2},{5,3},{6,4},{7,5},{8,14},{9,15},{10,... | collective-permute-start | bytes 393224 | tf_op jit(solution)/shard_map/ppermute | solution.py:575
  61.8 2.0 %scan_pieces.1 = (f32[32,40,128]{2,1,0:T(8,128)}, f32[2,32,128]{2,1,0:T(8,128)S(1)}, f32[32,128]{1,0:T(8,128)S(1)}) custom-call(f32[32,24,128]{2,1,0:T(8,128)} %all-to-all-done.refs_0_), custom_call_target="tpu_custom_call" | custom-call | flops 1000000000 | bytes 1048576 | tf_op jit(solution)/shard_map/scan_pieces/pallas_call | solution.py:210
  63.8 8.8 %all-to-all-start.1 = ((f32[32,40,128]{2,1,0:T(8,128)}), f32[32,40,128]{2,1,0:T(8,128)S(1)}, u32[]{:S(2)}, u32[]{:S(2)}) async-start(f32[32,40,128]{2,1,0:T(8,128)} %get-tuple-element.87), calls=%async_computation.1 | async-start | bytes 1310720 | tf_op jit(solution)/shard_map/all_to_all | solution.py:579
  72.7 3.1 %collective-permute-start.13 = (bf16[4096,128]{1,0:T(8,128)(2,1)S(1)}, bf16[4096,128]{1,0:T(8,128)(2,1)S(1)}, u32[]{:S(2)}, u32[]{:S(2)}) collective-permute-start(bf16[4096,128]{1,0:T(8,128)(2,1)S(1)} %constant_dynamic-update-slice_fusion.2.refs_1_), channel_id=1, source_target_pairs={{0,1},{1,0},{2,3},{3,2},{4,5},{5,4},{6,7},{7,6},{8,9},{9,8},{10,11... | collective-permute-start | bytes 3145736 | tf_op jit(solution)/shard_map/ppermute | solution.py:575
  81.5 5.0 %late_terms.1 = (f32[96,8,128,128]{3,2,1,0:T(8,128)}, f32[1,128,1024]{2,1,0:T(8,128)}) custom-call(s32[21]{0:T(128)S(1)} %concatenate.9.refs_0_.where_ref, bf16[4096,128]{1,0:T(8,128)(2,1)S(1)} %constant_dynamic-update-slice_fusion.2.refs_1_, bf16[4096,128]{1,0:T(8,128)(2,1)S(1)} %collective-permute-done.13.refs_2_, ...), custom_call_target="tpu_custom_call", output_to_operand_aliasing={{0}: (12, {})} | custom-call | flops 100000000 | bytes 1048576 | tf_op jit(solution)/shard_map/late_terms/pallas_call | solution.py:210
  87.1 6.3 %collective-permute-start.18 = (f32[8,32,128]{2,1,0:T(8,128)S(1)}, f32[8,32,128]{2,1,0:T(8,128)S(1)}, u32[]{:S(2)}, u32[]{:S(2)}) collective-permute-start(f32[8,32,128]{2,1,0:T(8,128)S(1)} %get-tuple-element.108), channel_id=1, source_target_pairs={{0,7},{1,6},{2,1},{3,0},{4,3},{5,2},{6,5},{7,4},{8,15},{9,14},{10,... | collective-permute-start | bytes 393224 | tf_op jit(solution)/shard_map/ppermute | solution.py:575
  95.0 5.7 %most_outputs.1 = (f32[8,128,1024]{2,1,0:T(8,128)S(1)}, f32[128,1024]{1,0:T(8,128)S(1)}, f32[24,128]{1,0:T(8,128)S(1)}) custom-call(s32[21]{0:T(128)S(1)} %concatenate.9.refs_0_.where_ref, f32[32,40,128]{2,1,0:T(8,128)S(1)} %all-to-all-done.1.back_ref, f32[96,8,128,128]{3,2,1,0:T(8,128)} %get-tuple-element.101.store_hbm), custom_call_target="tpu_custom_call" | custom-call | flops 5000000000 | bytes 1048576 | tf_op jit(solution)/shard_map/most_outputs/pallas_call | solution.py:459
  100.7 1.6 %collective-permute-done.19.before_ref = f32[8,32,128]{2,1,0:T(8,128)S(1)} collective-permute-done((f32[8,32,128]{2,1,0:T(8,128)S(1)}, f32[8,32,128]{2,1,0:T(8,128)S(1)}, u32[]{:S(2)}, u32[]{:S(2)}) %collective-permute-start.19) | collective-permute-done | bytes 131104 | tf_op jit(solution)/shard_map/ppermute | solution.py:575
  102.3 3.1 %last_outputs.1 = (f32[1,8,128,1024]{3,2,1,0:T(8,128)}, f32[1,128,1024]{2,1,0:T(8,128)}) custom-call(s32[21]{0:T(128)S(1)} %concatenate.9.refs_0_.where_ref, f32[8,128,1024]{2,1,0:T(8,128)S(1)} %get-tuple-element.102.most_ref, f32[128,1024]{1,0:T(8,128)S(1)} %get-tuple-element.103.most_seg_ref, f32[24,128]{1,0:T(8,128)S(1)} %get-tuple-element.104.coef_ref, ...), custom_call_target="tpu_custom_call" | custom-call | flops 3000000000 | bytes 1048576 | tf_op jit(solution)/shard_map/last_outputs/pallas_call | solution.py:477
  (51 shorter events, 16.1 us)
Async XLA Ops:
  0.6 10.3 %collective-permute-start.3 = (bf16[2048,128]{1,0:T(8,128)(2,1)}, bf16[2048,128]{1,0:T(8,128)(2,1)S(1)}, u32[]{:S(2)}, u32[]{:S(2)}) collective-permute-start(bf16[2048,128]{1,0:T(8,128)(2,1)} %refs_1_.1), channel_id=1, source_target_pairs={{0,1},{1,0},{2,3},{3,2},{4,5},{5,4},{6,7},{7,6},{8,9},{9,8},{10,11... | collective-permute-start | bytes 1572872 | tf_op jit(solution)/shard_map/ppermute | solution.py:575
  4.0 14.9 %collective-permute-start = (bf16[2048,128]{1,0:T(8,128)(2,1)}, bf16[2048,128]{1,0:T(8,128)(2,1)S(1)}, u32[]{:S(2)}, u32[]{:S(2)}) collective-permute-start(bf16[2048,128]{1,0:T(8,128)(2,1)} %refs_1_.1), channel_id=1, source_target_pairs={{0,2},{1,3},{2,4},{3,5},{4,6},{5,7},{6,0},{7,1},{8,10},{9,11},{10,... | collective-permute-start | bytes 1572872 | tf_op jit(solution)/shard_map/ppermute | solution.py:575
  4.0 14.9 %collective-permute-start.1 = (bf16[2048,128]{1,0:T(8,128)(2,1)}, bf16[2048,128]{1,0:T(8,128)(2,1)S(1)}, u32[]{:S(2)}, u32[]{:S(2)}) collective-permute-start(bf16[2048,128]{1,0:T(8,128)(2,1)} %refs_1_.1), channel_id=1, source_target_pairs={{0,6},{1,7},{2,0},{3,1},{4,2},{5,3},{6,4},{7,5},{8,14},{9,15},{10,... | collective-permute-start | bytes 1572872 | tf_op jit(solution)/shard_map/ppermute | solution.py:575
  7.7 8.4 %collective-permute-start.2 = (bf16[1024,128]{1,0:T(8,128)(2,1)S(1)}, bf16[1024,128]{1,0:T(8,128)(2,1)S(1)}, u32[]{:S(2)}, u32[]{:S(2)}) collective-permute-start(bf16[1024,128]{1,0:T(8,128)(2,1)S(1)} %slice.24), channel_id=1, source_target_pairs={{0,8},{8,16},{16,24},{24,32},{32,40},{40,48},{48,56},{56,64},{64,7... | collective-permute-start | bytes 786440 | tf_op jit(solution)/shard_map/ppermute | solution.py:599
  11.0 1.0 copy-start.2
  18.9 3.8 %collective-permute-start.7 = (bf16[2048,128]{1,0:T(8,128)(2,1)S(1)}, bf16[2048,128]{1,0:T(8,128)(2,1)S(1)}, u32[]{:S(2)}, u32[]{:S(2)}) collective-permute-start(bf16[2048,128]{1,0:T(8,128)(2,1)S(1)} %collective-permute-done.refs_2_), channel_id=1, source_target_pairs={{0,1},{1,0},{2,3},{3,2},{4,5},{5,4},{6,7},{7,6},{8,9},{9,8},{10,11... | collective-permute-start | bytes 1572872 | tf_op jit(solution)/shard_map/ppermute | solution.py:575
  19.7 6.7 %collective-permute-start.6 = (bf16[2048,128]{1,0:T(8,128)(2,1)S(1)}, bf16[2048,128]{1,0:T(8,128)(2,1)S(1)}, u32[]{:S(2)}, u32[]{:S(2)}) collective-permute-start(bf16[2048,128]{1,0:T(8,128)(2,1)S(1)} %collective-permute-done.1.refs_1_), channel_id=1, source_target_pairs={{0,1},{1,0},{2,3},{3,2},{4,5},{5,4},{6,7},{7,6},{8,9},{9,8},{10,11... | collective-permute-start | bytes 1572872 | tf_op jit(solution)/shard_map/ppermute | solution.py:575
  19.8 8.7 %collective-permute-start.4 = (bf16[1024,128]{1,0:T(8,128)(2,1)S(1)}, bf16[1024,128]{1,0:T(8,128)(2,1)S(1)}, u32[]{:S(2)}, u32[]{:S(2)}) collective-permute-start(bf16[1024,128]{1,0:T(8,128)(2,1)S(1)} %slice.25), channel_id=1, source_target_pairs={{0,2},{1,3},{2,4},{3,5},{4,6},{5,7},{6,0},{7,1},{8,10},{9,11},{10,... | collective-permute-start | bytes 786440 | tf_op jit(solution)/shard_map/ppermute | solution.py:575
  19.9 8.6 %collective-permute-start.5 = (bf16[1024,128]{1,0:T(8,128)(2,1)S(1)}, bf16[1024,128]{1,0:T(8,128)(2,1)S(1)}, u32[]{:S(2)}, u32[]{:S(2)}) collective-permute-start(bf16[1024,128]{1,0:T(8,128)(2,1)S(1)} %slice.26), channel_id=1, source_target_pairs={{0,6},{1,7},{2,0},{3,1},{4,2},{5,3},{6,4},{7,5},{8,14},{9,15},{10,... | collective-permute-start | bytes 786440 | tf_op jit(solution)/shard_map/ppermute | solution.py:575
  28.5 3.0 %collective-permute-start.8 = (bf16[2048,128]{1,0:T(8,128)(2,1)S(1)}, bf16[2048,128]{1,0:T(8,128)(2,1)S(1)}, u32[]{:S(2)}, u32[]{:S(2)}) collective-permute-start(bf16[2048,128]{1,0:T(8,128)(2,1)S(1)} %constant_dynamic-update-slice_fusion.refs_1_), channel_id=1, source_target_pairs={{0,1},{1,0},{2,3},{3,2},{4,5},{5,4},{6,7},{7,6},{8,9},{9,8},{10,11... | collective-permute-start | bytes 1572872 | tf_op jit(solution)/shard_map/ppermute | solution.py:575
  35.1 23.8 %all-to-all-start = ((f32[32,24,128]{2,1,0:T(8,128)}), f32[32,24,128]{2,1,0:T(8,128)}, u32[]{:S(2)}, u32[]{:S(2)}) async-start(f32[32,24,128]{2,1,0:T(8,128)} %get-tuple-element.74), calls=%async_computation | async-start | bytes 786432 | tf_op jit(solution)/shard_map/all_to_all | solution.py:579
  44.7 6.0 %copy-start.1 = (bf16[2048,256]{1,0:T(8,128)(2,1)S(1)}, bf16[2048,256]{1,0:T(8,128)(2,1)}, u32[]{:S(2)}) copy-start(bf16[2048,256]{1,0:T(8,128)(2,1)} %copy-done) | copy-start | bytes 3145732
  47.7 8.0 %collective-permute-start.10 = (bf16[1024,128]{1,0:T(8,128)(2,1)S(1)}, bf16[1024,128]{1,0:T(8,128)(2,1)S(1)}, u32[]{:S(2)}, u32[]{:S(2)}) collective-permute-start(bf16[1024,128]{1,0:T(8,128)(2,1)S(1)} %collective-permute-done.2), channel_id=1, source_target_pairs={{0,6},{1,7},{2,0},{3,1},{4,2},{5,3},{6,4},{7,5},{8,14},{9,15},{10,... | collective-permute-start | bytes 786440 | tf_op jit(solution)/shard_map/ppermute | solution.py:575
  50.7 8.2 %collective-permute-start.9 = (bf16[1024,128]{1,0:T(8,128)(2,1)S(1)}, bf16[1024,128]{1,0:T(8,128)(2,1)S(1)}, u32[]{:S(2)}, u32[]{:S(2)}) collective-permute-start(bf16[1024,128]{1,0:T(8,128)(2,1)S(1)} %collective-permute-done.2), channel_id=1, source_target_pairs={{0,2},{1,3},{2,4},{3,5},{4,6},{5,7},{6,0},{7,1},{8,10},{9,11},{10,... | collective-permute-start | bytes 786440 | tf_op jit(solution)/shard_map/ppermute | solution.py:575
  58.9 13.7 %collective-permute-start.11 = (bf16[512,128]{1,0:T(8,128)(2,1)S(1)}, bf16[512,128]{1,0:T(8,128)(2,1)S(1)}, u32[]{:S(2)}, u32[]{:S(2)}) collective-permute-start(bf16[512,128]{1,0:T(8,128)(2,1)S(1)} %slice.27), channel_id=1, source_target_pairs={{0,2},{1,3},{2,4},{3,5},{4,6},{5,7},{6,0},{7,1},{8,10},{9,11},{10,... | collective-permute-start | bytes 393224 | tf_op jit(solution)/shard_map/ppermute | solution.py:575
  59.1 13.6 %collective-permute-start.12 = (bf16[512,128]{1,0:T(8,128)(2,1)S(1)}, bf16[512,128]{1,0:T(8,128)(2,1)S(1)}, u32[]{:S(2)}, u32[]{:S(2)}) collective-permute-start(bf16[512,128]{1,0:T(8,128)(2,1)S(1)} %slice.28), channel_id=1, source_target_pairs={{0,6},{1,7},{2,0},{3,1},{4,2},{5,3},{6,4},{7,5},{8,14},{9,15},{10,... | collective-permute-start | bytes 393224 | tf_op jit(solution)/shard_map/ppermute | solution.py:575
  63.8 23.3 %all-to-all-start.1 = ((f32[32,40,128]{2,1,0:T(8,128)}), f32[32,40,128]{2,1,0:T(8,128)S(1)}, u32[]{:S(2)}, u32[]{:S(2)}) async-start(f32[32,40,128]{2,1,0:T(8,128)} %get-tuple-element.87), calls=%async_computation.1 | async-start | bytes 1310720 | tf_op jit(solution)/shard_map/all_to_all | solution.py:579
  72.7 8.8 %collective-permute-start.13 = (bf16[4096,128]{1,0:T(8,128)(2,1)S(1)}, bf16[4096,128]{1,0:T(8,128)(2,1)S(1)}, u32[]{:S(2)}, u32[]{:S(2)}) collective-permute-start(bf16[4096,128]{1,0:T(8,128)(2,1)S(1)} %constant_dynamic-update-slice_fusion.2.refs_1_), channel_id=1, source_target_pairs={{0,1},{1,0},{2,3},{3,2},{4,5},{5,4},{6,7},{7,6},{8,9},{9,8},{10,11... | collective-permute-start | bytes 3145736 | tf_op jit(solution)/shard_map/ppermute | solution.py:575
  75.8 3.1 %collective-permute-start.14 = (f32[2,32,128]{2,1,0:T(8,128)S(1)}, f32[2,32,128]{2,1,0:T(8,128)S(1)}, u32[]{:S(2)}, u32[]{:S(2)}) collective-permute-start(f32[2,32,128]{2,1,0:T(8,128)S(1)} %get-tuple-element.94.refs_7_), channel_id=1, source_target_pairs={{0,6},{1,7},{2,0},{3,1},{4,2},{5,3},{6,4},{7,5},{8,14},{9,15},{10,... | collective-permute-start | bytes 98312 | tf_op jit(solution)/shard_map/ppermute | solution.py:575
  75.8 4.3 %collective-permute-start.15 = (f32[2,32,128]{2,1,0:T(8,128)S(1)}, f32[2,32,128]{2,1,0:T(8,128)S(1)}, u32[]{:S(2)}, u32[]{:S(2)}) collective-permute-start(f32[2,32,128]{2,1,0:T(8,128)S(1)} %get-tuple-element.94.refs_7_), channel_id=1, source_target_pairs={{0,2},{1,3},{2,4},{3,5},{4,6},{5,7},{6,0},{7,1},{8,10},{9,11},{10,... | collective-permute-start | bytes 98312 | tf_op jit(solution)/shard_map/ppermute | solution.py:575
  77.3 4.3 %collective-permute-start.16 = (f32[2,32,128]{2,1,0:T(8,128)S(1)}, f32[2,32,128]{2,1,0:T(8,128)S(1)}, u32[]{:S(2)}, u32[]{:S(2)}) collective-permute-start(f32[2,32,128]{2,1,0:T(8,128)S(1)} %get-tuple-element.94.refs_7_), channel_id=1, source_target_pairs={{0,4},{1,5},{2,6},{3,7},{4,0},{5,1},{6,2},{7,3},{8,12},{9,13},{10,... | collective-permute-start | bytes 98312 | tf_op jit(solution)/shard_map/ppermute | solution.py:575
  87.1 13.6 %collective-permute-start.18 = (f32[8,32,128]{2,1,0:T(8,128)S(1)}, f32[8,32,128]{2,1,0:T(8,128)S(1)}, u32[]{:S(2)}, u32[]{:S(2)}) collective-permute-start(f32[8,32,128]{2,1,0:T(8,128)S(1)} %get-tuple-element.108), channel_id=1, source_target_pairs={{0,7},{1,6},{2,1},{3,0},{4,3},{5,2},{6,5},{7,4},{8,15},{9,14},{10,... | collective-permute-start | bytes 393224 | tf_op jit(solution)/shard_map/ppermute | solution.py:575
  93.5 8.9 %collective-permute-start.19 = (f32[8,32,128]{2,1,0:T(8,128)S(1)}, f32[8,32,128]{2,1,0:T(8,128)S(1)}, u32[]{:S(2)}, u32[]{:S(2)}) collective-permute-start(f32[8,32,128]{2,1,0:T(8,128)S(1)} %get-tuple-element.107), channel_id=1, source_target_pairs={{0,2},{1,3},{2,4},{3,5},{4,6},{5,7},{6,0},{7,1},{8,10},{9,11},{10,... | collective-permute-start | bytes 393224 | tf_op jit(solution)/shard_map/ppermute | solution.py:575
  95.0 7.3 %collective-permute-start.17 = (f32[32,8,128]{2,1,0:T(8,128)S(1)}, f32[32,8,128]{2,1,0:T(8,128)S(1)}, u32[]{:S(2)}, u32[]{:S(2)}) collective-permute-start(f32[32,8,128]{2,1,0:T(8,128)S(1)} %slice.29), channel_id=1, source_target_pairs={{0,4},{1,5},{2,6},{3,7},{4,1},{5,0},{6,3},{7,2},{8,12},{9,13},{10,... | collective-permute-start | bytes 393224 | tf_op jit(solution)/shard_map/ppermute | solution.py:575
  (1 other events, 1.0 us)

commit v5 on v4

--- a/solution.py
+++ b/solution.py
@@ -125,14 +125,18 @@
     left_part(where_ref, flipped, cent_ref, left_ref, sums_ref)
 
 
-def side_kernel(where_ref, first_ref, second_ref, flip_ref, gram_ref, stat_ref, cent_ref):
+def side_kernel(
+    where_ref, first_ref, second_ref, flip_ref, left_ref, sums_ref, gram_ref, stat_ref, cent_ref
+):
     center_pair(first_ref, second_ref, 0, WIDTH, cent_ref, stat_ref)
-    gram_ref[0] = jnp.dot(flip_ref[...], cent_ref[...], preferred_element_type=F32)
+    flipped = flip_ref[...]
+    gram_ref[0] = jnp.dot(flipped, cent_ref[...], preferred_element_type=F32)
+    left_part(where_ref, flipped, cent_ref, left_ref, sums_ref)
 
 
 def far_kernel(
     where_ref, first_ref, second_ref, flip_ref, total_ref, spread0_ref, spread1_ref, rider_ref,
-    gram_ref, stat_ref, out_ref, cent_ref, held_ref,
+    gram_ref, stat_ref, out_ref, held_ref, cent_ref,
 ):
     rider = rider_ref[0:4, :]
     for q in range(BLOCKS):
@@ -149,7 +153,8 @@
         out_ref[q, 16:20, :] = held_ref[4 * q : 4 * q + 4, :]
 
 
-def rest_kernel(where_ref, cent_ref, flip_ref, left_ref, sums_ref):
+def rest_kernel(where_ref, first_ref, second_ref, flip_ref, left_ref, sums_ref, cent_ref, stat_ref):
+    center_pair(first_ref, second_ref, 0, WIDTH, cent_ref, stat_ref)
     left_part(where_ref, flip_ref[...], cent_ref, left_ref, sums_ref)
 
 
@@ -375,7 +380,10 @@
                 (store_hbm.at[10, :, pl.ds(0, 40)], cols_ref),
                 (store_hbm.at[11, 0], turned_ref),
                 (store_hbm.at[11, 1, pl.ds(0, 24)], coef_ref),
-                (store_hbm.at[pl.ds(0, 8)], left_ref),
+                *(
+                    (store_hbm.at[pl.ds(0, 8), j], left_ref.at[:, j])
+                    for j in range(SPLITS)
+                ),
             )
         )
     ]
@@ -404,8 +412,8 @@
         for i in range(3):
             value = value + turned[i] * cols_ref[u, 32 + i : 33 + i, :]
         seg_ref[:, shard_lanes(where_ref, u)] = value
-    loads[5].wait()
     for j in range(SPLITS):
+        loads[5 + j].wait()
         turned = spread_out(range(j, 32, 8))
         a, b = coef_ref[j : j + 1, :], coef_ref[8 + j : 9 + j, :]
         for u in range(8):
@@ -463,7 +471,7 @@
         in_specs=[SM, whole(*back.shape), HBM],
         out_specs=[whole(*value.shape) for value in MOST],
         scratch_shapes=[pltpu.VMEM(value.shape, F32) for value in buffers]
-        + [pltpu.SemaphoreType.DMA((6,))],
+        + [pltpu.SemaphoreType.DMA((5 + SPLITS,))],
         compiler_params=params(24),
         cost_estimate=cost(5),
         name="most_outputs",
@@ -626,29 +634,31 @@
         pair=1,
         scratch=[((ROWS, PAIR), BF16)],
     )
-    cent_shape = array(ROWS, PAIR, dtype=BF16)
-    gram, stat, side = call(
+    store, sums, gram, stat = call(
         side_kernel,
         "side_pair",
         [where, ahead_other, behind, flipped],
-        ALL[1:] + [cent_shape],
-        stored=(0, 1),
-        kept=(gram, stat),
+        ALL,
+        store=store,
+        puts=((SHARD_PAIR, pl.ds(6, 2)),),
+        stored=(0, 1, 2),
+        kept=(sums, gram, stat),
         pair=3,
-        us=0.1,
+        scratch=[((ROWS, PAIR), BF16)],
+        us=2,
     )
     far_low, far_high, stat = lax.optimization_barrier((far_low, far_high, stat))
     far = jnp.concatenate([far_low, far_high], axis=0)
     far_other = to_chan(far, lambda s: s ^ 1)
-    gram, stat, pieces, cent = call(
+    gram, stat, pieces = call(
         far_kernel,
         "far_pair",
         [where, far, far_other, flipped, total, spread0, spread1, rider],
-        ALL[1:] + [array(BLOCKS, 24, WIDTH), cent_shape],
-        stored=(0, 1, 3),
+        ALL[1:] + [array(BLOCKS, 24, WIDTH)],
+        stored=(0, 1),
         kept=(gram, stat),
         pair=2,
-        scratch=[((WIDTH, WIDTH), F32)],
+        scratch=[((WIDTH, WIDTH), F32), ((ROWS, PAIR), BF16)],
         us=0.1,
     )
     arrived = exchange(pieces)
@@ -656,39 +666,23 @@
     store, sums = call(
         rest_kernel,
         "rest_left",
-        [where, after(side, cent), late_flipped],
-        ALL[:1],
-        store=store,
-        puts=((SHARD_PAIR, pl.ds(6, 2)),),
-        fetched=(2,),
-        stored=(0,),
-        kept=(sums,),
-        pair=3,
-        us=4,
-    )
-    prior = after(prior, sums)
-    prior_behind = to_chan(prior, lambda s: s + 2)
-    prior_ahead = to_chan(prior, lambda s: s - 2)
-    store, sums = call(
-        rest_kernel,
-        "rest_left",
-        [where, cent, late_flipped],
+        [where, after(far, pieces), far_other, late_flipped],
         ALL[:1],
         store=store,
         puts=((SHARD_PAIR, pl.ds(4, 2)),),
-        fetched=(1, 2),
+        fetched=(3,),
         stored=(0,),
         kept=(sums,),
         pair=2,
-        us=2,
-    )
-    arrived, prior_behind, prior_ahead, sums = lax.optimization_barrier(
-        (arrived, prior_behind, prior_ahead, sums)
-    )
-    half = HALO // 2
-    prior_low = to_chan(prior_behind[:half], lambda s: s + 2)
-    prior_high = to_chan(prior_ahead[half:], lambda s: s - 2)
-    prior = jnp.concatenate([prior, prior_ahead, prior_low, prior_high, prior_behind], axis=0)
+        scratch=[((ROWS, PAIR), BF16), ((1, 8, PAIR), F32)],
+        us=4,
+    )
+    prior = after(prior, sums)
+    prior_ahead = to_chan(prior, lambda s: s - 2)
+    prior_behind = to_chan(prior, lambda s: s + 2)
+    prior_far = to_chan(prior, lambda s: s + 4)
+    arrived, prior_ahead = lax.optimization_barrier((arrived, prior_ahead))
+    prior = jnp.concatenate([prior, prior_ahead, prior_far, prior_behind], axis=0)
     prior_other = to_chan(prior, lambda s: s ^ 1)
     scanned, own_means, flags = call(
         scan_kernel,

time: 106 us -> 106 us (level)
  local copies, waits for them, and re-layouts: 4.02 us -> 6.34 us
  Pallas kernels: 34.1 us -> 32 us
    unnamed x11 -> x12, local copies, waits for them, and re-layouts: 2.12 us -> 3.76 us
    pallas_call x8 -> x7, Pallas kernels: 25.3 us -> 23.9 us  [call(): pl.pallas_call(body, out_shape=[STORE] * first + outputs, grid=(1,), in_s...]
    ppermute x19 -> x18, starting transfers between devices: 29.4 us -> 28.6 us  [to_chan(): lax.ppermute(value, 'chan', [(s, target(s) % count) for s in range(count)])]
    ppermute x19 -> x18, waiting for transfers between devices: 15.5 us -> 15.9 us  [to_chan(): lax.ppermute(value, 'chan', [(s, target(s) % count) for s in range(count)])]
  transfers between devices with their start and end apart: 22 -> 21, of which waited for: 10 -> 6; matrix products, arithmetic and copies ran while one was open for 2% -> 4% of each run, Pallas kernels for 27% -> 25%
where the time goes in v5:
time: 106 us; the launch traced here: 105 us
  starting transfers between devices  49.4 us (47%)
  Pallas kernels  32 us (30%)
  waiting for transfers between devices  15.9 us (15%)
  local copies, waits for them, and re-layouts  6.34 us (6%)
  between operations  1.82 us (2%)
    ppermute x18, starting transfers between devices, to_chan(): lax.ppermute(value, 'chan', [(s, target(s) % count) for s in range(count)])  28.6 us
    pallas_call x7, Pallas kernels, call(): pl.pallas_call(body, out_shape=[STORE] * first + outputs, grid=(1,), in_s...  23.9 us
    all_to_all x2, starting transfers between devices, exchange(): return lax.all_to_all(value, 'tm', 0, 0, tiled=True)  19 us
    ppermute x18, waiting for transfers between devices, to_chan(): lax.ppermute(value, 'chan', [(s, target(s) % count) for s in range(count)])  15.9 us
    pallas_call x1, Pallas kernels, most_outputs(): pl.pallas_call(most_kernel, out_shape=MOST, grid=(1,), in_specs=[SM, whol...  5 us
    unnamed x12, local copies, waits for them, and re-layouts  3.76 us
    pallas_call x1, Pallas kernels, last_outputs(): pl.pallas_call(last_kernel, out_shape=OUTPUTS, grid=(1,), in_specs=[SM] +...  3.11 us
  transfers between devices with their start and end apart: 21, of which 6 were waited for; matrix products, arithmetic and copies ran while one was open for 4% of the time, Pallas kernels for 25%

profile of v5, /device:TPU:1, one launch (start us, length us, event | category | flops | bytes accessed | tf_op | source)
XLA Modules:
  0.0 105.5 jit_solution(3157156983373790511)
XLA Ops:
  0.6 3.3 %collective-permute-start.3 = (bf16[2048,128]{1,0:T(8,128)(2,1)}, bf16[2048,128]{1,0:T(8,128)(2,1)S(1)}, u32[]{:S(2)}, u32[]{:S(2)}) collective-permute-start(bf16[2048,128]{1,0:T(8,128)(2,1)} %refs_1_.1), channel_id=1, source_target_pairs={{0,1},{1,0},{2,3},{3,2},{4,5},{5,4},{6,7},{7,6},{8,9},{9,8},{10,11... | collective-permute-start | bytes 1572872 | tf_op jit(solution)/shard_map/ppermute | solution.py:583
  4.0 2.7 %collective-permute-start.1 = (bf16[2048,128]{1,0:T(8,128)(2,1)}, bf16[2048,128]{1,0:T(8,128)(2,1)S(1)}, u32[]{:S(2)}, u32[]{:S(2)}) collective-permute-start(bf16[2048,128]{1,0:T(8,128)(2,1)} %refs_1_.1), channel_id=1, source_target_pairs={{0,6},{1,7},{2,0},{3,1},{4,2},{5,3},{6,4},{7,5},{8,14},{9,15},{10,... | collective-permute-start | bytes 1572872 | tf_op jit(solution)/shard_map/ppermute | solution.py:583
  6.6 1.7 %slice.18 = bf16[1024,128]{1,0:T(8,128)(2,1)} slice(bf16[2048,128]{1,0:T(8,128)(2,1)} %refs_1_.1), slice={[1024:2048], [0:128]} | slice | bytes 524288 | tf_op jit(solution)/shard_map/slice | solution.py:607
  8.4 1.8 %collective-permute-start.2 = (bf16[1024,128]{1,0:T(8,128)(2,1)}, bf16[1024,128]{1,0:T(8,128)(2,1)S(1)}, u32[]{:S(2)}, u32[]{:S(2)}) collective-permute-start(bf16[1024,128]{1,0:T(8,128)(2,1)} %slice.18), channel_id=1, source_target_pairs={{0,8},{8,16},{16,24},{24,32},{32,40},{40,48},{48,56},{56,64},{64,7... | collective-permute-start | bytes 786440 | tf_op jit(solution)/shard_map/ppermute | solution.py:607
  12.7 4.1 %first_pair.1 = (f32[96,8,128,128]{3,2,1,0:T(8,128)}, f32[4,8,256]{2,1,0:T(8,128)S(1)}, f32[4,128,256]{2,1,0:T(8,128)S(1)}, f32[4,8,256]{2,1,0:T(8,128)S(1)}, bf...) custom-call(s32[21]{0:T(128)S(1)} %concatenate.9.refs_0_.where_ref, ...), custom_call_target="tpu_custom_call" | custom-call | flops 3000000000 | bytes 1048576 | tf_op jit(solution)/shard_map/first_pair/pallas_call | solution.py:215
  16.8 2.1 %collective-permute-done.refs_2_ = bf16[2048,128]{1,0:T(8,128)(2,1)S(1)} collective-permute-done((bf16[2048,128]{1,0:T(8,128)(2,1)}, bf16[2048,128]{1,0:T(8,128)(2,1)S(1)}, u32[]{:S(2)}, u32[]{:S(2)}) %collective-permute-start) | collective-permute-done | bytes 524320 | tf_op jit(solution)/shard_map/ppermute | solution.py:583
  19.9 2.8 %collective-permute-start.5 = (bf16[1024,128]{1,0:T(8,128)(2,1)S(1)}, bf16[1024,128]{1,0:T(8,128)(2,1)S(1)}, u32[]{:S(2)}, u32[]{:S(2)}) collective-permute-start(bf16[1024,128]{1,0:T(8,128)(2,1)S(1)} %slice.20), channel_id=1, source_target_pairs={{0,6},{1,7},{2,0},{3,1},{4,2},{5,3},{6,4},{7,5},{8,14},{9,15},{10,... | collective-permute-start | bytes 786440 | tf_op jit(solution)/shard_map/ppermute | solution.py:583
  22.6 3.8 %near_pair.1 = (f32[96,8,128,128]{3,2,1,0:T(8,128)}, f32[4,8,256]{2,1,0:T(8,128)S(1)}, f32[4,128,256]{2,1,0:T(8,128)S(1)}, f32[4,8,256]{2,1,0:T(8,128)S(1)}, f32[128,256]{1,0:T(8,128)S(1)}) custom-call(s32[21]{0:T(128)S(1)} %concatenate.9.refs_0_.where_ref, ...), custom_call_target="tpu_custom_call", output_to_operand_aliasing={{0}: (5, {}), {1}: (6, {}), {2}: (7, {}), {3}: (8, {})} | custom-call | flops 3000000000 | bytes 1048576 | tf_op jit(solution)/shard_map/near_pair/pallas_call | solution.py:215
  26.4 3.8 %side_pair.1 = (f32[96,8,128,128]{3,2,1,0:T(8,128)}, f32[4,8,256]{2,1,0:T(8,128)S(1)}, f32[4,128,256]{2,1,0:T(8,128)S(1)}, f32[4,8,256]{2,1,0:T(8,128)S(1)}) custom-call(s32[21]{0:T(128)S(1)} %concatenate.9.refs_0_.where_ref, ...), custom_call_target="tpu_custom_call", output_to_operand_aliasing={{0}: (4, {}), {1}: (5, {}), {2}: (6, {}), {3}: (7, {})} | custom-call | flops 2000000000 | bytes 1048576 | tf_op jit(solution)/shard_map/side_pair/pallas_call | solution.py:215
  31.4 1.5 %collective-permute-done.8.refs_2_ = bf16[2048,128]{1,0:T(8,128)(2,1)S(1)} collective-permute-done((bf16[2048,128]{1,0:T(8,128)(2,1)S(1)}, bf16[2048,128]{1,0:T(8,128)(2,1)S(1)}, u32[]{:S(2)}, u32[]{:S(2)}) %collective-permute-start.8) | collective-permute-done | bytes 524320 | tf_op jit(solution)/shard_map/ppermute | solution.py:583
  33.0 2.5 %far_pair.1 = (f32[4,128,256]{2,1,0:T(8,128)S(1)}, f32[4,8,256]{2,1,0:T(8,128)S(1)}, f32[32,24,128]{2,1,0:T(8,128)}) custom-call(s32[21]{0:T(128)S(1)} %concatenate.9.refs_0_.where_ref, bf16[2048,128]{1,0:T(8,128)(2,1)S(1)} %constant_dynamic-update-slice_fusion.refs_1_, ...), custom_call_target="tpu_custom_call", output_to_operand_aliasing={{0}: (8, {}), {1}: (9, {})} | custom-call | flops 100000000 | bytes 1048576 | tf_op jit(solution)/shard_map/far_pair/pallas_call | solution.py:215
  35.5 10.4 %all-to-all-start = ((f32[32,24,128]{2,1,0:T(8,128)}), f32[32,24,128]{2,1,0:T(8,128)S(1)}, u32[]{:S(2)}, u32[]{:S(2)}) async-start(f32[32,24,128]{2,1,0:T(8,128)} %get-tuple-element.72), calls=%async_computation | async-start | bytes 786432 | tf_op jit(solution)/shard_map/all_to_all | solution.py:587
  45.9 3.7 %rest_left.1 = (f32[96,8,128,128]{3,2,1,0:T(8,128)}, f32[4,8,256]{2,1,0:T(8,128)S(1)}) custom-call(s32[21]{0:T(128)S(1)} %concatenate.9.refs_0_.where_ref, bf16[2048,128]{1,0:T(8,128)(2,1)S(1)} %constant_dynamic-update-slice_fusion.refs_1_, bf16[2048,128]{1,0:T(8,128)(2,1)S(1)} %collective-permute-done.8.refs_2_, ...), custom_call_target="tpu_custom_call", output_to_operand_aliasing={{0}: (4, {}), {1}: (5, {})} | custom-call | flops 4000000000 | bytes 1048576 | tf_op jit(solution)/shard_map/rest_left/pallas_call | solution.py:215
  49.7 1.4 %collective-permute-start.9 = (bf16[1024,128]{1,0:T(8,128)(2,1)S(1)}, bf16[1024,128]{1,0:T(8,128)(2,1)S(1)}, u32[]{:S(2)}, u32[]{:S(2)}) collective-permute-start(bf16[1024,128]{1,0:T(8,128)(2,1)S(1)} %copy-done.2), channel_id=1, source_target_pairs={{0,6},{1,7},{2,0},{3,1},{4,2},{5,3},{6,4},{7,5},{8,14},{9,15},{10,... | collective-permute-start | bytes 786440 | tf_op jit(solution)/shard_map/ppermute | solution.py:583
  51.8 5.2 %collective-permute-done.9 = bf16[1024,128]{1,0:T(8,128)(2,1)S(1)} collective-permute-done((bf16[1024,128]{1,0:T(8,128)(2,1)S(1)}, bf16[1024,128]{1,0:T(8,128)(2,1)S(1)}, u32[]{:S(2)}, u32[]{:S(2)}) %collective-permute-start.9) | collective-permute-done | bytes 262176 | tf_op jit(solution)/shard_map/ppermute | solution.py:583
  58.8 8.6 %all-to-all-start.1 = ((f32[32,40,128]{2,1,0:T(8,128)}), f32[32,40,128]{2,1,0:T(8,128)S(1)}, u32[]{:S(2)}, u32[]{:S(2)}) async-start(f32[32,40,128]{2,1,0:T(8,128)} %get-tuple-element.81), calls=%async_computation.1 | async-start | bytes 1310720 | tf_op jit(solution)/shard_map/all_to_all | solution.py:587
  69.5 3.7 %collective-permute-start.12 = (bf16[4096,128]{1,0:T(8,128)(2,1)S(1)}, bf16[4096,128]{1,0:T(8,128)(2,1)S(1)}, u32[]{:S(2)}, u32[]{:S(2)}) collective-permute-start(bf16[4096,128]{1,0:T(8,128)(2,1)S(1)} %constant_dynamic-update-slice_fusion.2.refs_1_), channel_id=1, source_target_pairs={{0,1},{1,0},{2,3},{3,2},{4,5},{5,4},{6,7},{7,6},{8,9},{9,8},{10,11... | collective-permute-start | bytes 3145736 | tf_op jit(solution)/shard_map/ppermute | solution.py:583
  73.1 6.7 %collective-permute-start.13 = (f32[2,32,128]{2,1,0:T(8,128)S(1)}, f32[2,32,128]{2,1,0:T(8,128)S(1)}, u32[]{:S(2)}, u32[]{:S(2)}) collective-permute-start(f32[2,32,128]{2,1,0:T(8,128)S(1)} %get-tuple-element.86.refs_7_), channel_id=1, source_target_pairs={{0,6},{1,7},{2,0},{3,1},{4,2},{5,3},{6,4},{7,5},{8,14},{9,15},{10,... | collective-permute-start | bytes 98312 | tf_op jit(solution)/shard_map/ppermute | solution.py:583
  81.0 3.1 %collective-permute-done.14.refs_9_ = f32[2,32,128]{2,1,0:T(8,128)S(1)} collective-permute-done((f32[2,32,128]{2,1,0:T(8,128)S(1)}, f32[2,32,128]{2,1,0:T(8,128)S(1)}, u32[]{:S(2)}, u32[]{:S(2)}) %collective-permute-start.14) | collective-permute-done | bytes 32800 | tf_op jit(solution)/shard_map/ppermute | solution.py:583
  84.4 5.0 %late_terms.1 = (f32[96,8,128,128]{3,2,1,0:T(8,128)}, f32[1,128,1024]{2,1,0:T(8,128)}) custom-call(s32[21]{0:T(128)S(1)} %concatenate.9.refs_0_.where_ref, bf16[4096,128]{1,0:T(8,128)(2,1)S(1)} %constant_dynamic-update-slice_fusion.2.refs_1_, bf16[4096,128]{1,0:T(8,128)(2,1)S(1)} %collective-permute-done.12.refs_2_, ...), custom_call_target="tpu_custom_call", output_to_operand_aliasing={{0}: (12, {})} | custom-call | flops 100000000 | bytes 1048576 | tf_op jit(solution)/shard_map/late_terms/pallas_call | solution.py:215
  89.4 4.1 %collective-permute-start.17 = (f32[8,32,128]{2,1,0:T(8,128)S(1)}, f32[8,32,128]{2,1,0:T(8,128)S(1)}, u32[]{:S(2)}, u32[]{:S(2)}) collective-permute-start(f32[8,32,128]{2,1,0:T(8,128)S(1)} %get-tuple-element.100), channel_id=1, source_target_pairs={{0,7},{1,6},{2,1},{3,0},{4,3},{5,2},{6,5},{7,4},{8,15},{9,14},{10,... | collective-permute-start | bytes 393224 | tf_op jit(solution)/shard_map/ppermute | solution.py:583
  93.5 5.0 %most_outputs.1 = (f32[8,128,1024]{2,1,0:T(8,128)S(1)}, f32[128,1024]{1,0:T(8,128)S(1)}, f32[24,128]{1,0:T(8,128)S(1)}) custom-call(s32[21]{0:T(128)S(1)} %concatenate.9.refs_0_.where_ref, f32[32,40,128]{2,1,0:T(8,128)S(1)} %all-to-all-done.1.back_ref, f32[96,8,128,128]{3,2,1,0:T(8,128)} %get-tuple-element.93.store_hbm), custom_call_target="tpu_custom_call" | custom-call | flops 5000000000 | bytes 1048576 | tf_op jit(solution)/shard_map/most_outputs/pallas_call | solution.py:467
  98.6 3.6 %collective-permute-done.18.before_ref = f32[8,32,128]{2,1,0:T(8,128)S(1)} collective-permute-done((f32[8,32,128]{2,1,0:T(8,128)S(1)}, f32[8,32,128]{2,1,0:T(8,128)S(1)}, u32[]{:S(2)}, u32[]{:S(2)}) %collective-permute-start.18) | collective-permute-done | bytes 131104 | tf_op jit(solution)/shard_map/ppermute | solution.py:583
  102.2 3.1 %last_outputs.1 = (f32[1,8,128,1024]{3,2,1,0:T(8,128)}, f32[1,128,1024]{2,1,0:T(8,128)}) custom-call(s32[21]{0:T(128)S(1)} %concatenate.9.refs_0_.where_ref, f32[8,128,1024]{2,1,0:T(8,128)S(1)} %get-tuple-element.94.most_ref, f32[128,1024]{1,0:T(8,128)S(1)} %get-tuple-element.95.most_seg_ref, f32[24,128]{1,0:T(8,128)S(1)} %get-tuple-element.96.coef_ref, ...), custom_call_target="tpu_custom_call" | custom-call | flops 3000000000 | bytes 1048576 | tf_op jit(solution)/shard_map/last_outputs/pallas_call | solution.py:485
  (47 shorter events, 9.9 us)
Async XLA Ops:
  0.6 11.0 %collective-permute-start.3 = (bf16[2048,128]{1,0:T(8,128)(2,1)}, bf16[2048,128]{1,0:T(8,128)(2,1)S(1)}, u32[]{:S(2)}, u32[]{:S(2)}) collective-permute-start(bf16[2048,128]{1,0:T(8,128)(2,1)} %refs_1_.1), channel_id=1, source_target_pairs={{0,1},{1,0},{2,3},{3,2},{4,5},{5,4},{6,7},{7,6},{8,9},{9,8},{10,11... | collective-permute-start | bytes 1572872 | tf_op jit(solution)/shard_map/ppermute | solution.py:583
  4.0 14.9 %collective-permute-start = (bf16[2048,128]{1,0:T(8,128)(2,1)}, bf16[2048,128]{1,0:T(8,128)(2,1)S(1)}, u32[]{:S(2)}, u32[]{:S(2)}) collective-permute-start(bf16[2048,128]{1,0:T(8,128)(2,1)} %refs_1_.1), channel_id=1, source_target_pairs={{0,2},{1,3},{2,4},{3,5},{4,6},{5,7},{6,0},{7,1},{8,10},{9,11},{10,... | collective-permute-start | bytes 1572872 | tf_op jit(solution)/shard_map/ppermute | solution.py:583
  4.0 14.9 %collective-permute-start.1 = (bf16[2048,128]{1,0:T(8,128)(2,1)}, bf16[2048,128]{1,0:T(8,128)(2,1)S(1)}, u32[]{:S(2)}, u32[]{:S(2)}) collective-permute-start(bf16[2048,128]{1,0:T(8,128)(2,1)} %refs_1_.1), channel_id=1, source_target_pairs={{0,6},{1,7},{2,0},{3,1},{4,2},{5,3},{6,4},{7,5},{8,14},{9,15},{10,... | collective-permute-start | bytes 1572872 | tf_op jit(solution)/shard_map/ppermute | solution.py:583
  8.4 8.4 %collective-permute-start.2 = (bf16[1024,128]{1,0:T(8,128)(2,1)}, bf16[1024,128]{1,0:T(8,128)(2,1)S(1)}, u32[]{:S(2)}, u32[]{:S(2)}) collective-permute-start(bf16[1024,128]{1,0:T(8,128)(2,1)} %slice.18), channel_id=1, source_target_pairs={{0,8},{8,16},{16,24},{24,32},{32,40},{40,48},{48,56},{56,64},{64,7... | collective-permute-start | bytes 786440 | tf_op jit(solution)/shard_map/ppermute | solution.py:607
  11.6 1.0 copy-start
  16.8 13.5 %copy-start.1 = (bf16[1024,128]{1,0:T(8,128)(2,1)}, bf16[1024,128]{1,0:T(8,128)(2,1)S(1)}, u32[]{:S(2)}) copy-start(bf16[1024,128]{1,0:T(8,128)(2,1)S(1)} %collective-permute-done.2) | copy-start | bytes 786436
  18.9 3.8 %collective-permute-start.7 = (bf16[2048,128]{1,0:T(8,128)(2,1)S(1)}, bf16[2048,128]{1,0:T(8,128)(2,1)S(1)}, u32[]{:S(2)}, u32[]{:S(2)}) collective-permute-start(bf16[2048,128]{1,0:T(8,128)(2,1)S(1)} %collective-permute-done.refs_2_), channel_id=1, source_target_pairs={{0,1},{1,0},{2,3},{3,2},{4,5},{5,4},{6,7},{7,6},{8,9},{9,8},{10,11... | collective-permute-start | bytes 1572872 | tf_op jit(solution)/shard_map/ppermute | solution.py:583
  19.7 6.7 %collective-permute-start.6 = (bf16[2048,128]{1,0:T(8,128)(2,1)S(1)}, bf16[2048,128]{1,0:T(8,128)(2,1)S(1)}, u32[]{:S(2)}, u32[]{:S(2)}) collective-permute-start(bf16[2048,128]{1,0:T(8,128)(2,1)S(1)} %collective-permute-done.1.refs_1_), channel_id=1, source_target_pairs={{0,1},{1,0},{2,3},{3,2},{4,5},{5,4},{6,7},{7,6},{8,9},{9,8},{10,11... | collective-permute-start | bytes 1572872 | tf_op jit(solution)/shard_map/ppermute | solution.py:583
  19.8 10.5 %collective-permute-start.4 = (bf16[1024,128]{1,0:T(8,128)(2,1)S(1)}, bf16[1024,128]{1,0:T(8,128)(2,1)S(1)}, u32[]{:S(2)}, u32[]{:S(2)}) collective-permute-start(bf16[1024,128]{1,0:T(8,128)(2,1)S(1)} %slice.19), channel_id=1, source_target_pairs={{0,2},{1,3},{2,4},{3,5},{4,6},{5,7},{6,0},{7,1},{8,10},{9,11},{10,... | collective-permute-start | bytes 786440 | tf_op jit(solution)/shard_map/ppermute | solution.py:583
  19.9 10.4 %collective-permute-start.5 = (bf16[1024,128]{1,0:T(8,128)(2,1)S(1)}, bf16[1024,128]{1,0:T(8,128)(2,1)S(1)}, u32[]{:S(2)}, u32[]{:S(2)}) collective-permute-start(bf16[1024,128]{1,0:T(8,128)(2,1)S(1)} %slice.20), channel_id=1, source_target_pairs={{0,6},{1,7},{2,0},{3,1},{4,2},{5,3},{6,4},{7,5},{8,14},{9,15},{10,... | collective-permute-start | bytes 786440 | tf_op jit(solution)/shard_map/ppermute | solution.py:583
  30.3 19.4 %copy-start.2 = (bf16[1024,128]{1,0:T(8,128)(2,1)S(1)}, bf16[1024,128]{1,0:T(8,128)(2,1)}, u32[]{:S(2)}) copy-start(bf16[1024,128]{1,0:T(8,128)(2,1)} %copy-done.1) | copy-start | bytes 786436
  30.4 2.6 %collective-permute-start.8 = (bf16[2048,128]{1,0:T(8,128)(2,1)S(1)}, bf16[2048,128]{1,0:T(8,128)(2,1)S(1)}, u32[]{:S(2)}, u32[]{:S(2)}) collective-permute-start(bf16[2048,128]{1,0:T(8,128)(2,1)S(1)} %constant_dynamic-update-slice_fusion.refs_1_), channel_id=1, source_target_pairs={{0,1},{1,0},{2,3},{3,2},{4,5},{5,4},{6,7},{7,6},{8,9},{9,8},{10,11... | collective-permute-start | bytes 1572872 | tf_op jit(solution)/shard_map/ppermute | solution.py:583
  35.5 22.2 %all-to-all-start = ((f32[32,24,128]{2,1,0:T(8,128)}), f32[32,24,128]{2,1,0:T(8,128)S(1)}, u32[]{:S(2)}, u32[]{:S(2)}) async-start(f32[32,24,128]{2,1,0:T(8,128)} %get-tuple-element.72), calls=%async_computation | async-start | bytes 786432 | tf_op jit(solution)/shard_map/all_to_all | solution.py:587
  49.7 7.4 %collective-permute-start.9 = (bf16[1024,128]{1,0:T(8,128)(2,1)S(1)}, bf16[1024,128]{1,0:T(8,128)(2,1)S(1)}, u32[]{:S(2)}, u32[]{:S(2)}) collective-permute-start(bf16[1024,128]{1,0:T(8,128)(2,1)S(1)} %copy-done.2), channel_id=1, source_target_pairs={{0,6},{1,7},{2,0},{3,1},{4,2},{5,3},{6,4},{7,5},{8,14},{9,15},{10,... | collective-permute-start | bytes 786440 | tf_op jit(solution)/shard_map/ppermute | solution.py:583
  51.0 17.4 %collective-permute-start.10 = (bf16[1024,128]{1,0:T(8,128)(2,1)S(1)}, bf16[1024,128]{1,0:T(8,128)(2,1)}, u32[]{:S(2)}, u32[]{:S(2)}) collective-permute-start(bf16[1024,128]{1,0:T(8,128)(2,1)S(1)} %copy-done.2), channel_id=1, source_target_pairs={{0,4},{1,5},{2,6},{3,7},{4,0},{5,1},{6,2},{7,3},{8,12},{9,13},{10,... | collective-permute-start | bytes 786440 | tf_op jit(solution)/shard_map/ppermute | solution.py:583
  51.1 18.3 %collective-permute-start.11 = (bf16[1024,128]{1,0:T(8,128)(2,1)S(1)}, bf16[1024,128]{1,0:T(8,128)(2,1)S(1)}, u32[]{:S(2)}, u32[]{:S(2)}) collective-permute-start(bf16[1024,128]{1,0:T(8,128)(2,1)S(1)} %copy-done.2), channel_id=1, source_target_pairs={{0,2},{1,3},{2,4},{3,5},{4,6},{5,7},{6,0},{7,1},{8,10},{9,11},{10,... | collective-permute-start | bytes 786440 | tf_op jit(solution)/shard_map/ppermute | solution.py:583
  58.8 30.6 %all-to-all-start.1 = ((f32[32,40,128]{2,1,0:T(8,128)}), f32[32,40,128]{2,1,0:T(8,128)S(1)}, u32[]{:S(2)}, u32[]{:S(2)}) async-start(f32[32,40,128]{2,1,0:T(8,128)} %get-tuple-element.81), calls=%async_computation.1 | async-start | bytes 1310720 | tf_op jit(solution)/shard_map/all_to_all | solution.py:587
  69.5 14.9 %collective-permute-start.12 = (bf16[4096,128]{1,0:T(8,128)(2,1)S(1)}, bf16[4096,128]{1,0:T(8,128)(2,1)S(1)}, u32[]{:S(2)}, u32[]{:S(2)}) collective-permute-start(bf16[4096,128]{1,0:T(8,128)(2,1)S(1)} %constant_dynamic-update-slice_fusion.2.refs_1_), channel_id=1, source_target_pairs={{0,1},{1,0},{2,3},{3,2},{4,5},{5,4},{6,7},{7,6},{8,9},{9,8},{10,11... | collective-permute-start | bytes 3145736 | tf_op jit(solution)/shard_map/ppermute | solution.py:583
  73.1 7.9 %collective-permute-start.13 = (f32[2,32,128]{2,1,0:T(8,128)S(1)}, f32[2,32,128]{2,1,0:T(8,128)S(1)}, u32[]{:S(2)}, u32[]{:S(2)}) collective-permute-start(f32[2,32,128]{2,1,0:T(8,128)S(1)} %get-tuple-element.86.refs_7_), channel_id=1, source_target_pairs={{0,6},{1,7},{2,0},{3,1},{4,2},{5,3},{6,4},{7,5},{8,14},{9,15},{10,... | collective-permute-start | bytes 98312 | tf_op jit(solution)/shard_map/ppermute | solution.py:583
  79.8 4.3 %collective-permute-start.14 = (f32[2,32,128]{2,1,0:T(8,128)S(1)}, f32[2,32,128]{2,1,0:T(8,128)S(1)}, u32[]{:S(2)}, u32[]{:S(2)}) collective-permute-start(f32[2,32,128]{2,1,0:T(8,128)S(1)} %get-tuple-element.86.refs_7_), channel_id=1, source_target_pairs={{0,2},{1,3},{2,4},{3,5},{4,6},{5,7},{6,0},{7,1},{8,10},{9,11},{10,... | collective-permute-start | bytes 98312 | tf_op jit(solution)/shard_map/ppermute | solution.py:583
  79.8 4.6 %collective-permute-start.15 = (f32[2,32,128]{2,1,0:T(8,128)S(1)}, f32[2,32,128]{2,1,0:T(8,128)S(1)}, u32[]{:S(2)}, u32[]{:S(2)}) collective-permute-start(f32[2,32,128]{2,1,0:T(8,128)S(1)} %get-tuple-element.86.refs_7_), channel_id=1, source_target_pairs={{0,4},{1,5},{2,6},{3,7},{4,0},{5,1},{6,2},{7,3},{8,12},{9,13},{10,... | collective-permute-start | bytes 98312 | tf_op jit(solution)/shard_map/ppermute | solution.py:583
  89.4 9.1 %collective-permute-start.17 = (f32[8,32,128]{2,1,0:T(8,128)S(1)}, f32[8,32,128]{2,1,0:T(8,128)S(1)}, u32[]{:S(2)}, u32[]{:S(2)}) collective-permute-start(f32[8,32,128]{2,1,0:T(8,128)S(1)} %get-tuple-element.100), channel_id=1, source_target_pairs={{0,7},{1,6},{2,1},{3,0},{4,3},{5,2},{6,5},{7,4},{8,15},{9,14},{10,... | collective-permute-start | bytes 393224 | tf_op jit(solution)/shard_map/ppermute | solution.py:583
  93.5 8.6 %collective-permute-start.18 = (f32[8,32,128]{2,1,0:T(8,128)S(1)}, f32[8,32,128]{2,1,0:T(8,128)S(1)}, u32[]{:S(2)}, u32[]{:S(2)}) collective-permute-start(f32[8,32,128]{2,1,0:T(8,128)S(1)} %get-tuple-element.99), channel_id=1, source_target_pairs={{0,2},{1,3},{2,4},{3,5},{4,6},{5,7},{6,0},{7,1},{8,10},{9,11},{10,... | collective-permute-start | bytes 393224 | tf_op jit(solution)/shard_map/ppermute | solution.py:583
  93.5 8.6 %collective-permute-start.16 = (f32[32,8,128]{2,1,0:T(8,128)S(1)}, f32[32,8,128]{2,1,0:T(8,128)S(1)}, u32[]{:S(2)}, u32[]{:S(2)}) collective-permute-start(f32[32,8,128]{2,1,0:T(8,128)S(1)} %slice.21), channel_id=1, source_target_pairs={{0,4},{1,5},{2,6},{3,7},{4,1},{5,0},{6,3},{7,2},{8,12},{9,13},{10,... | collective-permute-start | bytes 393224 | tf_op jit(solution)/shard_map/ppermute | solution.py:583
  (1 other events, 0.7 us)

commit v6 on v5

--- a/solution.py
+++ b/solution.py
@@ -497,13 +497,8 @@
 
 
 def window_kernel(
-    where_ref, mine_ref, other_ref, gram_ref, stat_ref, total_ref,
-    out_ref, cent_ref, flip_ref, sum_ref,
-):
-    halves = (
-        (mine_ref, 0), (other_ref, 0), (mine_ref, HALO), (other_ref, 3 * HALO),
-        (mine_ref, 2 * HALO), (other_ref, 2 * HALO), (other_ref, HALO), (mine_ref, 3 * HALO),
-    )
+    where_ref, halves, gram_ref, stat_ref, total_ref, out_ref, cent_ref, flip_ref, sum_ref,
+):
     live = jnp.where(where_ref[0] > 0, 1.0, 0.0).astype(F32)
     core = where_ref[2]
     at = pl.multiple_of(core * WIDTH, WIDTH)
@@ -514,11 +509,11 @@
     step = 256
     for r in range(CHIPS):
         lanes = (at, off) if r == 0 else (0, WIDTH)
-        for (raw, row), lane in zip(halves[2 * r : 2 * r + 2], lanes):
+        for raw, lane in zip(halves[2 * r : 2 * r + 2], lanes):
             mean = stat_ref[r, 0:1, pl.ds(lane, WIDTH)]
 
-            def shift(i, _, raw=raw, row=row, lane=lane, mean=mean):
-                piece = (raw[pl.ds(row + i * step, step), :].astype(F32) - mean) * live
+            def shift(i, _, raw=raw, lane=lane, mean=mean):
+                piece = (raw[pl.ds(i * step, step), :].astype(F32) - mean) * live
                 cent_ref[pl.ds(i * step, step), pl.ds(lane, WIDTH)] = piece.astype(BF16)
                 return 0
 
@@ -539,7 +534,8 @@
 
 
 def late_kernel(
-    where_ref, mine_ref, other_ref, total_ref, sums_ref, gram_ref, stat_ref, own_ref, ahead_ref, behind_ref, far_ref, flags_ref,
+    where_ref, h0, h1, h2, h3, h4, h5, h6, h7, total_ref, sums_ref, gram_ref, stat_ref,
+    own_ref, ahead_ref, behind_ref, far_ref, flags_ref,
     turned_ref, cols_ref, coef_ref, before_ref, after_ref, window_ref, vectors, cent_ref, flip_ref, sum_ref,
 ):
     prep_kernel(
@@ -547,16 +543,17 @@
         turned_ref, cols_ref, coef_ref, before_ref, after_ref, vectors,
     )
     window_kernel(
-        where_ref, mine_ref, other_ref, gram_ref, stat_ref, total_ref, window_ref, cent_ref, flip_ref, sum_ref
-    )
-
-
-def late_terms(where, mine, other, total, sums, gram, stat, means, flags, store):
+        where_ref, (h0, h1, h2, h3, h4, h5, h6, h7), gram_ref, stat_ref, total_ref,
+        window_ref, cent_ref, flip_ref, sum_ref,
+    )
+
+
+def late_terms(where, halves, total, sums, gram, stat, means, flags, store):
     square = (8, WIDTH, WIDTH)
     return call(
         late_kernel,
         "late_terms",
-        [where, mine, other, total, sums, gram, stat, *means, flags],
+        [where, *halves, total, sums, gram, stat, *means, flags],
         [array(1, WIDTH, CHIPS * PAIR)],
         store=store,
         puts=(
@@ -566,7 +563,7 @@
             (square, 8),
             (square, 9),
         ),
-        fetched=(3, 4, 5, 6, 7, 11),
+        fetched=(9, 10, 11, 12, 13, 17),
         stored=(0,),
         scratch=[
             ((WIDTH, WIDTH), F32),
@@ -681,9 +678,7 @@
     prior_ahead = to_chan(prior, lambda s: s - 2)
     prior_behind = to_chan(prior, lambda s: s + 2)
     prior_far = to_chan(prior, lambda s: s + 4)
-    arrived, prior_ahead = lax.optimization_barrier((arrived, prior_ahead))
-    prior = jnp.concatenate([prior, prior_ahead, prior_far, prior_behind], axis=0)
-    prior_other = to_chan(prior, lambda s: s ^ 1)
+    arrived = after(arrived, sums)
     scanned, own_means, flags = call(
         scan_kernel,
         "scan_pieces",
@@ -697,8 +692,12 @@
     behind_means = to_chan(own_means, lambda s: s + 2)
     far_means = to_chan(own_means, lambda s: s + 4)
     means = (own_means, ahead_means, behind_means, far_means)
+    halo = (prior, prior_ahead, prior_far, prior_behind)
+    halo, means = lax.optimization_barrier((halo, means))
+    mine, other = halo, [to_chan(value, lambda s: s ^ 1) for value in halo]
+    halves = (mine[0], other[0], mine[1], other[3], mine[2], other[2], other[1], mine[3])
     store, window_cov = late_terms(
-        where, prior, prior_other, late_total, sums, gram, stat, means, flags, store
+        where, halves, late_total, sums, gram, stat, means, flags, store
     )
     back, store, window_cov = lax.optimization_barrier((back, store, window_cov))
     before = to_chan(back[16:24, 0:32], lambda s: s + 2)

time: 106 us -> 105 us (level)
  waiting for transfers between devices: 15.9 us -> 26.5 us
  starting transfers between devices: 49.4 us -> 41.2 us
  local copies, waits for them, and re-layouts: 6.34 us -> 2.9 us
    all_to_all x2, waiting for transfers between devices: 0.01 us -> 7.88 us  [exchange(): return lax.all_to_all(value, 'tm', 0, 0, tiled=True)]
    ppermute x18 -> x21, starting transfers between devices: 28.6 us -> 22.1 us  [to_chan(): lax.ppermute(value, 'chan', [(s, target(s) % count) for s in range(count)])]
    ppermute x18 -> x21, waiting for transfers between devices: 15.9 us -> 18.6 us  [to_chan(): lax.ppermute(value, 'chan', [(s, target(s) % count) for s in range(count)])]
    unnamed x12 -> x3, local copies, waits for them, and re-layouts: 3.76 us -> 1.06 us
    all_to_all x2, starting transfers between devices: 19 us -> 17.2 us  [exchange(): return lax.all_to_all(value, 'tm', 0, 0, tiled=True)]
  transfers between devices with their start and end apart: 21 -> 24, of which waited for: 6 -> 11; matrix products, arithmetic and copies ran while one was open for 4% -> 2% of each run, Pallas kernels for 25% -> 24%
where the time goes in v6:
time: 105 us; the launch traced here: 104 us
  starting transfers between devices  41.2 us (39%)
  Pallas kernels  32.1 us (31%)
  waiting for transfers between devices  26.5 us (25%)
  local copies, waits for them, and re-layouts  2.9 us (3%)
  between operations  1.76 us (2%)
    pallas_call x7, Pallas kernels, call(): pl.pallas_call(body, out_shape=[STORE] * first + outputs, grid=(1,), in_s...  24 us
    ppermute x21, starting transfers between devices, to_chan(): lax.ppermute(value, 'chan', [(s, target(s) % count) for s in range(count)])  22.1 us
    ppermute x21, waiting for transfers between devices, to_chan(): lax.ppermute(value, 'chan', [(s, target(s) % count) for s in range(count)])  18.6 us
    all_to_all x2, starting transfers between devices, exchange(): return lax.all_to_all(value, 'tm', 0, 0, tiled=True)  17.2 us
    all_to_all x2, waiting for transfers between devices, exchange(): return lax.all_to_all(value, 'tm', 0, 0, tiled=True)  7.88 us
    pallas_call x1, Pallas kernels, most_outputs(): pl.pallas_call(most_kernel, out_shape=MOST, grid=(1,), in_specs=[SM, whol...  5 us
    pallas_call x1, Pallas kernels, last_outputs(): pl.pallas_call(last_kernel, out_shape=OUTPUTS, grid=(1,), in_specs=[SM] +...  3.12 us
  transfers between devices with their start and end apart: 24, of which 11 were waited for; matrix products, arithmetic and copies ran while one was open for 2% of the time, Pallas kernels for 24%

profile of v6, /device:TPU:1, one launch (start us, length us, event | category | flops | bytes accessed | tf_op | source)
XLA Modules:
  0.0 104.4 jit_solution(13657429837351710350)
XLA Ops:
  0.6 3.3 %collective-permute-start.3 = (bf16[2048,128]{1,0:T(8,128)(2,1)}, bf16[2048,128]{1,0:T(8,128)(2,1)S(1)}, u32[]{:S(2)}, u32[]{:S(2)}) collective-permute-start(bf16[2048,128]{1,0:T(8,128)(2,1)} %refs_1_.1), channel_id=1, source_target_pairs={{0,1},{1,0},{2,3},{3,2},{4,5},{5,4},{6,7},{7,6},{8,9},{9,8},{10,11... | collective-permute-start | bytes 1572872 | tf_op jit(solution)/shard_map/ppermute | solution.py:580
  4.0 2.7 %collective-permute-start.1 = (bf16[2048,128]{1,0:T(8,128)(2,1)}, bf16[2048,128]{1,0:T(8,128)(2,1)S(1)}, u32[]{:S(2)}, u32[]{:S(2)}) collective-permute-start(bf16[2048,128]{1,0:T(8,128)(2,1)} %refs_1_.1), channel_id=1, source_target_pairs={{0,6},{1,7},{2,0},{3,1},{4,2},{5,3},{6,4},{7,5},{8,14},{9,15},{10,... | collective-permute-start | bytes 1572872 | tf_op jit(solution)/shard_map/ppermute | solution.py:580
  7.7 1.8 %collective-permute-start.2 = (bf16[1024,128]{1,0:T(8,128)(2,1)S(1)}, bf16[1024,128]{1,0:T(8,128)(2,1)S(1)}, u32[]{:S(2)}, u32[]{:S(2)}) collective-permute-start(bf16[1024,128]{1,0:T(8,128)(2,1)S(1)} %slice.18), channel_id=1, source_target_pairs={{0,8},{8,16},{16,24},{24,32},{32,40},{40,48},{48,56},{56,64},{64,7... | collective-permute-start | bytes 786440 | tf_op jit(solution)/shard_map/ppermute | solution.py:604
  12.0 4.1 %first_pair.1 = (f32[96,8,128,128]{3,2,1,0:T(8,128)}, f32[4,8,256]{2,1,0:T(8,128)S(1)}, f32[4,128,256]{2,1,0:T(8,128)S(1)}, f32[4,8,256]{2,1,0:T(8,128)S(1)}, bf...) custom-call(s32[21]{0:T(128)S(1)} %concatenate.6.refs_0_.where_ref, ...), custom_call_target="tpu_custom_call" | custom-call | flops 3000000000 | bytes 1048576 | tf_op jit(solution)/shard_map/first_pair/pallas_call | solution.py:215
  16.1 2.8 %collective-permute-done.refs_2_ = bf16[2048,128]{1,0:T(8,128)(2,1)S(1)} collective-permute-done((bf16[2048,128]{1,0:T(8,128)(2,1)}, bf16[2048,128]{1,0:T(8,128)(2,1)S(1)}, u32[]{:S(2)}, u32[]{:S(2)}) %collective-permute-start) | collective-permute-done | bytes 524320 | tf_op jit(solution)/shard_map/ppermute | solution.py:580
  19.9 2.8 %collective-permute-start.5 = (bf16[1024,128]{1,0:T(8,128)(2,1)S(1)}, bf16[1024,128]{1,0:T(8,128)(2,1)S(1)}, u32[]{:S(2)}, u32[]{:S(2)}) collective-permute-start(bf16[1024,128]{1,0:T(8,128)(2,1)S(1)} %slice.20), channel_id=1, source_target_pairs={{0,6},{1,7},{2,0},{3,1},{4,2},{5,3},{6,4},{7,5},{8,14},{9,15},{10,... | collective-permute-start | bytes 786440 | tf_op jit(solution)/shard_map/ppermute | solution.py:580
  22.6 3.8 %near_pair.1 = (f32[96,8,128,128]{3,2,1,0:T(8,128)}, f32[4,8,256]{2,1,0:T(8,128)S(1)}, f32[4,128,256]{2,1,0:T(8,128)S(1)}, f32[4,8,256]{2,1,0:T(8,128)S(1)}, f32[128,256]{1,0:T(8,128)S(1)}) custom-call(s32[21]{0:T(128)S(1)} %concatenate.6.refs_0_.where_ref, ...), custom_call_target="tpu_custom_call", output_to_operand_aliasing={{0}: (5, {}), {1}: (6, {}), {2}: (7, {}), {3}: (8, {})} | custom-call | flops 3000000000 | bytes 1048576 | tf_op jit(solution)/shard_map/near_pair/pallas_call | solution.py:215
  26.5 3.8 %side_pair.1 = (f32[96,8,128,128]{3,2,1,0:T(8,128)}, f32[4,8,256]{2,1,0:T(8,128)S(1)}, f32[4,128,256]{2,1,0:T(8,128)S(1)}, f32[4,8,256]{2,1,0:T(8,128)S(1)}) custom-call(s32[21]{0:T(128)S(1)} %concatenate.6.refs_0_.where_ref, ...), custom_call_target="tpu_custom_call", output_to_operand_aliasing={{0}: (4, {}), {1}: (5, {}), {2}: (6, {}), {3}: (7, {})} | custom-call | flops 2000000000 | bytes 1048576 | tf_op jit(solution)/shard_map/side_pair/pallas_call | solution.py:215
  31.5 1.5 %collective-permute-done.8.refs_2_ = bf16[2048,128]{1,0:T(8,128)(2,1)S(1)} collective-permute-done((bf16[2048,128]{1,0:T(8,128)(2,1)S(1)}, bf16[2048,128]{1,0:T(8,128)(2,1)S(1)}, u32[]{:S(2)}, u32[]{:S(2)}) %collective-permute-start.8) | collective-permute-done | bytes 524320 | tf_op jit(solution)/shard_map/ppermute | solution.py:580
  33.0 2.5 %far_pair.1 = (f32[4,128,256]{2,1,0:T(8,128)S(1)}, f32[4,8,256]{2,1,0:T(8,128)S(1)}, f32[32,24,128]{2,1,0:T(8,128)}) custom-call(s32[21]{0:T(128)S(1)} %concatenate.6.refs_0_.where_ref, bf16[2048,128]{1,0:T(8,128)(2,1)S(1)} %constant_dynamic-update-slice_fusion.refs_1_, ...), custom_call_target="tpu_custom_call", output_to_operand_aliasing={{0}: (8, {}), {1}: (9, {})} | custom-call | flops 100000000 | bytes 1048576 | tf_op jit(solution)/shard_map/far_pair/pallas_call | solution.py:215
  35.6 9.7 %all-to-all-start = ((f32[32,24,128]{2,1,0:T(8,128)}), f32[32,24,128]{2,1,0:T(8,128)S(1)}, u32[]{:S(2)}, u32[]{:S(2)}) async-start(f32[32,24,128]{2,1,0:T(8,128)} %get-tuple-element.79), calls=%async_computation | async-start | bytes 786432 | tf_op jit(solution)/shard_map/all_to_all | solution.py:584
  45.2 3.7 %rest_left.1 = (f32[96,8,128,128]{3,2,1,0:T(8,128)}, f32[4,8,256]{2,1,0:T(8,128)S(1)}) custom-call(s32[21]{0:T(128)S(1)} %concatenate.6.refs_0_.where_ref, bf16[2048,128]{1,0:T(8,128)(2,1)S(1)} %constant_dynamic-update-slice_fusion.refs_1_, bf16[2048,128]{1,0:T(8,128)(2,1)S(1)} %collective-permute-done.8.refs_2_, ...), custom_call_target="tpu_custom_call", output_to_operand_aliasing={{0}: (4, {}), {1}: (5, {})} | custom-call | flops 4000000000 | bytes 1048576 | tf_op jit(solution)/shard_map/rest_left/pallas_call | solution.py:215
  49.0 7.9 %all-to-all-done.refs_0_ = f32[32,24,128]{2,1,0:T(8,128)S(1)} async-done(((f32[32,24,128]{2,1,0:T(8,128)}), f32[32,24,128]{2,1,0:T(8,128)S(1)}, u32[]{:S(2)}, u32[]{:S(2)}) %all-to-all-start) | async-done | bytes 393248 | tf_op jit(solution)/shard_map/all_to_all | solution.py:584
  57.8 7.6 %all-to-all-start.1 = ((f32[32,40,128]{2,1,0:T(8,128)}), f32[32,40,128]{2,1,0:T(8,128)S(1)}, u32[]{:S(2)}, u32[]{:S(2)}) async-start(f32[32,40,128]{2,1,0:T(8,128)} %get-tuple-element.86), calls=%async_computation.1 | async-start | bytes 1310720 | tf_op jit(solution)/shard_map/all_to_all | solution.py:584
  65.4 1.3 %collective-permute-start.10 = (bf16[1024,128]{1,0:T(8,128)(2,1)S(1)}, bf16[1024,128]{1,0:T(8,128)(2,1)S(1)}, u32[]{:S(2)}, u32[]{:S(2)}) collective-permute-start(bf16[1024,128]{1,0:T(8,128)(2,1)S(1)} %collective-permute-done.2.refs_1_), channel_id=1, source_target_pairs={{0,4},{1,5},{2,6},{3,7},{4,0},{5,1},{6,2},{7,3},{8,12},{9,13},{10,... | collective-permute-start | bytes 786440 | tf_op jit(solution)/shard_map/ppermute | solution.py:580
  67.6 1.9 %collective-permute-start.9 = (bf16[1024,128]{1,0:T(8,128)(2,1)S(1)}, bf16[1024,128]{1,0:T(8,128)(2,1)S(1)}, u32[]{:S(2)}, u32[]{:S(2)}) collective-permute-start(bf16[1024,128]{1,0:T(8,128)(2,1)S(1)} %collective-permute-done.2.refs_1_), channel_id=1, source_target_pairs={{0,6},{1,7},{2,0},{3,1},{4,2},{5,3},{6,4},{7,5},{8,14},{9,15},{10,... | collective-permute-start | bytes 786440 | tf_op jit(solution)/shard_map/ppermute | solution.py:580
  69.5 1.4 %collective-permute-start.13 = (f32[2,32,128]{2,1,0:T(8,128)S(1)}, f32[2,32,128]{2,1,0:T(8,128)S(1)}, u32[]{:S(2)}, u32[]{:S(2)}) collective-permute-start(f32[2,32,128]{2,1,0:T(8,128)S(1)} %get-tuple-element.97.refs_13_), channel_id=1, source_target_pairs={{0,2},{1,3},{2,4},{3,5},{4,6},{5,7},{6,0},{7,1},{8,10},{9,11},{10,... | collective-permute-start | bytes 98312 | tf_op jit(solution)/shard_map/ppermute | solution.py:580
  70.9 2.7 %collective-permute-done.10.refs_5_ = bf16[1024,128]{1,0:T(8,128)(2,1)S(1)} collective-permute-done((bf16[1024,128]{1,0:T(8,128)(2,1)S(1)}, bf16[1024,128]{1,0:T(8,128)(2,1)S(1)}, u32[]{:S(2)}, u32[]{:S(2)}) %collective-permute-start.10) | collective-permute-done | bytes 262176 | tf_op jit(solution)/shard_map/ppermute | solution.py:580
  74.8 6.4 %collective-permute-done.11.refs_8_ = bf16[1024,128]{1,0:T(8,128)(2,1)S(1)} collective-permute-done((bf16[1024,128]{1,0:T(8,128)(2,1)S(1)}, bf16[1024,128]{1,0:T(8,128)(2,1)S(1)}, u32[]{:S(2)}, u32[]{:S(2)}) %collective-permute-start.11) | collective-permute-done | bytes 262176 | tf_op jit(solution)/shard_map/ppermute | solution.py:580
  85.3 5.0 %late_terms.1 = (f32[96,8,128,128]{3,2,1,0:T(8,128)}, f32[1,128,1024]{2,1,0:T(8,128)}) custom-call(s32[21]{0:T(128)S(1)} %concatenate.6.refs_0_.where_ref, bf16[1024,128]{1,0:T(8,128)(2,1)S(1)} %collective-permute-done.2.refs_1_, bf16[1024,128]{1,0:T(8,128)(2,1)S(1)} %collective-permute-done.15.refs_2_, ...), custom_call_target="tpu_custom_call", output_to_operand_aliasing={{0}: (18, {})} | custom-call | flops 100000000 | bytes 1048576 | tf_op jit(solution)/shard_map/late_terms/pallas_call | solution.py:215
  90.3 1.8 %collective-permute-start.20 = (f32[8,32,128]{2,1,0:T(8,128)S(1)}, f32[8,32,128]{2,1,0:T(8,128)S(1)}, u32[]{:S(2)}, u32[]{:S(2)}) collective-permute-start(f32[8,32,128]{2,1,0:T(8,128)S(1)} %get-tuple-element.114), channel_id=1, source_target_pairs={{0,7},{1,6},{2,1},{3,0},{4,3},{5,2},{6,5},{7,4},{8,15},{9,14},{10,... | collective-permute-start | bytes 393224 | tf_op jit(solution)/shard_map/ppermute | solution.py:580
  93.4 5.0 %most_outputs.1 = (f32[8,128,1024]{2,1,0:T(8,128)S(1)}, f32[128,1024]{1,0:T(8,128)S(1)}, f32[24,128]{1,0:T(8,128)S(1)}) custom-call(s32[21]{0:T(128)S(1)} %concatenate.6.refs_0_.where_ref, f32[32,40,128]{2,1,0:T(8,128)S(1)} %all-to-all-done.1.back_ref, f32[96,8,128,128]{3,2,1,0:T(8,128)} %get-tuple-element.107.store_hbm), custom_call_target="tpu_custom_call" | custom-call | flops 5000000000 | bytes 1048576 | tf_op jit(solution)/shard_map/most_outputs/pallas_call | solution.py:467
  98.4 2.7 %collective-permute-done.21.before_ref = f32[8,32,128]{2,1,0:T(8,128)S(1)} collective-permute-done((f32[8,32,128]{2,1,0:T(8,128)S(1)}, f32[8,32,128]{2,1,0:T(8,128)S(1)}, u32[]{:S(2)}, u32[]{:S(2)}) %collective-permute-start.21) | collective-permute-done | bytes 131104 | tf_op jit(solution)/shard_map/ppermute | solution.py:580
  101.1 3.1 %last_outputs.1 = (f32[1,8,128,1024]{3,2,1,0:T(8,128)}, f32[1,128,1024]{2,1,0:T(8,128)}) custom-call(s32[21]{0:T(128)S(1)} %concatenate.6.refs_0_.where_ref, f32[8,128,1024]{2,1,0:T(8,128)S(1)} %get-tuple-element.108.most_ref, f32[128,1024]{1,0:T(8,128)S(1)} %get-tuple-element.109.most_seg_ref, f32[24,128]{1,0:T(8,128)S(1)} %get-tuple-element.110.coef_ref, ...), custom_call_target="tpu_custom_call" | custom-call | flops 3000000000 | bytes 1048576 | tf_op jit(solution)/shard_map/last_outputs/pallas_call | solution.py:485
  (43 shorter events, 13.4 us)
Async XLA Ops:
  0.6 10.3 %collective-permute-start.3 = (bf16[2048,128]{1,0:T(8,128)(2,1)}, bf16[2048,128]{1,0:T(8,128)(2,1)S(1)}, u32[]{:S(2)}, u32[]{:S(2)}) collective-permute-start(bf16[2048,128]{1,0:T(8,128)(2,1)} %refs_1_.1), channel_id=1, source_target_pairs={{0,1},{1,0},{2,3},{3,2},{4,5},{5,4},{6,7},{7,6},{8,9},{9,8},{10,11... | collective-permute-start | bytes 1572872 | tf_op jit(solution)/shard_map/ppermute | solution.py:580
  4.0 14.9 %collective-permute-start = (bf16[2048,128]{1,0:T(8,128)(2,1)}, bf16[2048,128]{1,0:T(8,128)(2,1)S(1)}, u32[]{:S(2)}, u32[]{:S(2)}) collective-permute-start(bf16[2048,128]{1,0:T(8,128)(2,1)} %refs_1_.1), channel_id=1, source_target_pairs={{0,2},{1,3},{2,4},{3,5},{4,6},{5,7},{6,0},{7,1},{8,10},{9,11},{10,... | collective-permute-start | bytes 1572872 | tf_op jit(solution)/shard_map/ppermute | solution.py:580
  4.0 14.9 %collective-permute-start.1 = (bf16[2048,128]{1,0:T(8,128)(2,1)}, bf16[2048,128]{1,0:T(8,128)(2,1)S(1)}, u32[]{:S(2)}, u32[]{:S(2)}) collective-permute-start(bf16[2048,128]{1,0:T(8,128)(2,1)} %refs_1_.1), channel_id=1, source_target_pairs={{0,6},{1,7},{2,0},{3,1},{4,2},{5,3},{6,4},{7,5},{8,14},{9,15},{10,... | collective-permute-start | bytes 1572872 | tf_op jit(solution)/shard_map/ppermute | solution.py:580
  7.7 8.4 %collective-permute-start.2 = (bf16[1024,128]{1,0:T(8,128)(2,1)S(1)}, bf16[1024,128]{1,0:T(8,128)(2,1)S(1)}, u32[]{:S(2)}, u32[]{:S(2)}) collective-permute-start(bf16[1024,128]{1,0:T(8,128)(2,1)S(1)} %slice.18), channel_id=1, source_target_pairs={{0,8},{8,16},{16,24},{24,32},{32,40},{40,48},{48,56},{56,64},{64,7... | collective-permute-start | bytes 786440 | tf_op jit(solution)/shard_map/ppermute | solution.py:604
  18.9 3.8 %collective-permute-start.7 = (bf16[2048,128]{1,0:T(8,128)(2,1)S(1)}, bf16[2048,128]{1,0:T(8,128)(2,1)S(1)}, u32[]{:S(2)}, u32[]{:S(2)}) collective-permute-start(bf16[2048,128]{1,0:T(8,128)(2,1)S(1)} %collective-permute-done.refs_2_), channel_id=1, source_target_pairs={{0,1},{1,0},{2,3},{3,2},{4,5},{5,4},{6,7},{7,6},{8,9},{9,8},{10,11... | collective-permute-start | bytes 1572872 | tf_op jit(solution)/shard_map/ppermute | solution.py:580
  19.7 6.7 %collective-permute-start.6 = (bf16[2048,128]{1,0:T(8,128)(2,1)S(1)}, bf16[2048,128]{1,0:T(8,128)(2,1)S(1)}, u32[]{:S(2)}, u32[]{:S(2)}) collective-permute-start(bf16[2048,128]{1,0:T(8,128)(2,1)S(1)} %collective-permute-done.1.refs_1_), channel_id=1, source_target_pairs={{0,1},{1,0},{2,3},{3,2},{4,5},{5,4},{6,7},{7,6},{8,9},{9,8},{10,11... | collective-permute-start | bytes 1572872 | tf_op jit(solution)/shard_map/ppermute | solution.py:580
  19.8 10.5 %collective-permute-start.4 = (bf16[1024,128]{1,0:T(8,128)(2,1)S(1)}, bf16[1024,128]{1,0:T(8,128)(2,1)S(1)}, u32[]{:S(2)}, u32[]{:S(2)}) collective-permute-start(bf16[1024,128]{1,0:T(8,128)(2,1)S(1)} %slice.19), channel_id=1, source_target_pairs={{0,2},{1,3},{2,4},{3,5},{4,6},{5,7},{6,0},{7,1},{8,10},{9,11},{10,... | collective-permute-start | bytes 786440 | tf_op jit(solution)/shard_map/ppermute | solution.py:580
  19.9 10.4 %collective-permute-start.5 = (bf16[1024,128]{1,0:T(8,128)(2,1)S(1)}, bf16[1024,128]{1,0:T(8,128)(2,1)S(1)}, u32[]{:S(2)}, u32[]{:S(2)}) collective-permute-start(bf16[1024,128]{1,0:T(8,128)(2,1)S(1)} %slice.20), channel_id=1, source_target_pairs={{0,6},{1,7},{2,0},{3,1},{4,2},{5,3},{6,4},{7,5},{8,14},{9,15},{10,... | collective-permute-start | bytes 786440 | tf_op jit(solution)/shard_map/ppermute | solution.py:580
  30.4 2.6 %collective-permute-start.8 = (bf16[2048,128]{1,0:T(8,128)(2,1)S(1)}, bf16[2048,128]{1,0:T(8,128)(2,1)S(1)}, u32[]{:S(2)}, u32[]{:S(2)}) collective-permute-start(bf16[2048,128]{1,0:T(8,128)(2,1)S(1)} %constant_dynamic-update-slice_fusion.refs_1_), channel_id=1, source_target_pairs={{0,1},{1,0},{2,3},{3,2},{4,5},{5,4},{6,7},{7,6},{8,9},{9,8},{10,11... | collective-permute-start | bytes 1572872 | tf_op jit(solution)/shard_map/ppermute | solution.py:580
  35.6 21.3 %all-to-all-start = ((f32[32,24,128]{2,1,0:T(8,128)}), f32[32,24,128]{2,1,0:T(8,128)S(1)}, u32[]{:S(2)}, u32[]{:S(2)}) async-start(f32[32,24,128]{2,1,0:T(8,128)} %get-tuple-element.79), calls=%async_computation | async-start | bytes 786432 | tf_op jit(solution)/shard_map/all_to_all | solution.py:584
  57.8 32.4 %all-to-all-start.1 = ((f32[32,40,128]{2,1,0:T(8,128)}), f32[32,40,128]{2,1,0:T(8,128)S(1)}, u32[]{:S(2)}, u32[]{:S(2)}) async-start(f32[32,40,128]{2,1,0:T(8,128)} %get-tuple-element.86), calls=%async_computation.1 | async-start | bytes 1310720 | tf_op jit(solution)/shard_map/all_to_all | solution.py:584
  65.4 8.2 %collective-permute-start.10 = (bf16[1024,128]{1,0:T(8,128)(2,1)S(1)}, bf16[1024,128]{1,0:T(8,128)(2,1)S(1)}, u32[]{:S(2)}, u32[]{:S(2)}) collective-permute-start(bf16[1024,128]{1,0:T(8,128)(2,1)S(1)} %collective-permute-done.2.refs_1_), channel_id=1, source_target_pairs={{0,4},{1,5},{2,6},{3,7},{4,0},{5,1},{6,2},{7,3},{8,12},{9,13},{10,... | collective-permute-start | bytes 786440 | tf_op jit(solution)/shard_map/ppermute | solution.py:580
  66.7 14.5 %collective-permute-start.11 = (bf16[1024,128]{1,0:T(8,128)(2,1)S(1)}, bf16[1024,128]{1,0:T(8,128)(2,1)S(1)}, u32[]{:S(2)}, u32[]{:S(2)}) collective-permute-start(bf16[1024,128]{1,0:T(8,128)(2,1)S(1)} %collective-permute-done.2.refs_1_), channel_id=1, source_target_pairs={{0,2},{1,3},{2,4},{3,5},{4,6},{5,7},{6,0},{7,1},{8,10},{9,11},{10,... | collective-permute-start | bytes 786440 | tf_op jit(solution)/shard_map/ppermute | solution.py:580
  67.6 13.7 %collective-permute-start.9 = (bf16[1024,128]{1,0:T(8,128)(2,1)S(1)}, bf16[1024,128]{1,0:T(8,128)(2,1)S(1)}, u32[]{:S(2)}, u32[]{:S(2)}) collective-permute-start(bf16[1024,128]{1,0:T(8,128)(2,1)S(1)} %collective-permute-done.2.refs_1_), channel_id=1, source_target_pairs={{0,6},{1,7},{2,0},{3,1},{4,2},{5,3},{6,4},{7,5},{8,14},{9,15},{10,... | collective-permute-start | bytes 786440 | tf_op jit(solution)/shard_map/ppermute | solution.py:580
  69.4 11.8 %collective-permute-start.12 = (f32[2,32,128]{2,1,0:T(8,128)S(1)}, f32[2,32,128]{2,1,0:T(8,128)S(1)}, u32[]{:S(2)}, u32[]{:S(2)}) collective-permute-start(f32[2,32,128]{2,1,0:T(8,128)S(1)} %get-tuple-element.97.refs_13_), channel_id=1, source_target_pairs={{0,6},{1,7},{2,0},{3,1},{4,2},{5,3},{6,4},{7,5},{8,14},{9,15},{10,... | collective-permute-start | bytes 98312 | tf_op jit(solution)/shard_map/ppermute | solution.py:580
  69.5 12.5 %collective-permute-start.13 = (f32[2,32,128]{2,1,0:T(8,128)S(1)}, f32[2,32,128]{2,1,0:T(8,128)S(1)}, u32[]{:S(2)}, u32[]{:S(2)}) collective-permute-start(f32[2,32,128]{2,1,0:T(8,128)S(1)} %get-tuple-element.97.refs_13_), channel_id=1, source_target_pairs={{0,2},{1,3},{2,4},{3,5},{4,6},{5,7},{6,0},{7,1},{8,10},{9,11},{10,... | collective-permute-start | bytes 98312 | tf_op jit(solution)/shard_map/ppermute | solution.py:580
  73.6 8.3 %collective-permute-start.14 = (f32[2,32,128]{2,1,0:T(8,128)S(1)}, f32[2,32,128]{2,1,0:T(8,128)S(1)}, u32[]{:S(2)}, u32[]{:S(2)}) collective-permute-start(f32[2,32,128]{2,1,0:T(8,128)S(1)} %get-tuple-element.97.refs_13_), channel_id=1, source_target_pairs={{0,4},{1,5},{2,6},{3,7},{4,0},{5,1},{6,2},{7,3},{8,12},{9,13},{10,... | collective-permute-start | bytes 98312 | tf_op jit(solution)/shard_map/ppermute | solution.py:580
  81.9 2.2 %collective-permute-start.15 = (bf16[1024,128]{1,0:T(8,128)(2,1)S(1)}, bf16[1024,128]{1,0:T(8,128)(2,1)S(1)}, u32[]{:S(2)}, u32[]{:S(2)}) collective-permute-start(bf16[1024,128]{1,0:T(8,128)(2,1)S(1)} %collective-permute-done.2.refs_1_), channel_id=1, source_target_pairs={{0,1},{1,0},{2,3},{3,2},{4,5},{5,4},{6,7},{7,6},{8,9},{9,8},{10,11... | collective-permute-start | bytes 786440 | tf_op jit(solution)/shard_map/ppermute | solution.py:580
  83.0 1.5 %collective-permute-start.16 = (bf16[1024,128]{1,0:T(8,128)(2,1)S(1)}, bf16[1024,128]{1,0:T(8,128)(2,1)S(1)}, u32[]{:S(2)}, u32[]{:S(2)}) collective-permute-start(bf16[1024,128]{1,0:T(8,128)(2,1)S(1)} %collective-permute-done.11.refs_8_), channel_id=1, source_target_pairs={{0,1},{1,0},{2,3},{3,2},{4,5},{5,4},{6,7},{7,6},{8,9},{9,8},{10,11... | collective-permute-start | bytes 786440 | tf_op jit(solution)/shard_map/ppermute | solution.py:580
  83.0 1.9 %collective-permute-start.17 = (bf16[1024,128]{1,0:T(8,128)(2,1)S(1)}, bf16[1024,128]{1,0:T(8,128)(2,1)S(1)}, u32[]{:S(2)}, u32[]{:S(2)}) collective-permute-start(bf16[1024,128]{1,0:T(8,128)(2,1)S(1)} %collective-permute-done.10.refs_5_), channel_id=1, source_target_pairs={{0,1},{1,0},{2,3},{3,2},{4,5},{5,4},{6,7},{7,6},{8,9},{9,8},{10,11... | collective-permute-start | bytes 786440 | tf_op jit(solution)/shard_map/ppermute | solution.py:580
  83.5 1.8 %collective-permute-start.18 = (bf16[1024,128]{1,0:T(8,128)(2,1)S(1)}, bf16[1024,128]{1,0:T(8,128)(2,1)S(1)}, u32[]{:S(2)}, u32[]{:S(2)}) collective-permute-start(bf16[1024,128]{1,0:T(8,128)(2,1)S(1)} %collective-permute-done.9.refs_3_), channel_id=1, source_target_pairs={{0,1},{1,0},{2,3},{3,2},{4,5},{5,4},{6,7},{7,6},{8,9},{9,8},{10,11... | collective-permute-start | bytes 786440 | tf_op jit(solution)/shard_map/ppermute | solution.py:580
  90.3 8.0 %collective-permute-start.20 = (f32[8,32,128]{2,1,0:T(8,128)S(1)}, f32[8,32,128]{2,1,0:T(8,128)S(1)}, u32[]{:S(2)}, u32[]{:S(2)}) collective-permute-start(f32[8,32,128]{2,1,0:T(8,128)S(1)} %get-tuple-element.114), channel_id=1, source_target_pairs={{0,7},{1,6},{2,1},{3,0},{4,3},{5,2},{6,5},{7,4},{8,15},{9,14},{10,... | collective-permute-start | bytes 393224 | tf_op jit(solution)/shard_map/ppermute | solution.py:580
  92.1 9.0 %collective-permute-start.21 = (f32[8,32,128]{2,1,0:T(8,128)S(1)}, f32[8,32,128]{2,1,0:T(8,128)S(1)}, u32[]{:S(2)}, u32[]{:S(2)}) collective-permute-start(f32[8,32,128]{2,1,0:T(8,128)S(1)} %get-tuple-element.113), channel_id=1, source_target_pairs={{0,2},{1,3},{2,4},{3,5},{4,6},{5,7},{6,0},{7,1},{8,10},{9,11},{10,... | collective-permute-start | bytes 393224 | tf_op jit(solution)/shard_map/ppermute | solution.py:580
  92.1 9.0 %collective-permute-start.19 = (f32[32,8,128]{2,1,0:T(8,128)S(1)}, f32[32,8,128]{2,1,0:T(8,128)S(1)}, u32[]{:S(2)}, u32[]{:S(2)}) collective-permute-start(f32[32,8,128]{2,1,0:T(8,128)S(1)} %slice.21), channel_id=1, source_target_pairs={{0,4},{1,5},{2,6},{3,7},{4,1},{5,0},{6,3},{7,2},{8,12},{9,13},{10,... | collective-permute-start | bytes 393224 | tf_op jit(solution)/shard_map/ppermute | solution.py:580
  (1 other events, 1.0 us)

commit v7 on v6

--- a/solution.py
+++ b/solution.py
@@ -156,6 +156,23 @@
 def rest_kernel(where_ref, first_ref, second_ref, flip_ref, left_ref, sums_ref, cent_ref, stat_ref):
     center_pair(first_ref, second_ref, 0, WIDTH, cent_ref, stat_ref)
     left_part(where_ref, flip_ref[...], cent_ref, left_ref, sums_ref)
+
+
+def token_kernel(pieces_ref, out_ref):
+    out_ref[...] = jnp.zeros((8, WIDTH), F32)
+
+
+def token(pieces):
+    return pl.pallas_call(
+        token_kernel,
+        out_shape=array(8, WIDTH),
+        grid=(1,),
+        in_specs=[HBM],
+        out_specs=whole(8, WIDTH),
+        compiler_params=params(16),
+        cost_estimate=cost(4),
+        name="token",
+    )(pieces)
 
 
 ALL = [
@@ -674,11 +691,11 @@
         scratch=[((ROWS, PAIR), BF16), ((1, 8, PAIR), F32)],
         us=4,
     )
-    prior = after(prior, sums)
+    prior = after(prior, token(pieces))
     prior_ahead = to_chan(prior, lambda s: s - 2)
     prior_behind = to_chan(prior, lambda s: s + 2)
     prior_far = to_chan(prior, lambda s: s + 4)
-    arrived = after(arrived, sums)
+    arrived, prior_ahead, sums = lax.optimization_barrier((arrived, prior_ahead, sums))
     scanned, own_means, flags = call(
         scan_kernel,
         "scan_pieces",

time: 105 us -> 103 us (0.981)
  waiting for transfers between devices: 26.5 us -> 23.5 us
  local copies, waits for them, and re-layouts: 2.9 us -> 4.73 us
    all_to_all x2, waiting for transfers between devices: 7.88 us -> 4.33 us  [exchange(): return lax.all_to_all(value, 'tm', 0, 0, tiled=True)]
    unnamed x3 -> x7, local copies, waits for them, and re-layouts: 1.06 us -> 2.89 us
  transfers between devices with their start and end apart: 24 -> 24, of which waited for: 11 -> 12; matrix products, arithmetic and copies ran while one was open for 2% -> 2% of each run, Pallas kernels for 24% -> 25%
where the time goes in v7:
time: 103 us
  starting transfers between devices  41 us (40%)
  Pallas kernels  32.1 us (31%)
  waiting for transfers between devices  23.5 us (23%)
  local copies, waits for them, and re-layouts  4.73 us (5%)
  between operations  1.77 us (2%)
    pallas_call x7, Pallas kernels, call(): pl.pallas_call(body, out_shape=[STORE] * first + outputs, grid=(1,), in_s...  24 us
    ppermute x21, starting transfers between devices, to_chan(): lax.ppermute(value, 'chan', [(s, target(s) % count) for s in range(count)])  22.1 us
    ppermute x21, waiting for transfers between devices, to_chan(): lax.ppermute(value, 'chan', [(s, target(s) % count) for s in range(count)])  19.2 us
    all_to_all x2, starting transfers between devices, exchange(): return lax.all_to_all(value, 'tm', 0, 0, tiled=True)  17.1 us
    pallas_call x1, Pallas kernels, most_outputs(): pl.pallas_call(most_kernel, out_shape=MOST, grid=(1,), in_specs=[SM, whol...  5 us
    all_to_all x2, waiting for transfers between devices, exchange(): return lax.all_to_all(value, 'tm', 0, 0, tiled=True)  4.33 us
    pallas_call x1, Pallas kernels, last_outputs(): pl.pallas_call(last_kernel, out_shape=OUTPUTS, grid=(1,), in_specs=[SM] +...  3.12 us
    unnamed x7, local copies, waits for them, and re-layouts  2.89 us
  transfers between devices with their start and end apart: 24, of which 12 were waited for; matrix products, arithmetic and copies ran while one was open for 2% of the time, Pallas kernels for 25%

profile of v7, /device:TPU:1, one launch (start us, length us, event | category | flops | bytes accessed | tf_op | source)
XLA Modules:
  0.0 103.1 jit_solution(16445319502182020567)
XLA Ops:
  0.6 3.3 %collective-permute-start.3 = (bf16[2048,128]{1,0:T(8,128)(2,1)}, bf16[2048,128]{1,0:T(8,128)(2,1)S(1)}, u32[]{:S(2)}, u32[]{:S(2)}) collective-permute-start(bf16[2048,128]{1,0:T(8,128)(2,1)} %refs_1_.1), channel_id=1, source_target_pairs={{0,1},{1,0},{2,3},{3,2},{4,5},{5,4},{6,7},{7,6},{8,9},{9,8},{10,11... | collective-permute-start | bytes 1572872 | tf_op jit(solution)/shard_map/ppermute | solution.py:597
  4.0 2.7 %collective-permute-start.1 = (bf16[2048,128]{1,0:T(8,128)(2,1)}, bf16[2048,128]{1,0:T(8,128)(2,1)S(1)}, u32[]{:S(2)}, u32[]{:S(2)}) collective-permute-start(bf16[2048,128]{1,0:T(8,128)(2,1)} %refs_1_.1), channel_id=1, source_target_pairs={{0,6},{1,7},{2,0},{3,1},{4,2},{5,3},{6,4},{7,5},{8,14},{9,15},{10,... | collective-permute-start | bytes 1572872 | tf_op jit(solution)/shard_map/ppermute | solution.py:597
  7.7 1.8 %collective-permute-start.2 = (bf16[1024,128]{1,0:T(8,128)(2,1)S(1)}, bf16[1024,128]{1,0:T(8,128)(2,1)S(1)}, u32[]{:S(2)}, u32[]{:S(2)}) collective-permute-start(bf16[1024,128]{1,0:T(8,128)(2,1)S(1)} %slice.18), channel_id=1, source_target_pairs={{0,8},{8,16},{16,24},{24,32},{32,40},{40,48},{48,56},{56,64},{64,7... | collective-permute-start | bytes 786440 | tf_op jit(solution)/shard_map/ppermute | solution.py:621
  13.8 4.1 %first_pair.1 = (f32[96,8,128,128]{3,2,1,0:T(8,128)}, f32[4,8,256]{2,1,0:T(8,128)S(1)}, f32[4,128,256]{2,1,0:T(8,128)S(1)}, f32[4,8,256]{2,1,0:T(8,128)S(1)}, bf...) custom-call(s32[21]{0:T(128)S(1)} %concatenate.6.refs_0_.where_ref, ...), custom_call_target="tpu_custom_call" | custom-call | flops 3000000000 | bytes 1048576 | tf_op jit(solution)/shard_map/first_pair/pallas_call | solution.py:232
  19.9 2.8 %collective-permute-start.5 = (bf16[1024,128]{1,0:T(8,128)(2,1)S(1)}, bf16[1024,128]{1,0:T(8,128)(2,1)S(1)}, u32[]{:S(2)}, u32[]{:S(2)}) collective-permute-start(bf16[1024,128]{1,0:T(8,128)(2,1)S(1)} %slice.20), channel_id=1, source_target_pairs={{0,6},{1,7},{2,0},{3,1},{4,2},{5,3},{6,4},{7,5},{8,14},{9,15},{10,... | collective-permute-start | bytes 786440 | tf_op jit(solution)/shard_map/ppermute | solution.py:597
  22.6 3.8 %near_pair.1 = (f32[96,8,128,128]{3,2,1,0:T(8,128)}, f32[4,8,256]{2,1,0:T(8,128)S(1)}, f32[4,128,256]{2,1,0:T(8,128)S(1)}, f32[4,8,256]{2,1,0:T(8,128)S(1)}, f32[128,256]{1,0:T(8,128)S(1)}) custom-call(s32[21]{0:T(128)S(1)} %concatenate.6.refs_0_.where_ref, ...), custom_call_target="tpu_custom_call", output_to_operand_aliasing={{0}: (5, {}), {1}: (6, {}), {2}: (7, {}), {3}: (8, {})} | custom-call | flops 3000000000 | bytes 1048576 | tf_op jit(solution)/shard_map/near_pair/pallas_call | solution.py:232
  26.5 3.8 %side_pair.1 = (f32[96,8,128,128]{3,2,1,0:T(8,128)}, f32[4,8,256]{2,1,0:T(8,128)S(1)}, f32[4,128,256]{2,1,0:T(8,128)S(1)}, f32[4,8,256]{2,1,0:T(8,128)S(1)}) custom-call(s32[21]{0:T(128)S(1)} %concatenate.6.refs_0_.where_ref, ...), custom_call_target="tpu_custom_call", output_to_operand_aliasing={{0}: (4, {}), {1}: (5, {}), {2}: (6, {}), {3}: (7, {})} | custom-call | flops 2000000000 | bytes 1048576 | tf_op jit(solution)/shard_map/side_pair/pallas_call | solution.py:232
  31.5 1.5 %collective-permute-done.8.refs_2_ = bf16[2048,128]{1,0:T(8,128)(2,1)S(1)} collective-permute-done((bf16[2048,128]{1,0:T(8,128)(2,1)S(1)}, bf16[2048,128]{1,0:T(8,128)(2,1)S(1)}, u32[]{:S(2)}, u32[]{:S(2)}) %collective-permute-start.8) | collective-permute-done | bytes 524320 | tf_op jit(solution)/shard_map/ppermute | solution.py:597
  33.0 2.5 %far_pair.1 = (f32[4,128,256]{2,1,0:T(8,128)S(1)}, f32[4,8,256]{2,1,0:T(8,128)S(1)}, f32[32,24,128]{2,1,0:T(8,128)}) custom-call(s32[21]{0:T(128)S(1)} %concatenate.6.refs_0_.where_ref, bf16[2048,128]{1,0:T(8,128)(2,1)S(1)} %constant_dynamic-update-slice_fusion.refs_1_, ...), custom_call_target="tpu_custom_call", output_to_operand_aliasing={{0}: (8, {}), {1}: (9, {})} | custom-call | flops 100000000 | bytes 1048576 | tf_op jit(solution)/shard_map/far_pair/pallas_call | solution.py:232
  35.6 9.5 %all-to-all-start = ((f32[32,24,128]{2,1,0:T(8,128)}), f32[32,24,128]{2,1,0:T(8,128)S(1)}, u32[]{:S(2)}, u32[]{:S(2)}) async-start(f32[32,24,128]{2,1,0:T(8,128)} %get-tuple-element.80), calls=%async_computation | async-start | bytes 786432 | tf_op jit(solution)/shard_map/all_to_all | solution.py:601
  45.1 1.7 %collective-permute-start.9 = (bf16[1024,128]{1,0:T(8,128)(2,1)S(1)}, bf16[1024,128]{1,0:T(8,128)(2,1)S(1)}, u32[]{:S(2)}, u32[]{:S(2)}) collective-permute-start(bf16[1024,128]{1,0:T(8,128)(2,1)S(1)} %collective-permute-done.2.refs_1_), channel_id=1, source_target_pairs={{0,6},{1,7},{2,0},{3,1},{4,2},{5,3},{6,4},{7,5},{8,14},{9,15},{10,... | collective-permute-start | bytes 786440 | tf_op jit(solution)/shard_map/ppermute | solution.py:597
  46.8 3.7 %rest_left.1 = (f32[96,8,128,128]{3,2,1,0:T(8,128)}, f32[4,8,256]{2,1,0:T(8,128)S(1)}) custom-call(s32[21]{0:T(128)S(1)} %concatenate.6.refs_0_.where_ref, bf16[2048,128]{1,0:T(8,128)(2,1)S(1)} %constant_dynamic-update-slice_fusion.refs_1_, bf16[2048,128]{1,0:T(8,128)(2,1)S(1)} %collective-permute-done.8.refs_2_, ...), custom_call_target="tpu_custom_call", output_to_operand_aliasing={{0}: (4, {}), {1}: (5, {})} | custom-call | flops 4000000000 | bytes 1048576 | tf_op jit(solution)/shard_map/rest_left/pallas_call | solution.py:232
  50.5 2.0 %collective-permute-done.9.refs_3_ = bf16[1024,128]{1,0:T(8,128)(2,1)S(1)} collective-permute-done((bf16[1024,128]{1,0:T(8,128)(2,1)S(1)}, bf16[1024,128]{1,0:T(8,128)(2,1)S(1)}, u32[]{:S(2)}, u32[]{:S(2)}) %collective-permute-start.9) | collective-permute-done | bytes 262176 | tf_op jit(solution)/shard_map/ppermute | solution.py:597
  52.6 4.3 %all-to-all-done.refs_0_ = f32[32,24,128]{2,1,0:T(8,128)S(1)} async-done(((f32[32,24,128]{2,1,0:T(8,128)}), f32[32,24,128]{2,1,0:T(8,128)S(1)}, u32[]{:S(2)}, u32[]{:S(2)}) %all-to-all-start) | async-done | bytes 393248 | tf_op jit(solution)/shard_map/all_to_all | solution.py:601
  57.9 7.6 %all-to-all-start.1 = ((f32[32,40,128]{2,1,0:T(8,128)}), f32[32,40,128]{2,1,0:T(8,128)S(1)}, u32[]{:S(2)}, u32[]{:S(2)}) async-start(f32[32,40,128]{2,1,0:T(8,128)} %get-tuple-element.88), calls=%async_computation.1 | async-start | bytes 1310720 | tf_op jit(solution)/shard_map/all_to_all | solution.py:601
  65.5 1.3 %collective-permute-start.10 = (bf16[1024,128]{1,0:T(8,128)(2,1)S(1)}, bf16[1024,128]{1,0:T(8,128)(2,1)S(1)}, u32[]{:S(2)}, u32[]{:S(2)}) collective-permute-start(bf16[1024,128]{1,0:T(8,128)(2,1)S(1)} %collective-permute-done.2.refs_1_), channel_id=1, source_target_pairs={{0,4},{1,5},{2,6},{3,7},{4,0},{5,1},{6,2},{7,3},{8,12},{9,13},{10,... | collective-permute-start | bytes 786440 | tf_op jit(solution)/shard_map/ppermute | solution.py:597
  67.6 1.9 %collective-permute-start.12 = (f32[2,32,128]{2,1,0:T(8,128)S(1)}, f32[2,32,128]{2,1,0:T(8,128)S(1)}, u32[]{:S(2)}, u32[]{:S(2)}) collective-permute-start(f32[2,32,128]{2,1,0:T(8,128)S(1)} %get-tuple-element.99.refs_13_), channel_id=1, source_target_pairs={{0,6},{1,7},{2,0},{3,1},{4,2},{5,3},{6,4},{7,5},{8,14},{9,15},{10,... | collective-permute-start | bytes 98312 | tf_op jit(solution)/shard_map/ppermute | solution.py:597
  70.6 3.0 %collective-permute-done.10.refs_5_ = bf16[1024,128]{1,0:T(8,128)(2,1)S(1)} collective-permute-done((bf16[1024,128]{1,0:T(8,128)(2,1)S(1)}, bf16[1024,128]{1,0:T(8,128)(2,1)S(1)}, u32[]{:S(2)}, u32[]{:S(2)}) %collective-permute-start.10) | collective-permute-done | bytes 262176 | tf_op jit(solution)/shard_map/ppermute | solution.py:597
  73.6 7.6 %collective-permute-done.11.refs_8_ = bf16[1024,128]{1,0:T(8,128)(2,1)S(1)} collective-permute-done((bf16[1024,128]{1,0:T(8,128)(2,1)S(1)}, bf16[1024,128]{1,0:T(8,128)(2,1)S(1)}, u32[]{:S(2)}, u32[]{:S(2)}) %collective-permute-start.11) | collective-permute-done | bytes 262176 | tf_op jit(solution)/shard_map/ppermute | solution.py:597
  85.2 5.0 %late_terms.1 = (f32[96,8,128,128]{3,2,1,0:T(8,128)}, f32[1,128,1024]{2,1,0:T(8,128)}) custom-call(s32[21]{0:T(128)S(1)} %concatenate.6.refs_0_.where_ref, bf16[1024,128]{1,0:T(8,128)(2,1)S(1)} %collective-permute-done.2.refs_1_, bf16[1024,128]{1,0:T(8,128)(2,1)S(1)} %collective-permute-done.15.refs_2_, ...), custom_call_target="tpu_custom_call", output_to_operand_aliasing={{0}: (18, {})} | custom-call | flops 100000000 | bytes 1048576 | tf_op jit(solution)/shard_map/late_terms/pallas_call | solution.py:232
  90.5 1.5 %collective-permute-start.21 = (f32[8,32,128]{2,1,0:T(8,128)S(1)}, f32[8,32,128]{2,1,0:T(8,128)S(1)}, u32[]{:S(2)}, u32[]{:S(2)}) collective-permute-start(f32[8,32,128]{2,1,0:T(8,128)S(1)} %get-tuple-element.115), channel_id=1, source_target_pairs={{0,2},{1,3},{2,4},{3,5},{4,6},{5,7},{6,0},{7,1},{8,10},{9,11},{10,... | collective-permute-start | bytes 393224 | tf_op jit(solution)/shard_map/ppermute | solution.py:597
  93.2 5.0 %most_outputs.1 = (f32[8,128,1024]{2,1,0:T(8,128)S(1)}, f32[128,1024]{1,0:T(8,128)S(1)}, f32[24,128]{1,0:T(8,128)S(1)}) custom-call(s32[21]{0:T(128)S(1)} %concatenate.6.refs_0_.where_ref, f32[32,40,128]{2,1,0:T(8,128)S(1)} %all-to-all-done.1.back_ref, f32[96,8,128,128]{3,2,1,0:T(8,128)} %get-tuple-element.109.store_hbm), custom_call_target="tpu_custom_call" | custom-call | flops 5000000000 | bytes 1048576 | tf_op jit(solution)/shard_map/most_outputs/pallas_call | solution.py:484
  98.2 1.5 %collective-permute-done.19.opposite_ref = f32[32,8,128]{2,1,0:T(8,128)S(1)} collective-permute-done((f32[32,8,128]{2,1,0:T(8,128)S(1)}, f32[32,8,128]{2,1,0:T(8,128)S(1)}, u32[]{:S(2)}, u32[]{:S(2)}) %collective-permute-start.19) | collective-permute-done | bytes 131104 | tf_op jit(solution)/shard_map/ppermute | solution.py:597
  99.8 3.1 %last_outputs.1 = (f32[1,8,128,1024]{3,2,1,0:T(8,128)}, f32[1,128,1024]{2,1,0:T(8,128)}) custom-call(s32[21]{0:T(128)S(1)} %concatenate.6.refs_0_.where_ref, f32[8,128,1024]{2,1,0:T(8,128)S(1)} %get-tuple-element.110.most_ref, f32[128,1024]{1,0:T(8,128)S(1)} %get-tuple-element.111.most_seg_ref, f32[24,128]{1,0:T(8,128)S(1)} %get-tuple-element.112.coef_ref, ...), custom_call_target="tpu_custom_call" | custom-call | flops 3000000000 | bytes 1048576 | tf_op jit(solution)/shard_map/last_outputs/pallas_call | solution.py:502
  (47 shorter events, 16.1 us)
Async XLA Ops:
  0.6 10.3 %collective-permute-start.3 = (bf16[2048,128]{1,0:T(8,128)(2,1)}, bf16[2048,128]{1,0:T(8,128)(2,1)S(1)}, u32[]{:S(2)}, u32[]{:S(2)}) collective-permute-start(bf16[2048,128]{1,0:T(8,128)(2,1)} %refs_1_.1), channel_id=1, source_target_pairs={{0,1},{1,0},{2,3},{3,2},{4,5},{5,4},{6,7},{7,6},{8,9},{9,8},{10,11... | collective-permute-start | bytes 1572872 | tf_op jit(solution)/shard_map/ppermute | solution.py:597
  4.0 14.9 %collective-permute-start = (bf16[2048,128]{1,0:T(8,128)(2,1)}, bf16[2048,128]{1,0:T(8,128)(2,1)S(1)}, u32[]{:S(2)}, u32[]{:S(2)}) collective-permute-start(bf16[2048,128]{1,0:T(8,128)(2,1)} %refs_1_.1), channel_id=1, source_target_pairs={{0,2},{1,3},{2,4},{3,5},{4,6},{5,7},{6,0},{7,1},{8,10},{9,11},{10,... | collective-permute-start | bytes 1572872 | tf_op jit(solution)/shard_map/ppermute | solution.py:597
  4.0 14.9 %collective-permute-start.1 = (bf16[2048,128]{1,0:T(8,128)(2,1)}, bf16[2048,128]{1,0:T(8,128)(2,1)S(1)}, u32[]{:S(2)}, u32[]{:S(2)}) collective-permute-start(bf16[2048,128]{1,0:T(8,128)(2,1)} %refs_1_.1), channel_id=1, source_target_pairs={{0,6},{1,7},{2,0},{3,1},{4,2},{5,3},{6,4},{7,5},{8,14},{9,15},{10,... | collective-permute-start | bytes 1572872 | tf_op jit(solution)/shard_map/ppermute | solution.py:597
  7.7 10.3 %collective-permute-start.2 = (bf16[1024,128]{1,0:T(8,128)(2,1)S(1)}, bf16[1024,128]{1,0:T(8,128)(2,1)S(1)}, u32[]{:S(2)}, u32[]{:S(2)}) collective-permute-start(bf16[1024,128]{1,0:T(8,128)(2,1)S(1)} %slice.18), channel_id=1, source_target_pairs={{0,8},{8,16},{16,24},{24,32},{32,40},{40,48},{48,56},{56,64},{64,7... | collective-permute-start | bytes 786440 | tf_op jit(solution)/shard_map/ppermute | solution.py:621
  18.9 3.8 %collective-permute-start.7 = (bf16[2048,128]{1,0:T(8,128)(2,1)S(1)}, bf16[2048,128]{1,0:T(8,128)(2,1)S(1)}, u32[]{:S(2)}, u32[]{:S(2)}) collective-permute-start(bf16[2048,128]{1,0:T(8,128)(2,1)S(1)} %collective-permute-done.refs_2_), channel_id=1, source_target_pairs={{0,1},{1,0},{2,3},{3,2},{4,5},{5,4},{6,7},{7,6},{8,9},{9,8},{10,11... | collective-permute-start | bytes 1572872 | tf_op jit(solution)/shard_map/ppermute | solution.py:597
  19.7 6.7 %collective-permute-start.6 = (bf16[2048,128]{1,0:T(8,128)(2,1)S(1)}, bf16[2048,128]{1,0:T(8,128)(2,1)S(1)}, u32[]{:S(2)}, u32[]{:S(2)}) collective-permute-start(bf16[2048,128]{1,0:T(8,128)(2,1)S(1)} %collective-permute-done.1.refs_1_), channel_id=1, source_target_pairs={{0,1},{1,0},{2,3},{3,2},{4,5},{5,4},{6,7},{7,6},{8,9},{9,8},{10,11... | collective-permute-start | bytes 1572872 | tf_op jit(solution)/shard_map/ppermute | solution.py:597
  19.8 10.6 %collective-permute-start.4 = (bf16[1024,128]{1,0:T(8,128)(2,1)S(1)}, bf16[1024,128]{1,0:T(8,128)(2,1)S(1)}, u32[]{:S(2)}, u32[]{:S(2)}) collective-permute-start(bf16[1024,128]{1,0:T(8,128)(2,1)S(1)} %slice.19), channel_id=1, source_target_pairs={{0,2},{1,3},{2,4},{3,5},{4,6},{5,7},{6,0},{7,1},{8,10},{9,11},{10,... | collective-permute-start | bytes 786440 | tf_op jit(solution)/shard_map/ppermute | solution.py:597
  19.9 10.5 %collective-permute-start.5 = (bf16[1024,128]{1,0:T(8,128)(2,1)S(1)}, bf16[1024,128]{1,0:T(8,128)(2,1)S(1)}, u32[]{:S(2)}, u32[]{:S(2)}) collective-permute-start(bf16[1024,128]{1,0:T(8,128)(2,1)S(1)} %slice.20), channel_id=1, source_target_pairs={{0,6},{1,7},{2,0},{3,1},{4,2},{5,3},{6,4},{7,5},{8,14},{9,15},{10,... | collective-permute-start | bytes 786440 | tf_op jit(solution)/shard_map/ppermute | solution.py:597
  30.4 2.6 %collective-permute-start.8 = (bf16[2048,128]{1,0:T(8,128)(2,1)S(1)}, bf16[2048,128]{1,0:T(8,128)(2,1)S(1)}, u32[]{:S(2)}, u32[]{:S(2)}) collective-permute-start(bf16[2048,128]{1,0:T(8,128)(2,1)S(1)} %constant_dynamic-update-slice_fusion.refs_1_), channel_id=1, source_target_pairs={{0,1},{1,0},{2,3},{3,2},{4,5},{5,4},{6,7},{7,6},{8,9},{9,8},{10,11... | collective-permute-start | bytes 1572872 | tf_op jit(solution)/shard_map/ppermute | solution.py:597
  35.6 21.3 %all-to-all-start = ((f32[32,24,128]{2,1,0:T(8,128)}), f32[32,24,128]{2,1,0:T(8,128)S(1)}, u32[]{:S(2)}, u32[]{:S(2)}) async-start(f32[32,24,128]{2,1,0:T(8,128)} %get-tuple-element.80), calls=%async_computation | async-start | bytes 786432 | tf_op jit(solution)/shard_map/all_to_all | solution.py:601
  45.1 7.5 %collective-permute-start.9 = (bf16[1024,128]{1,0:T(8,128)(2,1)S(1)}, bf16[1024,128]{1,0:T(8,128)(2,1)S(1)}, u32[]{:S(2)}, u32[]{:S(2)}) collective-permute-start(bf16[1024,128]{1,0:T(8,128)(2,1)S(1)} %collective-permute-done.2.refs_1_), channel_id=1, source_target_pairs={{0,6},{1,7},{2,0},{3,1},{4,2},{5,3},{6,4},{7,5},{8,14},{9,15},{10,... | collective-permute-start | bytes 786440 | tf_op jit(solution)/shard_map/ppermute | solution.py:597
  57.9 32.2 %all-to-all-start.1 = ((f32[32,40,128]{2,1,0:T(8,128)}), f32[32,40,128]{2,1,0:T(8,128)S(1)}, u32[]{:S(2)}, u32[]{:S(2)}) async-start(f32[32,40,128]{2,1,0:T(8,128)} %get-tuple-element.88), calls=%async_computation.1 | async-start | bytes 1310720 | tf_op jit(solution)/shard_map/all_to_all | solution.py:601
  65.5 8.2 %collective-permute-start.10 = (bf16[1024,128]{1,0:T(8,128)(2,1)S(1)}, bf16[1024,128]{1,0:T(8,128)(2,1)S(1)}, u32[]{:S(2)}, u32[]{:S(2)}) collective-permute-start(bf16[1024,128]{1,0:T(8,128)(2,1)S(1)} %collective-permute-done.2.refs_1_), channel_id=1, source_target_pairs={{0,4},{1,5},{2,6},{3,7},{4,0},{5,1},{6,2},{7,3},{8,12},{9,13},{10,... | collective-permute-start | bytes 786440 | tf_op jit(solution)/shard_map/ppermute | solution.py:597
  66.8 14.5 %collective-permute-start.11 = (bf16[1024,128]{1,0:T(8,128)(2,1)S(1)}, bf16[1024,128]{1,0:T(8,128)(2,1)S(1)}, u32[]{:S(2)}, u32[]{:S(2)}) collective-permute-start(bf16[1024,128]{1,0:T(8,128)(2,1)S(1)} %collective-permute-done.2.refs_1_), channel_id=1, source_target_pairs={{0,2},{1,3},{2,4},{3,5},{4,6},{5,7},{6,0},{7,1},{8,10},{9,11},{10,... | collective-permute-start | bytes 786440 | tf_op jit(solution)/shard_map/ppermute | solution.py:597
  67.6 13.7 %collective-permute-start.12 = (f32[2,32,128]{2,1,0:T(8,128)S(1)}, f32[2,32,128]{2,1,0:T(8,128)S(1)}, u32[]{:S(2)}, u32[]{:S(2)}) collective-permute-start(f32[2,32,128]{2,1,0:T(8,128)S(1)} %get-tuple-element.99.refs_13_), channel_id=1, source_target_pairs={{0,6},{1,7},{2,0},{3,1},{4,2},{5,3},{6,4},{7,5},{8,14},{9,15},{10,... | collective-permute-start | bytes 98312 | tf_op jit(solution)/shard_map/ppermute | solution.py:597
  69.5 12.5 %collective-permute-start.13 = (f32[2,32,128]{2,1,0:T(8,128)S(1)}, f32[2,32,128]{2,1,0:T(8,128)S(1)}, u32[]{:S(2)}, u32[]{:S(2)}) collective-permute-start(f32[2,32,128]{2,1,0:T(8,128)S(1)} %get-tuple-element.99.refs_13_), channel_id=1, source_target_pairs={{0,2},{1,3},{2,4},{3,5},{4,6},{5,7},{6,0},{7,1},{8,10},{9,11},{10,... | collective-permute-start | bytes 98312 | tf_op jit(solution)/shard_map/ppermute | solution.py:597
  69.5 12.5 %collective-permute-start.14 = (f32[2,32,128]{2,1,0:T(8,128)S(1)}, f32[2,32,128]{2,1,0:T(8,128)S(1)}, u32[]{:S(2)}, u32[]{:S(2)}) collective-permute-start(f32[2,32,128]{2,1,0:T(8,128)S(1)} %get-tuple-element.99.refs_13_), channel_id=1, source_target_pairs={{0,4},{1,5},{2,6},{3,7},{4,0},{5,1},{6,2},{7,3},{8,12},{9,13},{10,... | collective-permute-start | bytes 98312 | tf_op jit(solution)/shard_map/ppermute | solution.py:597
  82.0 2.0 %collective-permute-start.15 = (bf16[1024,128]{1,0:T(8,128)(2,1)S(1)}, bf16[1024,128]{1,0:T(8,128)(2,1)S(1)}, u32[]{:S(2)}, u32[]{:S(2)}) collective-permute-start(bf16[1024,128]{1,0:T(8,128)(2,1)S(1)} %collective-permute-done.2.refs_1_), channel_id=1, source_target_pairs={{0,1},{1,0},{2,3},{3,2},{4,5},{5,4},{6,7},{7,6},{8,9},{9,8},{10,11... | collective-permute-start | bytes 786440 | tf_op jit(solution)/shard_map/ppermute | solution.py:597
  82.9 1.5 %collective-permute-start.16 = (bf16[1024,128]{1,0:T(8,128)(2,1)S(1)}, bf16[1024,128]{1,0:T(8,128)(2,1)S(1)}, u32[]{:S(2)}, u32[]{:S(2)}) collective-permute-start(bf16[1024,128]{1,0:T(8,128)(2,1)S(1)} %collective-permute-done.11.refs_8_), channel_id=1, source_target_pairs={{0,1},{1,0},{2,3},{3,2},{4,5},{5,4},{6,7},{7,6},{8,9},{9,8},{10,11... | collective-permute-start | bytes 786440 | tf_op jit(solution)/shard_map/ppermute | solution.py:597
  82.9 1.9 %collective-permute-start.17 = (bf16[1024,128]{1,0:T(8,128)(2,1)S(1)}, bf16[1024,128]{1,0:T(8,128)(2,1)S(1)}, u32[]{:S(2)}, u32[]{:S(2)}) collective-permute-start(bf16[1024,128]{1,0:T(8,128)(2,1)S(1)} %collective-permute-done.10.refs_5_), channel_id=1, source_target_pairs={{0,1},{1,0},{2,3},{3,2},{4,5},{5,4},{6,7},{7,6},{8,9},{9,8},{10,11... | collective-permute-start | bytes 786440 | tf_op jit(solution)/shard_map/ppermute | solution.py:597
  83.4 1.8 %collective-permute-start.18 = (bf16[1024,128]{1,0:T(8,128)(2,1)S(1)}, bf16[1024,128]{1,0:T(8,128)(2,1)S(1)}, u32[]{:S(2)}, u32[]{:S(2)}) collective-permute-start(bf16[1024,128]{1,0:T(8,128)(2,1)S(1)} %collective-permute-done.9.refs_3_), channel_id=1, source_target_pairs={{0,1},{1,0},{2,3},{3,2},{4,5},{5,4},{6,7},{7,6},{8,9},{9,8},{10,11... | collective-permute-start | bytes 786440 | tf_op jit(solution)/shard_map/ppermute | solution.py:597
  90.2 8.0 %collective-permute-start.20 = (f32[8,32,128]{2,1,0:T(8,128)S(1)}, f32[8,32,128]{2,1,0:T(8,128)S(1)}, u32[]{:S(2)}, u32[]{:S(2)}) collective-permute-start(f32[8,32,128]{2,1,0:T(8,128)S(1)} %get-tuple-element.116), channel_id=1, source_target_pairs={{0,7},{1,6},{2,1},{3,0},{4,3},{5,2},{6,5},{7,4},{8,15},{9,14},{10,... | collective-permute-start | bytes 393224 | tf_op jit(solution)/shard_map/ppermute | solution.py:597
  90.5 7.8 %collective-permute-start.21 = (f32[8,32,128]{2,1,0:T(8,128)S(1)}, f32[8,32,128]{2,1,0:T(8,128)S(1)}, u32[]{:S(2)}, u32[]{:S(2)}) collective-permute-start(f32[8,32,128]{2,1,0:T(8,128)S(1)} %get-tuple-element.115), channel_id=1, source_target_pairs={{0,2},{1,3},{2,4},{3,5},{4,6},{5,7},{6,0},{7,1},{8,10},{9,11},{10,... | collective-permute-start | bytes 393224 | tf_op jit(solution)/shard_map/ppermute | solution.py:597
  92.0 7.8 %collective-permute-start.19 = (f32[32,8,128]{2,1,0:T(8,128)S(1)}, f32[32,8,128]{2,1,0:T(8,128)S(1)}, u32[]{:S(2)}, u32[]{:S(2)}) collective-permute-start(f32[32,8,128]{2,1,0:T(8,128)S(1)} %slice.21), channel_id=1, source_target_pairs={{0,4},{1,5},{2,6},{3,7},{4,1},{5,0},{6,3},{7,2},{8,12},{9,13},{10,... | collective-permute-start | bytes 393224 | tf_op jit(solution)/shard_map/ppermute | solution.py:597
  (3 other events, 2.9 us)

commit v8 on v7

--- a/solution.py
+++ b/solution.py
@@ -695,7 +695,9 @@
     prior_ahead = to_chan(prior, lambda s: s - 2)
     prior_behind = to_chan(prior, lambda s: s + 2)
     prior_far = to_chan(prior, lambda s: s + 4)
-    arrived, prior_ahead, sums = lax.optimization_barrier((arrived, prior_ahead, sums))
+    arrived, prior_ahead, prior_behind, sums = lax.optimization_barrier(
+        (arrived, prior_ahead, prior_behind, sums)
+    )
     scanned, own_means, flags = call(
         scan_kernel,
         "scan_pieces",
@@ -705,6 +707,7 @@
         us=1,
     )
     back = exchange(scanned)
+    own_means, prior_far = lax.optimization_barrier((own_means, prior_far))
     ahead_means = to_chan(own_means, lambda s: s - 2)
     behind_means = to_chan(own_means, lambda s: s + 2)
     far_means = to_chan(own_means, lambda s: s + 4)

time: 103 us -> 106 us (1.029)
  starting transfers between devices: 41 us -> 45.1 us
  local copies, waits for them, and re-layouts: 4.73 us -> 2.9 us
    ppermute x21, starting transfers between devices: 22.1 us -> 26.2 us  [to_chan(): lax.ppermute(value, 'chan', [(s, target(s) % count) for s in range(count)])]
    unnamed x7 -> x3, local copies, waits for them, and re-layouts: 2.89 us -> 1.06 us
    ppermute x21, waiting for transfers between devices: 19.2 us -> 21 us  [to_chan(): lax.ppermute(value, 'chan', [(s, target(s) % count) for s in range(count)])]
    all_to_all x2, waiting for transfers between devices: 4.33 us -> 3.11 us  [exchange(): return lax.all_to_all(value, 'tm', 0, 0, tiled=True)]
  transfers between devices with their start and end apart: 24 -> 24, of which waited for: 12 -> 13; matrix products, arithmetic and copies ran while one was open for 2% -> 2% of each run, Pallas kernels for 25% -> 24%
where the time goes in v8:
time: 106 us
  starting transfers between devices  45.1 us (43%)
  Pallas kernels  32.1 us (30%)
  waiting for transfers between devices  24.1 us (23%)
  local copies, waits for them, and re-layouts  2.9 us (3%)
  between operations  1.77 us (2%)
    ppermute x21, starting transfers between devices, to_chan(): lax.ppermute(value, 'chan', [(s, target(s) % count) for s in range(count)])  26.2 us
    pallas_call x7, Pallas kernels, call(): pl.pallas_call(body, out_shape=[STORE] * first + outputs, grid=(1,), in_s...  24 us
    ppermute x21, waiting for transfers between devices, to_chan(): lax.ppermute(value, 'chan', [(s, target(s) % count) for s in range(count)])  21 us
    all_to_all x2, starting transfers between devices, exchange(): return lax.all_to_all(value, 'tm', 0, 0, tiled=True)  17.1 us
    pallas_call x1, Pallas kernels, most_outputs(): pl.pallas_call(most_kernel, out_shape=MOST, grid=(1,), in_specs=[SM, whol...  5 us
    pallas_call x1, Pallas kernels, last_outputs(): pl.pallas_call(last_kernel, out_shape=OUTPUTS, grid=(1,), in_specs=[SM] +...  3.12 us
    all_to_all x2, waiting for transfers between devices, exchange(): return lax.all_to_all(value, 'tm', 0, 0, tiled=True)  3.11 us
  transfers between devices with their start and end apart: 24, of which 13 were waited for; matrix products, arithmetic and copies ran while one was open for 2% of the time, Pallas kernels for 24%

profile of v8, /device:TPU:1, one launch (start us, length us, event | category | flops | bytes accessed | tf_op | source)
XLA Modules:
  0.0 105.9 jit_solution(2644429747068977685)
XLA Ops:
  0.6 3.3 %collective-permute-start.3 = (bf16[2048,128]{1,0:T(8,128)(2,1)}, bf16[2048,128]{1,0:T(8,128)(2,1)S(1)}, u32[]{:S(2)}, u32[]{:S(2)}) collective-permute-start(bf16[2048,128]{1,0:T(8,128)(2,1)} %refs_1_.1), channel_id=1, source_target_pairs={{0,1},{1,0},{2,3},{3,2},{4,5},{5,4},{6,7},{7,6},{8,9},{9,8},{10,11... | collective-permute-start | bytes 1572872 | tf_op jit(solution)/shard_map/ppermute | solution.py:597
  4.0 2.7 %collective-permute-start.1 = (bf16[2048,128]{1,0:T(8,128)(2,1)}, bf16[2048,128]{1,0:T(8,128)(2,1)S(1)}, u32[]{:S(2)}, u32[]{:S(2)}) collective-permute-start(bf16[2048,128]{1,0:T(8,128)(2,1)} %refs_1_.1), channel_id=1, source_target_pairs={{0,6},{1,7},{2,0},{3,1},{4,2},{5,3},{6,4},{7,5},{8,14},{9,15},{10,... | collective-permute-start | bytes 1572872 | tf_op jit(solution)/shard_map/ppermute | solution.py:597
  7.7 1.8 %collective-permute-start.2 = (bf16[1024,128]{1,0:T(8,128)(2,1)S(1)}, bf16[1024,128]{1,0:T(8,128)(2,1)S(1)}, u32[]{:S(2)}, u32[]{:S(2)}) collective-permute-start(bf16[1024,128]{1,0:T(8,128)(2,1)S(1)} %slice.18), channel_id=1, source_target_pairs={{0,8},{8,16},{16,24},{24,32},{32,40},{40,48},{48,56},{56,64},{64,7... | collective-permute-start | bytes 786440 | tf_op jit(solution)/shard_map/ppermute | solution.py:621
  12.0 4.1 %first_pair.1 = (f32[96,8,128,128]{3,2,1,0:T(8,128)}, f32[4,8,256]{2,1,0:T(8,128)S(1)}, f32[4,128,256]{2,1,0:T(8,128)S(1)}, f32[4,8,256]{2,1,0:T(8,128)S(1)}, bf...) custom-call(s32[21]{0:T(128)S(1)} %concatenate.6.refs_0_.where_ref, ...), custom_call_target="tpu_custom_call" | custom-call | flops 3000000000 | bytes 1048576 | tf_op jit(solution)/shard_map/first_pair/pallas_call | solution.py:232
  16.1 2.8 %collective-permute-done.refs_2_ = bf16[2048,128]{1,0:T(8,128)(2,1)S(1)} collective-permute-done((bf16[2048,128]{1,0:T(8,128)(2,1)}, bf16[2048,128]{1,0:T(8,128)(2,1)S(1)}, u32[]{:S(2)}, u32[]{:S(2)}) %collective-permute-start) | collective-permute-done | bytes 524320 | tf_op jit(solution)/shard_map/ppermute | solution.py:597
  19.9 2.8 %collective-permute-start.5 = (bf16[1024,128]{1,0:T(8,128)(2,1)S(1)}, bf16[1024,128]{1,0:T(8,128)(2,1)S(1)}, u32[]{:S(2)}, u32[]{:S(2)}) collective-permute-start(bf16[1024,128]{1,0:T(8,128)(2,1)S(1)} %slice.20), channel_id=1, source_target_pairs={{0,6},{1,7},{2,0},{3,1},{4,2},{5,3},{6,4},{7,5},{8,14},{9,15},{10,... | collective-permute-start | bytes 786440 | tf_op jit(solution)/shard_map/ppermute | solution.py:597
  22.6 3.8 %near_pair.1 = (f32[96,8,128,128]{3,2,1,0:T(8,128)}, f32[4,8,256]{2,1,0:T(8,128)S(1)}, f32[4,128,256]{2,1,0:T(8,128)S(1)}, f32[4,8,256]{2,1,0:T(8,128)S(1)}, f32[128,256]{1,0:T(8,128)S(1)}) custom-call(s32[21]{0:T(128)S(1)} %concatenate.6.refs_0_.where_ref, ...), custom_call_target="tpu_custom_call", output_to_operand_aliasing={{0}: (5, {}), {1}: (6, {}), {2}: (7, {}), {3}: (8, {})} | custom-call | flops 3000000000 | bytes 1048576 | tf_op jit(solution)/shard_map/near_pair/pallas_call | solution.py:232
  26.5 3.8 %side_pair.1 = (f32[96,8,128,128]{3,2,1,0:T(8,128)}, f32[4,8,256]{2,1,0:T(8,128)S(1)}, f32[4,128,256]{2,1,0:T(8,128)S(1)}, f32[4,8,256]{2,1,0:T(8,128)S(1)}) custom-call(s32[21]{0:T(128)S(1)} %concatenate.6.refs_0_.where_ref, ...), custom_call_target="tpu_custom_call", output_to_operand_aliasing={{0}: (4, {}), {1}: (5, {}), {2}: (6, {}), {3}: (7, {})} | custom-call | flops 2000000000 | bytes 1048576 | tf_op jit(solution)/shard_map/side_pair/pallas_call | solution.py:232
  31.5 1.5 %collective-permute-done.8.refs_2_ = bf16[2048,128]{1,0:T(8,128)(2,1)S(1)} collective-permute-done((bf16[2048,128]{1,0:T(8,128)(2,1)S(1)}, bf16[2048,128]{1,0:T(8,128)(2,1)S(1)}, u32[]{:S(2)}, u32[]{:S(2)}) %collective-permute-start.8) | collective-permute-done | bytes 524320 | tf_op jit(solution)/shard_map/ppermute | solution.py:597
  33.0 2.5 %far_pair.1 = (f32[4,128,256]{2,1,0:T(8,128)S(1)}, f32[4,8,256]{2,1,0:T(8,128)S(1)}, f32[32,24,128]{2,1,0:T(8,128)}) custom-call(s32[21]{0:T(128)S(1)} %concatenate.6.refs_0_.where_ref, bf16[2048,128]{1,0:T(8,128)(2,1)S(1)} %constant_dynamic-update-slice_fusion.refs_1_, ...), custom_call_target="tpu_custom_call", output_to_operand_aliasing={{0}: (8, {}), {1}: (9, {})} | custom-call | flops 100000000 | bytes 1048576 | tf_op jit(solution)/shard_map/far_pair/pallas_call | solution.py:232
  35.6 9.5 %all-to-all-start = ((f32[32,24,128]{2,1,0:T(8,128)}), f32[32,24,128]{2,1,0:T(8,128)S(1)}, u32[]{:S(2)}, u32[]{:S(2)}) async-start(f32[32,24,128]{2,1,0:T(8,128)} %get-tuple-element.83), calls=%async_computation | async-start | bytes 786432 | tf_op jit(solution)/shard_map/all_to_all | solution.py:601
  45.3 2.7 %collective-permute-start.9 = (bf16[1024,128]{1,0:T(8,128)(2,1)S(1)}, bf16[1024,128]{1,0:T(8,128)(2,1)S(1)}, u32[]{:S(2)}, u32[]{:S(2)}) collective-permute-start(bf16[1024,128]{1,0:T(8,128)(2,1)S(1)} %collective-permute-done.2.refs_1_), channel_id=1, source_target_pairs={{0,6},{1,7},{2,0},{3,1},{4,2},{5,3},{6,4},{7,5},{8,14},{9,15},{10,... | collective-permute-start | bytes 786440 | tf_op jit(solution)/shard_map/ppermute | solution.py:597
  48.0 3.7 %rest_left.1 = (f32[96,8,128,128]{3,2,1,0:T(8,128)}, f32[4,8,256]{2,1,0:T(8,128)S(1)}) custom-call(s32[21]{0:T(128)S(1)} %concatenate.6.refs_0_.where_ref, bf16[2048,128]{1,0:T(8,128)(2,1)S(1)} %constant_dynamic-update-slice_fusion.refs_1_, bf16[2048,128]{1,0:T(8,128)(2,1)S(1)} %collective-permute-done.8.refs_2_, ...), custom_call_target="tpu_custom_call", output_to_operand_aliasing={{0}: (4, {}), {1}: (5, {})} | custom-call | flops 4000000000 | bytes 1048576 | tf_op jit(solution)/shard_map/rest_left/pallas_call | solution.py:232
  51.7 2.0 %collective-permute-done.10.refs_8_ = bf16[1024,128]{1,0:T(8,128)(2,1)S(1)} collective-permute-done((bf16[1024,128]{1,0:T(8,128)(2,1)S(1)}, bf16[1024,128]{1,0:T(8,128)(2,1)S(1)}, u32[]{:S(2)}, u32[]{:S(2)}) %collective-permute-start.10) | collective-permute-done | bytes 262176 | tf_op jit(solution)/shard_map/ppermute | solution.py:597
  53.7 3.1 %all-to-all-done.refs_0_ = f32[32,24,128]{2,1,0:T(8,128)S(1)} async-done(((f32[32,24,128]{2,1,0:T(8,128)}), f32[32,24,128]{2,1,0:T(8,128)S(1)}, u32[]{:S(2)}, u32[]{:S(2)}) %all-to-all-start) | async-done | bytes 393248 | tf_op jit(solution)/shard_map/all_to_all | solution.py:601
  57.8 7.6 %all-to-all-start.1 = ((f32[32,40,128]{2,1,0:T(8,128)}), f32[32,40,128]{2,1,0:T(8,128)S(1)}, u32[]{:S(2)}, u32[]{:S(2)}) async-start(f32[32,40,128]{2,1,0:T(8,128)} %get-tuple-element.91), calls=%async_computation.1 | async-start | bytes 1310720 | tf_op jit(solution)/shard_map/all_to_all | solution.py:601
  66.7 6.8 %collective-permute-done.11.refs_5_ = bf16[1024,128]{1,0:T(8,128)(2,1)S(1)} collective-permute-done((bf16[1024,128]{1,0:T(8,128)(2,1)S(1)}, bf16[1024,128]{1,0:T(8,128)(2,1)S(1)}, u32[]{:S(2)}, u32[]{:S(2)}) %collective-permute-start.11) | collective-permute-done | bytes 262176 | tf_op jit(solution)/shard_map/ppermute | solution.py:597
  76.6 2.4 %collective-permute-done.13.refs_15_ = f32[2,32,128]{2,1,0:T(8,128)S(1)} collective-permute-done((f32[2,32,128]{2,1,0:T(8,128)S(1)}, f32[2,32,128]{2,1,0:T(8,128)S(1)}, u32[]{:S(2)}, u32[]{:S(2)}) %collective-permute-start.13) | collective-permute-done | bytes 32800 | tf_op jit(solution)/shard_map/ppermute | solution.py:597
  79.3 3.9 %collective-permute-start.15 = (bf16[1024,128]{1,0:T(8,128)(2,1)S(1)}, bf16[1024,128]{1,0:T(8,128)(2,1)S(1)}, u32[]{:S(2)}, u32[]{:S(2)}) collective-permute-start(bf16[1024,128]{1,0:T(8,128)(2,1)S(1)} %collective-permute-done.2.refs_1_), channel_id=1, source_target_pairs={{0,1},{1,0},{2,3},{3,2},{4,5},{5,4},{6,7},{7,6},{8,9},{9,8},{10,11... | collective-permute-start | bytes 786440 | tf_op jit(solution)/shard_map/ppermute | solution.py:597
  85.5 5.0 %late_terms.1 = (f32[96,8,128,128]{3,2,1,0:T(8,128)}, f32[1,128,1024]{2,1,0:T(8,128)}) custom-call(s32[21]{0:T(128)S(1)} %concatenate.6.refs_0_.where_ref, bf16[1024,128]{1,0:T(8,128)(2,1)S(1)} %collective-permute-done.2.refs_1_, bf16[1024,128]{1,0:T(8,128)(2,1)S(1)} %collective-permute-done.15.refs_2_, ...), custom_call_target="tpu_custom_call", output_to_operand_aliasing={{0}: (18, {})} | custom-call | flops 100000000 | bytes 1048576 | tf_op jit(solution)/shard_map/late_terms/pallas_call | solution.py:232
  90.5 3.0 %collective-permute-start.20 = (f32[8,32,128]{2,1,0:T(8,128)S(1)}, f32[8,32,128]{2,1,0:T(8,128)S(1)}, u32[]{:S(2)}, u32[]{:S(2)}) collective-permute-start(f32[8,32,128]{2,1,0:T(8,128)S(1)} %get-tuple-element.122), channel_id=1, source_target_pairs={{0,7},{1,6},{2,1},{3,0},{4,3},{5,2},{6,5},{7,4},{8,15},{9,14},{10,... | collective-permute-start | bytes 393224 | tf_op jit(solution)/shard_map/ppermute | solution.py:597
  94.5 5.0 %most_outputs.1 = (f32[8,128,1024]{2,1,0:T(8,128)S(1)}, f32[128,1024]{1,0:T(8,128)S(1)}, f32[24,128]{1,0:T(8,128)S(1)}) custom-call(s32[21]{0:T(128)S(1)} %concatenate.6.refs_0_.where_ref, f32[32,40,128]{2,1,0:T(8,128)S(1)} %all-to-all-done.1.back_ref, f32[96,8,128,128]{3,2,1,0:T(8,128)} %get-tuple-element.115.store_hbm), custom_call_target="tpu_custom_call" | custom-call | flops 5000000000 | bytes 1048576 | tf_op jit(solution)/shard_map/most_outputs/pallas_call | solution.py:484
  99.6 3.1 %collective-permute-done.21.before_ref = f32[8,32,128]{2,1,0:T(8,128)S(1)} collective-permute-done((f32[8,32,128]{2,1,0:T(8,128)S(1)}, f32[8,32,128]{2,1,0:T(8,128)S(1)}, u32[]{:S(2)}, u32[]{:S(2)}) %collective-permute-start.21) | collective-permute-done | bytes 131104 | tf_op jit(solution)/shard_map/ppermute | solution.py:597
  102.6 3.1 %last_outputs.1 = (f32[1,8,128,1024]{3,2,1,0:T(8,128)}, f32[1,128,1024]{2,1,0:T(8,128)}) custom-call(s32[21]{0:T(128)S(1)} %concatenate.6.refs_0_.where_ref, f32[8,128,1024]{2,1,0:T(8,128)S(1)} %get-tuple-element.116.most_ref, f32[128,1024]{1,0:T(8,128)S(1)} %get-tuple-element.117.most_seg_ref, f32[24,128]{1,0:T(8,128)S(1)} %get-tuple-element.118.coef_ref, ...), custom_call_target="tpu_custom_call" | custom-call | flops 3000000000 | bytes 1048576 | tf_op jit(solution)/shard_map/last_outputs/pallas_call | solution.py:502
  (43 shorter events, 14.2 us)
Async XLA Ops:
  0.6 10.3 %collective-permute-start.3 = (bf16[2048,128]{1,0:T(8,128)(2,1)}, bf16[2048,128]{1,0:T(8,128)(2,1)S(1)}, u32[]{:S(2)}, u32[]{:S(2)}) collective-permute-start(bf16[2048,128]{1,0:T(8,128)(2,1)} %refs_1_.1), channel_id=1, source_target_pairs={{0,1},{1,0},{2,3},{3,2},{4,5},{5,4},{6,7},{7,6},{8,9},{9,8},{10,11... | collective-permute-start | bytes 1572872 | tf_op jit(solution)/shard_map/ppermute | solution.py:597
  4.0 14.9 %collective-permute-start = (bf16[2048,128]{1,0:T(8,128)(2,1)}, bf16[2048,128]{1,0:T(8,128)(2,1)S(1)}, u32[]{:S(2)}, u32[]{:S(2)}) collective-permute-start(bf16[2048,128]{1,0:T(8,128)(2,1)} %refs_1_.1), channel_id=1, source_target_pairs={{0,2},{1,3},{2,4},{3,5},{4,6},{5,7},{6,0},{7,1},{8,10},{9,11},{10,... | collective-permute-start | bytes 1572872 | tf_op jit(solution)/shard_map/ppermute | solution.py:597
  4.0 14.9 %collective-permute-start.1 = (bf16[2048,128]{1,0:T(8,128)(2,1)}, bf16[2048,128]{1,0:T(8,128)(2,1)S(1)}, u32[]{:S(2)}, u32[]{:S(2)}) collective-permute-start(bf16[2048,128]{1,0:T(8,128)(2,1)} %refs_1_.1), channel_id=1, source_target_pairs={{0,6},{1,7},{2,0},{3,1},{4,2},{5,3},{6,4},{7,5},{8,14},{9,15},{10,... | collective-permute-start | bytes 1572872 | tf_op jit(solution)/shard_map/ppermute | solution.py:597
  7.7 8.4 %collective-permute-start.2 = (bf16[1024,128]{1,0:T(8,128)(2,1)S(1)}, bf16[1024,128]{1,0:T(8,128)(2,1)S(1)}, u32[]{:S(2)}, u32[]{:S(2)}) collective-permute-start(bf16[1024,128]{1,0:T(8,128)(2,1)S(1)} %slice.18), channel_id=1, source_target_pairs={{0,8},{8,16},{16,24},{24,32},{32,40},{40,48},{48,56},{56,64},{64,7... | collective-permute-start | bytes 786440 | tf_op jit(solution)/shard_map/ppermute | solution.py:621
  18.9 3.8 %collective-permute-start.7 = (bf16[2048,128]{1,0:T(8,128)(2,1)S(1)}, bf16[2048,128]{1,0:T(8,128)(2,1)S(1)}, u32[]{:S(2)}, u32[]{:S(2)}) collective-permute-start(bf16[2048,128]{1,0:T(8,128)(2,1)S(1)} %collective-permute-done.refs_2_), channel_id=1, source_target_pairs={{0,1},{1,0},{2,3},{3,2},{4,5},{5,4},{6,7},{7,6},{8,9},{9,8},{10,11... | collective-permute-start | bytes 1572872 | tf_op jit(solution)/shard_map/ppermute | solution.py:597
  19.7 6.7 %collective-permute-start.6 = (bf16[2048,128]{1,0:T(8,128)(2,1)S(1)}, bf16[2048,128]{1,0:T(8,128)(2,1)S(1)}, u32[]{:S(2)}, u32[]{:S(2)}) collective-permute-start(bf16[2048,128]{1,0:T(8,128)(2,1)S(1)} %collective-permute-done.1.refs_1_), channel_id=1, source_target_pairs={{0,1},{1,0},{2,3},{3,2},{4,5},{5,4},{6,7},{7,6},{8,9},{9,8},{10,11... | collective-permute-start | bytes 1572872 | tf_op jit(solution)/shard_map/ppermute | solution.py:597
  19.8 10.5 %collective-permute-start.4 = (bf16[1024,128]{1,0:T(8,128)(2,1)S(1)}, bf16[1024,128]{1,0:T(8,128)(2,1)S(1)}, u32[]{:S(2)}, u32[]{:S(2)}) collective-permute-start(bf16[1024,128]{1,0:T(8,128)(2,1)S(1)} %slice.19), channel_id=1, source_target_pairs={{0,2},{1,3},{2,4},{3,5},{4,6},{5,7},{6,0},{7,1},{8,10},{9,11},{10,... | collective-permute-start | bytes 786440 | tf_op jit(solution)/shard_map/ppermute | solution.py:597
  19.9 10.4 %collective-permute-start.5 = (bf16[1024,128]{1,0:T(8,128)(2,1)S(1)}, bf16[1024,128]{1,0:T(8,128)(2,1)S(1)}, u32[]{:S(2)}, u32[]{:S(2)}) collective-permute-start(bf16[1024,128]{1,0:T(8,128)(2,1)S(1)} %slice.20), channel_id=1, source_target_pairs={{0,6},{1,7},{2,0},{3,1},{4,2},{5,3},{6,4},{7,5},{8,14},{9,15},{10,... | collective-permute-start | bytes 786440 | tf_op jit(solution)/shard_map/ppermute | solution.py:597
  30.4 2.6 %collective-permute-start.8 = (bf16[2048,128]{1,0:T(8,128)(2,1)S(1)}, bf16[2048,128]{1,0:T(8,128)(2,1)S(1)}, u32[]{:S(2)}, u32[]{:S(2)}) collective-permute-start(bf16[2048,128]{1,0:T(8,128)(2,1)S(1)} %constant_dynamic-update-slice_fusion.refs_1_), channel_id=1, source_target_pairs={{0,1},{1,0},{2,3},{3,2},{4,5},{5,4},{6,7},{7,6},{8,9},{9,8},{10,11... | collective-permute-start | bytes 1572872 | tf_op jit(solution)/shard_map/ppermute | solution.py:597
  35.6 21.3 %all-to-all-start = ((f32[32,24,128]{2,1,0:T(8,128)}), f32[32,24,128]{2,1,0:T(8,128)S(1)}, u32[]{:S(2)}, u32[]{:S(2)}) async-start(f32[32,24,128]{2,1,0:T(8,128)} %get-tuple-element.83), calls=%async_computation | async-start | bytes 786432 | tf_op jit(solution)/shard_map/all_to_all | solution.py:601
  45.0 8.7 %collective-permute-start.10 = (bf16[1024,128]{1,0:T(8,128)(2,1)S(1)}, bf16[1024,128]{1,0:T(8,128)(2,1)S(1)}, u32[]{:S(2)}, u32[]{:S(2)}) collective-permute-start(bf16[1024,128]{1,0:T(8,128)(2,1)S(1)} %collective-permute-done.2.refs_1_), channel_id=1, source_target_pairs={{0,2},{1,3},{2,4},{3,5},{4,6},{5,7},{6,0},{7,1},{8,10},{9,11},{10,... | collective-permute-start | bytes 786440 | tf_op jit(solution)/shard_map/ppermute | solution.py:597
  45.3 8.4 %collective-permute-start.9 = (bf16[1024,128]{1,0:T(8,128)(2,1)S(1)}, bf16[1024,128]{1,0:T(8,128)(2,1)S(1)}, u32[]{:S(2)}, u32[]{:S(2)}) collective-permute-start(bf16[1024,128]{1,0:T(8,128)(2,1)S(1)} %collective-permute-done.2.refs_1_), channel_id=1, source_target_pairs={{0,6},{1,7},{2,0},{3,1},{4,2},{5,3},{6,4},{7,5},{8,14},{9,15},{10,... | collective-permute-start | bytes 786440 | tf_op jit(solution)/shard_map/ppermute | solution.py:597
  57.8 32.6 %all-to-all-start.1 = ((f32[32,40,128]{2,1,0:T(8,128)}), f32[32,40,128]{2,1,0:T(8,128)S(1)}, u32[]{:S(2)}, u32[]{:S(2)}) async-start(f32[32,40,128]{2,1,0:T(8,128)} %get-tuple-element.91), calls=%async_computation.1 | async-start | bytes 1310720 | tf_op jit(solution)/shard_map/all_to_all | solution.py:601
  65.4 8.1 %collective-permute-start.11 = (bf16[1024,128]{1,0:T(8,128)(2,1)S(1)}, bf16[1024,128]{1,0:T(8,128)(2,1)S(1)}, u32[]{:S(2)}, u32[]{:S(2)}) collective-permute-start(bf16[1024,128]{1,0:T(8,128)(2,1)S(1)} %collective-permute-done.2.refs_1_), channel_id=1, source_target_pairs={{0,4},{1,5},{2,6},{3,7},{4,0},{5,1},{6,2},{7,3},{8,12},{9,13},{10,... | collective-permute-start | bytes 786440 | tf_op jit(solution)/shard_map/ppermute | solution.py:597
  73.5 3.1 %collective-permute-start.12 = (f32[2,32,128]{2,1,0:T(8,128)S(1)}, f32[2,32,128]{2,1,0:T(8,128)S(1)}, u32[]{:S(2)}, u32[]{:S(2)}) collective-permute-start(f32[2,32,128]{2,1,0:T(8,128)S(1)} %get-tuple-element.105.refs_13_), channel_id=1, source_target_pairs={{0,6},{1,7},{2,0},{3,1},{4,2},{5,3},{6,4},{7,5},{8,14},{9,15},{10,... | collective-permute-start | bytes 98312 | tf_op jit(solution)/shard_map/ppermute | solution.py:597
  74.7 4.3 %collective-permute-start.13 = (f32[2,32,128]{2,1,0:T(8,128)S(1)}, f32[2,32,128]{2,1,0:T(8,128)S(1)}, u32[]{:S(2)}, u32[]{:S(2)}) collective-permute-start(f32[2,32,128]{2,1,0:T(8,128)S(1)} %get-tuple-element.105.refs_13_), channel_id=1, source_target_pairs={{0,2},{1,3},{2,4},{3,5},{4,6},{5,7},{6,0},{7,1},{8,10},{9,11},{10,... | collective-permute-start | bytes 98312 | tf_op jit(solution)/shard_map/ppermute | solution.py:597
  75.0 4.3 %collective-permute-start.14 = (f32[2,32,128]{2,1,0:T(8,128)S(1)}, f32[2,32,128]{2,1,0:T(8,128)S(1)}, u32[]{:S(2)}, u32[]{:S(2)}) collective-permute-start(f32[2,32,128]{2,1,0:T(8,128)S(1)} %get-tuple-element.105.refs_13_), channel_id=1, source_target_pairs={{0,4},{1,5},{2,6},{3,7},{4,0},{5,1},{6,2},{7,3},{8,12},{9,13},{10,... | collective-permute-start | bytes 98312 | tf_op jit(solution)/shard_map/ppermute | solution.py:597
  79.3 5.1 %collective-permute-start.15 = (bf16[1024,128]{1,0:T(8,128)(2,1)S(1)}, bf16[1024,128]{1,0:T(8,128)(2,1)S(1)}, u32[]{:S(2)}, u32[]{:S(2)}) collective-permute-start(bf16[1024,128]{1,0:T(8,128)(2,1)S(1)} %collective-permute-done.2.refs_1_), channel_id=1, source_target_pairs={{0,1},{1,0},{2,3},{3,2},{4,5},{5,4},{6,7},{7,6},{8,9},{9,8},{10,11... | collective-permute-start | bytes 786440 | tf_op jit(solution)/shard_map/ppermute | solution.py:597
  83.2 1.5 %collective-permute-start.16 = (bf16[1024,128]{1,0:T(8,128)(2,1)S(1)}, bf16[1024,128]{1,0:T(8,128)(2,1)S(1)}, u32[]{:S(2)}, u32[]{:S(2)}) collective-permute-start(bf16[1024,128]{1,0:T(8,128)(2,1)S(1)} %collective-permute-done.10.refs_8_), channel_id=1, source_target_pairs={{0,1},{1,0},{2,3},{3,2},{4,5},{5,4},{6,7},{7,6},{8,9},{9,8},{10,11... | collective-permute-start | bytes 786440 | tf_op jit(solution)/shard_map/ppermute | solution.py:597
  83.2 1.9 %collective-permute-start.17 = (bf16[1024,128]{1,0:T(8,128)(2,1)S(1)}, bf16[1024,128]{1,0:T(8,128)(2,1)S(1)}, u32[]{:S(2)}, u32[]{:S(2)}) collective-permute-start(bf16[1024,128]{1,0:T(8,128)(2,1)S(1)} %collective-permute-done.11.refs_5_), channel_id=1, source_target_pairs={{0,1},{1,0},{2,3},{3,2},{4,5},{5,4},{6,7},{7,6},{8,9},{9,8},{10,11... | collective-permute-start | bytes 786440 | tf_op jit(solution)/shard_map/ppermute | solution.py:597
  83.7 1.8 %collective-permute-start.18 = (bf16[1024,128]{1,0:T(8,128)(2,1)S(1)}, bf16[1024,128]{1,0:T(8,128)(2,1)S(1)}, u32[]{:S(2)}, u32[]{:S(2)}) collective-permute-start(bf16[1024,128]{1,0:T(8,128)(2,1)S(1)} %collective-permute-done.9.refs_3_), channel_id=1, source_target_pairs={{0,1},{1,0},{2,3},{3,2},{4,5},{5,4},{6,7},{7,6},{8,9},{9,8},{10,11... | collective-permute-start | bytes 786440 | tf_op jit(solution)/shard_map/ppermute | solution.py:597
  90.5 9.0 %collective-permute-start.20 = (f32[8,32,128]{2,1,0:T(8,128)S(1)}, f32[8,32,128]{2,1,0:T(8,128)S(1)}, u32[]{:S(2)}, u32[]{:S(2)}) collective-permute-start(f32[8,32,128]{2,1,0:T(8,128)S(1)} %get-tuple-element.122), channel_id=1, source_target_pairs={{0,7},{1,6},{2,1},{3,0},{4,3},{5,2},{6,5},{7,4},{8,15},{9,14},{10,... | collective-permute-start | bytes 393224 | tf_op jit(solution)/shard_map/ppermute | solution.py:597
  93.5 9.1 %collective-permute-start.21 = (f32[8,32,128]{2,1,0:T(8,128)S(1)}, f32[8,32,128]{2,1,0:T(8,128)S(1)}, u32[]{:S(2)}, u32[]{:S(2)}) collective-permute-start(f32[8,32,128]{2,1,0:T(8,128)S(1)} %get-tuple-element.121), channel_id=1, source_target_pairs={{0,2},{1,3},{2,4},{3,5},{4,6},{5,7},{6,0},{7,1},{8,10},{9,11},{10,... | collective-permute-start | bytes 393224 | tf_op jit(solution)/shard_map/ppermute | solution.py:597
  93.5 9.1 %collective-permute-start.19 = (f32[32,8,128]{2,1,0:T(8,128)S(1)}, f32[32,8,128]{2,1,0:T(8,128)S(1)}, u32[]{:S(2)}, u32[]{:S(2)}) collective-permute-start(f32[32,8,128]{2,1,0:T(8,128)S(1)} %slice.21), channel_id=1, source_target_pairs={{0,4},{1,5},{2,6},{3,7},{4,1},{5,0},{6,3},{7,2},{8,12},{9,13},{10,... | collective-permute-start | bytes 393224 | tf_op jit(solution)/shard_map/ppermute | solution.py:597
  (1 other events, 1.0 us)

commit v9 on v8

--- a/solution.py
+++ b/solution.py
@@ -526,15 +526,17 @@
     step = 256
     for r in range(CHIPS):
         lanes = (at, off) if r == 0 else (0, WIDTH)
-        for raw, lane in zip(halves[2 * r : 2 * r + 2], lanes):
+        for raws, lane in zip(halves[2 * r : 2 * r + 2], lanes):
             mean = stat_ref[r, 0:1, pl.ds(lane, WIDTH)]
-
-            def shift(i, _, raw=raw, lane=lane, mean=mean):
-                piece = (raw[pl.ds(i * step, step), :].astype(F32) - mean) * live
-                cent_ref[pl.ds(i * step, step), pl.ds(lane, WIDTH)] = piece.astype(BF16)
-                return 0
-
-            lax.fori_loop(0, HALO // step, shift, 0, unroll=2)
+            for index, raw in enumerate(raws):
+                rows = raw.shape[0]
+
+                def shift(i, _, raw=raw, first=index * rows, lane=lane, mean=mean):
+                    piece = (raw[pl.ds(i * step, step), :].astype(F32) - mean) * live
+                    cent_ref[pl.ds(first + i * step, step), pl.ds(lane, WIDTH)] = piece.astype(BF16)
+                    return 0
+
+                lax.fori_loop(0, rows // step, shift, 0, unroll=2)
         if r == 0:
             flip_ref[...] = cent_ref[:, pl.ds(at, WIDTH)].T
             flipped = flip_ref[...]
@@ -551,7 +553,7 @@
 
 
 def late_kernel(
-    where_ref, h0, h1, h2, h3, h4, h5, h6, h7, total_ref, sums_ref, gram_ref, stat_ref,
+    where_ref, m0, m1, m2, m3, m4, o0, o1, o2, o3, o4, total_ref, sums_ref, gram_ref, stat_ref,
     own_ref, ahead_ref, behind_ref, far_ref, flags_ref,
     turned_ref, cols_ref, coef_ref, before_ref, after_ref, window_ref, vectors, cent_ref, flip_ref, sum_ref,
 ):
@@ -560,7 +562,8 @@
         turned_ref, cols_ref, coef_ref, before_ref, after_ref, vectors,
     )
     window_kernel(
-        where_ref, (h0, h1, h2, h3, h4, h5, h6, h7), gram_ref, stat_ref, total_ref,
+        where_ref, ((m0,), (o0,), (m1,), (o4,), (m2, m3), (o2, o3), (o1,), (m4,)),
+        gram_ref, stat_ref, total_ref,
         window_ref, cent_ref, flip_ref, sum_ref,
     )
 
@@ -580,7 +583,7 @@
             (square, 8),
             (square, 9),
         ),
-        fetched=(9, 10, 11, 12, 13, 17),
+        fetched=(11, 12, 13, 14, 15, 19),
         stored=(0,),
         scratch=[
             ((WIDTH, WIDTH), F32),
@@ -694,10 +697,12 @@
     prior = after(prior, token(pieces))
     prior_ahead = to_chan(prior, lambda s: s - 2)
     prior_behind = to_chan(prior, lambda s: s + 2)
-    prior_far = to_chan(prior, lambda s: s + 4)
     arrived, prior_ahead, prior_behind, sums = lax.optimization_barrier(
         (arrived, prior_ahead, prior_behind, sums)
     )
+    half = HALO // 2
+    prior_low = to_chan(prior_behind[:half], lambda s: s + 2)
+    prior_high = to_chan(prior_ahead[half:], lambda s: s - 2)
     scanned, own_means, flags = call(
         scan_kernel,
         "scan_pieces",
@@ -706,16 +711,16 @@
         stored=(0, 1, 2),
         us=1,
     )
+    scanned, prior_low, prior_high = lax.optimization_barrier((scanned, prior_low, prior_high))
     back = exchange(scanned)
-    own_means, prior_far = lax.optimization_barrier((own_means, prior_far))
     ahead_means = to_chan(own_means, lambda s: s - 2)
     behind_means = to_chan(own_means, lambda s: s + 2)
     far_means = to_chan(own_means, lambda s: s + 4)
     means = (own_means, ahead_means, behind_means, far_means)
-    halo = (prior, prior_ahead, prior_far, prior_behind)
+    halo = (prior, prior_ahead, prior_low, prior_high, prior_behind)
     halo, means = lax.optimization_barrier((halo, means))
     mine, other = halo, [to_chan(value, lambda s: s ^ 1) for value in halo]
-    halves = (mine[0], other[0], mine[1], other[3], mine[2], other[2], other[1], mine[3])
+    halves = (*mine, *other)
     store, window_cov = late_terms(
         where, halves, late_total, sums, gram, stat, means, flags, store
     )

time: 106 us -> 105 us (level)
  waiting for transfers between devices: 24.1 us -> 17.6 us
  starting transfers between devices: 45.1 us -> 50.5 us
    ppermute x21 -> x23, waiting for transfers between devices: 21 us -> 14.4 us  [to_chan(): lax.ppermute(value, 'chan', [(s, target(s) % count) for s in range(count)])]
    ppermute x21 -> x23, starting transfers between devices: 26.2 us -> 31.3 us  [to_chan(): lax.ppermute(value, 'chan', [(s, target(s) % count) for s in range(count)])]
  transfers between devices with their start and end apart: 24 -> 26, of which waited for: 13 -> 9; matrix products, arithmetic and copies ran while one was open for 2% -> 2% of each run, Pallas kernels for 24% -> 25%
where the time goes in v9:
time: 105 us
  starting transfers between devices  50.5 us (48%)
  Pallas kernels  31.8 us (30%)
  waiting for transfers between devices  17.6 us (17%)
  local copies, waits for them, and re-layouts  2.92 us (3%)
  between operations  1.79 us (2%)
    ppermute x23, starting transfers between devices, to_chan(): lax.ppermute(value, 'chan', [(s, target(s) % count) for s in range(count)])  31.3 us
    pallas_call x7, Pallas kernels, call(): pl.pallas_call(body, out_shape=[STORE] * first + outputs, grid=(1,), in_s...  23.7 us
    all_to_all x2, starting transfers between devices, exchange(): return lax.all_to_all(value, 'tm', 0, 0, tiled=True)  17.4 us
    ppermute x23, waiting for transfers between devices, to_chan(): lax.ppermute(value, 'chan', [(s, target(s) % count) for s in range(count)])  14.4 us
    pallas_call x1, Pallas kernels, most_outputs(): pl.pallas_call(most_kernel, out_shape=MOST, grid=(1,), in_specs=[SM, whol...  5 us
    pallas_call x1, Pallas kernels, last_outputs(): pl.pallas_call(last_kernel, out_shape=OUTPUTS, grid=(1,), in_specs=[SM] +...  3.12 us
    all_to_all x2, waiting for transfers between devices, exchange(): return lax.all_to_all(value, 'tm', 0, 0, tiled=True)  3.11 us
  transfers between devices with their start and end apart: 26, of which 9 were waited for; matrix products, arithmetic and copies ran while one was open for 2% of the time, Pallas kernels for 25%

profile of v9, /device:TPU:1, one launch (start us, length us, event | category | flops | bytes accessed | tf_op | source)
XLA Modules:
  0.0 104.6 jit_solution(4522263699793271017)
XLA Ops:
  0.6 3.3 %collective-permute-start.3 = (bf16[2048,128]{1,0:T(8,128)(2,1)}, bf16[2048,128]{1,0:T(8,128)(2,1)S(1)}, u32[]{:S(2)}, u32[]{:S(2)}) collective-permute-start(bf16[2048,128]{1,0:T(8,128)(2,1)} %refs_1_.1), channel_id=1, source_target_pairs={{0,1},{1,0},{2,3},{3,2},{4,5},{5,4},{6,7},{7,6},{8,9},{9,8},{10,11... | collective-permute-start | bytes 1572872 | tf_op jit(solution)/shard_map/ppermute | solution.py:600
  4.0 2.7 %collective-permute-start.1 = (bf16[2048,128]{1,0:T(8,128)(2,1)}, bf16[2048,128]{1,0:T(8,128)(2,1)S(1)}, u32[]{:S(2)}, u32[]{:S(2)}) collective-permute-start(bf16[2048,128]{1,0:T(8,128)(2,1)} %refs_1_.1), channel_id=1, source_target_pairs={{0,6},{1,7},{2,0},{3,1},{4,2},{5,3},{6,4},{7,5},{8,14},{9,15},{10,... | collective-permute-start | bytes 1572872 | tf_op jit(solution)/shard_map/ppermute | solution.py:600
  7.7 1.8 %collective-permute-start.2 = (bf16[1024,128]{1,0:T(8,128)(2,1)S(1)}, bf16[1024,128]{1,0:T(8,128)(2,1)S(1)}, u32[]{:S(2)}, u32[]{:S(2)}) collective-permute-start(bf16[1024,128]{1,0:T(8,128)(2,1)S(1)} %slice.24), channel_id=1, source_target_pairs={{0,8},{8,16},{16,24},{24,32},{32,40},{40,48},{48,56},{56,64},{64,7... | collective-permute-start | bytes 786440 | tf_op jit(solution)/shard_map/ppermute | solution.py:624
  12.0 4.1 %first_pair.1 = (f32[96,8,128,128]{3,2,1,0:T(8,128)}, f32[4,8,256]{2,1,0:T(8,128)S(1)}, f32[4,128,256]{2,1,0:T(8,128)S(1)}, f32[4,8,256]{2,1,0:T(8,128)S(1)}, bf...) custom-call(s32[21]{0:T(128)S(1)} %concatenate.6.refs_0_.where_ref, ...), custom_call_target="tpu_custom_call" | custom-call | flops 3000000000 | bytes 1048576 | tf_op jit(solution)/shard_map/first_pair/pallas_call | solution.py:232
  16.1 2.8 %collective-permute-done.refs_2_ = bf16[2048,128]{1,0:T(8,128)(2,1)S(1)} collective-permute-done((bf16[2048,128]{1,0:T(8,128)(2,1)}, bf16[2048,128]{1,0:T(8,128)(2,1)S(1)}, u32[]{:S(2)}, u32[]{:S(2)}) %collective-permute-start) | collective-permute-done | bytes 524320 | tf_op jit(solution)/shard_map/ppermute | solution.py:600
  19.9 2.8 %collective-permute-start.5 = (bf16[1024,128]{1,0:T(8,128)(2,1)S(1)}, bf16[1024,128]{1,0:T(8,128)(2,1)S(1)}, u32[]{:S(2)}, u32[]{:S(2)}) collective-permute-start(bf16[1024,128]{1,0:T(8,128)(2,1)S(1)} %slice.26), channel_id=1, source_target_pairs={{0,6},{1,7},{2,0},{3,1},{4,2},{5,3},{6,4},{7,5},{8,14},{9,15},{10,... | collective-permute-start | bytes 786440 | tf_op jit(solution)/shard_map/ppermute | solution.py:600
  22.6 3.8 %near_pair.1 = (f32[96,8,128,128]{3,2,1,0:T(8,128)}, f32[4,8,256]{2,1,0:T(8,128)S(1)}, f32[4,128,256]{2,1,0:T(8,128)S(1)}, f32[4,8,256]{2,1,0:T(8,128)S(1)}, f32[128,256]{1,0:T(8,128)S(1)}) custom-call(s32[21]{0:T(128)S(1)} %concatenate.6.refs_0_.where_ref, ...), custom_call_target="tpu_custom_call", output_to_operand_aliasing={{0}: (5, {}), {1}: (6, {}), {2}: (7, {}), {3}: (8, {})} | custom-call | flops 3000000000 | bytes 1048576 | tf_op jit(solution)/shard_map/near_pair/pallas_call | solution.py:232
  26.5 3.8 %side_pair.1 = (f32[96,8,128,128]{3,2,1,0:T(8,128)}, f32[4,8,256]{2,1,0:T(8,128)S(1)}, f32[4,128,256]{2,1,0:T(8,128)S(1)}, f32[4,8,256]{2,1,0:T(8,128)S(1)}) custom-call(s32[21]{0:T(128)S(1)} %concatenate.6.refs_0_.where_ref, ...), custom_call_target="tpu_custom_call", output_to_operand_aliasing={{0}: (4, {}), {1}: (5, {}), {2}: (6, {}), {3}: (7, {})} | custom-call | flops 2000000000 | bytes 1048576 | tf_op jit(solution)/shard_map/side_pair/pallas_call | solution.py:232
  33.0 2.5 %far_pair.1 = (f32[4,128,256]{2,1,0:T(8,128)S(1)}, f32[4,8,256]{2,1,0:T(8,128)S(1)}, f32[32,24,128]{2,1,0:T(8,128)}) custom-call(s32[21]{0:T(128)S(1)} %concatenate.6.refs_0_.where_ref, bf16[2048,128]{1,0:T(8,128)(2,1)S(1)} %constant_dynamic-update-slice_fusion.refs_1_, ...), custom_call_target="tpu_custom_call", output_to_operand_aliasing={{0}: (8, {}), {1}: (9, {})} | custom-call | flops 100000000 | bytes 1048576 | tf_op jit(solution)/shard_map/far_pair/pallas_call | solution.py:232
  35.6 9.5 %all-to-all-start = ((f32[32,24,128]{2,1,0:T(8,128)}), f32[32,24,128]{2,1,0:T(8,128)S(1)}, u32[]{:S(2)}, u32[]{:S(2)}) async-start(f32[32,24,128]{2,1,0:T(8,128)} %get-tuple-element.85), calls=%async_computation | async-start | bytes 786432 | tf_op jit(solution)/shard_map/all_to_all | solution.py:604
  45.3 2.7 %collective-permute-start.9 = (bf16[1024,128]{1,0:T(8,128)(2,1)S(1)}, bf16[1024,128]{1,0:T(8,128)(2,1)S(1)}, u32[]{:S(2)}, u32[]{:S(2)}) collective-permute-start(bf16[1024,128]{1,0:T(8,128)(2,1)S(1)} %collective-permute-done.2.refs_1_), channel_id=1, source_target_pairs={{0,6},{1,7},{2,0},{3,1},{4,2},{5,3},{6,4},{7,5},{8,14},{9,15},{10,... | collective-permute-start | bytes 786440 | tf_op jit(solution)/shard_map/ppermute | solution.py:600
  48.0 3.7 %rest_left.1 = (f32[96,8,128,128]{3,2,1,0:T(8,128)}, f32[4,8,256]{2,1,0:T(8,128)S(1)}) custom-call(s32[21]{0:T(128)S(1)} %concatenate.6.refs_0_.where_ref, bf16[2048,128]{1,0:T(8,128)(2,1)S(1)} %constant_dynamic-update-slice_fusion.refs_1_, bf16[2048,128]{1,0:T(8,128)(2,1)S(1)} %collective-permute-done.8.refs_2_, ...), custom_call_target="tpu_custom_call", output_to_operand_aliasing={{0}: (4, {}), {1}: (5, {})} | custom-call | flops 4000000000 | bytes 1048576 | tf_op jit(solution)/shard_map/rest_left/pallas_call | solution.py:232
  51.7 2.0 %collective-permute-done.10.refs_5_ = bf16[1024,128]{1,0:T(8,128)(2,1)S(1)} collective-permute-done((bf16[1024,128]{1,0:T(8,128)(2,1)S(1)}, bf16[1024,128]{1,0:T(8,128)(2,1)S(1)}, u32[]{:S(2)}, u32[]{:S(2)}) %collective-permute-start.10) | collective-permute-done | bytes 262176 | tf_op jit(solution)/shard_map/ppermute | solution.py:600
  53.7 3.1 %all-to-all-done.refs_0_ = f32[32,24,128]{2,1,0:T(8,128)S(1)} async-done(((f32[32,24,128]{2,1,0:T(8,128)}), f32[32,24,128]{2,1,0:T(8,128)S(1)}, u32[]{:S(2)}, u32[]{:S(2)}) %all-to-all-start) | async-done | bytes 393248 | tf_op jit(solution)/shard_map/all_to_all | solution.py:604
  57.0 2.7 %collective-permute-start.12 = (bf16[512,128]{1,0:T(8,128)(2,1)S(1)}, bf16[512,128]{1,0:T(8,128)(2,1)S(1)}, u32[]{:S(2)}, u32[]{:S(2)}) collective-permute-start(bf16[512,128]{1,0:T(8,128)(2,1)S(1)} %slice.28), channel_id=1, source_target_pairs={{0,6},{1,7},{2,0},{3,1},{4,2},{5,3},{6,4},{7,5},{8,14},{9,15},{10,... | collective-permute-start | bytes 393224 | tf_op jit(solution)/shard_map/ppermute | solution.py:600
  62.0 7.9 %all-to-all-start.1 = ((f32[32,40,128]{2,1,0:T(8,128)}), f32[32,40,128]{2,1,0:T(8,128)S(1)}, u32[]{:S(2)}, u32[]{:S(2)}) async-start(f32[32,40,128]{2,1,0:T(8,128)} %get-tuple-element.96), calls=%async_computation.1 | async-start | bytes 1310720 | tf_op jit(solution)/shard_map/all_to_all | solution.py:604
  69.9 2.5 %collective-permute-start.13 = (f32[2,32,128]{2,1,0:T(8,128)S(1)}, f32[2,32,128]{2,1,0:T(8,128)S(1)}, u32[]{:S(2)}, u32[]{:S(2)}) collective-permute-start(f32[2,32,128]{2,1,0:T(8,128)S(1)} %get-tuple-element.109.refs_15_), channel_id=1, source_target_pairs={{0,6},{1,7},{2,0},{3,1},{4,2},{5,3},{6,4},{7,5},{8,14},{9,15},{10,... | collective-permute-start | bytes 98312 | tf_op jit(solution)/shard_map/ppermute | solution.py:600
  73.7 3.0 %collective-permute-done.14.refs_17_ = f32[2,32,128]{2,1,0:T(8,128)S(1)} collective-permute-done((f32[2,32,128]{2,1,0:T(8,128)S(1)}, f32[2,32,128]{2,1,0:T(8,128)S(1)}, u32[]{:S(2)}, u32[]{:S(2)}) %collective-permute-start.14) | collective-permute-done | bytes 32800 | tf_op jit(solution)/shard_map/ppermute | solution.py:600
  76.7 4.1 %collective-permute-start.16 = (bf16[1024,128]{1,0:T(8,128)(2,1)S(1)}, bf16[1024,128]{1,0:T(8,128)(2,1)S(1)}, u32[]{:S(2)}, u32[]{:S(2)}) collective-permute-start(bf16[1024,128]{1,0:T(8,128)(2,1)S(1)} %collective-permute-done.2.refs_1_), channel_id=1, source_target_pairs={{0,1},{1,0},{2,3},{3,2},{4,5},{5,4},{6,7},{7,6},{8,9},{9,8},{10,11... | collective-permute-start | bytes 786440 | tf_op jit(solution)/shard_map/ppermute | solution.py:600
  83.1 4.7 %late_terms.1 = (f32[96,8,128,128]{3,2,1,0:T(8,128)}, f32[1,128,1024]{2,1,0:T(8,128)}) custom-call(s32[21]{0:T(128)S(1)} %concatenate.6.refs_0_.where_ref, bf16[1024,128]{1,0:T(8,128)(2,1)S(1)} %collective-permute-done.2.refs_1_, bf16[1024,128]{1,0:T(8,128)(2,1)S(1)} %collective-permute-done.9.refs_2_, ...), custom_call_target="tpu_custom_call", output_to_operand_aliasing={{0}: (20, {})} | custom-call | flops 100000000 | bytes 1048576 | tf_op jit(solution)/shard_map/late_terms/pallas_call | solution.py:232
  87.9 5.3 %collective-permute-start.22 = (f32[8,32,128]{2,1,0:T(8,128)S(1)}, f32[8,32,128]{2,1,0:T(8,128)S(1)}, u32[]{:S(2)}, u32[]{:S(2)}) collective-permute-start(f32[8,32,128]{2,1,0:T(8,128)S(1)} %get-tuple-element.126), channel_id=1, source_target_pairs={{0,7},{1,6},{2,1},{3,0},{4,3},{5,2},{6,5},{7,4},{8,15},{9,14},{10,... | collective-permute-start | bytes 393224 | tf_op jit(solution)/shard_map/ppermute | solution.py:600
  93.7 5.0 %most_outputs.1 = (f32[8,128,1024]{2,1,0:T(8,128)S(1)}, f32[128,1024]{1,0:T(8,128)S(1)}, f32[24,128]{1,0:T(8,128)S(1)}) custom-call(s32[21]{0:T(128)S(1)} %concatenate.6.refs_0_.where_ref, f32[32,40,128]{2,1,0:T(8,128)S(1)} %all-to-all-done.1.back_ref, f32[96,8,128,128]{3,2,1,0:T(8,128)} %get-tuple-element.119.store_hbm), custom_call_target="tpu_custom_call" | custom-call | flops 5000000000 | bytes 1048576 | tf_op jit(solution)/shard_map/most_outputs/pallas_call | solution.py:484
  98.7 2.5 %collective-permute-done.23.before_ref = f32[8,32,128]{2,1,0:T(8,128)S(1)} collective-permute-done((f32[8,32,128]{2,1,0:T(8,128)S(1)}, f32[8,32,128]{2,1,0:T(8,128)S(1)}, u32[]{:S(2)}, u32[]{:S(2)}) %collective-permute-start.23) | collective-permute-done | bytes 131104 | tf_op jit(solution)/shard_map/ppermute | solution.py:600
  101.3 3.1 %last_outputs.1 = (f32[1,8,128,1024]{3,2,1,0:T(8,128)}, f32[1,128,1024]{2,1,0:T(8,128)}) custom-call(s32[21]{0:T(128)S(1)} %concatenate.6.refs_0_.where_ref, f32[8,128,1024]{2,1,0:T(8,128)S(1)} %get-tuple-element.120.most_ref, f32[128,1024]{1,0:T(8,128)S(1)} %get-tuple-element.121.most_seg_ref, f32[24,128]{1,0:T(8,128)S(1)} %get-tuple-element.122.coef_ref, ...), custom_call_target="tpu_custom_call" | custom-call | flops 3000000000 | bytes 1048576 | tf_op jit(solution)/shard_map/last_outputs/pallas_call | solution.py:502
  (49 shorter events, 13.3 us)
Async XLA Ops:
  0.6 10.3 %collective-permute-start.3 = (bf16[2048,128]{1,0:T(8,128)(2,1)}, bf16[2048,128]{1,0:T(8,128)(2,1)S(1)}, u32[]{:S(2)}, u32[]{:S(2)}) collective-permute-start(bf16[2048,128]{1,0:T(8,128)(2,1)} %refs_1_.1), channel_id=1, source_target_pairs={{0,1},{1,0},{2,3},{3,2},{4,5},{5,4},{6,7},{7,6},{8,9},{9,8},{10,11... | collective-permute-start | bytes 1572872 | tf_op jit(solution)/shard_map/ppermute | solution.py:600
  4.0 14.9 %collective-permute-start = (bf16[2048,128]{1,0:T(8,128)(2,1)}, bf16[2048,128]{1,0:T(8,128)(2,1)S(1)}, u32[]{:S(2)}, u32[]{:S(2)}) collective-permute-start(bf16[2048,128]{1,0:T(8,128)(2,1)} %refs_1_.1), channel_id=1, source_target_pairs={{0,2},{1,3},{2,4},{3,5},{4,6},{5,7},{6,0},{7,1},{8,10},{9,11},{10,... | collective-permute-start | bytes 1572872 | tf_op jit(solution)/shard_map/ppermute | solution.py:600
  4.0 14.9 %collective-permute-start.1 = (bf16[2048,128]{1,0:T(8,128)(2,1)}, bf16[2048,128]{1,0:T(8,128)(2,1)S(1)}, u32[]{:S(2)}, u32[]{:S(2)}) collective-permute-start(bf16[2048,128]{1,0:T(8,128)(2,1)} %refs_1_.1), channel_id=1, source_target_pairs={{0,6},{1,7},{2,0},{3,1},{4,2},{5,3},{6,4},{7,5},{8,14},{9,15},{10,... | collective-permute-start | bytes 1572872 | tf_op jit(solution)/shard_map/ppermute | solution.py:600
  7.7 8.4 %collective-permute-start.2 = (bf16[1024,128]{1,0:T(8,128)(2,1)S(1)}, bf16[1024,128]{1,0:T(8,128)(2,1)S(1)}, u32[]{:S(2)}, u32[]{:S(2)}) collective-permute-start(bf16[1024,128]{1,0:T(8,128)(2,1)S(1)} %slice.24), channel_id=1, source_target_pairs={{0,8},{8,16},{16,24},{24,32},{32,40},{40,48},{48,56},{56,64},{64,7... | collective-permute-start | bytes 786440 | tf_op jit(solution)/shard_map/ppermute | solution.py:624
  18.9 3.8 %collective-permute-start.7 = (bf16[2048,128]{1,0:T(8,128)(2,1)S(1)}, bf16[2048,128]{1,0:T(8,128)(2,1)S(1)}, u32[]{:S(2)}, u32[]{:S(2)}) collective-permute-start(bf16[2048,128]{1,0:T(8,128)(2,1)S(1)} %collective-permute-done.refs_2_), channel_id=1, source_target_pairs={{0,1},{1,0},{2,3},{3,2},{4,5},{5,4},{6,7},{7,6},{8,9},{9,8},{10,11... | collective-permute-start | bytes 1572872 | tf_op jit(solution)/shard_map/ppermute | solution.py:600
  19.7 6.7 %collective-permute-start.6 = (bf16[2048,128]{1,0:T(8,128)(2,1)S(1)}, bf16[2048,128]{1,0:T(8,128)(2,1)S(1)}, u32[]{:S(2)}, u32[]{:S(2)}) collective-permute-start(bf16[2048,128]{1,0:T(8,128)(2,1)S(1)} %collective-permute-done.1.refs_1_), channel_id=1, source_target_pairs={{0,1},{1,0},{2,3},{3,2},{4,5},{5,4},{6,7},{7,6},{8,9},{9,8},{10,11... | collective-permute-start | bytes 1572872 | tf_op jit(solution)/shard_map/ppermute | solution.py:600
  19.8 10.6 %collective-permute-start.4 = (bf16[1024,128]{1,0:T(8,128)(2,1)S(1)}, bf16[1024,128]{1,0:T(8,128)(2,1)S(1)}, u32[]{:S(2)}, u32[]{:S(2)}) collective-permute-start(bf16[1024,128]{1,0:T(8,128)(2,1)S(1)} %slice.25), channel_id=1, source_target_pairs={{0,2},{1,3},{2,4},{3,5},{4,6},{5,7},{6,0},{7,1},{8,10},{9,11},{10,... | collective-permute-start | bytes 786440 | tf_op jit(solution)/shard_map/ppermute | solution.py:600
  19.9 10.5 %collective-permute-start.5 = (bf16[1024,128]{1,0:T(8,128)(2,1)S(1)}, bf16[1024,128]{1,0:T(8,128)(2,1)S(1)}, u32[]{:S(2)}, u32[]{:S(2)}) collective-permute-start(bf16[1024,128]{1,0:T(8,128)(2,1)S(1)} %slice.26), channel_id=1, source_target_pairs={{0,6},{1,7},{2,0},{3,1},{4,2},{5,3},{6,4},{7,5},{8,14},{9,15},{10,... | collective-permute-start | bytes 786440 | tf_op jit(solution)/shard_map/ppermute | solution.py:600
  30.4 2.6 %collective-permute-start.8 = (bf16[2048,128]{1,0:T(8,128)(2,1)S(1)}, bf16[2048,128]{1,0:T(8,128)(2,1)S(1)}, u32[]{:S(2)}, u32[]{:S(2)}) collective-permute-start(bf16[2048,128]{1,0:T(8,128)(2,1)S(1)} %constant_dynamic-update-slice_fusion.refs_1_), channel_id=1, source_target_pairs={{0,1},{1,0},{2,3},{3,2},{4,5},{5,4},{6,7},{7,6},{8,9},{9,8},{10,11... | collective-permute-start | bytes 1572872 | tf_op jit(solution)/shard_map/ppermute | solution.py:600
  35.6 21.3 %all-to-all-start = ((f32[32,24,128]{2,1,0:T(8,128)}), f32[32,24,128]{2,1,0:T(8,128)S(1)}, u32[]{:S(2)}, u32[]{:S(2)}) async-start(f32[32,24,128]{2,1,0:T(8,128)} %get-tuple-element.85), calls=%async_computation | async-start | bytes 786432 | tf_op jit(solution)/shard_map/all_to_all | solution.py:604
  45.1 8.7 %collective-permute-start.10 = (bf16[1024,128]{1,0:T(8,128)(2,1)S(1)}, bf16[1024,128]{1,0:T(8,128)(2,1)S(1)}, u32[]{:S(2)}, u32[]{:S(2)}) collective-permute-start(bf16[1024,128]{1,0:T(8,128)(2,1)S(1)} %collective-permute-done.2.refs_1_), channel_id=1, source_target_pairs={{0,2},{1,3},{2,4},{3,5},{4,6},{5,7},{6,0},{7,1},{8,10},{9,11},{10,... | collective-permute-start | bytes 786440 | tf_op jit(solution)/shard_map/ppermute | solution.py:600
  45.3 8.4 %collective-permute-start.9 = (bf16[1024,128]{1,0:T(8,128)(2,1)S(1)}, bf16[1024,128]{1,0:T(8,128)(2,1)S(1)}, u32[]{:S(2)}, u32[]{:S(2)}) collective-permute-start(bf16[1024,128]{1,0:T(8,128)(2,1)S(1)} %collective-permute-done.2.refs_1_), channel_id=1, source_target_pairs={{0,6},{1,7},{2,0},{3,1},{4,2},{5,3},{6,4},{7,5},{8,14},{9,15},{10,... | collective-permute-start | bytes 786440 | tf_op jit(solution)/shard_map/ppermute | solution.py:600
  56.9 5.1 %collective-permute-start.11 = (bf16[512,128]{1,0:T(8,128)(2,1)S(1)}, bf16[512,128]{1,0:T(8,128)(2,1)S(1)}, u32[]{:S(2)}, u32[]{:S(2)}) collective-permute-start(bf16[512,128]{1,0:T(8,128)(2,1)S(1)} %slice.27), channel_id=1, source_target_pairs={{0,2},{1,3},{2,4},{3,5},{4,6},{5,7},{6,0},{7,1},{8,10},{9,11},{10,... | collective-permute-start | bytes 393224 | tf_op jit(solution)/shard_map/ppermute | solution.py:600
  57.0 5.0 %collective-permute-start.12 = (bf16[512,128]{1,0:T(8,128)(2,1)S(1)}, bf16[512,128]{1,0:T(8,128)(2,1)S(1)}, u32[]{:S(2)}, u32[]{:S(2)}) collective-permute-start(bf16[512,128]{1,0:T(8,128)(2,1)S(1)} %slice.28), channel_id=1, source_target_pairs={{0,6},{1,7},{2,0},{3,1},{4,2},{5,3},{6,4},{7,5},{8,14},{9,15},{10,... | collective-permute-start | bytes 393224 | tf_op jit(solution)/shard_map/ppermute | solution.py:600
  62.0 25.9 %all-to-all-start.1 = ((f32[32,40,128]{2,1,0:T(8,128)}), f32[32,40,128]{2,1,0:T(8,128)S(1)}, u32[]{:S(2)}, u32[]{:S(2)}) async-start(f32[32,40,128]{2,1,0:T(8,128)} %get-tuple-element.96), calls=%async_computation.1 | async-start | bytes 1310720 | tf_op jit(solution)/shard_map/all_to_all | solution.py:604
  69.9 3.8 %collective-permute-start.13 = (f32[2,32,128]{2,1,0:T(8,128)S(1)}, f32[2,32,128]{2,1,0:T(8,128)S(1)}, u32[]{:S(2)}, u32[]{:S(2)}) collective-permute-start(f32[2,32,128]{2,1,0:T(8,128)S(1)} %get-tuple-element.109.refs_15_), channel_id=1, source_target_pairs={{0,6},{1,7},{2,0},{3,1},{4,2},{5,3},{6,4},{7,5},{8,14},{9,15},{10,... | collective-permute-start | bytes 98312 | tf_op jit(solution)/shard_map/ppermute | solution.py:600
  72.4 4.3 %collective-permute-start.14 = (f32[2,32,128]{2,1,0:T(8,128)S(1)}, f32[2,32,128]{2,1,0:T(8,128)S(1)}, u32[]{:S(2)}, u32[]{:S(2)}) collective-permute-start(f32[2,32,128]{2,1,0:T(8,128)S(1)} %get-tuple-element.109.refs_15_), channel_id=1, source_target_pairs={{0,2},{1,3},{2,4},{3,5},{4,6},{5,7},{6,0},{7,1},{8,10},{9,11},{10,... | collective-permute-start | bytes 98312 | tf_op jit(solution)/shard_map/ppermute | solution.py:600
  72.4 4.3 %collective-permute-start.15 = (f32[2,32,128]{2,1,0:T(8,128)S(1)}, f32[2,32,128]{2,1,0:T(8,128)S(1)}, u32[]{:S(2)}, u32[]{:S(2)}) collective-permute-start(f32[2,32,128]{2,1,0:T(8,128)S(1)} %get-tuple-element.109.refs_15_), channel_id=1, source_target_pairs={{0,4},{1,5},{2,6},{3,7},{4,0},{5,1},{6,2},{7,3},{8,12},{9,13},{10,... | collective-permute-start | bytes 98312 | tf_op jit(solution)/shard_map/ppermute | solution.py:600
  76.7 6.4 %collective-permute-start.16 = (bf16[1024,128]{1,0:T(8,128)(2,1)S(1)}, bf16[1024,128]{1,0:T(8,128)(2,1)S(1)}, u32[]{:S(2)}, u32[]{:S(2)}) collective-permute-start(bf16[1024,128]{1,0:T(8,128)(2,1)S(1)} %collective-permute-done.2.refs_1_), channel_id=1, source_target_pairs={{0,1},{1,0},{2,3},{3,2},{4,5},{5,4},{6,7},{7,6},{8,9},{9,8},{10,11... | collective-permute-start | bytes 786440 | tf_op jit(solution)/shard_map/ppermute | solution.py:600
  80.8 2.3 %collective-permute-start.17 = (bf16[1024,128]{1,0:T(8,128)(2,1)S(1)}, bf16[1024,128]{1,0:T(8,128)(2,1)S(1)}, u32[]{:S(2)}, u32[]{:S(2)}) collective-permute-start(bf16[1024,128]{1,0:T(8,128)(2,1)S(1)} %collective-permute-done.9.refs_2_), channel_id=1, source_target_pairs={{0,1},{1,0},{2,3},{3,2},{4,5},{5,4},{6,7},{7,6},{8,9},{9,8},{10,11... | collective-permute-start | bytes 786440 | tf_op jit(solution)/shard_map/ppermute | solution.py:600
  80.9 2.3 %collective-permute-start.20 = (bf16[1024,128]{1,0:T(8,128)(2,1)S(1)}, bf16[1024,128]{1,0:T(8,128)(2,1)S(1)}, u32[]{:S(2)}, u32[]{:S(2)}) collective-permute-start(bf16[1024,128]{1,0:T(8,128)(2,1)S(1)} %collective-permute-done.10.refs_5_), channel_id=1, source_target_pairs={{0,1},{1,0},{2,3},{3,2},{4,5},{5,4},{6,7},{7,6},{8,9},{9,8},{10,11... | collective-permute-start | bytes 786440 | tf_op jit(solution)/shard_map/ppermute | solution.py:600
  87.9 10.8 %collective-permute-start.22 = (f32[8,32,128]{2,1,0:T(8,128)S(1)}, f32[8,32,128]{2,1,0:T(8,128)S(1)}, u32[]{:S(2)}, u32[]{:S(2)}) collective-permute-start(f32[8,32,128]{2,1,0:T(8,128)S(1)} %get-tuple-element.126), channel_id=1, source_target_pairs={{0,7},{1,6},{2,1},{3,0},{4,3},{5,2},{6,5},{7,4},{8,15},{9,14},{10,... | collective-permute-start | bytes 393224 | tf_op jit(solution)/shard_map/ppermute | solution.py:600
  93.2 8.1 %collective-permute-start.23 = (f32[8,32,128]{2,1,0:T(8,128)S(1)}, f32[8,32,128]{2,1,0:T(8,128)S(1)}, u32[]{:S(2)}, u32[]{:S(2)}) collective-permute-start(f32[8,32,128]{2,1,0:T(8,128)S(1)} %get-tuple-element.125), channel_id=1, source_target_pairs={{0,2},{1,3},{2,4},{3,5},{4,6},{5,7},{6,0},{7,1},{8,10},{9,11},{10,... | collective-permute-start | bytes 393224 | tf_op jit(solution)/shard_map/ppermute | solution.py:600
  93.2 8.1 %collective-permute-start.21 = (f32[32,8,128]{2,1,0:T(8,128)S(1)}, f32[32,8,128]{2,1,0:T(8,128)S(1)}, u32[]{:S(2)}, u32[]{:S(2)}) collective-permute-start(f32[32,8,128]{2,1,0:T(8,128)S(1)} %slice.29), channel_id=1, source_target_pairs={{0,4},{1,5},{2,6},{3,7},{4,1},{5,0},{6,3},{7,2},{8,12},{9,13},{10,... | collective-permute-start | bytes 393224 | tf_op jit(solution)/shard_map/ppermute | solution.py:600
  (3 other events, 4.4 us)

commit v10 on v7

--- a/solution.py
+++ b/solution.py
@@ -710,7 +710,6 @@
     far_means = to_chan(own_means, lambda s: s + 4)
     means = (own_means, ahead_means, behind_means, far_means)
     halo = (prior, prior_ahead, prior_far, prior_behind)
-    halo, means = lax.optimization_barrier((halo, means))
     mine, other = halo, [to_chan(value, lambda s: s ^ 1) for value in halo]
     halves = (mine[0], other[0], mine[1], other[3], mine[2], other[2], other[1], mine[3])
     store, window_cov = late_terms(

time: 103 us -> 108 us (1.049)
  starting transfers between devices: 41 us -> 47.8 us
  waiting for transfers between devices: 23.5 us -> 20.9 us
    ppermute x21, starting transfers between devices: 22.1 us -> 28.9 us  [to_chan(): lax.ppermute(value, 'chan', [(s, target(s) % count) for s in range(count)])]
    ppermute x21, waiting for transfers between devices: 19.2 us -> 16.6 us  [to_chan(): lax.ppermute(value, 'chan', [(s, target(s) % count) for s in range(count)])]
  transfers between devices with their start and end apart: 24 -> 24, of which waited for: 12 -> 10; matrix products, arithmetic and copies ran while one was open for 2% -> 2% of each run, Pallas kernels for 25% -> 24%
where the time goes in v10:
time: 108 us; the launch traced here: 107 us
  starting transfers between devices  47.8 us (44%)
  Pallas kernels  32.1 us (30%)
  waiting for transfers between devices  20.9 us (19%)
  local copies, waits for them, and re-layouts  4.73 us (4%)
  between operations  1.77 us (2%)
    ppermute x21, starting transfers between devices, to_chan(): lax.ppermute(value, 'chan', [(s, target(s) % count) for s in range(count)])  28.9 us
    pallas_call x7, Pallas kernels, call(): pl.pallas_call(body, out_shape=[STORE] * first + outputs, grid=(1,), in_s...  24 us
    all_to_all x2, starting transfers between devices, exchange(): return lax.all_to_all(value, 'tm', 0, 0, tiled=True)  17.1 us
    ppermute x21, waiting for transfers between devices, to_chan(): lax.ppermute(value, 'chan', [(s, target(s) % count) for s in range(count)])  16.6 us
    pallas_call x1, Pallas kernels, most_outputs(): pl.pallas_call(most_kernel, out_shape=MOST, grid=(1,), in_specs=[SM, whol...  5 us
    all_to_all x2, waiting for transfers between devices, exchange(): return lax.all_to_all(value, 'tm', 0, 0, tiled=True)  4.33 us
    pallas_call x1, Pallas kernels, last_outputs(): pl.pallas_call(last_kernel, out_shape=OUTPUTS, grid=(1,), in_specs=[SM] +...  3.12 us
    unnamed x7, local copies, waits for them, and re-layouts  2.89 us
  transfers between devices with their start and end apart: 24, of which 10 were waited for; matrix products, arithmetic and copies ran while one was open for 2% of the time, Pallas kernels for 24%

profile of v10, /device:TPU:1, one launch (start us, length us, event | category | flops | bytes accessed | tf_op | source)
XLA Modules:
  0.0 107.4 jit_solution(12484138976063053433)
XLA Ops:
  0.6 3.3 %collective-permute-start.3 = (bf16[2048,128]{1,0:T(8,128)(2,1)}, bf16[2048,128]{1,0:T(8,128)(2,1)S(1)}, u32[]{:S(2)}, u32[]{:S(2)}) collective-permute-start(bf16[2048,128]{1,0:T(8,128)(2,1)} %refs_1_.1), channel_id=1, source_target_pairs={{0,1},{1,0},{2,3},{3,2},{4,5},{5,4},{6,7},{7,6},{8,9},{9,8},{10,11... | collective-permute-start | bytes 1572872 | tf_op jit(solution)/shard_map/ppermute | solution.py:597
  4.0 2.7 %collective-permute-start.1 = (bf16[2048,128]{1,0:T(8,128)(2,1)}, bf16[2048,128]{1,0:T(8,128)(2,1)S(1)}, u32[]{:S(2)}, u32[]{:S(2)}) collective-permute-start(bf16[2048,128]{1,0:T(8,128)(2,1)} %refs_1_.1), channel_id=1, source_target_pairs={{0,6},{1,7},{2,0},{3,1},{4,2},{5,3},{6,4},{7,5},{8,14},{9,15},{10,... | collective-permute-start | bytes 1572872 | tf_op jit(solution)/shard_map/ppermute | solution.py:597
  7.7 1.8 %collective-permute-start.2 = (bf16[1024,128]{1,0:T(8,128)(2,1)S(1)}, bf16[1024,128]{1,0:T(8,128)(2,1)S(1)}, u32[]{:S(2)}, u32[]{:S(2)}) collective-permute-start(bf16[1024,128]{1,0:T(8,128)(2,1)S(1)} %slice.18), channel_id=1, source_target_pairs={{0,8},{8,16},{16,24},{24,32},{32,40},{40,48},{48,56},{56,64},{64,7... | collective-permute-start | bytes 786440 | tf_op jit(solution)/shard_map/ppermute | solution.py:621
  13.8 4.1 %first_pair.1 = (f32[96,8,128,128]{3,2,1,0:T(8,128)}, f32[4,8,256]{2,1,0:T(8,128)S(1)}, f32[4,128,256]{2,1,0:T(8,128)S(1)}, f32[4,8,256]{2,1,0:T(8,128)S(1)}, bf...) custom-call(s32[21]{0:T(128)S(1)} %concatenate.6.refs_0_.where_ref, ...), custom_call_target="tpu_custom_call" | custom-call | flops 3000000000 | bytes 1048576 | tf_op jit(solution)/shard_map/first_pair/pallas_call | solution.py:232
  19.9 2.8 %collective-permute-start.5 = (bf16[1024,128]{1,0:T(8,128)(2,1)S(1)}, bf16[1024,128]{1,0:T(8,128)(2,1)S(1)}, u32[]{:S(2)}, u32[]{:S(2)}) collective-permute-start(bf16[1024,128]{1,0:T(8,128)(2,1)S(1)} %slice.20), channel_id=1, source_target_pairs={{0,6},{1,7},{2,0},{3,1},{4,2},{5,3},{6,4},{7,5},{8,14},{9,15},{10,... | collective-permute-start | bytes 786440 | tf_op jit(solution)/shard_map/ppermute | solution.py:597
  22.6 3.8 %near_pair.1 = (f32[96,8,128,128]{3,2,1,0:T(8,128)}, f32[4,8,256]{2,1,0:T(8,128)S(1)}, f32[4,128,256]{2,1,0:T(8,128)S(1)}, f32[4,8,256]{2,1,0:T(8,128)S(1)}, f32[128,256]{1,0:T(8,128)S(1)}) custom-call(s32[21]{0:T(128)S(1)} %concatenate.6.refs_0_.where_ref, ...), custom_call_target="tpu_custom_call", output_to_operand_aliasing={{0}: (5, {}), {1}: (6, {}), {2}: (7, {}), {3}: (8, {})} | custom-call | flops 3000000000 | bytes 1048576 | tf_op jit(solution)/shard_map/near_pair/pallas_call | solution.py:232
  26.5 3.8 %side_pair.1 = (f32[96,8,128,128]{3,2,1,0:T(8,128)}, f32[4,8,256]{2,1,0:T(8,128)S(1)}, f32[4,128,256]{2,1,0:T(8,128)S(1)}, f32[4,8,256]{2,1,0:T(8,128)S(1)}) custom-call(s32[21]{0:T(128)S(1)} %concatenate.6.refs_0_.where_ref, ...), custom_call_target="tpu_custom_call", output_to_operand_aliasing={{0}: (4, {}), {1}: (5, {}), {2}: (6, {}), {3}: (7, {})} | custom-call | flops 2000000000 | bytes 1048576 | tf_op jit(solution)/shard_map/side_pair/pallas_call | solution.py:232
  33.0 2.5 %far_pair.1 = (f32[4,128,256]{2,1,0:T(8,128)S(1)}, f32[4,8,256]{2,1,0:T(8,128)S(1)}, f32[32,24,128]{2,1,0:T(8,128)}) custom-call(s32[21]{0:T(128)S(1)} %concatenate.6.refs_0_.where_ref, bf16[2048,128]{1,0:T(8,128)(2,1)S(1)} %constant_dynamic-update-slice_fusion.refs_1_, ...), custom_call_target="tpu_custom_call", output_to_operand_aliasing={{0}: (8, {}), {1}: (9, {})} | custom-call | flops 100000000 | bytes 1048576 | tf_op jit(solution)/shard_map/far_pair/pallas_call | solution.py:232
  35.6 9.5 %all-to-all-start = ((f32[32,24,128]{2,1,0:T(8,128)}), f32[32,24,128]{2,1,0:T(8,128)S(1)}, u32[]{:S(2)}, u32[]{:S(2)}) async-start(f32[32,24,128]{2,1,0:T(8,128)} %get-tuple-element.72), calls=%async_computation | async-start | bytes 786432 | tf_op jit(solution)/shard_map/all_to_all | solution.py:601
  45.1 1.7 %collective-permute-start.9 = (bf16[1024,128]{1,0:T(8,128)(2,1)S(1)}, bf16[1024,128]{1,0:T(8,128)(2,1)S(1)}, u32[]{:S(2)}, u32[]{:S(2)}) collective-permute-start(bf16[1024,128]{1,0:T(8,128)(2,1)S(1)} %collective-permute-done.2.refs_1_), channel_id=1, source_target_pairs={{0,6},{1,7},{2,0},{3,1},{4,2},{5,3},{6,4},{7,5},{8,14},{9,15},{10,... | collective-permute-start | bytes 786440 | tf_op jit(solution)/shard_map/ppermute | solution.py:597
  46.8 3.7 %rest_left.1 = (f32[96,8,128,128]{3,2,1,0:T(8,128)}, f32[4,8,256]{2,1,0:T(8,128)S(1)}) custom-call(s32[21]{0:T(128)S(1)} %concatenate.6.refs_0_.where_ref, bf16[2048,128]{1,0:T(8,128)(2,1)S(1)} %constant_dynamic-update-slice_fusion.refs_1_, bf16[2048,128]{1,0:T(8,128)(2,1)S(1)} %collective-permute-done.8.refs_2_, ...), custom_call_target="tpu_custom_call", output_to_operand_aliasing={{0}: (4, {}), {1}: (5, {})} | custom-call | flops 4000000000 | bytes 1048576 | tf_op jit(solution)/shard_map/rest_left/pallas_call | solution.py:232
  50.5 2.0 %collective-permute-done.9.refs_3_ = bf16[1024,128]{1,0:T(8,128)(2,1)S(1)} collective-permute-done((bf16[1024,128]{1,0:T(8,128)(2,1)S(1)}, bf16[1024,128]{1,0:T(8,128)(2,1)S(1)}, u32[]{:S(2)}, u32[]{:S(2)}) %collective-permute-start.9) | collective-permute-done | bytes 262176 | tf_op jit(solution)/shard_map/ppermute | solution.py:597
  52.6 4.3 %all-to-all-done.refs_0_ = f32[32,24,128]{2,1,0:T(8,128)S(1)} async-done(((f32[32,24,128]{2,1,0:T(8,128)}), f32[32,24,128]{2,1,0:T(8,128)S(1)}, u32[]{:S(2)}, u32[]{:S(2)}) %all-to-all-start) | async-done | bytes 393248 | tf_op jit(solution)/shard_map/all_to_all | solution.py:601
  57.9 7.6 %all-to-all-start.1 = ((f32[32,40,128]{2,1,0:T(8,128)}), f32[32,40,128]{2,1,0:T(8,128)S(1)}, u32[]{:S(2)}, u32[]{:S(2)}) async-start(f32[32,40,128]{2,1,0:T(8,128)} %get-tuple-element.80), calls=%async_computation.1 | async-start | bytes 1310720 | tf_op jit(solution)/shard_map/all_to_all | solution.py:601
  65.6 2.6 %collective-permute-start.13 = (bf16[1024,128]{1,0:T(8,128)(2,1)S(1)}, bf16[1024,128]{1,0:T(8,128)(2,1)S(1)}, u32[]{:S(2)}, u32[]{:S(2)}) collective-permute-start(bf16[1024,128]{1,0:T(8,128)(2,1)S(1)} %collective-permute-done.2.refs_1_), channel_id=1, source_target_pairs={{0,4},{1,5},{2,6},{3,7},{4,0},{5,1},{6,2},{7,3},{8,12},{9,13},{10,... | collective-permute-start | bytes 786440 | tf_op jit(solution)/shard_map/ppermute | solution.py:597
  68.2 1.8 %collective-permute-start.10 = (bf16[1024,128]{1,0:T(8,128)(2,1)S(1)}, bf16[1024,128]{1,0:T(8,128)(2,1)S(1)}, u32[]{:S(2)}, u32[]{:S(2)}) collective-permute-start(bf16[1024,128]{1,0:T(8,128)(2,1)S(1)} %collective-permute-done.2.refs_1_), channel_id=1, source_target_pairs={{0,1},{1,0},{2,3},{3,2},{4,5},{5,4},{6,7},{7,6},{8,9},{9,8},{10,11... | collective-permute-start | bytes 786440 | tf_op jit(solution)/shard_map/ppermute | solution.py:597
  70.0 3.3 %collective-permute-done.11.refs_8_ = bf16[1024,128]{1,0:T(8,128)(2,1)S(1)} collective-permute-done((bf16[1024,128]{1,0:T(8,128)(2,1)S(1)}, bf16[1024,128]{1,0:T(8,128)(2,1)S(1)}, u32[]{:S(2)}, u32[]{:S(2)}) %collective-permute-start.11) | collective-permute-done | bytes 262176 | tf_op jit(solution)/shard_map/ppermute | solution.py:597
  73.3 3.9 %collective-permute-start.12 = (bf16[1024,128]{1,0:T(8,128)(2,1)S(1)}, bf16[1024,128]{1,0:T(8,128)(2,1)S(1)}, u32[]{:S(2)}, u32[]{:S(2)}) collective-permute-start(bf16[1024,128]{1,0:T(8,128)(2,1)S(1)} %collective-permute-done.11.refs_8_), channel_id=1, source_target_pairs={{0,1},{1,0},{2,3},{3,2},{4,5},{5,4},{6,7},{7,6},{8,9},{9,8},{10,11... | collective-permute-start | bytes 786440 | tf_op jit(solution)/shard_map/ppermute | solution.py:597
  78.9 2.2 %collective-permute-start.14 = (bf16[1024,128]{1,0:T(8,128)(2,1)S(1)}, bf16[1024,128]{1,0:T(8,128)(2,1)S(1)}, u32[]{:S(2)}, u32[]{:S(2)}) collective-permute-start(bf16[1024,128]{1,0:T(8,128)(2,1)S(1)} %collective-permute-done.13.refs_5_), channel_id=1, source_target_pairs={{0,1},{1,0},{2,3},{3,2},{4,5},{5,4},{6,7},{7,6},{8,9},{9,8},{10,11... | collective-permute-start | bytes 786440 | tf_op jit(solution)/shard_map/ppermute | solution.py:597
  86.9 5.0 %late_terms.1 = (f32[96,8,128,128]{3,2,1,0:T(8,128)}, f32[1,128,1024]{2,1,0:T(8,128)}) custom-call(s32[21]{0:T(128)S(1)} %concatenate.6.refs_0_.where_ref, bf16[1024,128]{1,0:T(8,128)(2,1)S(1)} %collective-permute-done.2.refs_1_, bf16[1024,128]{1,0:T(8,128)(2,1)S(1)} %collective-permute-done.10.refs_2_, ...), custom_call_target="tpu_custom_call", output_to_operand_aliasing={{0}: (18, {})} | custom-call | flops 100000000 | bytes 1048576 | tf_op jit(solution)/shard_map/late_terms/pallas_call | solution.py:232
  91.9 3.1 %collective-permute-start.20 = (f32[8,32,128]{2,1,0:T(8,128)S(1)}, f32[8,32,128]{2,1,0:T(8,128)S(1)}, u32[]{:S(2)}, u32[]{:S(2)}) collective-permute-start(f32[8,32,128]{2,1,0:T(8,128)S(1)} %get-tuple-element.100), channel_id=1, source_target_pairs={{0,7},{1,6},{2,1},{3,0},{4,3},{5,2},{6,5},{7,4},{8,15},{9,14},{10,... | collective-permute-start | bytes 393224 | tf_op jit(solution)/shard_map/ppermute | solution.py:597
  95.9 5.0 %most_outputs.1 = (f32[8,128,1024]{2,1,0:T(8,128)S(1)}, f32[128,1024]{1,0:T(8,128)S(1)}, f32[24,128]{1,0:T(8,128)S(1)}) custom-call(s32[21]{0:T(128)S(1)} %concatenate.6.refs_0_.where_ref, f32[32,40,128]{2,1,0:T(8,128)S(1)} %all-to-all-done.1.back_ref, f32[96,8,128,128]{3,2,1,0:T(8,128)} %get-tuple-element.93.store_hbm), custom_call_target="tpu_custom_call" | custom-call | flops 5000000000 | bytes 1048576 | tf_op jit(solution)/shard_map/most_outputs/pallas_call | solution.py:484
  100.9 3.2 %collective-permute-done.21.before_ref = f32[8,32,128]{2,1,0:T(8,128)S(1)} collective-permute-done((f32[8,32,128]{2,1,0:T(8,128)S(1)}, f32[8,32,128]{2,1,0:T(8,128)S(1)}, u32[]{:S(2)}, u32[]{:S(2)}) %collective-permute-start.21) | collective-permute-done | bytes 131104 | tf_op jit(solution)/shard_map/ppermute | solution.py:597
  104.1 3.1 %last_outputs.1 = (f32[1,8,128,1024]{3,2,1,0:T(8,128)}, f32[1,128,1024]{2,1,0:T(8,128)}) custom-call(s32[21]{0:T(128)S(1)} %concatenate.6.refs_0_.where_ref, f32[8,128,1024]{2,1,0:T(8,128)S(1)} %get-tuple-element.94.most_ref, f32[128,1024]{1,0:T(8,128)S(1)} %get-tuple-element.95.most_seg_ref, f32[24,128]{1,0:T(8,128)S(1)} %get-tuple-element.96.coef_ref, ...), custom_call_target="tpu_custom_call" | custom-call | flops 3000000000 | bytes 1048576 | tf_op jit(solution)/shard_map/last_outputs/pallas_call | solution.py:502
  (47 shorter events, 18.5 us)
Async XLA Ops:
  0.6 10.3 %collective-permute-start.3 = (bf16[2048,128]{1,0:T(8,128)(2,1)}, bf16[2048,128]{1,0:T(8,128)(2,1)S(1)}, u32[]{:S(2)}, u32[]{:S(2)}) collective-permute-start(bf16[2048,128]{1,0:T(8,128)(2,1)} %refs_1_.1), channel_id=1, source_target_pairs={{0,1},{1,0},{2,3},{3,2},{4,5},{5,4},{6,7},{7,6},{8,9},{9,8},{10,11... | collective-permute-start | bytes 1572872 | tf_op jit(solution)/shard_map/ppermute | solution.py:597
  4.0 14.9 %collective-permute-start = (bf16[2048,128]{1,0:T(8,128)(2,1)}, bf16[2048,128]{1,0:T(8,128)(2,1)S(1)}, u32[]{:S(2)}, u32[]{:S(2)}) collective-permute-start(bf16[2048,128]{1,0:T(8,128)(2,1)} %refs_1_.1), channel_id=1, source_target_pairs={{0,2},{1,3},{2,4},{3,5},{4,6},{5,7},{6,0},{7,1},{8,10},{9,11},{10,... | collective-permute-start | bytes 1572872 | tf_op jit(solution)/shard_map/ppermute | solution.py:597
  4.0 14.9 %collective-permute-start.1 = (bf16[2048,128]{1,0:T(8,128)(2,1)}, bf16[2048,128]{1,0:T(8,128)(2,1)S(1)}, u32[]{:S(2)}, u32[]{:S(2)}) collective-permute-start(bf16[2048,128]{1,0:T(8,128)(2,1)} %refs_1_.1), channel_id=1, source_target_pairs={{0,6},{1,7},{2,0},{3,1},{4,2},{5,3},{6,4},{7,5},{8,14},{9,15},{10,... | collective-permute-start | bytes 1572872 | tf_op jit(solution)/shard_map/ppermute | solution.py:597
  7.7 10.3 %collective-permute-start.2 = (bf16[1024,128]{1,0:T(8,128)(2,1)S(1)}, bf16[1024,128]{1,0:T(8,128)(2,1)S(1)}, u32[]{:S(2)}, u32[]{:S(2)}) collective-permute-start(bf16[1024,128]{1,0:T(8,128)(2,1)S(1)} %slice.18), channel_id=1, source_target_pairs={{0,8},{8,16},{16,24},{24,32},{32,40},{40,48},{48,56},{56,64},{64,7... | collective-permute-start | bytes 786440 | tf_op jit(solution)/shard_map/ppermute | solution.py:621
  18.9 3.8 %collective-permute-start.7 = (bf16[2048,128]{1,0:T(8,128)(2,1)S(1)}, bf16[2048,128]{1,0:T(8,128)(2,1)S(1)}, u32[]{:S(2)}, u32[]{:S(2)}) collective-permute-start(bf16[2048,128]{1,0:T(8,128)(2,1)S(1)} %collective-permute-done.refs_2_), channel_id=1, source_target_pairs={{0,1},{1,0},{2,3},{3,2},{4,5},{5,4},{6,7},{7,6},{8,9},{9,8},{10,11... | collective-permute-start | bytes 1572872 | tf_op jit(solution)/shard_map/ppermute | solution.py:597
  19.7 6.7 %collective-permute-start.6 = (bf16[2048,128]{1,0:T(8,128)(2,1)S(1)}, bf16[2048,128]{1,0:T(8,128)(2,1)S(1)}, u32[]{:S(2)}, u32[]{:S(2)}) collective-permute-start(bf16[2048,128]{1,0:T(8,128)(2,1)S(1)} %collective-permute-done.1.refs_1_), channel_id=1, source_target_pairs={{0,1},{1,0},{2,3},{3,2},{4,5},{5,4},{6,7},{7,6},{8,9},{9,8},{10,11... | collective-permute-start | bytes 1572872 | tf_op jit(solution)/shard_map/ppermute | solution.py:597
  19.8 10.6 %collective-permute-start.4 = (bf16[1024,128]{1,0:T(8,128)(2,1)S(1)}, bf16[1024,128]{1,0:T(8,128)(2,1)S(1)}, u32[]{:S(2)}, u32[]{:S(2)}) collective-permute-start(bf16[1024,128]{1,0:T(8,128)(2,1)S(1)} %slice.19), channel_id=1, source_target_pairs={{0,2},{1,3},{2,4},{3,5},{4,6},{5,7},{6,0},{7,1},{8,10},{9,11},{10,... | collective-permute-start | bytes 786440 | tf_op jit(solution)/shard_map/ppermute | solution.py:597
  19.9 10.5 %collective-permute-start.5 = (bf16[1024,128]{1,0:T(8,128)(2,1)S(1)}, bf16[1024,128]{1,0:T(8,128)(2,1)S(1)}, u32[]{:S(2)}, u32[]{:S(2)}) collective-permute-start(bf16[1024,128]{1,0:T(8,128)(2,1)S(1)} %slice.20), channel_id=1, source_target_pairs={{0,6},{1,7},{2,0},{3,1},{4,2},{5,3},{6,4},{7,5},{8,14},{9,15},{10,... | collective-permute-start | bytes 786440 | tf_op jit(solution)/shard_map/ppermute | solution.py:597
  30.4 2.6 %collective-permute-start.8 = (bf16[2048,128]{1,0:T(8,128)(2,1)S(1)}, bf16[2048,128]{1,0:T(8,128)(2,1)S(1)}, u32[]{:S(2)}, u32[]{:S(2)}) collective-permute-start(bf16[2048,128]{1,0:T(8,128)(2,1)S(1)} %constant_dynamic-update-slice_fusion.refs_1_), channel_id=1, source_target_pairs={{0,1},{1,0},{2,3},{3,2},{4,5},{5,4},{6,7},{7,6},{8,9},{9,8},{10,11... | collective-permute-start | bytes 1572872 | tf_op jit(solution)/shard_map/ppermute | solution.py:597
  35.6 21.3 %all-to-all-start = ((f32[32,24,128]{2,1,0:T(8,128)}), f32[32,24,128]{2,1,0:T(8,128)S(1)}, u32[]{:S(2)}, u32[]{:S(2)}) async-start(f32[32,24,128]{2,1,0:T(8,128)} %get-tuple-element.72), calls=%async_computation | async-start | bytes 786432 | tf_op jit(solution)/shard_map/all_to_all | solution.py:601
  45.1 7.5 %collective-permute-start.9 = (bf16[1024,128]{1,0:T(8,128)(2,1)S(1)}, bf16[1024,128]{1,0:T(8,128)(2,1)S(1)}, u32[]{:S(2)}, u32[]{:S(2)}) collective-permute-start(bf16[1024,128]{1,0:T(8,128)(2,1)S(1)} %collective-permute-done.2.refs_1_), channel_id=1, source_target_pairs={{0,6},{1,7},{2,0},{3,1},{4,2},{5,3},{6,4},{7,5},{8,14},{9,15},{10,... | collective-permute-start | bytes 786440 | tf_op jit(solution)/shard_map/ppermute | solution.py:597
  57.9 34.0 %all-to-all-start.1 = ((f32[32,40,128]{2,1,0:T(8,128)}), f32[32,40,128]{2,1,0:T(8,128)S(1)}, u32[]{:S(2)}, u32[]{:S(2)}) async-start(f32[32,40,128]{2,1,0:T(8,128)} %get-tuple-element.80), calls=%async_computation.1 | async-start | bytes 1310720 | tf_op jit(solution)/shard_map/all_to_all | solution.py:601
  65.5 7.9 %collective-permute-start.11 = (bf16[1024,128]{1,0:T(8,128)(2,1)S(1)}, bf16[1024,128]{1,0:T(8,128)(2,1)S(1)}, u32[]{:S(2)}, u32[]{:S(2)}) collective-permute-start(bf16[1024,128]{1,0:T(8,128)(2,1)S(1)} %collective-permute-done.2.refs_1_), channel_id=1, source_target_pairs={{0,2},{1,3},{2,4},{3,5},{4,6},{5,7},{6,0},{7,1},{8,10},{9,11},{10,... | collective-permute-start | bytes 786440 | tf_op jit(solution)/shard_map/ppermute | solution.py:597
  65.6 13.3 %collective-permute-start.13 = (bf16[1024,128]{1,0:T(8,128)(2,1)S(1)}, bf16[1024,128]{1,0:T(8,128)(2,1)S(1)}, u32[]{:S(2)}, u32[]{:S(2)}) collective-permute-start(bf16[1024,128]{1,0:T(8,128)(2,1)S(1)} %collective-permute-done.2.refs_1_), channel_id=1, source_target_pairs={{0,4},{1,5},{2,6},{3,7},{4,0},{5,1},{6,2},{7,3},{8,12},{9,13},{10,... | collective-permute-start | bytes 786440 | tf_op jit(solution)/shard_map/ppermute | solution.py:597
  68.2 12.9 %collective-permute-start.10 = (bf16[1024,128]{1,0:T(8,128)(2,1)S(1)}, bf16[1024,128]{1,0:T(8,128)(2,1)S(1)}, u32[]{:S(2)}, u32[]{:S(2)}) collective-permute-start(bf16[1024,128]{1,0:T(8,128)(2,1)S(1)} %collective-permute-done.2.refs_1_), channel_id=1, source_target_pairs={{0,1},{1,0},{2,3},{3,2},{4,5},{5,4},{6,7},{7,6},{8,9},{9,8},{10,11... | collective-permute-start | bytes 786440 | tf_op jit(solution)/shard_map/ppermute | solution.py:597
  73.3 9.2 %collective-permute-start.12 = (bf16[1024,128]{1,0:T(8,128)(2,1)S(1)}, bf16[1024,128]{1,0:T(8,128)(2,1)S(1)}, u32[]{:S(2)}, u32[]{:S(2)}) collective-permute-start(bf16[1024,128]{1,0:T(8,128)(2,1)S(1)} %collective-permute-done.11.refs_8_), channel_id=1, source_target_pairs={{0,1},{1,0},{2,3},{3,2},{4,5},{5,4},{6,7},{7,6},{8,9},{9,8},{10,11... | collective-permute-start | bytes 786440 | tf_op jit(solution)/shard_map/ppermute | solution.py:597
  78.9 4.0 %collective-permute-start.14 = (bf16[1024,128]{1,0:T(8,128)(2,1)S(1)}, bf16[1024,128]{1,0:T(8,128)(2,1)S(1)}, u32[]{:S(2)}, u32[]{:S(2)}) collective-permute-start(bf16[1024,128]{1,0:T(8,128)(2,1)S(1)} %collective-permute-done.13.refs_5_), channel_id=1, source_target_pairs={{0,1},{1,0},{2,3},{3,2},{4,5},{5,4},{6,7},{7,6},{8,9},{9,8},{10,11... | collective-permute-start | bytes 786440 | tf_op jit(solution)/shard_map/ppermute | solution.py:597
  81.1 5.8 %collective-permute-start.15 = (bf16[1024,128]{1,0:T(8,128)(2,1)S(1)}, bf16[1024,128]{1,0:T(8,128)(2,1)S(1)}, u32[]{:S(2)}, u32[]{:S(2)}) collective-permute-start(bf16[1024,128]{1,0:T(8,128)(2,1)S(1)} %collective-permute-done.9.refs_3_), channel_id=1, source_target_pairs={{0,1},{1,0},{2,3},{3,2},{4,5},{5,4},{6,7},{7,6},{8,9},{9,8},{10,11... | collective-permute-start | bytes 786440 | tf_op jit(solution)/shard_map/ppermute | solution.py:597
  81.1 3.1 %collective-permute-start.16 = (f32[2,32,128]{2,1,0:T(8,128)S(1)}, f32[2,32,128]{2,1,0:T(8,128)S(1)}, u32[]{:S(2)}, u32[]{:S(2)}) collective-permute-start(f32[2,32,128]{2,1,0:T(8,128)S(1)} %get-tuple-element.86.refs_13_), channel_id=1, source_target_pairs={{0,6},{1,7},{2,0},{3,1},{4,2},{5,3},{6,4},{7,5},{8,14},{9,15},{10,... | collective-permute-start | bytes 98312 | tf_op jit(solution)/shard_map/ppermute | solution.py:597
  81.1 4.3 %collective-permute-start.17 = (f32[2,32,128]{2,1,0:T(8,128)S(1)}, f32[2,32,128]{2,1,0:T(8,128)S(1)}, u32[]{:S(2)}, u32[]{:S(2)}) collective-permute-start(f32[2,32,128]{2,1,0:T(8,128)S(1)} %get-tuple-element.86.refs_13_), channel_id=1, source_target_pairs={{0,2},{1,3},{2,4},{3,5},{4,6},{5,7},{6,0},{7,1},{8,10},{9,11},{10,... | collective-permute-start | bytes 98312 | tf_op jit(solution)/shard_map/ppermute | solution.py:597
  82.6 4.3 %collective-permute-start.18 = (f32[2,32,128]{2,1,0:T(8,128)S(1)}, f32[2,32,128]{2,1,0:T(8,128)S(1)}, u32[]{:S(2)}, u32[]{:S(2)}) collective-permute-start(f32[2,32,128]{2,1,0:T(8,128)S(1)} %get-tuple-element.86.refs_13_), channel_id=1, source_target_pairs={{0,4},{1,5},{2,6},{3,7},{4,0},{5,1},{6,2},{7,3},{8,12},{9,13},{10,... | collective-permute-start | bytes 98312 | tf_op jit(solution)/shard_map/ppermute | solution.py:597
  91.9 9.0 %collective-permute-start.20 = (f32[8,32,128]{2,1,0:T(8,128)S(1)}, f32[8,32,128]{2,1,0:T(8,128)S(1)}, u32[]{:S(2)}, u32[]{:S(2)}) collective-permute-start(f32[8,32,128]{2,1,0:T(8,128)S(1)} %get-tuple-element.100), channel_id=1, source_target_pairs={{0,7},{1,6},{2,1},{3,0},{4,3},{5,2},{6,5},{7,4},{8,15},{9,14},{10,... | collective-permute-start | bytes 393224 | tf_op jit(solution)/shard_map/ppermute | solution.py:597
  95.0 9.0 %collective-permute-start.21 = (f32[8,32,128]{2,1,0:T(8,128)S(1)}, f32[8,32,128]{2,1,0:T(8,128)S(1)}, u32[]{:S(2)}, u32[]{:S(2)}) collective-permute-start(f32[8,32,128]{2,1,0:T(8,128)S(1)} %get-tuple-element.99), channel_id=1, source_target_pairs={{0,2},{1,3},{2,4},{3,5},{4,6},{5,7},{6,0},{7,1},{8,10},{9,11},{10,... | collective-permute-start | bytes 393224 | tf_op jit(solution)/shard_map/ppermute | solution.py:597
  95.6 8.5 %collective-permute-start.19 = (f32[32,8,128]{2,1,0:T(8,128)S(1)}, f32[32,8,128]{2,1,0:T(8,128)S(1)}, u32[]{:S(2)}, u32[]{:S(2)}) collective-permute-start(f32[32,8,128]{2,1,0:T(8,128)S(1)} %slice.21), channel_id=1, source_target_pairs={{0,4},{1,5},{2,6},{3,7},{4,1},{5,0},{6,3},{7,2},{8,12},{9,13},{10,... | collective-permute-start | bytes 393224 | tf_op jit(solution)/shard_map/ppermute | solution.py:597
  (3 other events, 2.9 us)

commit v11 on v7

--- a/solution.py
+++ b/solution.py
@@ -695,7 +695,9 @@
     prior_ahead = to_chan(prior, lambda s: s - 2)
     prior_behind = to_chan(prior, lambda s: s + 2)
     prior_far = to_chan(prior, lambda s: s + 4)
-    arrived, prior_ahead, sums = lax.optimization_barrier((arrived, prior_ahead, sums))
+    arrived, prior_ahead, prior_behind, prior_far, sums = lax.optimization_barrier(
+        (arrived, prior_ahead, prior_behind, prior_far, sums)
+    )
     scanned, own_means, flags = call(
         scan_kernel,
         "scan_pieces",

time: 103 us -> 106 us (1.029)
  starting transfers between devices: 41 us -> 49 us
  waiting for transfers between devices: 23.5 us -> 19.1 us
  local copies, waits for them, and re-layouts: 4.73 us -> 2.9 us
    ppermute x21, starting transfers between devices: 22.1 us -> 28.4 us  [to_chan(): lax.ppermute(value, 'chan', [(s, target(s) % count) for s in range(count)])]
    all_to_all x2, waiting for transfers between devices: 4.33 us -> 0.01 us  [exchange(): return lax.all_to_all(value, 'tm', 0, 0, tiled=True)]
    unnamed x7 -> x3, local copies, waits for them, and re-layouts: 2.89 us -> 1.06 us
    all_to_all x2, starting transfers between devices: 17.1 us -> 18.7 us  [exchange(): return lax.all_to_all(value, 'tm', 0, 0, tiled=True)]
where the time goes in v11:
time: 106 us; the launch traced here: 105 us
  starting transfers between devices  49 us (46%)
  Pallas kernels  32.5 us (31%)
  waiting for transfers between devices  19.1 us (18%)
  local copies, waits for them, and re-layouts  2.9 us (3%)
  between operations  1.77 us (2%)
    ppermute x21, starting transfers between devices, to_chan(): lax.ppermute(value, 'chan', [(s, target(s) % count) for s in range(count)])  28.4 us
    pallas_call x7, Pallas kernels, call(): pl.pallas_call(body, out_shape=[STORE] * first + outputs, grid=(1,), in_s...  24.4 us
    ppermute x21, waiting for transfers between devices, to_chan(): lax.ppermute(value, 'chan', [(s, target(s) % count) for s in range(count)])  19.1 us
    all_to_all x2, starting transfers between devices, exchange(): return lax.all_to_all(value, 'tm', 0, 0, tiled=True)  18.7 us
    pallas_call x1, Pallas kernels, most_outputs(): pl.pallas_call(most_kernel, out_shape=MOST, grid=(1,), in_specs=[SM, whol...  5 us
    pallas_call x1, Pallas kernels, last_outputs(): pl.pallas_call(last_kernel, out_shape=OUTPUTS, grid=(1,), in_specs=[SM] +...  3.12 us
  transfers between devices with their start and end apart: 24, of which 12 were waited for; matrix products, arithmetic and copies ran while one was open for 2% of the time, Pallas kernels for 25%

profile of v11, /device:TPU:1, one launch (start us, length us, event | category | flops | bytes accessed | tf_op | source)
XLA Modules:
  0.0 105.3 jit_solution(5304082399614432808)
XLA Ops:
  0.6 3.3 %collective-permute-start.3 = (bf16[2048,128]{1,0:T(8,128)(2,1)}, bf16[2048,128]{1,0:T(8,128)(2,1)S(1)}, u32[]{:S(2)}, u32[]{:S(2)}) collective-permute-start(bf16[2048,128]{1,0:T(8,128)(2,1)} %refs_1_.1), channel_id=1, source_target_pairs={{0,1},{1,0},{2,3},{3,2},{4,5},{5,4},{6,7},{7,6},{8,9},{9,8},{10,11... | collective-permute-start | bytes 1572872 | tf_op jit(solution)/shard_map/ppermute | solution.py:597
  4.0 2.7 %collective-permute-start.1 = (bf16[2048,128]{1,0:T(8,128)(2,1)}, bf16[2048,128]{1,0:T(8,128)(2,1)S(1)}, u32[]{:S(2)}, u32[]{:S(2)}) collective-permute-start(bf16[2048,128]{1,0:T(8,128)(2,1)} %refs_1_.1), channel_id=1, source_target_pairs={{0,6},{1,7},{2,0},{3,1},{4,2},{5,3},{6,4},{7,5},{8,14},{9,15},{10,... | collective-permute-start | bytes 1572872 | tf_op jit(solution)/shard_map/ppermute | solution.py:597
  7.7 1.8 %collective-permute-start.2 = (bf16[1024,128]{1,0:T(8,128)(2,1)S(1)}, bf16[1024,128]{1,0:T(8,128)(2,1)S(1)}, u32[]{:S(2)}, u32[]{:S(2)}) collective-permute-start(bf16[1024,128]{1,0:T(8,128)(2,1)S(1)} %slice.18), channel_id=1, source_target_pairs={{0,8},{8,16},{16,24},{24,32},{32,40},{40,48},{48,56},{56,64},{64,7... | collective-permute-start | bytes 786440 | tf_op jit(solution)/shard_map/ppermute | solution.py:621
  12.0 4.1 %first_pair.1 = (f32[96,8,128,128]{3,2,1,0:T(8,128)}, f32[4,8,256]{2,1,0:T(8,128)S(1)}, f32[4,128,256]{2,1,0:T(8,128)S(1)}, f32[4,8,256]{2,1,0:T(8,128)S(1)}, bf...) custom-call(s32[21]{0:T(128)S(1)} %concatenate.6.refs_0_.where_ref, ...), custom_call_target="tpu_custom_call" | custom-call | flops 3000000000 | bytes 1048576 | tf_op jit(solution)/shard_map/first_pair/pallas_call | solution.py:232
  16.1 2.8 %collective-permute-done.refs_2_ = bf16[2048,128]{1,0:T(8,128)(2,1)S(1)} collective-permute-done((bf16[2048,128]{1,0:T(8,128)(2,1)}, bf16[2048,128]{1,0:T(8,128)(2,1)S(1)}, u32[]{:S(2)}, u32[]{:S(2)}) %collective-permute-start) | collective-permute-done | bytes 524320 | tf_op jit(solution)/shard_map/ppermute | solution.py:597
  19.9 2.8 %collective-permute-start.5 = (bf16[1024,128]{1,0:T(8,128)(2,1)S(1)}, bf16[1024,128]{1,0:T(8,128)(2,1)S(1)}, u32[]{:S(2)}, u32[]{:S(2)}) collective-permute-start(bf16[1024,128]{1,0:T(8,128)(2,1)S(1)} %slice.20), channel_id=1, source_target_pairs={{0,6},{1,7},{2,0},{3,1},{4,2},{5,3},{6,4},{7,5},{8,14},{9,15},{10,... | collective-permute-start | bytes 786440 | tf_op jit(solution)/shard_map/ppermute | solution.py:597
  22.6 3.8 %near_pair.1 = (f32[96,8,128,128]{3,2,1,0:T(8,128)}, f32[4,8,256]{2,1,0:T(8,128)S(1)}, f32[4,128,256]{2,1,0:T(8,128)S(1)}, f32[4,8,256]{2,1,0:T(8,128)S(1)}, f32[128,256]{1,0:T(8,128)S(1)}) custom-call(s32[21]{0:T(128)S(1)} %concatenate.6.refs_0_.where_ref, ...), custom_call_target="tpu_custom_call", output_to_operand_aliasing={{0}: (5, {}), {1}: (6, {}), {2}: (7, {}), {3}: (8, {})} | custom-call | flops 3000000000 | bytes 1048576 | tf_op jit(solution)/shard_map/near_pair/pallas_call | solution.py:232
  26.5 3.8 %side_pair.1 = (f32[96,8,128,128]{3,2,1,0:T(8,128)}, f32[4,8,256]{2,1,0:T(8,128)S(1)}, f32[4,128,256]{2,1,0:T(8,128)S(1)}, f32[4,8,256]{2,1,0:T(8,128)S(1)}) custom-call(s32[21]{0:T(128)S(1)} %concatenate.6.refs_0_.where_ref, ...), custom_call_target="tpu_custom_call", output_to_operand_aliasing={{0}: (4, {}), {1}: (5, {}), {2}: (6, {}), {3}: (7, {})} | custom-call | flops 2000000000 | bytes 1048576 | tf_op jit(solution)/shard_map/side_pair/pallas_call | solution.py:232
  31.5 1.5 %collective-permute-done.8.refs_2_ = bf16[2048,128]{1,0:T(8,128)(2,1)S(1)} collective-permute-done((bf16[2048,128]{1,0:T(8,128)(2,1)S(1)}, bf16[2048,128]{1,0:T(8,128)(2,1)S(1)}, u32[]{:S(2)}, u32[]{:S(2)}) %collective-permute-start.8) | collective-permute-done | bytes 524320 | tf_op jit(solution)/shard_map/ppermute | solution.py:597
  33.0 2.5 %far_pair.1 = (f32[4,128,256]{2,1,0:T(8,128)S(1)}, f32[4,8,256]{2,1,0:T(8,128)S(1)}, f32[32,24,128]{2,1,0:T(8,128)}) custom-call(s32[21]{0:T(128)S(1)} %concatenate.6.refs_0_.where_ref, bf16[2048,128]{1,0:T(8,128)(2,1)S(1)} %constant_dynamic-update-slice_fusion.refs_1_, ...), custom_call_target="tpu_custom_call", output_to_operand_aliasing={{0}: (8, {}), {1}: (9, {})} | custom-call | flops 100000000 | bytes 1048576 | tf_op jit(solution)/shard_map/far_pair/pallas_call | solution.py:232
  35.6 9.5 %all-to-all-start = ((f32[32,24,128]{2,1,0:T(8,128)}), f32[32,24,128]{2,1,0:T(8,128)S(1)}, u32[]{:S(2)}, u32[]{:S(2)}) async-start(f32[32,24,128]{2,1,0:T(8,128)} %get-tuple-element.82), calls=%async_computation | async-start | bytes 786432 | tf_op jit(solution)/shard_map/all_to_all | solution.py:601
  45.3 2.6 %collective-permute-start.11 = (bf16[1024,128]{1,0:T(8,128)(2,1)S(1)}, bf16[1024,128]{1,0:T(8,128)(2,1)S(1)}, u32[]{:S(2)}, u32[]{:S(2)}) collective-permute-start(bf16[1024,128]{1,0:T(8,128)(2,1)S(1)} %collective-permute-done.2.refs_1_), channel_id=1, source_target_pairs={{0,4},{1,5},{2,6},{3,7},{4,0},{5,1},{6,2},{7,3},{8,12},{9,13},{10,... | collective-permute-start | bytes 786440 | tf_op jit(solution)/shard_map/ppermute | solution.py:597
  48.6 3.7 %rest_left.1 = (f32[96,8,128,128]{3,2,1,0:T(8,128)}, f32[4,8,256]{2,1,0:T(8,128)S(1)}) custom-call(s32[21]{0:T(128)S(1)} %concatenate.6.refs_0_.where_ref, bf16[2048,128]{1,0:T(8,128)(2,1)S(1)} %constant_dynamic-update-slice_fusion.refs_1_, bf16[2048,128]{1,0:T(8,128)(2,1)S(1)} %collective-permute-done.8.refs_2_, ...), custom_call_target="tpu_custom_call", output_to_operand_aliasing={{0}: (4, {}), {1}: (5, {})} | custom-call | flops 4000000000 | bytes 1048576 | tf_op jit(solution)/shard_map/rest_left/pallas_call | solution.py:232
  52.3 1.4 %collective-permute-done.10.refs_8_ = bf16[1024,128]{1,0:T(8,128)(2,1)S(1)} collective-permute-done((bf16[1024,128]{1,0:T(8,128)(2,1)S(1)}, bf16[1024,128]{1,0:T(8,128)(2,1)S(1)}, u32[]{:S(2)}, u32[]{:S(2)}) %collective-permute-start.10) | collective-permute-done | bytes 262176 | tf_op jit(solution)/shard_map/ppermute | solution.py:597
  53.7 5.6 %collective-permute-done.11.refs_5_ = bf16[1024,128]{1,0:T(8,128)(2,1)S(1)} collective-permute-done((bf16[1024,128]{1,0:T(8,128)(2,1)S(1)}, bf16[1024,128]{1,0:T(8,128)(2,1)S(1)}, u32[]{:S(2)}, u32[]{:S(2)}) %collective-permute-start.11) | collective-permute-done | bytes 262176 | tf_op jit(solution)/shard_map/ppermute | solution.py:597
  60.9 9.2 %all-to-all-start.1 = ((f32[32,40,128]{2,1,0:T(8,128)}), f32[32,40,128]{2,1,0:T(8,128)S(1)}, u32[]{:S(2)}, u32[]{:S(2)}) async-start(f32[32,40,128]{2,1,0:T(8,128)} %get-tuple-element.90), calls=%async_computation.1 | async-start | bytes 1310720 | tf_op jit(solution)/shard_map/all_to_all | solution.py:601
  70.2 3.6 %collective-permute-start.12 = (f32[2,32,128]{2,1,0:T(8,128)S(1)}, f32[2,32,128]{2,1,0:T(8,128)S(1)}, u32[]{:S(2)}, u32[]{:S(2)}) collective-permute-start(f32[2,32,128]{2,1,0:T(8,128)S(1)} %get-tuple-element.103.refs_13_), channel_id=1, source_target_pairs={{0,6},{1,7},{2,0},{3,1},{4,2},{5,3},{6,4},{7,5},{8,14},{9,15},{10,... | collective-permute-start | bytes 98312 | tf_op jit(solution)/shard_map/ppermute | solution.py:597
  75.1 3.0 %collective-permute-done.13.refs_15_ = f32[2,32,128]{2,1,0:T(8,128)S(1)} collective-permute-done((f32[2,32,128]{2,1,0:T(8,128)S(1)}, f32[2,32,128]{2,1,0:T(8,128)S(1)}, u32[]{:S(2)}, u32[]{:S(2)}) %collective-permute-start.13) | collective-permute-done | bytes 32800 | tf_op jit(solution)/shard_map/ppermute | solution.py:597
  78.2 2.1 %collective-permute-start.15 = (bf16[1024,128]{1,0:T(8,128)(2,1)S(1)}, bf16[1024,128]{1,0:T(8,128)(2,1)S(1)}, u32[]{:S(2)}, u32[]{:S(2)}) collective-permute-start(bf16[1024,128]{1,0:T(8,128)(2,1)S(1)} %collective-permute-done.2.refs_1_), channel_id=1, source_target_pairs={{0,1},{1,0},{2,3},{3,2},{4,5},{5,4},{6,7},{7,6},{8,9},{9,8},{10,11... | collective-permute-start | bytes 786440 | tf_op jit(solution)/shard_map/ppermute | solution.py:597
  82.8 5.4 %late_terms.1 = (f32[96,8,128,128]{3,2,1,0:T(8,128)}, f32[1,128,1024]{2,1,0:T(8,128)}) custom-call(s32[21]{0:T(128)S(1)} %concatenate.6.refs_0_.where_ref, bf16[1024,128]{1,0:T(8,128)(2,1)S(1)} %collective-permute-done.2.refs_1_, bf16[1024,128]{1,0:T(8,128)(2,1)S(1)} %collective-permute-done.15.refs_2_, ...), custom_call_target="tpu_custom_call", output_to_operand_aliasing={{0}: (18, {})} | custom-call | flops 100000000 | bytes 1048576 | tf_op jit(solution)/shard_map/late_terms/pallas_call | solution.py:232
  88.3 6.5 %collective-permute-start.20 = (f32[8,32,128]{2,1,0:T(8,128)S(1)}, f32[8,32,128]{2,1,0:T(8,128)S(1)}, u32[]{:S(2)}, u32[]{:S(2)}) collective-permute-start(f32[8,32,128]{2,1,0:T(8,128)S(1)} %get-tuple-element.120), channel_id=1, source_target_pairs={{0,7},{1,6},{2,1},{3,0},{4,3},{5,2},{6,5},{7,4},{8,15},{9,14},{10,... | collective-permute-start | bytes 393224 | tf_op jit(solution)/shard_map/ppermute | solution.py:597
  94.8 5.0 %most_outputs.1 = (f32[8,128,1024]{2,1,0:T(8,128)S(1)}, f32[128,1024]{1,0:T(8,128)S(1)}, f32[24,128]{1,0:T(8,128)S(1)}) custom-call(s32[21]{0:T(128)S(1)} %concatenate.6.refs_0_.where_ref, f32[32,40,128]{2,1,0:T(8,128)S(1)} %all-to-all-done.1.back_ref, f32[96,8,128,128]{3,2,1,0:T(8,128)} %get-tuple-element.113.store_hbm), custom_call_target="tpu_custom_call" | custom-call | flops 5000000000 | bytes 1048576 | tf_op jit(solution)/shard_map/most_outputs/pallas_call | solution.py:484
  99.8 2.1 %collective-permute-done.21.before_ref = f32[8,32,128]{2,1,0:T(8,128)S(1)} collective-permute-done((f32[8,32,128]{2,1,0:T(8,128)S(1)}, f32[8,32,128]{2,1,0:T(8,128)S(1)}, u32[]{:S(2)}, u32[]{:S(2)}) %collective-permute-start.21) | collective-permute-done | bytes 131104 | tf_op jit(solution)/shard_map/ppermute | solution.py:597
  102.0 3.1 %last_outputs.1 = (f32[1,8,128,1024]{3,2,1,0:T(8,128)}, f32[1,128,1024]{2,1,0:T(8,128)}) custom-call(s32[21]{0:T(128)S(1)} %concatenate.6.refs_0_.where_ref, f32[8,128,1024]{2,1,0:T(8,128)S(1)} %get-tuple-element.114.most_ref, f32[128,1024]{1,0:T(8,128)S(1)} %get-tuple-element.115.most_seg_ref, f32[24,128]{1,0:T(8,128)S(1)} %get-tuple-element.116.coef_ref, ...), custom_call_target="tpu_custom_call" | custom-call | flops 3000000000 | bytes 1048576 | tf_op jit(solution)/shard_map/last_outputs/pallas_call | solution.py:502
  (43 shorter events, 11.4 us)
Async XLA Ops:
  0.6 10.3 %collective-permute-start.3 = (bf16[2048,128]{1,0:T(8,128)(2,1)}, bf16[2048,128]{1,0:T(8,128)(2,1)S(1)}, u32[]{:S(2)}, u32[]{:S(2)}) collective-permute-start(bf16[2048,128]{1,0:T(8,128)(2,1)} %refs_1_.1), channel_id=1, source_target_pairs={{0,1},{1,0},{2,3},{3,2},{4,5},{5,4},{6,7},{7,6},{8,9},{9,8},{10,11... | collective-permute-start | bytes 1572872 | tf_op jit(solution)/shard_map/ppermute | solution.py:597
  4.0 14.9 %collective-permute-start = (bf16[2048,128]{1,0:T(8,128)(2,1)}, bf16[2048,128]{1,0:T(8,128)(2,1)S(1)}, u32[]{:S(2)}, u32[]{:S(2)}) collective-permute-start(bf16[2048,128]{1,0:T(8,128)(2,1)} %refs_1_.1), channel_id=1, source_target_pairs={{0,2},{1,3},{2,4},{3,5},{4,6},{5,7},{6,0},{7,1},{8,10},{9,11},{10,... | collective-permute-start | bytes 1572872 | tf_op jit(solution)/shard_map/ppermute | solution.py:597
  4.0 14.9 %collective-permute-start.1 = (bf16[2048,128]{1,0:T(8,128)(2,1)}, bf16[2048,128]{1,0:T(8,128)(2,1)S(1)}, u32[]{:S(2)}, u32[]{:S(2)}) collective-permute-start(bf16[2048,128]{1,0:T(8,128)(2,1)} %refs_1_.1), channel_id=1, source_target_pairs={{0,6},{1,7},{2,0},{3,1},{4,2},{5,3},{6,4},{7,5},{8,14},{9,15},{10,... | collective-permute-start | bytes 1572872 | tf_op jit(solution)/shard_map/ppermute | solution.py:597
  7.7 8.4 %collective-permute-start.2 = (bf16[1024,128]{1,0:T(8,128)(2,1)S(1)}, bf16[1024,128]{1,0:T(8,128)(2,1)S(1)}, u32[]{:S(2)}, u32[]{:S(2)}) collective-permute-start(bf16[1024,128]{1,0:T(8,128)(2,1)S(1)} %slice.18), channel_id=1, source_target_pairs={{0,8},{8,16},{16,24},{24,32},{32,40},{40,48},{48,56},{56,64},{64,7... | collective-permute-start | bytes 786440 | tf_op jit(solution)/shard_map/ppermute | solution.py:621
  18.9 3.8 %collective-permute-start.7 = (bf16[2048,128]{1,0:T(8,128)(2,1)S(1)}, bf16[2048,128]{1,0:T(8,128)(2,1)S(1)}, u32[]{:S(2)}, u32[]{:S(2)}) collective-permute-start(bf16[2048,128]{1,0:T(8,128)(2,1)S(1)} %collective-permute-done.refs_2_), channel_id=1, source_target_pairs={{0,1},{1,0},{2,3},{3,2},{4,5},{5,4},{6,7},{7,6},{8,9},{9,8},{10,11... | collective-permute-start | bytes 1572872 | tf_op jit(solution)/shard_map/ppermute | solution.py:597
  19.7 6.7 %collective-permute-start.6 = (bf16[2048,128]{1,0:T(8,128)(2,1)S(1)}, bf16[2048,128]{1,0:T(8,128)(2,1)S(1)}, u32[]{:S(2)}, u32[]{:S(2)}) collective-permute-start(bf16[2048,128]{1,0:T(8,128)(2,1)S(1)} %collective-permute-done.1.refs_1_), channel_id=1, source_target_pairs={{0,1},{1,0},{2,3},{3,2},{4,5},{5,4},{6,7},{7,6},{8,9},{9,8},{10,11... | collective-permute-start | bytes 1572872 | tf_op jit(solution)/shard_map/ppermute | solution.py:597
  19.8 10.5 %collective-permute-start.4 = (bf16[1024,128]{1,0:T(8,128)(2,1)S(1)}, bf16[1024,128]{1,0:T(8,128)(2,1)S(1)}, u32[]{:S(2)}, u32[]{:S(2)}) collective-permute-start(bf16[1024,128]{1,0:T(8,128)(2,1)S(1)} %slice.19), channel_id=1, source_target_pairs={{0,2},{1,3},{2,4},{3,5},{4,6},{5,7},{6,0},{7,1},{8,10},{9,11},{10,... | collective-permute-start | bytes 786440 | tf_op jit(solution)/shard_map/ppermute | solution.py:597
  19.9 10.4 %collective-permute-start.5 = (bf16[1024,128]{1,0:T(8,128)(2,1)S(1)}, bf16[1024,128]{1,0:T(8,128)(2,1)S(1)}, u32[]{:S(2)}, u32[]{:S(2)}) collective-permute-start(bf16[1024,128]{1,0:T(8,128)(2,1)S(1)} %slice.20), channel_id=1, source_target_pairs={{0,6},{1,7},{2,0},{3,1},{4,2},{5,3},{6,4},{7,5},{8,14},{9,15},{10,... | collective-permute-start | bytes 786440 | tf_op jit(solution)/shard_map/ppermute | solution.py:597
  30.4 2.6 %collective-permute-start.8 = (bf16[2048,128]{1,0:T(8,128)(2,1)S(1)}, bf16[2048,128]{1,0:T(8,128)(2,1)S(1)}, u32[]{:S(2)}, u32[]{:S(2)}) collective-permute-start(bf16[2048,128]{1,0:T(8,128)(2,1)S(1)} %constant_dynamic-update-slice_fusion.refs_1_), channel_id=1, source_target_pairs={{0,1},{1,0},{2,3},{3,2},{4,5},{5,4},{6,7},{7,6},{8,9},{9,8},{10,11... | collective-permute-start | bytes 1572872 | tf_op jit(solution)/shard_map/ppermute | solution.py:597
  35.6 24.4 %all-to-all-start = ((f32[32,24,128]{2,1,0:T(8,128)}), f32[32,24,128]{2,1,0:T(8,128)S(1)}, u32[]{:S(2)}, u32[]{:S(2)}) async-start(f32[32,24,128]{2,1,0:T(8,128)} %get-tuple-element.82), calls=%async_computation | async-start | bytes 786432 | tf_op jit(solution)/shard_map/all_to_all | solution.py:601
  45.0 8.7 %collective-permute-start.10 = (bf16[1024,128]{1,0:T(8,128)(2,1)S(1)}, bf16[1024,128]{1,0:T(8,128)(2,1)S(1)}, u32[]{:S(2)}, u32[]{:S(2)}) collective-permute-start(bf16[1024,128]{1,0:T(8,128)(2,1)S(1)} %collective-permute-done.2.refs_1_), channel_id=1, source_target_pairs={{0,2},{1,3},{2,4},{3,5},{4,6},{5,7},{6,0},{7,1},{8,10},{9,11},{10,... | collective-permute-start | bytes 786440 | tf_op jit(solution)/shard_map/ppermute | solution.py:597
  45.3 14.0 %collective-permute-start.11 = (bf16[1024,128]{1,0:T(8,128)(2,1)S(1)}, bf16[1024,128]{1,0:T(8,128)(2,1)S(1)}, u32[]{:S(2)}, u32[]{:S(2)}) collective-permute-start(bf16[1024,128]{1,0:T(8,128)(2,1)S(1)} %collective-permute-done.2.refs_1_), channel_id=1, source_target_pairs={{0,4},{1,5},{2,6},{3,7},{4,0},{5,1},{6,2},{7,3},{8,12},{9,13},{10,... | collective-permute-start | bytes 786440 | tf_op jit(solution)/shard_map/ppermute | solution.py:597
  47.9 12.0 %collective-permute-start.9 = (bf16[1024,128]{1,0:T(8,128)(2,1)S(1)}, bf16[1024,128]{1,0:T(8,128)(2,1)}, u32[]{:S(2)}, u32[]{:S(2)}) collective-permute-start(bf16[1024,128]{1,0:T(8,128)(2,1)S(1)} %collective-permute-done.2.refs_1_), channel_id=1, source_target_pairs={{0,6},{1,7},{2,0},{3,1},{4,2},{5,3},{6,4},{7,5},{8,14},{9,15},{10,... | collective-permute-start | bytes 786440 | tf_op jit(solution)/shard_map/ppermute | solution.py:597
  60.9 27.3 %all-to-all-start.1 = ((f32[32,40,128]{2,1,0:T(8,128)}), f32[32,40,128]{2,1,0:T(8,128)S(1)}, u32[]{:S(2)}, u32[]{:S(2)}) async-start(f32[32,40,128]{2,1,0:T(8,128)} %get-tuple-element.90), calls=%async_computation.1 | async-start | bytes 1310720 | tf_op jit(solution)/shard_map/all_to_all | solution.py:601
  70.2 4.9 %collective-permute-start.12 = (f32[2,32,128]{2,1,0:T(8,128)S(1)}, f32[2,32,128]{2,1,0:T(8,128)S(1)}, u32[]{:S(2)}, u32[]{:S(2)}) collective-permute-start(f32[2,32,128]{2,1,0:T(8,128)S(1)} %get-tuple-element.103.refs_13_), channel_id=1, source_target_pairs={{0,6},{1,7},{2,0},{3,1},{4,2},{5,3},{6,4},{7,5},{8,14},{9,15},{10,... | collective-permute-start | bytes 98312 | tf_op jit(solution)/shard_map/ppermute | solution.py:597
  73.8 4.3 %collective-permute-start.13 = (f32[2,32,128]{2,1,0:T(8,128)S(1)}, f32[2,32,128]{2,1,0:T(8,128)S(1)}, u32[]{:S(2)}, u32[]{:S(2)}) collective-permute-start(f32[2,32,128]{2,1,0:T(8,128)S(1)} %get-tuple-element.103.refs_13_), channel_id=1, source_target_pairs={{0,2},{1,3},{2,4},{3,5},{4,6},{5,7},{6,0},{7,1},{8,10},{9,11},{10,... | collective-permute-start | bytes 98312 | tf_op jit(solution)/shard_map/ppermute | solution.py:597
  73.8 4.4 %collective-permute-start.14 = (f32[2,32,128]{2,1,0:T(8,128)S(1)}, f32[2,32,128]{2,1,0:T(8,128)S(1)}, u32[]{:S(2)}, u32[]{:S(2)}) collective-permute-start(f32[2,32,128]{2,1,0:T(8,128)S(1)} %get-tuple-element.103.refs_13_), channel_id=1, source_target_pairs={{0,4},{1,5},{2,6},{3,7},{4,0},{5,1},{6,2},{7,3},{8,12},{9,13},{10,... | collective-permute-start | bytes 98312 | tf_op jit(solution)/shard_map/ppermute | solution.py:597
  78.2 3.3 %collective-permute-start.15 = (bf16[1024,128]{1,0:T(8,128)(2,1)S(1)}, bf16[1024,128]{1,0:T(8,128)(2,1)S(1)}, u32[]{:S(2)}, u32[]{:S(2)}) collective-permute-start(bf16[1024,128]{1,0:T(8,128)(2,1)S(1)} %collective-permute-done.2.refs_1_), channel_id=1, source_target_pairs={{0,1},{1,0},{2,3},{3,2},{4,5},{5,4},{6,7},{7,6},{8,9},{9,8},{10,11... | collective-permute-start | bytes 786440 | tf_op jit(solution)/shard_map/ppermute | solution.py:597
  80.3 1.5 %collective-permute-start.16 = (bf16[1024,128]{1,0:T(8,128)(2,1)S(1)}, bf16[1024,128]{1,0:T(8,128)(2,1)S(1)}, u32[]{:S(2)}, u32[]{:S(2)}) collective-permute-start(bf16[1024,128]{1,0:T(8,128)(2,1)S(1)} %collective-permute-done.10.refs_8_), channel_id=1, source_target_pairs={{0,1},{1,0},{2,3},{3,2},{4,5},{5,4},{6,7},{7,6},{8,9},{9,8},{10,11... | collective-permute-start | bytes 786440 | tf_op jit(solution)/shard_map/ppermute | solution.py:597
  80.3 2.3 %collective-permute-start.17 = (bf16[1024,128]{1,0:T(8,128)(2,1)S(1)}, bf16[1024,128]{1,0:T(8,128)(2,1)S(1)}, u32[]{:S(2)}, u32[]{:S(2)}) collective-permute-start(bf16[1024,128]{1,0:T(8,128)(2,1)S(1)} %collective-permute-done.11.refs_5_), channel_id=1, source_target_pairs={{0,1},{1,0},{2,3},{3,2},{4,5},{5,4},{6,7},{7,6},{8,9},{9,8},{10,11... | collective-permute-start | bytes 786440 | tf_op jit(solution)/shard_map/ppermute | solution.py:597
  80.8 2.0 %collective-permute-start.18 = (bf16[1024,128]{1,0:T(8,128)(2,1)}, bf16[1024,128]{1,0:T(8,128)(2,1)S(1)}, u32[]{:S(2)}, u32[]{:S(2)}) collective-permute-start(bf16[1024,128]{1,0:T(8,128)(2,1)} %collective-permute-done.9.refs_3_), channel_id=1, source_target_pairs={{0,1},{1,0},{2,3},{3,2},{4,5},{5,4},{6,7},{7,6},{8,9},{9,8},{10,11... | collective-permute-start | bytes 786440 | tf_op jit(solution)/shard_map/ppermute | solution.py:597
  88.3 11.6 %collective-permute-start.20 = (f32[8,32,128]{2,1,0:T(8,128)S(1)}, f32[8,32,128]{2,1,0:T(8,128)S(1)}, u32[]{:S(2)}, u32[]{:S(2)}) collective-permute-start(f32[8,32,128]{2,1,0:T(8,128)S(1)} %get-tuple-element.120), channel_id=1, source_target_pairs={{0,7},{1,6},{2,1},{3,0},{4,3},{5,2},{6,5},{7,4},{8,15},{9,14},{10,... | collective-permute-start | bytes 393224 | tf_op jit(solution)/shard_map/ppermute | solution.py:597
  94.8 7.2 %collective-permute-start.21 = (f32[8,32,128]{2,1,0:T(8,128)S(1)}, f32[8,32,128]{2,1,0:T(8,128)S(1)}, u32[]{:S(2)}, u32[]{:S(2)}) collective-permute-start(f32[8,32,128]{2,1,0:T(8,128)S(1)} %get-tuple-element.119), channel_id=1, source_target_pairs={{0,2},{1,3},{2,4},{3,5},{4,6},{5,7},{6,0},{7,1},{8,10},{9,11},{10,... | collective-permute-start | bytes 393224 | tf_op jit(solution)/shard_map/ppermute | solution.py:597
  94.8 7.2 %collective-permute-start.19 = (f32[32,8,128]{2,1,0:T(8,128)S(1)}, f32[32,8,128]{2,1,0:T(8,128)S(1)}, u32[]{:S(2)}, u32[]{:S(2)}) collective-permute-start(f32[32,8,128]{2,1,0:T(8,128)S(1)} %slice.21), channel_id=1, source_target_pairs={{0,4},{1,5},{2,6},{3,7},{4,1},{5,0},{6,3},{7,2},{8,12},{9,13},{10,... | collective-permute-start | bytes 393224 | tf_op jit(solution)/shard_map/ppermute | solution.py:597
  (1 other events, 1.0 us)
